TPU v7x, 32 devices: a whole 2x2x4 slice. The times are simulated.
32 devices in a mesh: grp: 2 (over x), lat: 2 (over core), lon: 8 (over z, y).
Axes of the slice: x: 2, y: 2, z: 4, core: 2. Of those that a mesh axis runs over, the one named last changes fastest.
Arguments:
- fields: bfloat16 [256, 128, 768], P(('grp', 'lat'), 'lon'), parts along dimension 0, may hold values from -6 to 6
- ocean: int32 [256, 128], P(('grp', 'lat'), 'lon'), parts along dimension 0, may hold values 0 or 1
- w_query1: bfloat16 [768, 768], replicated, may hold values from -4 to 4
- w_key1: bfloat16 [768, 768], replicated, may hold values from -4 to 4
- w_value1: bfloat16 [768, 768], replicated, may hold values from -0.21875 to 0.21875
- w_out1: bfloat16 [768, 768], replicated, may hold values from -0.21875 to 0.21875
- w_query2: bfloat16 [768, 768], replicated, may hold values from -4 to 4
- w_key2: bfloat16 [768, 768], replicated, may hold values from -4 to 4
- w_value2: bfloat16 [768, 768], replicated, may hold values from -0.21875 to 0.21875
- w_out2: bfloat16 [768, 768], replicated, may hold values from -0.21875 to 0.21875
Outputs:
- forecast: bfloat16 [256, 128, 768], P(('grp', 'lat'), 'lon'), parts along dimension 0
There are 2 independent parts, one for each index of `grp`. A program takes and returns all parts, laid end to end along the dimension named above; an argument that names none is the same for every part. Nothing has to cross between parts.
All inputs are finite; a program needn't handle non-finite values. No bound on the sum of `ocean` on one device may be relied on, other than what follows from the above.
Results may differ from a plain program's by a relative error of at most 0.006.
Values may be sent and summed in bfloat16 or wider, within the bound.
No kernel may reach another device: no remote copies, remote signals or barrier semaphores. Data moves between devices by JAX's collectives and lax.ppermute only.
A program may use at most 128 MiB of HBM per device.

v0:
```python
import jax
import jax.numpy as jnp
from jax import lax
from jax.sharding import PartitionSpec as P

HEADS = 12


EPS = 1e-05
NEG = -1e30


def passed_along(value, axis, steps):
    count = lax.axis_size(axis)
    pairs = [(source, (source + steps) % count) for source in range(count)]
    return lax.ppermute(value, axis, pairs)


def norm_rows(a):
    af = a.astype(jnp.float32)
    mean = jnp.mean(af, -1, keepdims=True)
    var = jnp.mean((af - mean) * (af - mean), -1, keepdims=True)
    return ((af - mean) * lax.rsqrt(var + EPS)).astype(jnp.bfloat16)


def project(h, weight):
    return jnp.dot(h, weight, preferred_element_type=jnp.float32).astype(jnp.bfloat16)


def masked_softmax(scores, key_ok, land_query):
    top = jnp.max(jnp.where(key_ok, scores, NEG), -1, keepdims=True)
    expo = jnp.where(key_ok, jnp.exp(scores - top), 0.0)
    total = jnp.sum(expo, -1, keepdims=True) + land_query[..., None]
    return (expo / total).astype(jnp.bfloat16)


def window_attend(query, keys, values, flags):
    rows, cols, width = query.shape
    nh = HEADS
    hd = width // nh
    scale = hd ** (-0.5)

    def tiles(a):
        a = a.reshape(rows // 8, 8, cols // 8, 8, nh, hd).transpose(0, 2, 4, 1, 3, 5)
        return a.reshape(rows // 8, cols // 8, nh, 64, hd)

    marks = (
        flags.reshape(rows // 8, 8, cols // 8, 8)
        .transpose(0, 2, 1, 3)
        .reshape(rows // 8, cols // 8, 64)
    )
    key_ok = (marks > 0)[:, :, None, None, :]
    land_query = (marks <= 0).astype(jnp.float32)[:, :, None, :]
    scores = (
        jnp.einsum(
            "abhqd,abhkd->abhqk", tiles(query), tiles(keys), preferred_element_type=jnp.float32
        )
        * scale
    )
    probs = masked_softmax(scores, key_ok, land_query)
    outs = jnp.einsum(
        "abhqk,abhkd->abhqd", probs, tiles(values), preferred_element_type=jnp.float32
    )
    outs = outs * (1.0 - land_query)[..., None]
    outs = outs.astype(jnp.bfloat16).reshape(rows // 8, cols // 8, nh, 8, 8, hd)
    return outs.transpose(0, 3, 1, 4, 2, 5).reshape(rows, cols, width)


def row_attend(query, keys, values, flags):
    rows, length, width = query.shape
    nh = HEADS
    hd = width // nh
    scale = hd ** (-0.5)
    key_ok = (flags > 0)[:, None, :]
    land_query = (flags <= 0).astype(jnp.float32)

    def head(index):
        qh = lax.dynamic_slice_in_dim(query, index * hd, hd, 2)
        kh = lax.dynamic_slice_in_dim(keys, index * hd, hd, 2)
        vh = lax.dynamic_slice_in_dim(values, index * hd, hd, 2)
        scores = jnp.einsum("rqd,rkd->rqk", qh, kh, preferred_element_type=jnp.float32) * scale
        probs = masked_softmax(scores, key_ok, land_query)
        return jnp.einsum("rqk,rkd->rqd", probs, vh, preferred_element_type=jnp.float32)

    outs = lax.map(head, jnp.arange(nh, dtype=jnp.int32))
    outs = outs.transpose(1, 2, 0, 3).reshape(rows, length, width)
    return (outs * (1.0 - land_query)[..., None]).astype(jnp.bfloat16)


def attend_columns(columns, marks, w_query1, w_key1, w_value1):
    return window_attend(
        project(columns, w_query1), project(columns, w_key1), project(columns, w_value1), marks
    )


def on_device(
    fields, ocean, w_query1, w_key1, w_value1, w_out1, w_query2, w_key2, w_value2, w_out2
):
    rows, cols, width = fields.shape
    normed = norm_rows(fields)
    marks = ocean.astype(jnp.bfloat16)
    edge_feats, edge_marks = passed_along((normed[:, cols - 4 :], marks[:, cols - 4 :]), "lon", 1)
    columns = jnp.concatenate([edge_feats, normed[:, : cols - 4]], 1)
    column_marks = jnp.concatenate([edge_marks, marks[:, : cols - 4]], 1)
    extended = attend_columns(columns, column_marks, w_query1, w_key1, w_value1)
    returned = passed_along(extended[:, :4], "lon", -1)
    o1 = jnp.concatenate([extended[:, 4:], returned], 1)
    y1 = (
        fields.astype(jnp.float32) + jnp.dot(o1, w_out1, preferred_element_type=jnp.float32)
    ).astype(jnp.bfloat16)
    h2 = norm_rows(y1)
    q2 = project(h2, w_query2)
    k2 = project(h2, w_key2)
    v2 = project(h2, w_value2)
    row_q, row_k, row_v, row_marks = (
        lax.all_to_all(q2, "lon", split_axis=0, concat_axis=1, tiled=True),
        lax.all_to_all(k2, "lon", split_axis=0, concat_axis=1, tiled=True),
        lax.all_to_all(v2, "lon", split_axis=0, concat_axis=1, tiled=True),
        lax.all_to_all(marks, "lon", split_axis=0, concat_axis=1, tiled=True),
    )
    row_out = row_attend(row_q, row_k, row_v, row_marks)
    o2 = lax.all_to_all(row_out, "lon", split_axis=1, concat_axis=0, tiled=True)
    return (
        y1.astype(jnp.float32) + jnp.dot(o2, w_out2, preferred_element_type=jnp.float32)
    ).astype(jnp.bfloat16)


def solution(mesh):
    in_specs = (
        P(("grp", "lat"), "lon", None),
        P(("grp", "lat"), "lon"),
        P(),
        P(),
        P(),
        P(),
        P(),
        P(),
        P(),
        P(),
    )
    out_specs = P(("grp", "lat"), "lon", None)
    return jax.shard_map(
        on_device, mesh=mesh, in_specs=in_specs, out_specs=out_specs, check_vma=False
    )
```

profile of v0, /device:TPU:0, one launch (start us, length us, event | category | flops | bytes accessed | tf_op | source)
XLA Modules:
  0.0 330.1 jit_solution(7208995526217545636)
XLA Ops:
  0.0 1.8 convert_reduce_fusion.1
  4.4 3.0 collective-permute-start.1
  7.6 1.5 collective-permute-start
  9.2 10.7 %collective-permute-done = bf16[64,4]{1,0:T(8,128)(2,1)S(1)} collective-permute-done((bf16[64,4]{1,0:T(8,128)(2,1)S(1)}, bf16[64,4]{1,0:T(8,128)(2,1)S(1)}, u32[]{:S(2)}, u32[]{:S(2)}) %collective-permute-start) | collective-permute-done | bytes 544 | tf_op jit(solution)/shard_map/ppermute | solution.py:16
  20.6 4.6 %convolution_convert_fusion.5 = bf16[64,16,768]{2,1,0:T(8,128)(2,1)} fusion(bf16[768,768]{1,0:T(8,128)(2,1)} %param.14, bf16[64,12,768]{2,1,0:T(8,128)(2,1)} %bitcast.111, bf16[64,4,768]{2,1,0:T(4,128)(2,1)} %collective-permute-done.1), kind=kOutput, calls=%fused_computation.66 | convolution fusion | flops 1211891712 | bytes 4325376 | tf_op jit(solution)/shard_map/dot_general | solution.py:27
  25.3 5.9 %reshape.124 = bf16[8,8,2,8,12,64]{5,4,3,2,1,0:T(8,128)(2,1)} reshape(bf16[64,16,768]{2,1,0:T(8,128)(2,1)} %convolution_convert_fusion.5) | data formatting | bytes 3145728 | tf_op jit(solution)/shard_map/reshape | solution.py:44
  31.1 4.7 %convolution_convert_fusion.4 = bf16[64,16,768]{2,1,0:T(8,128)(2,1)} fusion(bf16[768,768]{1,0:T(8,128)(2,1)} %param.15, bf16[64,12,768]{2,1,0:T(8,128)(2,1)} %bitcast.112, bf16[64,4,768]{2,1,0:T(4,128)(2,1)} %collective-permute-done.1), kind=kOutput, calls=%fused_computation.65 | convolution fusion | flops 1211891712 | bytes 4325376 | tf_op jit(solution)/shard_map/dot_general | solution.py:27
  35.8 5.9 %reshape.126 = bf16[8,8,2,8,12,64]{5,4,3,2,1,0:T(8,128)(2,1)} reshape(bf16[64,16,768]{2,1,0:T(8,128)(2,1)} %convolution_convert_fusion.4) | data formatting | bytes 3145728 | tf_op jit(solution)/shard_map/reshape | solution.py:44
  41.7 4.6 %convolution_convert_fusion.3 = bf16[64,16,768]{2,1,0:T(8,128)(2,1)} fusion(bf16[768,768]{1,0:T(8,128)(2,1)} %param.16, bf16[64,12,768]{2,1,0:T(8,128)(2,1)} %bitcast.113, bf16[64,4,768]{2,1,0:T(4,128)(2,1)} %collective-permute-done.1), kind=kOutput, calls=%fused_computation.64 | convolution fusion | flops 1211891712 | bytes 4325376 | tf_op jit(solution)/shard_map/dot_general | solution.py:27
  46.3 5.9 %reshape.128 = bf16[8,8,2,8,12,64]{5,4,3,2,1,0:T(8,128)(2,1)} reshape(bf16[64,16,768]{2,1,0:T(8,128)(2,1)} %convolution_convert_fusion.3) | data formatting | bytes 3145728 | tf_op jit(solution)/shard_map/reshape | solution.py:44
  52.3 5.2 %fusion.42 = f32[8,2,12,64,64]{3,4,2,1,0:T(8,128)S(1)} fusion(bf16[8,2,12,8,8,64]{5,2,4,1,3,0:T(8,128)(2,1)} %bitcast.104, bf16[8,2,12,8,8,64]{5,2,4,1,3,0:T(8,128)(2,1)} %bitcast.103), kind=kOutput, calls=%fused_computation.51 | convolution fusion | flops 100663296 | bytes 6291456 | tf_op jit(solution)/shard_map/abhqd,abhkd->abhqk/dot_general | solution.py:55
  57.5 3.8 %fusion.76 = (f32[8,2,12,64]{3,2,1,0:T(8,128)S(1)}, f32[8,2,12,64,64]{3,4,2,1,0:T(8,128)S(1)}) fusion(f32[8,2,12,64,64]{3,4,2,1,0:T(8,128)S(1)} %fusion.42, pred[8,2,64]{2,1,0:T(4,128)(4,1)S(1)} %reshape.144), kind=kOutput, calls=%fused_computation.98 | output fusion | flops 4718655 | bytes 6341632 | tf_op jit(solution)/shard_map/sub | solution.py:32
  61.3 2.0 fusion.39
  63.4 5.7 %copy.139 = bf16[8,2,12,8,8,64]{5,2,4,1,3,0:T(8,128)(2,1)} copy(bf16[8,2,12,8,8,64]{5,4,3,2,1,0:T(8,128)(2,1)S(1)} %fusion.39) | data formatting | bytes 3145728 | tf_op jit(solution)/shard_map/reshape | solution.py:65
  69.1 6.1 %reshape.131 = bf16[64,16,768]{2,1,0:T(8,128)(2,1)} reshape(bf16[8,8,2,8,12,64]{5,4,3,2,1,0:T(8,128)(2,1)} %bitcast.102) | data formatting | bytes 3145728 | tf_op jit(solution)/shard_map/reshape | solution.py:66
  76.4 1.8 collective-permute-start.2
  78.8 3.3 %all-to-all-start = ((bf16[8,8,16]{2,1,0:T(8,128)(2,1)}), bf16[8,8,16]{2,1,0:T(8,128)(2,1)S(1)}, u32[]{:S(2)}, u32[]{:S(2)}) async-start(bf16[8,8,16]{2,1,0:T(8,128)(2,1)} %convert_bitcast_fusion.1), calls=%async_computation | async-start | bytes 32768 | tf_op jit(solution)/shard_map/all_to_all | solution.py:119
  82.1 2.0 slice.28
  84.2 2.9 collective-permute-done.2
  87.1 2.5 convert_reduce_fusion
  91.5 2.6 convolution_convert_fusion
  94.1 5.5 %all-to-all-start.3 = ((bf16[64,16,768]{2,1,0:T(8,128)(2,1)}), bf16[64,16,768]{2,1,0:T(8,128)(2,1)S(1)}, u32[]{:S(2)}, u32[]{:S(2)}) async-start(bf16[64,16,768]{2,1,0:T(8,128)(2,1)} %convolution_convert_fusion), calls=%async_computation.3 | async-start | bytes 3145728 | tf_op jit(solution)/shard_map/all_to_all | solution.py:118
  99.6 4.3 %convolution_convert_fusion.1 = bf16[64,16,768]{2,1,0:T(8,128)(2,1)} fusion(bf16[768,768]{1,0:T(8,128)(2,1)} %param.19, bf16[64,16,768]{2,1,0:T(8,128)(2,1)} %copy-done.5, f32[64,16]{1,0:T(8,128)S(1)} %add_rsqrt_fusion, f32[64,16]{1,0:T(8,128)S(1)} %broadcast_multiply_fusion), kind=kOutput, calls=%fused_computation.62 | convolution fusion | flops 1211891712 | bytes 4333568 | tf_op jit(solution)/shard_map/dot_general | solution.py:27
  103.9 31.0 %all-to-all-done.3 = bf16[64,16,768]{2,1,0:T(8,128)(2,1)S(1)} async-done(((bf16[64,16,768]{2,1,0:T(8,128)(2,1)}), bf16[64,16,768]{2,1,0:T(8,128)(2,1)S(1)}, u32[]{:S(2)}, u32[]{:S(2)}) %all-to-all-start.3) | async-done | bytes 1572896 | tf_op jit(solution)/shard_map/all_to_all | solution.py:118
  135.0 4.3 %all-to-all-start.2 = ((bf16[64,16,768]{2,1,0:T(8,128)(2,1)}), bf16[64,16,768]{2,1,0:T(8,128)(2,1)}, u32[]{:S(2)}, u32[]{:S(2)}) async-start(bf16[64,16,768]{2,1,0:T(8,128)(2,1)} %convolution_convert_fusion.1), calls=%async_computation.2 | async-start | bytes 3145728 | tf_op jit(solution)/shard_map/all_to_all | solution.py:117
  139.3 4.3 %convolution_convert_fusion.2 = bf16[64,16,768]{2,1,0:T(8,128)(2,1)} fusion(bf16[768,768]{1,0:T(8,128)(2,1)} %param.18, bf16[64,16,768]{2,1,0:T(8,128)(2,1)} %copy-done.5, f32[64,16]{1,0:T(8,128)S(1)} %add_rsqrt_fusion, f32[64,16]{1,0:T(8,128)S(1)} %broadcast_multiply_fusion), kind=kOutput, calls=%fused_computation.63 | convolution fusion | flops 1211891712 | bytes 4333568 | tf_op jit(solution)/shard_map/dot_general | solution.py:27
  143.6 32.1 %all-to-all-done.2 = bf16[64,16,768]{2,1,0:T(8,128)(2,1)} async-done(((bf16[64,16,768]{2,1,0:T(8,128)(2,1)}), bf16[64,16,768]{2,1,0:T(8,128)(2,1)}, u32[]{:S(2)}, u32[]{:S(2)}) %all-to-all-start.2) | async-done | bytes 1572896 | tf_op jit(solution)/shard_map/all_to_all | solution.py:117
  175.7 4.3 %all-to-all-start.1 = ((bf16[64,16,768]{2,1,0:T(8,128)(2,1)}), bf16[64,16,768]{2,1,0:T(8,128)(2,1)}, u32[]{:S(2)}, u32[]{:S(2)}) async-start(bf16[64,16,768]{2,1,0:T(8,128)(2,1)} %convolution_convert_fusion.2), calls=%async_computation.1 | async-start | bytes 3145728 | tf_op jit(solution)/shard_map/all_to_all | solution.py:116
  180.2 1.3 copy.104
  181.6 2.6 copy.107
  184.1 1.5 copy.102
  185.7 1.6 copy.106
  187.3 29.3 %all-to-all-done.1 = bf16[64,16,768]{2,1,0:T(8,128)(2,1)} async-done(((bf16[64,16,768]{2,1,0:T(8,128)(2,1)}), bf16[64,16,768]{2,1,0:T(8,128)(2,1)}, u32[]{:S(2)}, u32[]{:S(2)}) %all-to-all-start.1) | async-done | bytes 1572896 | tf_op jit(solution)/shard_map/all_to_all | solution.py:116
  216.6 1.5 copy.101
  218.2 1.6 copy.105
  219.7 60.0 %while.10 = (s32[]{:T(128)}, f32[12,8,128,64]{2,3,0,1:T(8,128)}, pred[8,1,128]{2,0,1:T(8,128)(4,1)S(1)}, s32[12]{0:T(128)S(1)}, bf16[8,128,768]{1,2,0:T(8,128)(2...) while((s32[]{:T(128)}, f32[12,8,128,64]{2,3,0,1:T(8,128)}, ...), condition=%wide.region_9.10_spmd, body=%wide.region_6.9_spmd.sunk | while | flops 34867460 | bytes 2777779 | solution.py:85
  221.0 1.3 convolution_multiply_fusion.2
  222.6 2.1 fusion.89
  226.0 1.3 convolution_multiply_fusion.2
  227.6 2.1 fusion.89
  231.0 1.3 convolution_multiply_fusion.2
  232.7 2.1 fusion.89
  236.0 1.3 convolution_multiply_fusion.2
  237.7 2.1 fusion.89
  241.0 1.3 convolution_multiply_fusion.2
  242.7 2.1 fusion.89
  246.0 1.3 convolution_multiply_fusion.2
  247.7 2.1 fusion.89
  251.0 1.3 convolution_multiply_fusion.2
  252.7 2.1 fusion.89
  256.0 1.3 convolution_multiply_fusion.2
  257.7 2.1 fusion.89
  261.0 1.3 convolution_multiply_fusion.2
  262.7 2.1 fusion.89
  266.0 1.3 convolution_multiply_fusion.2
  267.7 2.1 fusion.89
  271.0 1.3 convolution_multiply_fusion.2
  272.7 2.1 fusion.89
  276.1 1.3 convolution_multiply_fusion.2
  277.7 2.1 fusion.89
  279.8 3.3 fusion.40
  283.1 2.2 copy.109
  285.3 40.6 %all_to_all.85 = bf16[8,128,768]{2,0,1:T(8,128)(2,1)S(1)} all-to-all(bf16[8,128,768]{2,0,1:T(8,128)(2,1)S(1)} %copy.109), channel_id=1, replica_groups=mesh['grp'=2,'lat'=2,'lon'=8] {'lon'}, dimensions={1} | all-to-all | bytes 3145728 | tf_op jit(solution)/shard_map/all_to_all | solution.py:122
  327.6 2.5 fusion.37
  (93 shorter events, 20.9 us)
Async XLA Ops:
  0.0 87.1 %copy-start = (bf16[768,768]{1,0:T(8,128)(2,1)S(1)}, bf16[768,768]{1,0:T(8,128)(2,1)}, u32[]{:S(2)}) copy-start(bf16[768,768]{1,0:T(8,128)(2,1)} %param.17) | copy-start | bytes 3538948
  0.0 2.0 copy-start.2
  2.6 4.8 %copy-start.7 = (s32[64,16]{0,1:T(8,128)S(1)}, s32[64,16]{0,1:T(8,128)}, u32[]{:S(2)}) copy-start(s32[64,16]{0,1:T(8,128)} %param.13) | copy-start | bytes 12292
  3.0 1.1 copy-start.4
  4.4 16.2 %collective-permute-start.1 = (bf16[64,4,768]{2,1,0:T(4,128)(2,1)S(1)}, bf16[64,4,768]{2,1,0:T(4,128)(2,1)}, u32[]{:S(2)}, u32[]{:S(2)}) collective-permute-start(bf16[64,4,768]{2,1,0:T(4,128)(2,1)S(1)} %slice.26), channel_id=1, source_target_pairs={{0,1},{1,2},{2,3},{3,4},{4,5},{5,6},{6,7},{7,0},{8,9},{9,10},{10,1... | collective-permute-start | bytes 1179656 | tf_op jit(solution)/shard_map/ppermute | solution.py:16
  7.6 12.3 %collective-permute-start = (bf16[64,4]{1,0:T(8,128)(2,1)S(1)}, bf16[64,4]{1,0:T(8,128)(2,1)S(1)}, u32[]{:S(2)}, u32[]{:S(2)}) collective-permute-start(bf16[64,4]{1,0:T(8,128)(2,1)S(1)} %slice.24), channel_id=1, source_target_pairs={{0,1},{1,2},{2,3},{3,4},{4,5},{5,6},{6,7},{7,0},{8,9},{9,10},{10,1... | collective-permute-start | bytes 1544 | tf_op jit(solution)/shard_map/ppermute | solution.py:16
  57.5 3.8 %copy-start.3 = (bf16[8,8,2,8,12,64]{5,4,3,2,1,0:T(8,128)(2,1)S(1)}, bf16[8,8,2,8,12,64]{5,4,3,2,1,0:T(8,128)(2,1)}, u32[]{:S(2)}) copy-start(bf16[8,8,2,8,12,64]{5,4,3,2,1,0:T(8,128)(2,1)} %reshape.128) | copy-start | bytes 4718596
  76.4 10.7 %collective-permute-start.2 = (bf16[64,4,768]{2,1,0:T(4,128)(2,1)S(1)}, bf16[64,4,768]{2,1,0:T(4,128)(2,1)}, u32[]{:S(2)}, u32[]{:S(2)}) collective-permute-start(bf16[64,4,768]{2,1,0:T(4,128)(2,1)S(1)} %slice.29), channel_id=1, source_target_pairs={{0,7},{1,0},{2,1},{3,2},{4,3},{5,4},{6,5},{7,6},{8,15},{9,8},{10,9... | collective-permute-start | bytes 1179656 | tf_op jit(solution)/shard_map/ppermute | solution.py:16
  78.8 15.3 %all-to-all-start = ((bf16[8,8,16]{2,1,0:T(8,128)(2,1)}), bf16[8,8,16]{2,1,0:T(8,128)(2,1)S(1)}, u32[]{:S(2)}, u32[]{:S(2)}) async-start(bf16[8,8,16]{2,1,0:T(8,128)(2,1)} %convert_bitcast_fusion.1), calls=%async_computation | async-start | bytes 32768 | tf_op jit(solution)/shard_map/all_to_all | solution.py:119
  89.6 1.1 copy-start.5
  89.6 1.8 copy-start.8
  94.1 40.9 %all-to-all-start.3 = ((bf16[64,16,768]{2,1,0:T(8,128)(2,1)}), bf16[64,16,768]{2,1,0:T(8,128)(2,1)S(1)}, u32[]{:S(2)}, u32[]{:S(2)}) async-start(bf16[64,16,768]{2,1,0:T(8,128)(2,1)} %convolution_convert_fusion), calls=%async_computation.3 | async-start | bytes 3145728 | tf_op jit(solution)/shard_map/all_to_all | solution.py:118
  135.0 40.7 %all-to-all-start.2 = ((bf16[64,16,768]{2,1,0:T(8,128)(2,1)}), bf16[64,16,768]{2,1,0:T(8,128)(2,1)}, u32[]{:S(2)}, u32[]{:S(2)}) async-start(bf16[64,16,768]{2,1,0:T(8,128)(2,1)} %convolution_convert_fusion.1), calls=%async_computation.2 | async-start | bytes 3145728 | tf_op jit(solution)/shard_map/all_to_all | solution.py:117
  175.7 40.9 %all-to-all-start.1 = ((bf16[64,16,768]{2,1,0:T(8,128)(2,1)}), bf16[64,16,768]{2,1,0:T(8,128)(2,1)}, u32[]{:S(2)}, u32[]{:S(2)}) async-start(bf16[64,16,768]{2,1,0:T(8,128)(2,1)} %convolution_convert_fusion.2), calls=%async_computation.1 | async-start | bytes 3145728 | tf_op jit(solution)/shard_map/all_to_all | solution.py:116
  325.8 1.4 copy-start.6
  325.8 1.7 copy-start.9
  327.6 2.6 copy-start.1
where the time goes:
time: 332 us; the launch traced here: 330 us
  waiting for transfers between devices  106 us (32%)
  matrix products  78 us (23%)
  local copies, waits for them, and re-layouts  58.3 us (18%)
  blocking collectives  40.6 us (12%)
  starting transfers between devices  23.7 us (7%)
  other arithmetic  15.4 us (5%)
  loops' own time  7.79 us (2%)
    all_to_all x1, blocking collectives, on_device(): o2 = lax.all_to_all(row_out, 'lon', split_axis=1, concat_axis=0, tiled=True)  40.6 us
    all_to_all x1, waiting for transfers between devices, on_device(): lax.all_to_all(k2, 'lon', split_axis=0, concat_axis=1, tiled=True)  32.1 us
    all_to_all x1, waiting for transfers between devices, on_device(): lax.all_to_all(v2, 'lon', split_axis=0, concat_axis=1, tiled=True)  31 us
    all_to_all x1, waiting for transfers between devices, on_device(): lax.all_to_all(q2, 'lon', split_axis=0, concat_axis=1, tiled=True)  29.3 us
    dot_general x12, matrix products, head(): jnp.einsum('rqk,rkd->rqd', probs, vh, preferred_element_type=jnp.float32)  25.3 us
    dot_general x6, matrix products, project(): jnp.dot(h, weight, preferred_element_type=jnp.float32).astype(jnp.bfloat16)  25.2 us
    reshape x3, local copies, waits for them, and re-layouts, tiles(): a.reshape(rows // 8, 8, cols // 8, 8, nh, hd).transpose(0, 2, 4, 1, 3, 5)  17.7 us
    dot_general x12, matrix products, head(): jnp.einsum('rqd,rkd->rqk', qh, kh, preferred_element_type=jnp.float32)  15.1 us
  transfers between devices with their start and end apart: 7, of which 5 were waited for; matrix products, arithmetic and copies ran while one was open for 8% of the time, Pallas kernels for 0%

commit v1 on v0

--- a/solution.py
+++ b/solution.py
@@ -1,6 +1,10 @@
+import functools
+
 import jax
 import jax.numpy as jnp
 from jax import lax
+from jax.experimental import pallas as pl
+from jax.experimental.pallas import tpu as pltpu
 from jax.sharding import PartitionSpec as P
 
 HEADS = 12
@@ -8,6 +12,8 @@
 
 EPS = 1e-05
 NEG = -1e30
+
+GROUPS = (4, 4)
 
 
 def passed_along(value, axis, steps):
@@ -93,7 +99,7 @@
     )
 
 
-def on_device(
+def spread_rows(
     fields, ocean, w_query1, w_key1, w_value1, w_out1, w_query2, w_key2, w_value2, w_out2
 ):
     rows, cols, width = fields.shape
@@ -125,6 +131,211 @@
     ).astype(jnp.bfloat16)
 
 
+def normed_f32(a):
+    mean = jnp.mean(a, -1, keepdims=True)
+    centred = a - mean
+    var = jnp.mean(centred * centred, -1, keepdims=True)
+    return (centred * lax.rsqrt(var + EPS)).astype(jnp.bfloat16)
+
+
+def dot_f32(a, b):
+    return jnp.dot(a, b, preferred_element_type=jnp.float32)
+
+
+def pair_attend(q, k, v, key_bias, land_query):
+    n = q.shape[0]
+    low = lax.broadcasted_iota(jnp.int32, (n, 128), 1) < 64
+    zero = jnp.zeros_like(q)
+    both = jnp.concatenate([jnp.where(low, q, zero), jnp.where(low, zero, q)], 0)
+    scores = lax.dot_general(both, k, (((1,), (1,)), ((), ())), preferred_element_type=jnp.float32)
+    scores = scores + key_bias
+    top = jnp.max(scores, -1, keepdims=True)
+    expo = jnp.exp(scores - top).astype(jnp.bfloat16)
+    wide = jnp.concatenate([v, jnp.ones_like(v)], 1)
+    sums = dot_f32(expo, wide)
+    upper = jnp.where(low, sums[:n, :128], sums[n:, :128])
+    total = jnp.where(low, sums[:n, 128:], sums[n:, 128:]) + land_query
+    return (upper / total * (1.0 - land_query)).astype(jnp.bfloat16)
+
+
+def window_kernel(straddling, count, x_ref, bias_ref, land_ref, wq, wk, wv, wo, wq2, wk2, wv2,
+                  y_ref, q2_ref, k2_ref, v2_ref, held, q_s, k_s, v_s, o_s, rows_s, sems):
+    width = x_ref.shape[-1]
+    scale = (width // HEADS) ** (-0.5)
+    copies = [
+        pltpu.make_async_copy(source, held.at[i], sems.at[i])
+        for i, source in enumerate((wq, wk, wv, wo, wq2, wk2, wv2))
+    ]
+    for copy in copies:
+        copy.start()
+    x = x_ref[...].astype(jnp.float32)
+    if straddling:
+        column = lax.broadcasted_iota(jnp.int32, x.shape, 0) % 8
+        x = jnp.where(column < 4, x, jnp.concatenate([x[64:], x[:64]], 0))
+    h = normed_f32(x)
+    copies[0].wait()
+    q_s[...] = (dot_f32(h, held[0]) * scale).astype(jnp.bfloat16)
+    copies[1].wait()
+    k_s[...] = dot_f32(h, held[1]).astype(jnp.bfloat16)
+    copies[2].wait()
+    v_s[...] = dot_f32(h, held[2]).astype(jnp.bfloat16)
+    for w in range(count):
+        here = slice(64 * w, 64 * w + 64)
+        for p in range(HEADS // 2):
+            lanes = slice(128 * p, 128 * p + 128)
+            o_s[here, lanes] = pair_attend(
+                q_s[here, lanes], k_s[here, lanes], v_s[here, lanes],
+                bias_ref[w : w + 1, :], land_ref[here, :],
+            )
+    copies[3].wait()
+    y = (x + dot_f32(o_s[...], held[3])).astype(jnp.bfloat16).astype(jnp.float32)
+    for w in range(count):
+        for r in range(8):
+            at = 64 * w + 8 * r
+            rows_s[r, 8 * w : 8 * w + 8, :] = y[at : at + 8]
+    y = rows_s[...].reshape(8 * 8 * count, width)
+    y_ref[...] = y.astype(jnp.bfloat16).reshape(y_ref.shape)
+    h = normed_f32(y)
+    copies[4].wait()
+    q2_ref[...] = (dot_f32(h, held[4]) * scale).astype(jnp.bfloat16).reshape(q2_ref.shape)
+    copies[5].wait()
+    k2_ref[...] = dot_f32(h, held[5]).astype(jnp.bfloat16).reshape(k2_ref.shape)
+    copies[6].wait()
+    v2_ref[...] = dot_f32(h, held[6]).astype(jnp.bfloat16).reshape(v2_ref.shape)
+
+
+def window_layer(straddling, x, bias, land, weights):
+    count, width = bias.shape[0], x.shape[-1]
+    tokens = 64 * count
+    half = jax.ShapeDtypeStruct((8, 8 * count, width), jnp.bfloat16)
+    vmem = pl.BlockSpec(memory_space=pltpu.VMEM)
+    anywhere = pl.BlockSpec(memory_space=pl.ANY)
+    work = pltpu.VMEM((tokens, width), jnp.bfloat16)
+    return pl.pallas_call(
+        functools.partial(window_kernel, straddling, count),
+        out_shape=(half,) * 4,
+        in_specs=[vmem] * 3 + [anywhere] * 7,
+        out_specs=(vmem,) * 4,
+        scratch_shapes=[
+            pltpu.VMEM((7, width, width), jnp.bfloat16),
+            work, work, work, work,
+            pltpu.VMEM((8, 8 * count, width), jnp.float32),
+            pltpu.SemaphoreType.DMA((7,)),
+        ],
+        compiler_params=pltpu.CompilerParams(vmem_limit_bytes=40 * 1024 * 1024),
+        cost_estimate=pl.CostEstimate(
+            flops=2 * tokens * width * (7 * width + 512), bytes_accessed=16 << 20, transcendentals=tokens * 64 * HEADS
+        ),
+        name="window_layer",
+    )(x, bias, land, *weights)
+
+
+def row_kernel(rows, count, ya, yb, qa, qb, ka, kb, va, vb, bias_ref, land_ref, wo, out_ref, held, o_s, sem):
+    width = ya.shape[-1]
+    length = 16 * count
+    copy = pltpu.make_async_copy(wo, held, sem)
+    copy.start()
+    for r in range(rows):
+        here = slice(length * r, length * r + length)
+        for p in range(HEADS // 2):
+            lanes = slice(128 * p, 128 * p + 128)
+            q = jnp.concatenate([qa[r, :, lanes], qb[r, :, lanes]], 0)
+            k = jnp.concatenate([ka[r, :, lanes], kb[r, :, lanes]], 0)
+            v = jnp.concatenate([va[r, :, lanes], vb[r, :, lanes]], 0)
+            o_s[here, lanes] = pair_attend(q, k, v, bias_ref[r : r + 1, :], land_ref[here, :])
+    copy.wait()
+    added = dot_f32(o_s[...], held[...])
+    for r in range(rows):
+        at = length * r
+        fa = added[at : at + 8 * count] + ya[r].astype(jnp.float32)
+        fb = added[at + 8 * count : at + length] + yb[r].astype(jnp.float32)
+        column = lax.broadcasted_iota(jnp.int32, (8, width), 0)
+        for d in range(count):
+            before = (d + count - 1) % count
+            a = fa[8 * d : 8 * d + 8]
+            first = jnp.where(column < 4, a, fb[8 * before : 8 * before + 8])
+            last = jnp.where(column < 4, fb[8 * d : 8 * d + 8], a)
+            out_ref[d, r] = jnp.concatenate(
+                [pltpu.roll(first, 4, 0), pltpu.roll(last, 4, 0)], 0
+            ).astype(jnp.bfloat16)
+
+
+def row_layer(start, rows, count, halves, bias, land, w_out):
+    ya = halves[0]
+    width = ya.shape[-1]
+    length = 16 * count
+    vmem = pl.BlockSpec(memory_space=pltpu.VMEM)
+    anywhere = pl.BlockSpec(memory_space=pl.ANY)
+    step = start // rows
+    half = pl.BlockSpec((rows, 8 * count, width), lambda i: (step, 0, 0))
+    return pl.pallas_call(
+        functools.partial(row_kernel, rows, count),
+        out_shape=jax.ShapeDtypeStruct((count, rows, 16, width), jnp.bfloat16),
+        grid=(1,),
+        in_specs=[half] * 8 + [
+            pl.BlockSpec((rows, length), lambda i: (0, 0)),
+            pl.BlockSpec((rows * length, 1), lambda i: (0, 0)),
+            anywhere,
+        ],
+        out_specs=pl.BlockSpec((count, rows, 16, width), lambda i: (0, 0, 0, 0)),
+        scratch_shapes=[
+            pltpu.VMEM((width, width), jnp.bfloat16),
+            pltpu.VMEM((rows * length, width), jnp.bfloat16),
+            pltpu.SemaphoreType.DMA,
+        ],
+        compiler_params=pltpu.CompilerParams(vmem_limit_bytes=40 * 1024 * 1024),
+        cost_estimate=pl.CostEstimate(
+            flops=2 * rows * length * width * (width + 1024), bytes_accessed=8 << 20,
+            transcendentals=rows * length * length * HEADS,
+        ),
+        name="row_layer",
+    )(*halves, bias[start : start + rows], land[start * length : (start + rows) * length], w_out)
+
+
+def gathered_bands(
+    fields, ocean, w_query1, w_key1, w_value1, w_out1, w_query2, w_key2, w_value2, w_out2
+):
+    count = lax.axis_size("lon")
+    me = lax.axis_index("lon")
+
+    def regroup(a):
+        return lax.all_to_all(a, "lon", split_axis=0, concat_axis=0, tiled=True)
+
+    marks = lax.all_gather(ocean, "lon", axis=1, tiled=True)
+    rows, cols, width = fields.shape
+    first = regroup(fields[:, 4:12])
+    second = regroup(jnp.concatenate([fields[:, 12:], fields[:, :4]], 1))
+
+    band = lax.dynamic_slice_in_dim(marks, 8 * me, 8, 0)
+    band = jnp.roll(band, -4, 1).reshape(8, count, 2, 8)
+    land = (band <= 0).astype(jnp.float32)
+    by_window = land.transpose(2, 1, 0, 3).reshape(2, count, 64)
+    by_row = land.transpose(0, 2, 1, 3).reshape(8, 16 * count)
+
+    weights = (w_query1, w_key1, w_value1, w_out1, w_query2, w_key2, w_value2)
+    halves = [
+        window_layer(
+            i == 1, x.reshape(64 * count, width), by_window[i] * NEG, by_window[i].reshape(64 * count, 1), weights
+        )
+        for i, x in enumerate((first, second))
+    ]
+    joined = [half for pair in zip(*halves) for half in pair]
+    parts, start = [], 0
+    for size in GROUPS:
+        sent = row_layer(start, size, count, joined, by_row * NEG, by_row.reshape(8 * 16 * count, 1), w_out2)
+        back = regroup(sent.reshape(count * size, cols, width))
+        parts.append(back.reshape(count, size, cols, width))
+        start += size
+    return jnp.concatenate(parts, 1).reshape(rows, cols, width)
+
+
+def on_device(fields, *rest):
+    rows, cols, width = fields.shape
+    if rows == 8 * lax.axis_size("lon") and cols == 16 and width == 64 * HEADS:
+        return gathered_bands(fields, *rest)
+    return spread_rows(fields, *rest)
+
+
 def solution(mesh):
     in_specs = (
         P(("grp", "lat"), "lon", None),

time: 332 us -> 162 us (0.49)
  waiting for transfers between devices: 106 us -> 0.01 us
  matrix products: 78 us -> 0 us
  Pallas kernels: 0 us -> 42.8 us
  local copies, waits for them, and re-layouts: 58.3 us -> 37 us
  blocking collectives: 40.6 us -> 59.4 us
  other arithmetic: 15.4 us -> 3.8 us
  loops' own time: 7.79 us -> 0 us
  starting transfers between devices: 23.7 us -> 17.5 us
    all_to_all x4 -> x3, waiting for transfers between devices: 92.4 us -> 0.01 us  [regroup(): return lax.all_to_all(a, 'lon', split_axis=0, concat_axis=0, tiled=True)]
    dot_general x34 -> x0, matrix products: 78 us -> none  [the longest x12 25.3 us: head(): jnp.einsum('rqk,rkd->rqd', probs, vh, preferred_element_type=jnp.float32)]
    pallas_call x0 -> x4, Pallas kernels: none -> 42.8 us  [the longest x2 33 us: window_layer(): pl.pallas_call(functools.partial(window_kernel, straddling, count), out_s...]
    all_gather x0 -> x1, blocking collectives: none -> 40.3 us  [gathered_bands(): marks = lax.all_gather(ocean, 'lon', axis=1, tiled=True)]
    reshape x5 -> x0, local copies, waits for them, and re-layouts: 29.5 us -> none  [the longest x3 17.7 us: tiles(): a.reshape(rows // 8, 8, cols // 8, 8, nh, hd).transpose(0, 2, 4, 1, 3, 5)]
    unnamed x21 -> x66, local copies, waits for them, and re-layouts: 4.03 us -> 28 us
    all_to_all x1, blocking collectives: 40.6 us -> 19.1 us  [regroup(): return lax.all_to_all(a, 'lon', split_axis=0, concat_axis=0, tiled=True)]
    ppermute x3 -> x0, waiting for transfers between devices: 13.7 us -> none  [passed_along(): return lax.ppermute(value, axis, pairs)]
  transfers between devices with their start and end apart: 7 -> 3, of which waited for: 5 -> 0; matrix products, arithmetic and copies ran while one was open for 8% -> 5% of each run, Pallas kernels for 0% -> 13%
where the time goes in v1:
time: 162 us; the launch traced here: 161 us
  blocking collectives  59.4 us (37%)
  Pallas kernels  42.8 us (26%)
  local copies, waits for them, and re-layouts  37 us (23%)
  starting transfers between devices  17.5 us (11%)
  other arithmetic  3.8 us (2%)
    all_gather x1, blocking collectives, gathered_bands(): marks = lax.all_gather(ocean, 'lon', axis=1, tiled=True)  40.3 us
    pallas_call x2, Pallas kernels, window_layer(): pl.pallas_call(functools.partial(window_kernel, straddling, count), out_s...  33 us
    unnamed x66, local copies, waits for them, and re-layouts  28 us
    all_to_all x1, blocking collectives, regroup(): return lax.all_to_all(a, 'lon', split_axis=0, concat_axis=0, tiled=True)  19.1 us
    all_to_all x3, starting transfers between devices, regroup(): return lax.all_to_all(a, 'lon', split_axis=0, concat_axis=0, tiled=True)  17.5 us
    pallas_call x2, Pallas kernels, row_layer(): pl.pallas_call(functools.partial(row_kernel, rows, count), out_shape=jax....  9.75 us
  transfers between devices with their start and end apart: 3, of which 0 were waited for; matrix products, arithmetic and copies ran while one was open for 5% of the time, Pallas kernels for 13%

profile of v1, /device:TPU:0, one launch (start us, length us, event | category | flops | bytes accessed | tf_op | source)
XLA Modules:
  0.0 160.8 jit_solution(5428797375380764290)
XLA Ops:
  0.0 1.7 %fusion.1 = (bf16[64,4,768]{2,1,0:T(4,128)(2,1)S(1)}, bf16[64,4,768]{2,1,0:T(4,128)(2,1)S(1)}) fusion(bf16[64,16,768]{2,1,0:T(8,128)(2,1)} %param.10), kind=kLoop, calls=%fused_computation.10 | loop fusion | bytes 1572864 | tf_op jit(solution)/shard_map/slice | solution.py:307
  1.7 0.0 copy-start.31
  1.7 1.3 pad_maximum_fusion.1
  3.0 7.4 %all-to-all-start.1 = ((bf16[64,8,768]{2,1,0:T(8,128)(2,1)}), bf16[64,8,768]{2,1,0:T(8,128)(2,1)S(1)}, u32[]{:S(2)}, u32[]{:S(2)}) async-start(bf16[64,8,768]{2,1,0:T(8,128)(2,1)} %pad_maximum_fusion.1), calls=%async_computation.1 | async-start | bytes 1572864 | tf_op jit(solution)/shard_map/all_to_all | solution.py:302
  10.4 0.0 copy-done.31
  10.4 1.1 slice.51
  11.5 40.3 %all_gather.3 = s32[64,128]{0,1:T(8,128)S(1)} all-gather(s32[64,16]{0,1:T(8,128)S(1)} %copy-done.32), channel_id=1, replica_groups=mesh['grp'=2,'lat'=2,'lon'=8] {'lon'}, dimensions={1}, use_global_device_ids=true | all-gather | bytes 36864 | tf_op jit(solution)/shard_map/all_gather | solution.py:304
  51.8 0.1 dynamic-slice
  51.9 0.1 copy.26
  52.0 0.1 constant_dynamic-slice_fusion
  52.0 0.1 copy.27
  52.1 0.0 all-to-all-done.1
  52.1 4.2 %all-to-all-start = ((bf16[64,8,768]{2,1,0:T(8,128)(2,1)}), bf16[64,8,768]{2,1,0:T(8,128)(2,1)}, u32[]{:S(2)}, u32[]{:S(2)}) async-start(bf16[64,8,768]{2,1,0:T(8,128)(2,1)} %slice.51), calls=%async_computation | async-start | bytes 1572864 | tf_op jit(solution)/shard_map/all_to_all | solution.py:302
  56.4 0.1 fusion
  56.4 0.1 reshape.51
  56.6 0.6 fusion.3
  57.3 0.1 slice.63.bias_ref
  57.4 0.1 mul.16.bias_ref
  57.5 0.1 mul.18.bias_ref
  57.5 0.1 reshape_squeeze.9.land_ref
  57.7 0.8 reshape_squeeze.8.land_ref
  58.5 0.6 fusion.2
  59.1 0.8 slice.67.land_ref
  59.9 1.3 copy-done.17
  61.2 1.3 copy-done.19
  62.5 1.3 copy-done.21
  63.8 1.3 copy-done.23
  65.0 1.3 copy-done.25
  66.3 1.3 copy-done.27
  67.6 1.3 copy-done.29
  68.8 15.8 %window_layer.3 = (bf16[8,64,768]{2,1,0:T(8,128)(2,1)S(1)}, bf16[8,64,768]{2,1,0:T(8,128)(2,1)S(1)}, bf16[8,64,768]{2,1,0:T(8,128)(2,1)S(1)}, bf16[8,64,768]{2,1,0:T(8,128)(2,1)S(1)}) custom-call(bf16[512,768]{1,0:T(8,128)(2,1)S(1)} %bitcast.33, f32[8,64]{1,0:T(8,128)S(1)} %mul.18.bias_ref, f32[512,1]{1,0:T(8,128)S(1)} %reshape_squeeze.9.land_ref, ...), custom_call_target="tpu_custom_call" | custom-call | flops 4630511616 | bytes 16777216 | tf_op jit(solution)/shard_map/window_layer/pallas_call | solution.py:214
  84.7 0.0 copy-start.1
  84.7 0.9 copy-done.1
  85.6 0.0 all-to-all-done
  85.6 0.9 copy-done.16
  86.5 1.3 copy-done.18
  87.8 1.3 copy-done.20
  89.1 1.3 copy-done.22
  90.3 1.3 copy-done.24
  91.6 1.3 copy-done.26
  92.9 1.3 copy-done.28
  94.2 1.3 copy-done.30
  95.4 17.2 %window_layer.2 = (bf16[8,64,768]{2,1,0:T(8,128)(2,1)S(1)}, bf16[8,64,768]{2,1,0:T(8,128)(2,1)S(1)}, bf16[8,64,768]{2,1,0:T(8,128)(2,1)S(1)}, bf16[8,64,768]{2,1,0:T(8,128)(2,1)S(1)}) custom-call(bf16[512,768]{1,0:T(8,128)(2,1)} %bitcast.x_ref, f32[8,64]{1,0:T(8,128)S(1)} %mul.16.bias_ref, f32[512,1]{1,0:T(8,128)S(1)} %copy-done.16, ...), custom_call_target="tpu_custom_call" | custom-call | flops 4630511616 | bytes 16777216 | tf_op jit(solution)/shard_map/window_layer/pallas_call | solution.py:214
  112.6 0.0 copy-start.4
  112.6 0.0 copy-start.6
  112.6 0.0 copy-start.8
  112.6 0.0 copy-start.10
  112.7 5.0 %row_layer.3 = bf16[8,4,16,768]{3,2,1,0:T(8,128)(2,1)S(1)} custom-call(bf16[8,64,768]{2,1,0:T(8,128)(2,1)S(1)} %get-tuple-element.13.ya, bf16[8,64,768]{2,1,0:T(8,128)(2,1)S(1)} %get-tuple-element.14.yb, bf16[8,64,768]{2,1,0:T(8,128)(2,1)S(1)} %get-tuple-element.15.qa, bf16[8,64,768]{2,1,0:T(8,128)(2,1)S(1)} %get-tuple-element.16.qb, ...), custom_call_target="tpu_custom_call" | custom-call | flops 1409286144 | bytes 8388608 | tf_op jit(solution)/shard_map/row_layer/pallas_call | solution.py:271
  117.7 0.0 copy-start.12
  117.7 0.9 copy-done.12
  118.6 5.9 %all-to-all-start.3 = ((bf16[32,16,768]{2,1,0:T(8,128)(2,1)}), bf16[32,16,768]{2,1,0:T(8,128)(2,1)}, u32[]{:S(2)}, u32[]{:S(2)}) async-start(bf16[32,16,768]{2,1,0:T(8,128)(2,1)} %bitcast.31), calls=%async_computation.3 | async-start | bytes 1572864 | tf_op jit(solution)/shard_map/all_to_all | solution.py:302
  124.5 0.8 slice.59.bias_ref
  125.4 1.6 slice.66.land_ref
  127.0 1.1 copy-done.3
  128.1 1.1 copy-done.5
  129.2 1.1 copy-done.7
  130.4 1.1 copy-done.9
  131.5 1.1 copy-done.11
  132.6 0.9 copy-done.15
  133.6 4.8 %row_layer.2 = bf16[8,4,16,768]{3,2,1,0:T(8,128)(2,1)S(1)} custom-call(bf16[8,64,768]{2,1,0:T(8,128)(2,1)S(1)} %copy-done.5, bf16[8,64,768]{2,1,0:T(8,128)(2,1)S(1)} %get-tuple-element.14.yb, bf16[8,64,768]{2,1,0:T(8,128)(2,1)S(1)} %copy-done.7, bf16[8,64,768]{2,1,0:T(8,128)(2,1)S(1)} %get-tuple-element.16.qb, bf16[8,64,768]{2,1,0:T(8,128)(2,1)S(1)} %copy-done.9, ...), custom_call_target="tpu_custom_call" | custom-call | flops 1409286144 | bytes 8388608 | tf_op jit(solution)/shard_map/row_layer/pallas_call | solution.py:271
  138.4 0.9 copy-done.13
  139.2 0.0 all-to-all-done.3
  139.2 19.1 %all_to_all.20 = bf16[32,16,768]{2,1,0:T(8,128)(2,1)S(1)} all-to-all(bf16[32,16,768]{2,1,0:T(8,128)(2,1)} %bitcast.32), channel_id=1, replica_groups=mesh['grp'=2,'lat'=2,'lon'=8] {'lon'}, dimensions={0} | all-to-all | bytes 1572864 | tf_op jit(solution)/shard_map/all_to_all | solution.py:302
  158.4 2.4 %pad_maximum_fusion = bf16[8,8,16,768]{3,2,1,0:T(8,128)(2,1)} fusion(bf16[8,4,16,768]{3,2,1,0:T(8,128)(2,1)} %bitcast.7, bf16[8,4,16,768]{3,2,1,0:T(8,128)(2,1)S(1)} %bitcast.34), kind=kLoop, calls=%fused_computation | loop fusion | flops 786432 | bytes 3145728 | tf_op jit(solution)/shard_map/concatenate | solution.py:329
  (38 shorter events, 0.1 us)
Async XLA Ops:
  1.7 8.7 %copy-start.31 = (bf16[64,16,768]{2,1,0:T(8,128)(2,1)S(1)}, bf16[64,16,768]{2,1,0:T(8,128)(2,1)}, u32[]{:S(2)}) copy-start(bf16[64,16,768]{2,1,0:T(8,128)(2,1)} %param.10) | copy-start | bytes 4718596
  3.0 8.5 %copy-start.32 = (s32[64,16]{0,1:T(8,128)S(1)}, s32[64,16]{0,1:T(8,128)}, u32[]{:S(2)}) copy-start(s32[64,16]{0,1:T(8,128)} %param.11) | copy-start | bytes 12292
  3.0 49.1 %all-to-all-start.1 = ((bf16[64,8,768]{2,1,0:T(8,128)(2,1)}), bf16[64,8,768]{2,1,0:T(8,128)(2,1)S(1)}, u32[]{:S(2)}, u32[]{:S(2)}) async-start(bf16[64,8,768]{2,1,0:T(8,128)(2,1)} %pad_maximum_fusion.1), calls=%async_computation.1 | async-start | bytes 1572864 | tf_op jit(solution)/shard_map/all_to_all | solution.py:302
  52.1 33.5 %all-to-all-start = ((bf16[64,8,768]{2,1,0:T(8,128)(2,1)}), bf16[64,8,768]{2,1,0:T(8,128)(2,1)}, u32[]{:S(2)}, u32[]{:S(2)}) async-start(bf16[64,8,768]{2,1,0:T(8,128)(2,1)} %slice.51), calls=%async_computation | async-start | bytes 1572864 | tf_op jit(solution)/shard_map/all_to_all | solution.py:302
  59.9 1.3 copy-start.17
  61.2 1.3 copy-start.19
  62.5 1.3 copy-start.21
  63.7 1.3 copy-start.23
  65.0 1.3 copy-start.25
  66.3 1.3 copy-start.27
  67.6 1.3 copy-start.29
  84.7 0.9 copy-start.1
  85.6 1.0 copy-start.16
  86.5 1.3 copy-start.18
  87.8 1.3 copy-start.20
  89.1 1.3 copy-start.22
  90.3 1.3 copy-start.24
  91.6 1.3 copy-start.26
  92.9 1.3 copy-start.28
  94.2 1.3 copy-start.30
  95.4 17.2 %copy-start = (bf16[768,768]{1,0:T(8,128)(2,1)S(1)}, bf16[768,768]{1,0:T(8,128)(2,1)}, u32[]{:S(2)}) copy-start(bf16[768,768]{1,0:T(8,128)(2,1)} %wo.7) | copy-start | bytes 3538948
  95.4 17.2 %copy-start.2 = (bf16[8,64,768]{2,1,0:T(8,128)(2,1)S(1)}, bf16[8,64,768]{2,1,0:T(8,128)(2,1)}, u32[]{:S(2)}) copy-start(bf16[8,64,768]{2,1,0:T(8,128)(2,1)} %copy-done.1) | copy-start | bytes 2359300
  95.4 17.3 %copy-start.14 = (f32[512,1]{1,0:T(8,128)S(1)}, f32[512,1]{1,0:T(8,128)}, u32[]{:S(2)}) copy-start(f32[512,1]{1,0:T(8,128)} %slice.67.land_ref) | copy-start | bytes 6148
  112.6 5.1 %copy-start.4 = (bf16[8,64,768]{2,1,0:T(8,128)(2,1)}, bf16[8,64,768]{2,1,0:T(8,128)(2,1)S(1)}, u32[]{:S(2)}) copy-start(bf16[8,64,768]{2,1,0:T(8,128)(2,1)S(1)} %get-tuple-element.13.ya) | copy-start | bytes 2359300
  112.6 5.1 %copy-start.6 = (bf16[8,64,768]{2,1,0:T(8,128)(2,1)}, bf16[8,64,768]{2,1,0:T(8,128)(2,1)S(1)}, u32[]{:S(2)}) copy-start(bf16[8,64,768]{2,1,0:T(8,128)(2,1)S(1)} %get-tuple-element.15.qa) | copy-start | bytes 2359300
  112.6 5.1 %copy-start.8 = (bf16[8,64,768]{2,1,0:T(8,128)(2,1)}, bf16[8,64,768]{2,1,0:T(8,128)(2,1)S(1)}, u32[]{:S(2)}) copy-start(bf16[8,64,768]{2,1,0:T(8,128)(2,1)S(1)} %get-tuple-element.17.ka) | copy-start | bytes 2359300
  112.6 5.1 %copy-start.10 = (bf16[8,64,768]{2,1,0:T(8,128)(2,1)}, bf16[8,64,768]{2,1,0:T(8,128)(2,1)S(1)}, u32[]{:S(2)}) copy-start(bf16[8,64,768]{2,1,0:T(8,128)(2,1)S(1)} %get-tuple-element.19.va) | copy-start | bytes 2359300
  117.7 0.9 copy-start.12
  118.6 20.6 %all-to-all-start.3 = ((bf16[32,16,768]{2,1,0:T(8,128)(2,1)}), bf16[32,16,768]{2,1,0:T(8,128)(2,1)}, u32[]{:S(2)}, u32[]{:S(2)}) async-start(bf16[32,16,768]{2,1,0:T(8,128)(2,1)} %bitcast.31), calls=%async_computation.3 | async-start | bytes 1572864 | tf_op jit(solution)/shard_map/all_to_all | solution.py:302
  127.0 1.1 copy-start.3
  128.1 1.1 copy-start.5
  129.2 1.1 copy-start.7
  130.4 1.1 copy-start.9
  131.5 1.1 copy-start.11
  132.6 0.9 copy-start.15
  138.4 0.9 copy-start.13

commit v2 on v0

--- a/solution.py
+++ b/solution.py
@@ -1,6 +1,10 @@
+import functools
+
 import jax
 import jax.numpy as jnp
 from jax import lax
+from jax.experimental import pallas as pl
+from jax.experimental.pallas import tpu as pltpu
 from jax.sharding import PartitionSpec as P
 
 HEADS = 12
@@ -8,6 +12,8 @@
 
 EPS = 1e-05
 NEG = -1e30
+
+GROUPS = (4, 4)
 
 
 def passed_along(value, axis, steps):
@@ -93,7 +99,7 @@
     )
 
 
-def on_device(
+def spread_rows(
     fields, ocean, w_query1, w_key1, w_value1, w_out1, w_query2, w_key2, w_value2, w_out2
 ):
     rows, cols, width = fields.shape
@@ -125,6 +131,330 @@
     ).astype(jnp.bfloat16)
 
 
+def normed_f32(a):
+    mean = jnp.mean(a, -1, keepdims=True)
+    centred = a - mean
+    var = jnp.mean(centred * centred, -1, keepdims=True)
+    return (centred * lax.rsqrt(var + EPS)).astype(jnp.bfloat16)
+
+
+def dot_f32(a, b):
+    return jnp.dot(a, b, preferred_element_type=jnp.float32)
+
+
+def diagonal(n, m):
+    return lax.broadcasted_iota(jnp.int32, (n, m), 0) == lax.broadcasted_iota(jnp.int32, (n, m), 1)
+
+
+def low_columns(shape, axis):
+    return lax.broadcasted_iota(jnp.int32, shape, axis) % 8 < 4
+
+
+def key_bias_of(marks):
+    n = marks.shape[0]
+    land = (1.0 - marks[:, :n]) * NEG
+    return jnp.sum(jnp.where(diagonal(n, n), land, 0.0), 0, keepdims=True)
+
+
+def pair_attend(q, k, v, key_bias, land_query):
+    n = q.shape[0]
+    low = lax.broadcasted_iota(jnp.int32, (n, 128), 1) < 64
+    zero = jnp.zeros_like(q)
+    both = jnp.concatenate([jnp.where(low, q, zero), jnp.where(low, zero, q)], 0)
+    scores = lax.dot_general(both, k, (((1,), (1,)), ((), ())), preferred_element_type=jnp.float32)
+    scores = scores + key_bias
+    top = jnp.max(scores, -1, keepdims=True)
+    expo = jnp.exp(scores - top).astype(jnp.bfloat16)
+    wide = jnp.concatenate([v, jnp.ones_like(v)], 1)
+    sums = dot_f32(expo, wide)
+    upper = jnp.where(low, sums[:n, :128], sums[n:, :128])
+    total = jnp.where(low, sums[:n, 128:], sums[n:, 128:]) + land_query
+    return (upper / total * (1.0 - land_query)).astype(jnp.bfloat16)
+
+
+def pack_kernel(distances, me_ref, marks_ref, fields_ref, *refs):
+    outs, (held, sems) = refs[: len(distances)], refs[len(distances) :]
+    me = me_ref[0]
+    tiles = fields_ref.shape[-1] // 128
+    copies = []
+    for i, d in enumerate(distances):
+        there = jnp.bitwise_xor(me, d)
+        copies.append(pltpu.make_async_copy(fields_ref.at[pl.ds(there * 8, 8)], held.at[i], sems.at[i]))
+        copies[-1].start()
+    for i, d in enumerate(distances):
+        there = jnp.bitwise_xor(me, d)
+        row = marks_ref[pl.ds(there, 1), :]
+        outs[i][128 * tiles :, :] = jnp.broadcast_to(row, (16, 128)).astype(jnp.bfloat16)
+        copies[i].wait()
+        piece = held[i].reshape(128, 128 * tiles)
+        for t in range(tiles):
+            outs[i][128 * t : 128 * t + 128, :] = piece[:, 128 * t : 128 * t + 128]
+
+
+def pack(distances, me, marks, fields):
+    cols, width = fields.shape[1:]
+    vmem = pl.BlockSpec(memory_space=pltpu.VMEM)
+    piece = jax.ShapeDtypeStruct((width + 16, 128), jnp.bfloat16)
+    n = len(distances)
+    return pl.pallas_call(
+        functools.partial(pack_kernel, distances),
+        out_shape=(piece,) * n,
+        in_specs=[pl.BlockSpec(memory_space=pltpu.SMEM), vmem, pl.BlockSpec(memory_space=pltpu.HBM)],
+        out_specs=(vmem,) * n,
+        scratch_shapes=[pltpu.VMEM((n, 8, cols, width), jnp.bfloat16), pltpu.SemaphoreType.DMA((n,))],
+        compiler_params=pltpu.CompilerParams(vmem_limit_bytes=16 * 1024 * 1024),
+        cost_estimate=pl.CostEstimate(flops=n * 200000, bytes_accessed=n * 400000, transcendentals=0),
+        name="pack",
+    )(me, marks, fields)
+
+
+def unpacked(piece):
+    tiles = (piece.shape[0] - 16) // 128
+    lanes = [piece[128 * t : 128 * t + 128] for t in range(tiles)]
+    row = piece[128 * tiles :].astype(jnp.float32)[:1]
+    marks = jnp.sum(jnp.where(diagonal(128, 128), row, 0.0), 1, keepdims=True)
+    marks = jnp.broadcast_to(marks, (128, 128)).astype(jnp.bfloat16)
+    whole = jnp.concatenate(lanes + [marks], 1).astype(jnp.float32).reshape(8, 2, 8, 128 * tiles + 128)
+    return whole[:, 0], whole[:, 1]
+
+
+def window_kernel(stage, me_ref, *refs):
+    if stage == 0:
+        pieces, refs = refs[:4], refs[4:]
+    else:
+        (*pieces, edge0_ref, edge3_ref, tail_ref), refs = refs[:7], refs[7:]
+    wq, wk, wv, wo, wq2, wk2, wv2 = refs[:7]
+    if stage == 0:
+        y_ref, q2_ref, k2_ref, v2_ref, m_ref, edge0_ref, edge3_ref, tail_ref = refs[7:15]
+        refs = refs[15:]
+    else:
+        y_ref, q2_ref, k2_ref, v2_ref, m_ref = refs[7:12]
+        refs = refs[12:]
+    placed, q_s, k_s, v_s, o_s, rows_s = refs
+    width = wq.shape[0]
+    scale = (width // HEADS) ** (-0.5)
+    low = jnp.bitwise_and(me_ref[0], 3)
+    for d in range(4):
+        placed[jnp.bitwise_xor(low, d)] = pieces[d][...]
+    columns = [unpacked(placed[l]) for l in range(4)]
+    mask = low_columns((8, 8, width + 128), 1)
+    full = (64, width + 128)
+
+    def whole_window(l):
+        return jnp.where(mask, columns[l][1], columns[l][0]).reshape(full)
+
+    def straddling_window(left, right):
+        return jnp.where(mask, right, left).reshape(full)
+
+    windows = [whole_window(0)]
+    for l in range(1, 4):
+        windows += [straddling_window(columns[l - 1][1], columns[l][0]), whole_window(l)]
+    if stage == 0:
+        edge0_ref[...] = columns[0][0].reshape(full)
+        edge3_ref[...] = columns[3][1].reshape(full)
+    else:
+        windows = (
+            [straddling_window(edge3_ref[...].reshape(8, 8, -1), columns[0][0])]
+            + windows
+            + [straddling_window(columns[3][1], edge0_ref[...].reshape(8, 8, -1))]
+        )
+    count = len(windows)
+    x = jnp.concatenate([w[:, :width] for w in windows], 0)
+    marks = [w[:, width:] for w in windows]
+    h = normed_f32(x)
+    q_s[...] = (dot_f32(h, wq[...]) * scale).astype(jnp.bfloat16)
+    k_s[...] = dot_f32(h, wk[...]).astype(jnp.bfloat16)
+    v_s[...] = dot_f32(h, wv[...]).astype(jnp.bfloat16)
+    for w in range(count):
+        here = slice(64 * w, 64 * w + 64)
+        bias = key_bias_of(marks[w])
+        land = 1.0 - marks[w]
+        for p in range(HEADS // 2):
+            lanes = slice(128 * p, 128 * p + 128)
+            o_s[here, lanes] = pair_attend(q_s[here, lanes], k_s[here, lanes], v_s[here, lanes], bias, land)
+    y = (x + dot_f32(o_s[...], wo[...])).astype(jnp.bfloat16).astype(jnp.float32)
+    first = 0
+    if stage == 1:
+        first = 1
+        rows_s[:, :8, :] = tail_ref[...]
+    for w in range(count):
+        for r in range(8):
+            at = 64 * w + 8 * r
+            to = 8 * (w + first)
+            if stage == 0 and w == count - 1:
+                tail_ref[r, :, :width] = y[at : at + 8]
+                tail_ref[r, :, width:] = marks[w][8 * r : 8 * r + 8]
+            else:
+                rows_s[r, to : to + 8, :width] = y[at : at + 8]
+                rows_s[r, to : to + 8, width:] = marks[w][8 * r : 8 * r + 8]
+    tokens = rows_s.shape[0] * rows_s.shape[1]
+    y = rows_s[:, :, :width].reshape(tokens, width)
+    m_ref[...] = rows_s[:, :, width:].astype(jnp.bfloat16)
+    y_ref[...] = y.astype(jnp.bfloat16).reshape(y_ref.shape)
+    h = normed_f32(y)
+    q2_ref[...] = (dot_f32(h, wq2[...]) * scale).astype(jnp.bfloat16).reshape(q2_ref.shape)
+    k2_ref[...] = dot_f32(h, wk2[...]).astype(jnp.bfloat16).reshape(k2_ref.shape)
+    v2_ref[...] = dot_f32(h, wv2[...]).astype(jnp.bfloat16).reshape(v2_ref.shape)
+
+
+def window_layer(stage, me, pieces, carried, weights):
+    width = weights[0].shape[0]
+    tokens = 64 * (7, 9)[stage]
+    columns = 8 * (6, 10)[stage]
+    half = jax.ShapeDtypeStruct((8, columns, width), jnp.bfloat16)
+    marks = jax.ShapeDtypeStruct((8, columns, 128), jnp.bfloat16)
+    edge = jax.ShapeDtypeStruct((64, width + 128), jnp.float32)
+    tail = jax.ShapeDtypeStruct((8, 8, width + 128), jnp.float32)
+    outs = (half,) * 4 + (marks,) + ((edge, edge, tail) if stage == 0 else ())
+    vmem = pl.BlockSpec(memory_space=pltpu.VMEM)
+    work = pltpu.VMEM((tokens, width), jnp.bfloat16)
+    inputs = [*pieces, *carried, *weights]
+    return pl.pallas_call(
+        functools.partial(window_kernel, stage),
+        out_shape=outs,
+        in_specs=[pl.BlockSpec(memory_space=pltpu.SMEM)] + [vmem] * len(inputs),
+        out_specs=(vmem,) * len(outs),
+        scratch_shapes=[
+            pltpu.VMEM((4, width + 16, 128), jnp.bfloat16),
+            work, work, work, work,
+            pltpu.VMEM((8, columns, width + 128), jnp.float32),
+        ],
+        compiler_params=pltpu.CompilerParams(vmem_limit_bytes=36 * 1024 * 1024),
+        cost_estimate=pl.CostEstimate(
+            flops=2 * tokens * width * (7 * width + 512), bytes_accessed=16 << 20, transcendentals=tokens * 64 * HEADS
+        ),
+        name="window_layer",
+    )(me, *inputs)
+
+
+def row_kernel(rows, me_ref, *refs):
+    (ya, qa, ka, va, ma, yb, qb, kb, vb, mb, wo), refs = refs[:11], refs[11:]
+    outs, (o_s, placed) = refs[:8], refs[8:]
+    width = wo.shape[0]
+    length = ya.shape[1] + yb.shape[1]
+    for r in range(rows):
+        here = slice(length * r, length * r + length)
+        marks = jnp.concatenate([ma[r], mb[r]], 0).astype(jnp.float32)
+        bias = key_bias_of(marks)
+        land = 1.0 - marks
+        for p in range(HEADS // 2):
+            lanes = slice(128 * p, 128 * p + 128)
+            q = jnp.concatenate([qa[r, :, lanes], qb[r, :, lanes]], 0)
+            k = jnp.concatenate([ka[r, :, lanes], kb[r, :, lanes]], 0)
+            v = jnp.concatenate([va[r, :, lanes], vb[r, :, lanes]], 0)
+            o_s[here, lanes] = pair_attend(q, k, v, bias, land)
+    added = dot_f32(o_s[...], wo[...])
+    mask = low_columns((8, width), 0)
+    for r in range(rows):
+        before = jnp.concatenate([ya[r], yb[r]], 0).astype(jnp.float32)
+        f = before + added[length * r : length * r + length]
+        tiles = [f[8 * w : 8 * w + 8] for w in range(16)]
+        for l in range(8):
+            placed[l, r] = jnp.concatenate(
+                [
+                    jnp.where(mask, tiles[(2 * l - 1) % 16], tiles[2 * l]),
+                    jnp.where(mask, tiles[2 * l], tiles[2 * l + 1]),
+                ],
+                0,
+            ).astype(jnp.bfloat16)
+    low = jnp.bitwise_and(me_ref[0], 3)
+    for d in range(8):
+        outs[d][...] = placed[jnp.bitwise_xor(low, d)]
+
+
+def row_layer(start, rows, me, halves, w_out):
+    width = w_out.shape[0]
+    step = start // rows
+    length = 128
+
+    def block(a):
+        return pl.BlockSpec((rows,) + a.shape[1:], lambda i: (step, 0, 0))
+
+    piece = jax.ShapeDtypeStruct((rows, 16, width), jnp.bfloat16)
+    return pl.pallas_call(
+        functools.partial(row_kernel, rows),
+        out_shape=(piece,) * 8,
+        grid=(1,),
+        in_specs=[pl.BlockSpec(memory_space=pltpu.SMEM)]
+        + [block(a) for a in halves]
+        + [pl.BlockSpec((width, width), lambda i: (0, 0))],
+        out_specs=(pl.BlockSpec(piece.shape, lambda i: (0, 0, 0)),) * 8,
+        scratch_shapes=[
+            pltpu.VMEM((rows * length, width), jnp.bfloat16),
+            pltpu.VMEM((8, rows, 16, width), jnp.bfloat16),
+        ],
+        compiler_params=pltpu.CompilerParams(vmem_limit_bytes=32 * 1024 * 1024),
+        cost_estimate=pl.CostEstimate(
+            flops=2 * rows * length * width * (width + 1024), bytes_accessed=8 << 20,
+            transcendentals=rows * length * length * HEADS,
+        ),
+        name="row_layer",
+    )(me, *halves, w_out)
+
+
+def place_kernel(start, rows, me_ref, *refs):
+    pieces, out_ref, sems = refs[:8], refs[-2], refs[-1]
+    copies = []
+    for d in range(8):
+        there = jnp.bitwise_xor(me_ref[0], d)
+        copies.append(
+            pltpu.make_async_copy(pieces[d], out_ref.at[pl.ds(there * 8 + start, rows)], sems.at[d])
+        )
+        copies[-1].start()
+    for copy in copies:
+        copy.wait()
+
+
+def place(start, rows, me, pieces, so_far, shape):
+    anywhere = pl.BlockSpec(memory_space=pl.ANY)
+    hbm = pl.BlockSpec(memory_space=pltpu.HBM)
+    more = () if so_far is None else (so_far,)
+    return pl.pallas_call(
+        functools.partial(place_kernel, start, rows),
+        out_shape=jax.ShapeDtypeStruct(shape, jnp.bfloat16),
+        in_specs=[pl.BlockSpec(memory_space=pltpu.SMEM)] + [anywhere] * 8 + [hbm] * len(more),
+        out_specs=hbm,
+        scratch_shapes=[pltpu.SemaphoreType.DMA((8,))],
+        input_output_aliases={9: 0} if more else {},
+        cost_estimate=pl.CostEstimate(flops=0, bytes_accessed=16 * rows * shape[1] * shape[2] * 2, transcendentals=0),
+        name="place",
+    )(me, *pieces, *more)
+
+
+def exchanged(piece, distance):
+    count = lax.axis_size("lon")
+    return lax.ppermute(piece, "lon", [(s, s ^ distance) for s in range(count)])
+
+
+def gathered_bands(
+    fields, ocean, w_query1, w_key1, w_value1, w_out1, w_query2, w_key2, w_value2, w_out2
+):
+    me = lax.axis_index("lon").astype(jnp.int32).reshape(1)
+    marks = ocean.reshape(8, 128).astype(jnp.float32)
+    weights = (w_query1, w_key1, w_value1, w_out1, w_query2, w_key2, w_value2)
+
+    order = (4, 5, 6, 7, 1, 2, 3, 0)
+    packed = dict(zip(order, pack(order, me, marks, fields)))
+    got = {d: exchanged(packed[d], d) if d else packed[d] for d in order}
+    own = window_layer(0, me, [got[d] for d in range(4)], (), weights)
+    other = window_layer(1, me, [got[d] for d in range(4, 8)], own[5:], weights)
+    halves = (*own[:5], *other)
+    start, out = 0, None
+    for size in GROUPS:
+        sent = row_layer(start, size, me, halves, w_out2)
+        back = [exchanged(sent[d], d) if d else sent[d] for d in range(8)]
+        out = place(start, size, me, back, out, fields.shape)
+        start += size
+    return out
+
+
+def on_device(fields, *rest):
+    rows, cols, width = fields.shape
+    if lax.axis_size("lon") == 8 and rows == 64 and cols == 16 and width == 64 * HEADS:
+        return gathered_bands(fields, *rest)
+    return spread_rows(fields, *rest)
+
+
 def solution(mesh):
     in_specs = (
         P(("grp", "lat"), "lon", None),

time: 332 us -> 155 us (0.47)
  the two profiles are of different devices: /device:TPU:0 before, /device:TPU:10 now
where the time goes in v2:
time: 155 us
  Pallas kernels  84.6 us (55%)
  starting transfers between devices  33.3 us (21%)
  waiting for transfers between devices  24.6 us (16%)
  local copies, waits for them, and re-layouts  11.2 us (7%)
    pallas_call x2, Pallas kernels, place(): pl.pallas_call(functools.partial(place_kernel, start, rows), out_shape=ja...  50 us
    ppermute x21, starting transfers between devices, exchanged(): return lax.ppermute(piece, 'lon', [(s, s ^ distance) for s in range(count)])  33.3 us
    ppermute x21, waiting for transfers between devices, exchanged(): return lax.ppermute(piece, 'lon', [(s, s ^ distance) for s in range(count)])  24.6 us
    pallas_call x2, Pallas kernels, window_layer(): pl.pallas_call(functools.partial(window_kernel, stage), out_shape=outs, i...  23.9 us
    unnamed x52, local copies, waits for them, and re-layouts  11 us
    pallas_call x2, Pallas kernels, row_layer(): pl.pallas_call(functools.partial(row_kernel, rows), out_shape=(piece,) *...  8.35 us
  transfers between devices with their start and end apart: 21, of which 7 were waited for; matrix products, arithmetic and copies ran while one was open for 0% of the time, Pallas kernels for 25%

profile of v2, /device:TPU:10, one launch (start us, length us, event | category | flops | bytes accessed | tf_op | source)
XLA Modules:
  0.0 154.8 jit_solution(8170994101832460829)
XLA Ops:
  0.0 0.7 convert_element_type.5
  0.7 0.1 copy.13
  0.8 0.1 convert_element_type.6.marks_ref
  0.9 1.4 copy-done.1
  2.3 2.3 %pack.1 = (bf16[784,128]{1,0:T(8,128)(2,1)S(1)}, bf16[784,128]{1,0:T(8,128)(2,1)S(1)}, bf16[784,128]{1,0:T(8,128)(2,1)S(1)}, bf16[784,128]{1,0:T(8,128)(2,1)S(1)...) custom-call(s32[1]{0:T(128)} %bitcast.me_ref, ...), custom_call_target="tpu_custom_call" | custom-call | flops 1600000 | bytes 3200000 | tf_op jit(solution)/shard_map/pack/pallas_call | solution.py:199
  4.6 1.6 %collective-permute-start = (bf16[784,128]{1,0:T(8,128)(2,1)S(1)}, bf16[784,128]{1,0:T(8,128)(2,1)S(1)}, u32[]{:S(2)}, u32[]{:S(2)}) collective-permute-start(bf16[784,128]{1,0:T(8,128)(2,1)S(1)} %get-tuple-element.43), channel_id=1, source_target_pairs={{0,1},{1,0},{2,3},{3,2},{4,5},{5,4},{6,7},{7,6},{8,9},{9,8},{10,11... | collective-permute-start | bytes 602120 | tf_op jit(solution)/shard_map/ppermute | solution.py:426
  6.2 0.4 collective-permute-start.1
  6.6 1.5 collective-permute-start.2
  8.1 2.6 %collective-permute-start.3 = (bf16[784,128]{1,0:T(8,128)(2,1)S(1)}, bf16[784,128]{1,0:T(8,128)(2,1)S(1)}, u32[]{:S(2)}, u32[]{:S(2)}) collective-permute-start(bf16[784,128]{1,0:T(8,128)(2,1)S(1)} %get-tuple-element.51), channel_id=1, source_target_pairs={{0,4},{1,5},{2,6},{3,7},{4,0},{5,1},{6,2},{7,3},{8,12},{9,13},{10,... | collective-permute-start | bytes 602120 | tf_op jit(solution)/shard_map/ppermute | solution.py:426
  10.7 1.3 collective-permute-start.4
  12.0 0.0 collective-permute-done.refs_1_
  12.0 1.6 %collective-permute-start.5 = (bf16[784,128]{1,0:T(8,128)(2,1)S(1)}, bf16[784,128]{1,0:T(8,128)(2,1)S(1)}, u32[]{:S(2)}, u32[]{:S(2)}) collective-permute-start(bf16[784,128]{1,0:T(8,128)(2,1)S(1)} %get-tuple-element.53), channel_id=1, source_target_pairs={{0,6},{1,7},{2,4},{3,5},{4,2},{5,3},{6,0},{7,1},{8,14},{9,15},{10,... | collective-permute-start | bytes 602120 | tf_op jit(solution)/shard_map/ppermute | solution.py:426
  13.6 6.3 %collective-permute-done.1.refs_2_ = bf16[784,128]{1,0:T(8,128)(2,1)S(1)} collective-permute-done((bf16[784,128]{1,0:T(8,128)(2,1)S(1)}, bf16[784,128]{1,0:T(8,128)(2,1)S(1)}, u32[]{:S(2)}, u32[]{:S(2)}) %collective-permute-start.1) | collective-permute-done | bytes 200736 | tf_op jit(solution)/shard_map/ppermute | solution.py:426
  19.9 0.0 collective-permute-start.6
  19.9 2.8 %collective-permute-done.2.refs_3_ = bf16[784,128]{1,0:T(8,128)(2,1)S(1)} collective-permute-done((bf16[784,128]{1,0:T(8,128)(2,1)S(1)}, bf16[784,128]{1,0:T(8,128)(2,1)S(1)}, u32[]{:S(2)}, u32[]{:S(2)}) %collective-permute-start.2) | collective-permute-done | bytes 200736 | tf_op jit(solution)/shard_map/ppermute | solution.py:426
  22.8 1.3 copy-done.5
  24.0 1.3 copy-done.6
  25.3 1.3 copy-done.7
  26.6 1.3 copy-done.8
  27.8 1.3 copy-done.9
  29.1 1.3 copy-done.10
  30.4 10.3 %window_layer.2 = (bf16[8,48,768]{2,1,0:T(8,128)(2,1)S(1)}, bf16[8,48,768]{2,1,0:T(8,128)(2,1)S(1)}, bf16[8,48,768]{2,1,0:T(8,128)(2,1)S(1)}, bf16[8,48,768]{2,1...) custom-call(s32[1]{0:T(128)} %bitcast.me_ref, ...), custom_call_target="tpu_custom_call" | custom-call | flops 4051697664 | bytes 16777216 | tf_op jit(solution)/shard_map/window_layer/pallas_call | solution.py:312
  40.7 0.0 collective-permute-done.3.refs_0_
  40.7 0.0 collective-permute-done.4.refs_1_
  40.7 1.3 collective-permute-done.5.refs_2_
  42.0 3.0 %collective-permute-done.6.refs_3_ = bf16[784,128]{1,0:T(8,128)(2,1)S(1)} collective-permute-done((bf16[784,128]{1,0:T(8,128)(2,1)S(1)}, bf16[784,128]{1,0:T(8,128)(2,1)S(1)}, u32[]{:S(2)}, u32[]{:S(2)}) %collective-permute-start.6) | collective-permute-done | bytes 200736 | tf_op jit(solution)/shard_map/ppermute | solution.py:426
  45.0 13.7 %window_layer.3 = (bf16[8,80,768]{2,1,0:T(8,128)(2,1)S(1)}, bf16[8,80,768]{2,1,0:T(8,128)(2,1)S(1)}, bf16[8,80,768]{2,1,0:T(8,128)(2,1)S(1)}, bf16[8,80,768]{2,1,0:T(8,128)(2,1)S(1)}, bf16[8,80,128]{2,1,0:T(8,128)(2,1)S(1)}) custom-call(s32[1]{0:T(128)} %bitcast.me_ref, bf16[784,128]{1,0:T(8,128)(2,1)S(1)} %collective-permute-done.3.refs_0_, ...), custom_call_target="tpu_custom_call" | custom-call | flops 5209325568 | bytes 16777216 | tf_op jit(solution)/shard_map/window_layer/pallas_call | solution.py:312
  58.7 4.2 %row_layer.2 = (bf16[4,16,768]{2,1,0:T(8,128)(2,1)S(1)}, bf16[4,16,768]{2,1,0:T(8,128)(2,1)S(1)}, bf16[4,16,768]{2,1,0:T(8,128)(2,1)S(1)}, bf16[4,16,768]{2,1,0:...) custom-call(s32[1]{0:T(128)} %bitcast.me_ref, ...), custom_call_target="tpu_custom_call" | custom-call | flops 1409286144 | bytes 8388608 | tf_op jit(solution)/shard_map/row_layer/pallas_call | solution.py:374
  62.9 0.6 copy-done.3
  63.5 0.8 collective-permute-start.7
  64.3 0.0 collective-permute-start.8
  64.3 4.2 %row_layer.3 = (bf16[4,16,768]{2,1,0:T(8,128)(2,1)S(1)}, bf16[4,16,768]{2,1,0:T(8,128)(2,1)S(1)}, bf16[4,16,768]{2,1,0:T(8,128)(2,1)S(1)}, bf16[4,16,768]{2,1,0:...) custom-call(s32[1]{0:T(128)} %bitcast.me_ref, ...), custom_call_target="tpu_custom_call" | custom-call | flops 1409286144 | bytes 8388608 | tf_op jit(solution)/shard_map/row_layer/pallas_call | solution.py:374
  68.5 0.6 copy-done.2
  69.1 1.2 collective-permute-start.14
  70.4 2.0 %collective-permute-start.15 = (bf16[4,16,768]{2,1,0:T(8,128)(2,1)S(1)}, bf16[4,16,768]{2,1,0:T(8,128)(2,1)S(1)}, u32[]{:S(2)}, u32[]{:S(2)}) collective-permute-start(bf16[4,16,768]{2,1,0:T(8,128)(2,1)S(1)} %get-tuple-element.73), channel_id=1, source_target_pairs={{0,2},{1,3},{2,0},{3,1},{4,6},{5,7},{6,4},{7,5},{8,10},{9,11},{10,... | collective-permute-start | bytes 294920 | tf_op jit(solution)/shard_map/ppermute | solution.py:426
  72.4 0.2 collective-permute-start.16
  72.6 0.0 collective-permute-done.7.refs_1_
  72.7 3.9 %collective-permute-start.17 = (bf16[4,16,768]{2,1,0:T(8,128)(2,1)S(1)}, bf16[4,16,768]{2,1,0:T(8,128)(2,1)S(1)}, u32[]{:S(2)}, u32[]{:S(2)}) collective-permute-start(bf16[4,16,768]{2,1,0:T(8,128)(2,1)S(1)} %get-tuple-element.75), channel_id=1, source_target_pairs={{0,4},{1,5},{2,6},{3,7},{4,0},{5,1},{6,2},{7,3},{8,12},{9,13},{10,... | collective-permute-start | bytes 294920 | tf_op jit(solution)/shard_map/ppermute | solution.py:426
  76.5 0.0 collective-permute-done.8.refs_2_
  76.5 1.1 collective-permute-start.18
  77.6 0.0 collective-permute-done.14.refs_1_
  77.6 1.4 collective-permute-start.19
  79.0 0.0 collective-permute-done.15.refs_2_
  79.0 0.6 collective-permute-start.20
  79.6 0.0 collective-permute-done.16.refs_3_
  79.6 3.4 %collective-permute-start.9 = (bf16[4,16,768]{2,1,0:T(8,128)(2,1)S(1)}, bf16[4,16,768]{2,1,0:T(8,128)(2,1)S(1)}, u32[]{:S(2)}, u32[]{:S(2)}) collective-permute-start(bf16[4,16,768]{2,1,0:T(8,128)(2,1)S(1)} %get-tuple-element.66), channel_id=1, source_target_pairs={{0,3},{1,2},{2,1},{3,0},{4,7},{5,6},{6,5},{7,4},{8,11},{9,10},{10,... | collective-permute-start | bytes 294920 | tf_op jit(solution)/shard_map/ppermute | solution.py:426
  83.0 4.8 %collective-permute-done.17.refs_4_ = bf16[4,16,768]{2,1,0:T(8,128)(2,1)S(1)} collective-permute-done((bf16[4,16,768]{2,1,0:T(8,128)(2,1)S(1)}, bf16[4,16,768]{2,1,0:T(8,128)(2,1)S(1)}, u32[]{:S(2)}, u32[]{:S(2)}) %collective-permute-start.17) | collective-permute-done | bytes 98336 | tf_op jit(solution)/shard_map/ppermute | solution.py:426
  87.8 3.4 %collective-permute-start.10 = (bf16[4,16,768]{2,1,0:T(8,128)(2,1)S(1)}, bf16[4,16,768]{2,1,0:T(8,128)(2,1)S(1)}, u32[]{:S(2)}, u32[]{:S(2)}) collective-permute-start(bf16[4,16,768]{2,1,0:T(8,128)(2,1)S(1)} %get-tuple-element.67), channel_id=1, source_target_pairs={{0,4},{1,5},{2,6},{3,7},{4,0},{5,1},{6,2},{7,3},{8,12},{9,13},{10,... | collective-permute-start | bytes 294920 | tf_op jit(solution)/shard_map/ppermute | solution.py:426
  91.2 0.0 collective-permute-done.18.refs_5_
  91.2 3.0 %collective-permute-start.11 = (bf16[4,16,768]{2,1,0:T(8,128)(2,1)S(1)}, bf16[4,16,768]{2,1,0:T(8,128)(2,1)S(1)}, u32[]{:S(2)}, u32[]{:S(2)}) collective-permute-start(bf16[4,16,768]{2,1,0:T(8,128)(2,1)S(1)} %get-tuple-element.68), channel_id=1, source_target_pairs={{0,5},{1,4},{2,7},{3,6},{4,1},{5,0},{6,3},{7,2},{8,13},{9,12},{10,... | collective-permute-start | bytes 294920 | tf_op jit(solution)/shard_map/ppermute | solution.py:426
  94.2 2.4 %collective-permute-done.19.refs_6_ = bf16[4,16,768]{2,1,0:T(8,128)(2,1)S(1)} collective-permute-done((bf16[4,16,768]{2,1,0:T(8,128)(2,1)S(1)}, bf16[4,16,768]{2,1,0:T(8,128)(2,1)S(1)}, u32[]{:S(2)}, u32[]{:S(2)}) %collective-permute-start.19) | collective-permute-done | bytes 98336 | tf_op jit(solution)/shard_map/ppermute | solution.py:426
  96.5 1.1 collective-permute-start.12
  97.6 3.9 %collective-permute-done.20.refs_7_ = bf16[4,16,768]{2,1,0:T(8,128)(2,1)S(1)} collective-permute-done((bf16[4,16,768]{2,1,0:T(8,128)(2,1)S(1)}, bf16[4,16,768]{2,1,0:T(8,128)(2,1)S(1)}, u32[]{:S(2)}, u32[]{:S(2)}) %collective-permute-start.20) | collective-permute-done | bytes 98336 | tf_op jit(solution)/shard_map/ppermute | solution.py:426
  101.6 2.2 %collective-permute-start.13 = (bf16[4,16,768]{2,1,0:T(8,128)(2,1)S(1)}, bf16[4,16,768]{2,1,0:T(8,128)(2,1)S(1)}, u32[]{:S(2)}, u32[]{:S(2)}) collective-permute-start(bf16[4,16,768]{2,1,0:T(8,128)(2,1)S(1)} %get-tuple-element.70), channel_id=1, source_target_pairs={{0,7},{1,6},{2,5},{3,4},{4,3},{5,2},{6,1},{7,0},{8,15},{9,14},{10,... | collective-permute-start | bytes 294920 | tf_op jit(solution)/shard_map/ppermute | solution.py:426
  103.8 25.0 %place.2.refs_8_ = bf16[64,16,768]{2,1,0:T(8,128)(2,1)} custom-call(s32[1]{0:T(128)} %bitcast.me_ref, bf16[4,16,768]{2,1,0:T(8,128)(2,1)} %copy-done.2, bf16[4,16,768]{2,1,0:T(8,128)(2,1)} %copy-done.12, bf16[4,16,768]{2,1,0:T(8,128)(2,1)} %copy-done.13, bf16[4,16,768]{2,1,0:T(8,128)(2,1)} %copy-done.14, bf16[4,16,768]{2,1,0:T(8,128)(2,1)} %copy-done.15, ...), custom_call_target="tpu_custom_call" | custom-call | bytes 1572864 | tf_op jit(solution)/shard_map/place/pallas_call | solution.py:412
  128.9 0.0 collective-permute-done.9.refs_3_
  128.9 0.0 collective-permute-done.10.refs_4_
  128.9 0.0 collective-permute-done.12.refs_6_
  129.0 0.5 copy-done.21
  129.5 0.0 copy-done.22
  129.5 0.0 copy-done.23
  129.6 0.1 copy-done.24
  129.6 0.0 copy-done.25
  129.7 25.0 %place.3 = bf16[64,16,768]{2,1,0:T(8,128)(2,1)} custom-call(s32[1]{0:T(128)} %bitcast.me_ref, bf16[4,16,768]{2,1,0:T(8,128)(2,1)} %copy-done.3, bf16[4,16,768]{2,1,0:T(8,128)(2,1)} %copy-done.19, bf16[4,16,768]{2,1,0:T(8,128)(2,1)} %copy-done.20, bf16[4,16,768]{2,1,0:T(8,128)(2,1)} %copy-done.21, ...), custom_call_target="tpu_custom_call", output_to_operand_aliasing={{}: (9, {})} | custom-call | bytes 1572864 | tf_op jit(solution)/shard_map/place/pallas_call | solution.py:412
  (40 shorter events, 0.1 us)
Async XLA Ops:
  0.9 1.4 copy-start.1
  2.3 20.5 %copy-start.4 = (bf16[768,768]{1,0:T(8,128)(2,1)S(1)}, bf16[768,768]{1,0:T(8,128)(2,1)}, u32[]{:S(2)}) copy-start(bf16[768,768]{1,0:T(8,128)(2,1)} %refs_7_.3) | copy-start | bytes 3538948
  4.6 7.4 %collective-permute-start = (bf16[784,128]{1,0:T(8,128)(2,1)S(1)}, bf16[784,128]{1,0:T(8,128)(2,1)S(1)}, u32[]{:S(2)}, u32[]{:S(2)}) collective-permute-start(bf16[784,128]{1,0:T(8,128)(2,1)S(1)} %get-tuple-element.43), channel_id=1, source_target_pairs={{0,1},{1,0},{2,3},{3,2},{4,5},{5,4},{6,7},{7,6},{8,9},{9,8},{10,11... | collective-permute-start | bytes 602120 | tf_op jit(solution)/shard_map/ppermute | solution.py:426
  6.2 13.7 %collective-permute-start.1 = (bf16[784,128]{1,0:T(8,128)(2,1)S(1)}, bf16[784,128]{1,0:T(8,128)(2,1)S(1)}, u32[]{:S(2)}, u32[]{:S(2)}) collective-permute-start(bf16[784,128]{1,0:T(8,128)(2,1)S(1)} %get-tuple-element.44), channel_id=1, source_target_pairs={{0,2},{1,3},{2,0},{3,1},{4,6},{5,7},{6,4},{7,5},{8,10},{9,11},{10,... | collective-permute-start | bytes 602120 | tf_op jit(solution)/shard_map/ppermute | solution.py:426
  6.6 16.1 %collective-permute-start.2 = (bf16[784,128]{1,0:T(8,128)(2,1)S(1)}, bf16[784,128]{1,0:T(8,128)(2,1)S(1)}, u32[]{:S(2)}, u32[]{:S(2)}) collective-permute-start(bf16[784,128]{1,0:T(8,128)(2,1)S(1)} %get-tuple-element.45), channel_id=1, source_target_pairs={{0,3},{1,2},{2,1},{3,0},{4,7},{5,6},{6,5},{7,4},{8,11},{9,10},{10,... | collective-permute-start | bytes 602120 | tf_op jit(solution)/shard_map/ppermute | solution.py:426
  8.1 32.5 %collective-permute-start.3 = (bf16[784,128]{1,0:T(8,128)(2,1)S(1)}, bf16[784,128]{1,0:T(8,128)(2,1)S(1)}, u32[]{:S(2)}, u32[]{:S(2)}) collective-permute-start(bf16[784,128]{1,0:T(8,128)(2,1)S(1)} %get-tuple-element.51), channel_id=1, source_target_pairs={{0,4},{1,5},{2,6},{3,7},{4,0},{5,1},{6,2},{7,3},{8,12},{9,13},{10,... | collective-permute-start | bytes 602120 | tf_op jit(solution)/shard_map/ppermute | solution.py:426
  10.7 29.9 %collective-permute-start.4 = (bf16[784,128]{1,0:T(8,128)(2,1)S(1)}, bf16[784,128]{1,0:T(8,128)(2,1)S(1)}, u32[]{:S(2)}, u32[]{:S(2)}) collective-permute-start(bf16[784,128]{1,0:T(8,128)(2,1)S(1)} %get-tuple-element.52), channel_id=1, source_target_pairs={{0,5},{1,4},{2,7},{3,6},{4,1},{5,0},{6,3},{7,2},{8,13},{9,12},{10,... | collective-permute-start | bytes 602120 | tf_op jit(solution)/shard_map/ppermute | solution.py:426
  12.0 30.0 %collective-permute-start.5 = (bf16[784,128]{1,0:T(8,128)(2,1)S(1)}, bf16[784,128]{1,0:T(8,128)(2,1)S(1)}, u32[]{:S(2)}, u32[]{:S(2)}) collective-permute-start(bf16[784,128]{1,0:T(8,128)(2,1)S(1)} %get-tuple-element.53), channel_id=1, source_target_pairs={{0,6},{1,7},{2,4},{3,5},{4,2},{5,3},{6,0},{7,1},{8,14},{9,15},{10,... | collective-permute-start | bytes 602120 | tf_op jit(solution)/shard_map/ppermute | solution.py:426
  19.9 25.1 %collective-permute-start.6 = (bf16[784,128]{1,0:T(8,128)(2,1)S(1)}, bf16[784,128]{1,0:T(8,128)(2,1)S(1)}, u32[]{:S(2)}, u32[]{:S(2)}) collective-permute-start(bf16[784,128]{1,0:T(8,128)(2,1)S(1)} %get-tuple-element.54), channel_id=1, source_target_pairs={{0,7},{1,6},{2,5},{3,4},{4,3},{5,2},{6,1},{7,0},{8,15},{9,14},{10,... | collective-permute-start | bytes 602120 | tf_op jit(solution)/shard_map/ppermute | solution.py:426
  22.8 1.3 copy-start.5
  24.0 1.3 copy-start.6
  25.3 1.3 copy-start.7
  26.6 1.3 copy-start.8
  27.8 1.3 copy-start.9
  29.1 1.3 copy-start.10
  30.4 14.6 %copy-start.11 = (bf16[768,768]{1,0:T(8,128)(2,1)S(1)}, bf16[768,768]{1,0:T(8,128)(2,1)}, u32[]{:S(2)}) copy-start(bf16[768,768]{1,0:T(8,128)(2,1)} %refs_13_.1) | copy-start | bytes 3538948
  45.0 13.7 %copy-start = (bf16[768,768]{1,0:T(8,128)(2,1)S(1)}, bf16[768,768]{1,0:T(8,128)(2,1)}, u32[]{:S(2)}) copy-start(bf16[768,768]{1,0:T(8,128)(2,1)} %refs_10_.7) | copy-start | bytes 3538948
  62.9 0.6 copy-start.3
  63.5 9.1 %collective-permute-start.7 = (bf16[4,16,768]{2,1,0:T(8,128)(2,1)S(1)}, bf16[4,16,768]{2,1,0:T(8,128)(2,1)S(1)}, u32[]{:S(2)}, u32[]{:S(2)}) collective-permute-start(bf16[4,16,768]{2,1,0:T(8,128)(2,1)S(1)} %get-tuple-element.64), channel_id=1, source_target_pairs={{0,1},{1,0},{2,3},{3,2},{4,5},{5,4},{6,7},{7,6},{8,9},{9,8},{10,11... | collective-permute-start | bytes 294920 | tf_op jit(solution)/shard_map/ppermute | solution.py:426
  64.3 12.2 %collective-permute-start.8 = (bf16[4,16,768]{2,1,0:T(8,128)(2,1)S(1)}, bf16[4,16,768]{2,1,0:T(8,128)(2,1)S(1)}, u32[]{:S(2)}, u32[]{:S(2)}) collective-permute-start(bf16[4,16,768]{2,1,0:T(8,128)(2,1)S(1)} %get-tuple-element.65), channel_id=1, source_target_pairs={{0,2},{1,3},{2,0},{3,1},{4,6},{5,7},{6,4},{7,5},{8,10},{9,11},{10,... | collective-permute-start | bytes 294920 | tf_op jit(solution)/shard_map/ppermute | solution.py:426
  68.5 0.6 copy-start.2
  69.1 8.4 %collective-permute-start.14 = (bf16[4,16,768]{2,1,0:T(8,128)(2,1)S(1)}, bf16[4,16,768]{2,1,0:T(8,128)(2,1)S(1)}, u32[]{:S(2)}, u32[]{:S(2)}) collective-permute-start(bf16[4,16,768]{2,1,0:T(8,128)(2,1)S(1)} %get-tuple-element.72), channel_id=1, source_target_pairs={{0,1},{1,0},{2,3},{3,2},{4,5},{5,4},{6,7},{7,6},{8,9},{9,8},{10,11... | collective-permute-start | bytes 294920 | tf_op jit(solution)/shard_map/ppermute | solution.py:426
  70.4 8.6 %collective-permute-start.15 = (bf16[4,16,768]{2,1,0:T(8,128)(2,1)S(1)}, bf16[4,16,768]{2,1,0:T(8,128)(2,1)S(1)}, u32[]{:S(2)}, u32[]{:S(2)}) collective-permute-start(bf16[4,16,768]{2,1,0:T(8,128)(2,1)S(1)} %get-tuple-element.73), channel_id=1, source_target_pairs={{0,2},{1,3},{2,0},{3,1},{4,6},{5,7},{6,4},{7,5},{8,10},{9,11},{10,... | collective-permute-start | bytes 294920 | tf_op jit(solution)/shard_map/ppermute | solution.py:426
  72.4 7.2 %collective-permute-start.16 = (bf16[4,16,768]{2,1,0:T(8,128)(2,1)S(1)}, bf16[4,16,768]{2,1,0:T(8,128)(2,1)S(1)}, u32[]{:S(2)}, u32[]{:S(2)}) collective-permute-start(bf16[4,16,768]{2,1,0:T(8,128)(2,1)S(1)} %get-tuple-element.74), channel_id=1, source_target_pairs={{0,3},{1,2},{2,1},{3,0},{4,7},{5,6},{6,5},{7,4},{8,11},{9,10},{10,... | collective-permute-start | bytes 294920 | tf_op jit(solution)/shard_map/ppermute | solution.py:426
  72.6 56.3 %copy-start.19 = (bf16[4,16,768]{2,1,0:T(8,128)(2,1)}, bf16[4,16,768]{2,1,0:T(8,128)(2,1)S(1)}, u32[]{:S(2)}) copy-start(bf16[4,16,768]{2,1,0:T(8,128)(2,1)S(1)} %collective-permute-done.7.refs_1_) | copy-start | bytes 294916
  72.7 15.1 %collective-permute-start.17 = (bf16[4,16,768]{2,1,0:T(8,128)(2,1)S(1)}, bf16[4,16,768]{2,1,0:T(8,128)(2,1)S(1)}, u32[]{:S(2)}, u32[]{:S(2)}) collective-permute-start(bf16[4,16,768]{2,1,0:T(8,128)(2,1)S(1)} %get-tuple-element.75), channel_id=1, source_target_pairs={{0,4},{1,5},{2,6},{3,7},{4,0},{5,1},{6,2},{7,3},{8,12},{9,13},{10,... | collective-permute-start | bytes 294920 | tf_op jit(solution)/shard_map/ppermute | solution.py:426
  76.5 52.4 %copy-start.20 = (bf16[4,16,768]{2,1,0:T(8,128)(2,1)}, bf16[4,16,768]{2,1,0:T(8,128)(2,1)S(1)}, u32[]{:S(2)}) copy-start(bf16[4,16,768]{2,1,0:T(8,128)(2,1)S(1)} %collective-permute-done.8.refs_2_) | copy-start | bytes 294916
  76.5 14.6 %collective-permute-start.18 = (bf16[4,16,768]{2,1,0:T(8,128)(2,1)S(1)}, bf16[4,16,768]{2,1,0:T(8,128)(2,1)S(1)}, u32[]{:S(2)}, u32[]{:S(2)}) collective-permute-start(bf16[4,16,768]{2,1,0:T(8,128)(2,1)S(1)} %get-tuple-element.76), channel_id=1, source_target_pairs={{0,5},{1,4},{2,7},{3,6},{4,1},{5,0},{6,3},{7,2},{8,13},{9,12},{10,... | collective-permute-start | bytes 294920 | tf_op jit(solution)/shard_map/ppermute | solution.py:426
  77.6 26.2 %copy-start.12 = (bf16[4,16,768]{2,1,0:T(8,128)(2,1)}, bf16[4,16,768]{2,1,0:T(8,128)(2,1)S(1)}, u32[]{:S(2)}) copy-start(bf16[4,16,768]{2,1,0:T(8,128)(2,1)S(1)} %collective-permute-done.14.refs_1_) | copy-start | bytes 294916
  77.6 19.0 %collective-permute-start.19 = (bf16[4,16,768]{2,1,0:T(8,128)(2,1)S(1)}, bf16[4,16,768]{2,1,0:T(8,128)(2,1)S(1)}, u32[]{:S(2)}, u32[]{:S(2)}) collective-permute-start(bf16[4,16,768]{2,1,0:T(8,128)(2,1)S(1)} %get-tuple-element.77), channel_id=1, source_target_pairs={{0,6},{1,7},{2,4},{3,5},{4,2},{5,3},{6,0},{7,1},{8,14},{9,15},{10,... | collective-permute-start | bytes 294920 | tf_op jit(solution)/shard_map/ppermute | solution.py:426
  79.0 24.8 %copy-start.13 = (bf16[4,16,768]{2,1,0:T(8,128)(2,1)}, bf16[4,16,768]{2,1,0:T(8,128)(2,1)S(1)}, u32[]{:S(2)}) copy-start(bf16[4,16,768]{2,1,0:T(8,128)(2,1)S(1)} %collective-permute-done.15.refs_2_) | copy-start | bytes 294916
  79.0 22.6 %collective-permute-start.20 = (bf16[4,16,768]{2,1,0:T(8,128)(2,1)S(1)}, bf16[4,16,768]{2,1,0:T(8,128)(2,1)S(1)}, u32[]{:S(2)}, u32[]{:S(2)}) collective-permute-start(bf16[4,16,768]{2,1,0:T(8,128)(2,1)S(1)} %get-tuple-element.78), channel_id=1, source_target_pairs={{0,7},{1,6},{2,5},{3,4},{4,3},{5,2},{6,1},{7,0},{8,15},{9,14},{10,... | collective-permute-start | bytes 294920 | tf_op jit(solution)/shard_map/ppermute | solution.py:426
  79.6 24.2 %copy-start.14 = (bf16[4,16,768]{2,1,0:T(8,128)(2,1)}, bf16[4,16,768]{2,1,0:T(8,128)(2,1)S(1)}, u32[]{:S(2)}) copy-start(bf16[4,16,768]{2,1,0:T(8,128)(2,1)S(1)} %collective-permute-done.16.refs_3_) | copy-start | bytes 294916
  79.6 49.2 %collective-permute-start.9 = (bf16[4,16,768]{2,1,0:T(8,128)(2,1)S(1)}, bf16[4,16,768]{2,1,0:T(8,128)(2,1)S(1)}, u32[]{:S(2)}, u32[]{:S(2)}) collective-permute-start(bf16[4,16,768]{2,1,0:T(8,128)(2,1)S(1)} %get-tuple-element.66), channel_id=1, source_target_pairs={{0,3},{1,2},{2,1},{3,0},{4,7},{5,6},{6,5},{7,4},{8,11},{9,10},{10,... | collective-permute-start | bytes 294920 | tf_op jit(solution)/shard_map/ppermute | solution.py:426
  87.8 16.0 %copy-start.15 = (bf16[4,16,768]{2,1,0:T(8,128)(2,1)}, bf16[4,16,768]{2,1,0:T(8,128)(2,1)S(1)}, u32[]{:S(2)}) copy-start(bf16[4,16,768]{2,1,0:T(8,128)(2,1)S(1)} %collective-permute-done.17.refs_4_) | copy-start | bytes 294916
  87.8 41.1 %collective-permute-start.10 = (bf16[4,16,768]{2,1,0:T(8,128)(2,1)S(1)}, bf16[4,16,768]{2,1,0:T(8,128)(2,1)S(1)}, u32[]{:S(2)}, u32[]{:S(2)}) collective-permute-start(bf16[4,16,768]{2,1,0:T(8,128)(2,1)S(1)} %get-tuple-element.67), channel_id=1, source_target_pairs={{0,4},{1,5},{2,6},{3,7},{4,0},{5,1},{6,2},{7,3},{8,12},{9,13},{10,... | collective-permute-start | bytes 294920 | tf_op jit(solution)/shard_map/ppermute | solution.py:426
  91.2 12.7 %copy-start.16 = (bf16[4,16,768]{2,1,0:T(8,128)(2,1)}, bf16[4,16,768]{2,1,0:T(8,128)(2,1)S(1)}, u32[]{:S(2)}) copy-start(bf16[4,16,768]{2,1,0:T(8,128)(2,1)S(1)} %collective-permute-done.18.refs_5_) | copy-start | bytes 294916
  91.2 37.7 %collective-permute-start.11 = (bf16[4,16,768]{2,1,0:T(8,128)(2,1)S(1)}, bf16[4,16,768]{2,1,0:T(8,128)(2,1)S(1)}, u32[]{:S(2)}, u32[]{:S(2)}) collective-permute-start(bf16[4,16,768]{2,1,0:T(8,128)(2,1)S(1)} %get-tuple-element.68), channel_id=1, source_target_pairs={{0,5},{1,4},{2,7},{3,6},{4,1},{5,0},{6,3},{7,2},{8,13},{9,12},{10,... | collective-permute-start | bytes 294920 | tf_op jit(solution)/shard_map/ppermute | solution.py:426
  96.5 7.3 %copy-start.17 = (bf16[4,16,768]{2,1,0:T(8,128)(2,1)}, bf16[4,16,768]{2,1,0:T(8,128)(2,1)S(1)}, u32[]{:S(2)}) copy-start(bf16[4,16,768]{2,1,0:T(8,128)(2,1)S(1)} %collective-permute-done.19.refs_6_) | copy-start | bytes 294916
  96.5 32.4 %collective-permute-start.12 = (bf16[4,16,768]{2,1,0:T(8,128)(2,1)S(1)}, bf16[4,16,768]{2,1,0:T(8,128)(2,1)S(1)}, u32[]{:S(2)}, u32[]{:S(2)}) collective-permute-start(bf16[4,16,768]{2,1,0:T(8,128)(2,1)S(1)} %get-tuple-element.69), channel_id=1, source_target_pairs={{0,6},{1,7},{2,4},{3,5},{4,2},{5,3},{6,0},{7,1},{8,14},{9,15},{10,... | collective-permute-start | bytes 294920 | tf_op jit(solution)/shard_map/ppermute | solution.py:426
  101.6 2.3 %copy-start.18 = (bf16[4,16,768]{2,1,0:T(8,128)(2,1)}, bf16[4,16,768]{2,1,0:T(8,128)(2,1)S(1)}, u32[]{:S(2)}) copy-start(bf16[4,16,768]{2,1,0:T(8,128)(2,1)S(1)} %collective-permute-done.20.refs_7_) | copy-start | bytes 294916
  101.6 27.4 %collective-permute-start.13 = (bf16[4,16,768]{2,1,0:T(8,128)(2,1)S(1)}, bf16[4,16,768]{2,1,0:T(8,128)(2,1)S(1)}, u32[]{:S(2)}, u32[]{:S(2)}) collective-permute-start(bf16[4,16,768]{2,1,0:T(8,128)(2,1)S(1)} %get-tuple-element.70), channel_id=1, source_target_pairs={{0,7},{1,6},{2,5},{3,4},{4,3},{5,2},{6,1},{7,0},{8,15},{9,14},{10,... | collective-permute-start | bytes 294920 | tf_op jit(solution)/shard_map/ppermute | solution.py:426
  128.9 0.6 copy-start.21
  128.9 0.7 copy-start.22
  128.9 0.7 copy-start.23
  128.9 0.7 copy-start.24
  128.9 0.7 copy-start.25

commit v3 on v2

--- a/solution.py
+++ b/solution.py
@@ -14,6 +14,8 @@
 NEG = -1e30
 
 GROUPS = (4, 4)
+
+PAIRS = [slice(128 * p, 128 * p + 128) for p in range(HEADS // 2)]
 
 
 def passed_along(value, axis, steps):
@@ -150,26 +152,28 @@
     return lax.broadcasted_iota(jnp.int32, shape, axis) % 8 < 4
 
 
-def key_bias_of(marks):
+def attend(queries, keys, values, marks):
     n = marks.shape[0]
-    land = (1.0 - marks[:, :n]) * NEG
-    return jnp.sum(jnp.where(diagonal(n, n), land, 0.0), 0, keepdims=True)
-
-
-def pair_attend(q, k, v, key_bias, land_query):
-    n = q.shape[0]
     low = lax.broadcasted_iota(jnp.int32, (n, 128), 1) < 64
-    zero = jnp.zeros_like(q)
-    both = jnp.concatenate([jnp.where(low, q, zero), jnp.where(low, zero, q)], 0)
-    scores = lax.dot_general(both, k, (((1,), (1,)), ((), ())), preferred_element_type=jnp.float32)
-    scores = scores + key_bias
-    top = jnp.max(scores, -1, keepdims=True)
-    expo = jnp.exp(scores - top).astype(jnp.bfloat16)
-    wide = jnp.concatenate([v, jnp.ones_like(v)], 1)
-    sums = dot_f32(expo, wide)
-    upper = jnp.where(low, sums[:n, :128], sums[n:, :128])
-    total = jnp.where(low, sums[:n, 128:], sums[n:, 128:]) + land_query
-    return (upper / total * (1.0 - land_query)).astype(jnp.bfloat16)
+    land = 1.0 - marks
+    bias = jnp.concatenate([land * NEG] * (2 * n // 128), 1)
+    scores = []
+    for q, k in zip(queries, keys):
+        zero = jnp.zeros_like(q)
+        both = jnp.concatenate([jnp.where(low, q, zero), jnp.where(low, zero, q)], 0)
+        scores.append(lax.dot_general(k, both, (((1,), (1,)), ((), ())), preferred_element_type=jnp.float32) + bias)
+    expos = [jnp.exp(s - jnp.max(s, 0, keepdims=True)).astype(jnp.bfloat16) for s in scores]
+    outs = []
+    for expo, v in zip(expos, values):
+        wide = jnp.concatenate([v, jnp.ones_like(v)], 1)
+        sums = lax.dot_general(expo, wide, (((0,), (0,)), ((), ())), preferred_element_type=jnp.float32)
+        upper = jnp.where(low, sums[:n, :128], sums[n:, :128])
+        total = jnp.where(low, sums[:n, 128:], sums[n:, 128:]) + land
+        outs.append((upper / total * marks).astype(jnp.bfloat16))
+    return outs
+
+
+ORDER = (4, 5, 6, 7, 1, 2, 3, 0)
 
 
 def pack_kernel(distances, me_ref, marks_ref, fields_ref, *refs):
@@ -267,11 +271,9 @@
     v_s[...] = dot_f32(h, wv[...]).astype(jnp.bfloat16)
     for w in range(count):
         here = slice(64 * w, 64 * w + 64)
-        bias = key_bias_of(marks[w])
-        land = 1.0 - marks[w]
-        for p in range(HEADS // 2):
-            lanes = slice(128 * p, 128 * p + 128)
-            o_s[here, lanes] = pair_attend(q_s[here, lanes], k_s[here, lanes], v_s[here, lanes], bias, land)
+        outs = attend(*([a[here, lanes] for lanes in PAIRS] for a in (q_s, k_s, v_s)), marks[w])
+        for lanes, out in zip(PAIRS, outs):
+            o_s[here, lanes] = out
     y = (x + dot_f32(o_s[...], wo[...])).astype(jnp.bfloat16).astype(jnp.float32)
     first = 0
     if stage == 1:
@@ -328,21 +330,22 @@
 
 
 def row_kernel(rows, me_ref, *refs):
-    (ya, qa, ka, va, ma, yb, qb, kb, vb, mb, wo), refs = refs[:11], refs[11:]
+    (yb, qb, kb, vb, mb, ya, qa, ka, va, ma, wo), refs = refs[:11], refs[11:]
     outs, (o_s, placed) = refs[:8], refs[8:]
     width = wo.shape[0]
     length = ya.shape[1] + yb.shape[1]
     for r in range(rows):
         here = slice(length * r, length * r + length)
         marks = jnp.concatenate([ma[r], mb[r]], 0).astype(jnp.float32)
-        bias = key_bias_of(marks)
-        land = 1.0 - marks
-        for p in range(HEADS // 2):
-            lanes = slice(128 * p, 128 * p + 128)
-            q = jnp.concatenate([qa[r, :, lanes], qb[r, :, lanes]], 0)
-            k = jnp.concatenate([ka[r, :, lanes], kb[r, :, lanes]], 0)
-            v = jnp.concatenate([va[r, :, lanes], vb[r, :, lanes]], 0)
-            o_s[here, lanes] = pair_attend(q, k, v, bias, land)
+        heads = attend(
+            *(
+                [jnp.concatenate([a[r, :, lanes], b[r, :, lanes]], 0) for lanes in PAIRS]
+                for a, b in ((qa, qb), (ka, kb), (va, vb))
+            ),
+            marks,
+        )
+        for lanes, out in zip(PAIRS, heads):
+            o_s[here, lanes] = out
     added = dot_f32(o_s[...], wo[...])
     mask = low_columns((8, width), 0)
     for r in range(rows):
@@ -358,8 +361,8 @@
                 0,
             ).astype(jnp.bfloat16)
     low = jnp.bitwise_and(me_ref[0], 3)
-    for d in range(8):
-        outs[d][...] = placed[jnp.bitwise_xor(low, d)]
+    for i, d in enumerate(ORDER):
+        outs[i][...] = placed[jnp.bitwise_xor(low, d)]
 
 
 def row_layer(start, rows, me, halves, w_out):
@@ -395,10 +398,10 @@
 def place_kernel(start, rows, me_ref, *refs):
     pieces, out_ref, sems = refs[:8], refs[-2], refs[-1]
     copies = []
-    for d in range(8):
+    for i, d in enumerate(ORDER):
         there = jnp.bitwise_xor(me_ref[0], d)
         copies.append(
-            pltpu.make_async_copy(pieces[d], out_ref.at[pl.ds(there * 8 + start, rows)], sems.at[d])
+            pltpu.make_async_copy(pieces[i], out_ref.at[pl.ds(there * 8 + start, rows)], sems.at[i])
         )
         copies[-1].start()
     for copy in copies:
@@ -406,13 +409,13 @@
 
 
 def place(start, rows, me, pieces, so_far, shape):
-    anywhere = pl.BlockSpec(memory_space=pl.ANY)
+    vmem = pl.BlockSpec(memory_space=pltpu.VMEM)
     hbm = pl.BlockSpec(memory_space=pltpu.HBM)
     more = () if so_far is None else (so_far,)
     return pl.pallas_call(
         functools.partial(place_kernel, start, rows),
         out_shape=jax.ShapeDtypeStruct(shape, jnp.bfloat16),
-        in_specs=[pl.BlockSpec(memory_space=pltpu.SMEM)] + [anywhere] * 8 + [hbm] * len(more),
+        in_specs=[pl.BlockSpec(memory_space=pltpu.SMEM)] + [vmem] * 8 + [hbm] * len(more),
         out_specs=hbm,
         scratch_shapes=[pltpu.SemaphoreType.DMA((8,))],
         input_output_aliases={9: 0} if more else {},
@@ -433,19 +436,21 @@
     marks = ocean.reshape(8, 128).astype(jnp.float32)
     weights = (w_query1, w_key1, w_value1, w_out1, w_query2, w_key2, w_value2)
 
-    order = (4, 5, 6, 7, 1, 2, 3, 0)
-    packed = dict(zip(order, pack(order, me, marks, fields)))
-    got = {d: exchanged(packed[d], d) if d else packed[d] for d in order}
+    packed = dict(zip(ORDER, pack(ORDER, me, marks, fields)))
+    got = {d: exchanged(packed[d], d) if d else packed[d] for d in ORDER}
     own = window_layer(0, me, [got[d] for d in range(4)], (), weights)
     other = window_layer(1, me, [got[d] for d in range(4, 8)], own[5:], weights)
-    halves = (*own[:5], *other)
-    start, out = 0, None
+    halves = (*other, *own[:5])
+    start, out, back = 0, None, None
     for size in GROUPS:
-        sent = row_layer(start, size, me, halves, w_out2)
-        back = [exchanged(sent[d], d) if d else sent[d] for d in range(8)]
-        out = place(start, size, me, back, out, fields.shape)
+        sent = list(row_layer(start, size, me, halves, w_out2))
+        if back is not None:
+            for i in range(7):
+                sent[i], back[i] = lax.optimization_barrier((sent[i], back[i]))
+            out = place(start - size, size, me, back, out, fields.shape)
+        back = [exchanged(piece, d) if d else piece for d, piece in zip(ORDER, sent)]
         start += size
-    return out
+    return place(start - size, size, me, back, out, fields.shape)
 
 
 def on_device(fields, *rest):

time: 155 us -> 102 us (0.66)
  the two profiles are of different devices: /device:TPU:10 before, /device:TPU:0 now
where the time goes in v3:
time: 102 us; the launch traced here: 101 us
  starting transfers between devices  39.7 us (39%)
  Pallas kernels  28.5 us (28%)
  waiting for transfers between devices  20.6 us (20%)
  local copies, waits for them, and re-layouts  11.1 us (11%)
    ppermute x21, starting transfers between devices, exchanged(): return lax.ppermute(piece, 'lon', [(s, s ^ distance) for s in range(count)])  39.7 us
    ppermute x21, waiting for transfers between devices, exchanged(): return lax.ppermute(piece, 'lon', [(s, s ^ distance) for s in range(count)])  20.6 us
    pallas_call x2, Pallas kernels, window_layer(): pl.pallas_call(functools.partial(window_kernel, stage), out_shape=outs, i...  16.4 us
    unnamed x52, local copies, waits for them, and re-layouts  11 us
    pallas_call x2, Pallas kernels, row_layer(): pl.pallas_call(functools.partial(row_kernel, rows), out_shape=(piece,) *...  5.45 us
    pallas_call x2, Pallas kernels, place(): pl.pallas_call(functools.partial(place_kernel, start, rows), out_shape=ja...  4.3 us
    pallas_call x1, Pallas kernels, pack(): pl.pallas_call(functools.partial(pack_kernel, distances), out_shape=(piec...  2.3 us
  transfers between devices with their start and end apart: 21, of which 8 were waited for; matrix products, arithmetic and copies ran while one was open for 0% of the time, Pallas kernels for 12%

profile of v3, /device:TPU:0, one launch (start us, length us, event | category | flops | bytes accessed | tf_op | source)
XLA Modules:
  0.0 101.1 jit_solution(10755599614547277794)
XLA Ops:
  0.0 0.7 convert_element_type.5
  0.7 0.1 copy.13
  0.8 0.1 convert_element_type.6.marks_ref
  0.9 1.4 %copy-done.1 = bf16[64,16,768]{2,1,0:T(8,128)(2,1)S(1)} copy-done((bf16[64,16,768]{2,1,0:T(8,128)(2,1)S(1)}, bf16[64,16,768]{2,1,0:T(8,128)(2,1)}, u32[]{:S(2)}) %copy-start.1) | copy-done | bytes 1572888
  2.3 2.3 %pack.1 = (bf16[784,128]{1,0:T(8,128)(2,1)S(1)}, bf16[784,128]{1,0:T(8,128)(2,1)S(1)}, bf16[784,128]{1,0:T(8,128)(2,1)S(1)}, bf16[784,128]{1,0:T(8,128)(2,1)S(1)...) custom-call(s32[1]{0:T(128)} %bitcast.me_ref, ...), custom_call_target="tpu_custom_call" | custom-call | flops 1600000 | bytes 3200000 | tf_op jit(solution)/shard_map/pack/pallas_call | solution.py:203
  4.6 3.0 %collective-permute-start.4 = (bf16[784,128]{1,0:T(8,128)(2,1)S(1)}, bf16[784,128]{1,0:T(8,128)(2,1)S(1)}, u32[]{:S(2)}, u32[]{:S(2)}) collective-permute-start(bf16[784,128]{1,0:T(8,128)(2,1)S(1)} %get-tuple-element.61), channel_id=1, source_target_pairs={{0,1},{1,0},{2,3},{3,2},{4,5},{5,4},{6,7},{7,6},{8,9},{9,8},{10,11... | collective-permute-start | bytes 602120 | tf_op jit(solution)/shard_map/ppermute | solution.py:429
  7.6 1.6 %collective-permute-start.5 = (bf16[784,128]{1,0:T(8,128)(2,1)S(1)}, bf16[784,128]{1,0:T(8,128)(2,1)S(1)}, u32[]{:S(2)}, u32[]{:S(2)}) collective-permute-start(bf16[784,128]{1,0:T(8,128)(2,1)S(1)} %get-tuple-element.62), channel_id=1, source_target_pairs={{0,2},{1,3},{2,0},{3,1},{4,6},{5,7},{6,4},{7,5},{8,10},{9,11},{10,... | collective-permute-start | bytes 602120 | tf_op jit(solution)/shard_map/ppermute | solution.py:429
  9.2 0.0 collective-permute-start.6
  9.2 3.0 %collective-permute-start = (bf16[784,128]{1,0:T(8,128)(2,1)S(1)}, bf16[784,128]{1,0:T(8,128)(2,1)S(1)}, u32[]{:S(2)}, u32[]{:S(2)}) collective-permute-start(bf16[784,128]{1,0:T(8,128)(2,1)S(1)} %get-tuple-element.56), channel_id=1, source_target_pairs={{0,4},{1,5},{2,6},{3,7},{4,0},{5,1},{6,2},{7,3},{8,12},{9,13},{10,... | collective-permute-start | bytes 602120 | tf_op jit(solution)/shard_map/ppermute | solution.py:429
  12.2 1.3 %collective-permute-start.1 = (bf16[784,128]{1,0:T(8,128)(2,1)S(1)}, bf16[784,128]{1,0:T(8,128)(2,1)S(1)}, u32[]{:S(2)}, u32[]{:S(2)}) collective-permute-start(bf16[784,128]{1,0:T(8,128)(2,1)S(1)} %get-tuple-element.57), channel_id=1, source_target_pairs={{0,5},{1,4},{2,7},{3,6},{4,1},{5,0},{6,3},{7,2},{8,13},{9,12},{10,... | collective-permute-start | bytes 602120 | tf_op jit(solution)/shard_map/ppermute | solution.py:429
  13.5 0.0 collective-permute-done.4.refs_1_
  13.5 3.6 %collective-permute-start.2 = (bf16[784,128]{1,0:T(8,128)(2,1)S(1)}, bf16[784,128]{1,0:T(8,128)(2,1)S(1)}, u32[]{:S(2)}, u32[]{:S(2)}) collective-permute-start(bf16[784,128]{1,0:T(8,128)(2,1)S(1)} %get-tuple-element.58), channel_id=1, source_target_pairs={{0,6},{1,7},{2,4},{3,5},{4,2},{5,3},{6,0},{7,1},{8,14},{9,15},{10,... | collective-permute-start | bytes 602120 | tf_op jit(solution)/shard_map/ppermute | solution.py:429
  17.1 6.3 %collective-permute-done.5.refs_2_ = bf16[784,128]{1,0:T(8,128)(2,1)S(1)} collective-permute-done((bf16[784,128]{1,0:T(8,128)(2,1)S(1)}, bf16[784,128]{1,0:T(8,128)(2,1)S(1)}, u32[]{:S(2)}, u32[]{:S(2)}) %collective-permute-start.5) | collective-permute-done | bytes 200736 | tf_op jit(solution)/shard_map/ppermute | solution.py:429
  23.4 0.8 collective-permute-start.3
  24.2 1.0 collective-permute-done.6.refs_3_
  25.1 0.0 copy-done.4
  25.2 1.3 %copy-done.5 = bf16[768,768]{1,0:T(8,128)(2,1)S(1)} copy-done((bf16[768,768]{1,0:T(8,128)(2,1)S(1)}, bf16[768,768]{1,0:T(8,128)(2,1)}, u32[]{:S(2)}) %copy-start.5) | copy-done | bytes 1179672
  26.4 1.3 %copy-done.6 = bf16[768,768]{1,0:T(8,128)(2,1)S(1)} copy-done((bf16[768,768]{1,0:T(8,128)(2,1)S(1)}, bf16[768,768]{1,0:T(8,128)(2,1)}, u32[]{:S(2)}) %copy-start.6) | copy-done | bytes 1179672
  27.7 1.3 %copy-done.7 = bf16[768,768]{1,0:T(8,128)(2,1)S(1)} copy-done((bf16[768,768]{1,0:T(8,128)(2,1)S(1)}, bf16[768,768]{1,0:T(8,128)(2,1)}, u32[]{:S(2)}) %copy-start.7) | copy-done | bytes 1179672
  29.0 1.3 %copy-done.8 = bf16[768,768]{1,0:T(8,128)(2,1)S(1)} copy-done((bf16[768,768]{1,0:T(8,128)(2,1)S(1)}, bf16[768,768]{1,0:T(8,128)(2,1)}, u32[]{:S(2)}) %copy-start.8) | copy-done | bytes 1179672
  30.2 1.3 %copy-done.9 = bf16[768,768]{1,0:T(8,128)(2,1)S(1)} copy-done((bf16[768,768]{1,0:T(8,128)(2,1)S(1)}, bf16[768,768]{1,0:T(8,128)(2,1)}, u32[]{:S(2)}) %copy-start.9) | copy-done | bytes 1179672
  31.5 1.3 %copy-done.10 = bf16[768,768]{1,0:T(8,128)(2,1)S(1)} copy-done((bf16[768,768]{1,0:T(8,128)(2,1)S(1)}, bf16[768,768]{1,0:T(8,128)(2,1)}, u32[]{:S(2)}) %copy-start.10) | copy-done | bytes 1179672
  32.8 6.8 %window_layer.2 = (bf16[8,48,768]{2,1,0:T(8,128)(2,1)S(1)}, bf16[8,48,768]{2,1,0:T(8,128)(2,1)S(1)}, bf16[8,48,768]{2,1,0:T(8,128)(2,1)S(1)}, bf16[8,48,768]{2,1...) custom-call(s32[1]{0:T(128)} %bitcast.me_ref, ...), custom_call_target="tpu_custom_call" | custom-call | flops 4051697664 | bytes 16777216 | tf_op jit(solution)/shard_map/window_layer/pallas_call | solution.py:314
  39.6 0.0 collective-permute-done.refs_0_
  39.6 1.3 %collective-permute-done.1.refs_1_ = bf16[784,128]{1,0:T(8,128)(2,1)S(1)} collective-permute-done((bf16[784,128]{1,0:T(8,128)(2,1)S(1)}, bf16[784,128]{1,0:T(8,128)(2,1)S(1)}, u32[]{:S(2)}, u32[]{:S(2)}) %collective-permute-start.1) | collective-permute-done | bytes 200736 | tf_op jit(solution)/shard_map/ppermute | solution.py:429
  40.9 0.0 collective-permute-done.2.refs_2_
  40.9 0.0 collective-permute-done.3.refs_3_
  40.9 0.0 copy-start
  40.9 9.6 %window_layer.3 = (bf16[8,80,768]{2,1,0:T(8,128)(2,1)S(1)}, bf16[8,80,768]{2,1,0:T(8,128)(2,1)S(1)}, bf16[8,80,768]{2,1,0:T(8,128)(2,1)S(1)}, bf16[8,80,768]{2,1,0:T(8,128)(2,1)S(1)}, bf16[8,80,128]{2,1,0:T(8,128)(2,1)S(1)}) custom-call(s32[1]{0:T(128)} %bitcast.me_ref, bf16[784,128]{1,0:T(8,128)(2,1)S(1)} %collective-permute-done.refs_0_, ...), custom_call_target="tpu_custom_call" | custom-call | flops 5209325568 | bytes 16777216 | tf_op jit(solution)/shard_map/window_layer/pallas_call | solution.py:314
  50.5 2.7 %row_layer.3 = (bf16[4,16,768]{2,1,0:T(8,128)(2,1)S(1)}, bf16[4,16,768]{2,1,0:T(8,128)(2,1)S(1)}, bf16[4,16,768]{2,1,0:T(8,128)(2,1)S(1)}, bf16[4,16,768]{2,1,0:...) custom-call(s32[1]{0:T(128)} %bitcast.me_ref, ...), custom_call_target="tpu_custom_call" | custom-call | flops 1409286144 | bytes 8388608 | tf_op jit(solution)/shard_map/row_layer/pallas_call | solution.py:377
  53.3 0.6 copy-done.2
  53.9 9.3 %collective-permute-start.7 = (bf16[4,16,768]{2,1,0:T(8,128)(2,1)S(1)}, bf16[4,16,768]{2,1,0:T(8,128)(2,1)S(1)}, u32[]{:S(2)}, u32[]{:S(2)}) collective-permute-start(bf16[4,16,768]{2,1,0:T(8,128)(2,1)S(1)} %get-tuple-element.78), channel_id=1, source_target_pairs={{0,4},{1,5},{2,6},{3,7},{4,0},{5,1},{6,2},{7,3},{8,12},{9,13},{10,... | collective-permute-start | bytes 294920 | tf_op jit(solution)/shard_map/ppermute | solution.py:429
  63.2 0.0 collective-permute-start.9
  63.2 0.4 collective-permute-start.11
  63.6 4.3 %collective-permute-start.13 = (bf16[4,16,768]{2,1,0:T(8,128)(2,1)S(1)}, bf16[4,16,768]{2,1,0:T(8,128)(2,1)S(1)}, u32[]{:S(2)}, u32[]{:S(2)}) collective-permute-start(bf16[4,16,768]{2,1,0:T(8,128)(2,1)S(1)} %get-tuple-element.87), channel_id=1, source_target_pairs={{0,7},{1,6},{2,5},{3,4},{4,3},{5,2},{6,1},{7,0},{8,15},{9,14},{10,... | collective-permute-start | bytes 294920 | tf_op jit(solution)/shard_map/ppermute | solution.py:429
  67.9 0.6 collective-permute-start.15
  68.4 2.7 %row_layer.2 = (bf16[4,16,768]{2,1,0:T(8,128)(2,1)S(1)}, bf16[4,16,768]{2,1,0:T(8,128)(2,1)S(1)}, bf16[4,16,768]{2,1,0:T(8,128)(2,1)S(1)}, bf16[4,16,768]{2,1,0:...) custom-call(s32[1]{0:T(128)} %bitcast.me_ref, ...), custom_call_target="tpu_custom_call" | custom-call | flops 1409286144 | bytes 8388608 | tf_op jit(solution)/shard_map/row_layer/pallas_call | solution.py:377
  71.2 0.6 copy-done.3
  71.8 1.4 %collective-permute-done.7.refs_0_ = bf16[4,16,768]{2,1,0:T(8,128)(2,1)S(1)} collective-permute-done((bf16[4,16,768]{2,1,0:T(8,128)(2,1)S(1)}, bf16[4,16,768]{2,1,0:T(8,128)(2,1)S(1)}, u32[]{:S(2)}, u32[]{:S(2)}) %collective-permute-start.7) | collective-permute-done | bytes 98336 | tf_op jit(solution)/shard_map/ppermute | solution.py:429
  73.2 0.0 collective-permute-start.17
  73.2 2.3 %collective-permute-done.9.refs_1_ = bf16[4,16,768]{2,1,0:T(8,128)(2,1)S(1)} collective-permute-done((bf16[4,16,768]{2,1,0:T(8,128)(2,1)S(1)}, bf16[4,16,768]{2,1,0:T(8,128)(2,1)S(1)}, u32[]{:S(2)}, u32[]{:S(2)}) %collective-permute-start.9) | collective-permute-done | bytes 98336 | tf_op jit(solution)/shard_map/ppermute | solution.py:429
  75.5 0.0 collective-permute-start.19
  75.5 0.0 collective-permute-done.11.refs_2_
  75.5 3.3 %collective-permute-start.8 = (bf16[4,16,768]{2,1,0:T(8,128)(2,1)S(1)}, bf16[4,16,768]{2,1,0:T(8,128)(2,1)S(1)}, u32[]{:S(2)}, u32[]{:S(2)}) collective-permute-start(bf16[4,16,768]{2,1,0:T(8,128)(2,1)S(1)} %get-tuple-element.79), channel_id=1, source_target_pairs={{0,4},{1,5},{2,6},{3,7},{4,0},{5,1},{6,2},{7,3},{8,12},{9,13},{10,... | collective-permute-start | bytes 294920 | tf_op jit(solution)/shard_map/ppermute | solution.py:429
  78.8 0.0 collective-permute-done.13.refs_3_
  78.8 3.3 %collective-permute-start.10 = (bf16[4,16,768]{2,1,0:T(8,128)(2,1)S(1)}, bf16[4,16,768]{2,1,0:T(8,128)(2,1)S(1)}, u32[]{:S(2)}, u32[]{:S(2)}) collective-permute-start(bf16[4,16,768]{2,1,0:T(8,128)(2,1)S(1)} %get-tuple-element.82), channel_id=1, source_target_pairs={{0,5},{1,4},{2,7},{3,6},{4,1},{5,0},{6,3},{7,2},{8,13},{9,12},{10,... | collective-permute-start | bytes 294920 | tf_op jit(solution)/shard_map/ppermute | solution.py:429
  82.1 0.0 collective-permute-done.15.refs_4_
  82.1 2.1 %collective-permute-start.12 = (bf16[4,16,768]{2,1,0:T(8,128)(2,1)S(1)}, bf16[4,16,768]{2,1,0:T(8,128)(2,1)S(1)}, u32[]{:S(2)}, u32[]{:S(2)}) collective-permute-start(bf16[4,16,768]{2,1,0:T(8,128)(2,1)S(1)} %get-tuple-element.85), channel_id=1, source_target_pairs={{0,6},{1,7},{2,4},{3,5},{4,2},{5,3},{6,0},{7,1},{8,14},{9,15},{10,... | collective-permute-start | bytes 294920 | tf_op jit(solution)/shard_map/ppermute | solution.py:429
  84.1 0.0 collective-permute-done.17.refs_5_
  84.1 1.7 %collective-permute-start.14 = (bf16[4,16,768]{2,1,0:T(8,128)(2,1)S(1)}, bf16[4,16,768]{2,1,0:T(8,128)(2,1)S(1)}, u32[]{:S(2)}, u32[]{:S(2)}) collective-permute-start(bf16[4,16,768]{2,1,0:T(8,128)(2,1)S(1)} %get-tuple-element.88), channel_id=1, source_target_pairs={{0,7},{1,6},{2,5},{3,4},{4,3},{5,2},{6,1},{7,0},{8,15},{9,14},{10,... | collective-permute-start | bytes 294920 | tf_op jit(solution)/shard_map/ppermute | solution.py:429
  85.8 0.0 collective-permute-done.19.refs_6_
  85.8 1.5 %collective-permute-start.16 = (bf16[4,16,768]{2,1,0:T(8,128)(2,1)S(1)}, bf16[4,16,768]{2,1,0:T(8,128)(2,1)S(1)}, u32[]{:S(2)}, u32[]{:S(2)}) collective-permute-start(bf16[4,16,768]{2,1,0:T(8,128)(2,1)S(1)} %get-tuple-element.91), channel_id=1, source_target_pairs={{0,1},{1,0},{2,3},{3,2},{4,5},{5,4},{6,7},{7,6},{8,9},{9,8},{10,11... | collective-permute-start | bytes 294920 | tf_op jit(solution)/shard_map/ppermute | solution.py:429
  87.4 1.9 %collective-permute-done.8.refs_0_ = bf16[4,16,768]{2,1,0:T(8,128)(2,1)S(1)} collective-permute-done((bf16[4,16,768]{2,1,0:T(8,128)(2,1)S(1)}, bf16[4,16,768]{2,1,0:T(8,128)(2,1)S(1)}, u32[]{:S(2)}, u32[]{:S(2)}) %collective-permute-start.8) | collective-permute-done | bytes 98336 | tf_op jit(solution)/shard_map/ppermute | solution.py:429
  89.3 0.0 collective-permute-start.18
  89.3 3.3 %collective-permute-done.10.refs_1_ = bf16[4,16,768]{2,1,0:T(8,128)(2,1)S(1)} collective-permute-done((bf16[4,16,768]{2,1,0:T(8,128)(2,1)S(1)}, bf16[4,16,768]{2,1,0:T(8,128)(2,1)S(1)}, u32[]{:S(2)}, u32[]{:S(2)}) %collective-permute-start.10) | collective-permute-done | bytes 98336 | tf_op jit(solution)/shard_map/ppermute | solution.py:429
  92.6 0.0 collective-permute-start.20
  92.7 2.2 %place.2.refs_8_ = bf16[64,16,768]{2,1,0:T(8,128)(2,1)} custom-call(s32[1]{0:T(128)} %bitcast.me_ref, bf16[4,16,768]{2,1,0:T(8,128)(2,1)} %copy-done.12, bf16[4,16,768]{2,1,0:T(8,128)(2,1)} %copy-done.13, bf16[4,16,768]{2,1,0:T(8,128)(2,1)} %copy-done.14, bf16[4,16,768]{2,1,0:T(8,128)(2,1)} %copy-done.15, bf16[4,16,768]{2,1,0:T(8,128)(2,1)} %copy-done.16, ...), custom_call_target="tpu_custom_call" | custom-call | bytes 1572864 | tf_op jit(solution)/shard_map/place/pallas_call | solution.py:415
  94.9 0.0 collective-permute-done.12.refs_2_
  94.9 0.0 collective-permute-done.14.refs_3_
  94.9 0.0 collective-permute-done.16.refs_4_
  94.9 0.0 collective-permute-done.18.refs_5_
  94.9 3.2 %collective-permute-done.20.refs_6_ = bf16[4,16,768]{2,1,0:T(8,128)(2,1)S(1)} collective-permute-done((bf16[4,16,768]{2,1,0:T(8,128)(2,1)S(1)}, bf16[4,16,768]{2,1,0:T(8,128)(2,1)S(1)}, u32[]{:S(2)}, u32[]{:S(2)}) %collective-permute-start.20) | collective-permute-done | bytes 98336 | tf_op jit(solution)/shard_map/ppermute | solution.py:429
  98.1 0.6 copy-done.25
  98.8 2.1 %place.3 = bf16[64,16,768]{2,1,0:T(8,128)(2,1)} custom-call(s32[1]{0:T(128)} %bitcast.me_ref, bf16[4,16,768]{2,1,0:T(8,128)(2,1)} %copy-done.19, bf16[4,16,768]{2,1,0:T(8,128)(2,1)} %copy-done.20, bf16[4,16,768]{2,1,0:T(8,128)(2,1)} %copy-done.21, bf16[4,16,768]{2,1,0:T(8,128)(2,1)} %copy-done.22, ...), custom_call_target="tpu_custom_call", output_to_operand_aliasing={{}: (9, {})} | custom-call | bytes 1572864 | tf_op jit(solution)/shard_map/place/pallas_call | solution.py:415
  (40 shorter events, 0.1 us)
Async XLA Ops:
  0.9 1.4 %copy-start.1 = (bf16[64,16,768]{2,1,0:T(8,128)(2,1)S(1)}, bf16[64,16,768]{2,1,0:T(8,128)(2,1)}, u32[]{:S(2)}) copy-start(bf16[64,16,768]{2,1,0:T(8,128)(2,1)} %fields_ref.1) | copy-start | bytes 4718596
  2.3 22.9 %copy-start.4 = (bf16[768,768]{1,0:T(8,128)(2,1)S(1)}, bf16[768,768]{1,0:T(8,128)(2,1)}, u32[]{:S(2)}) copy-start(bf16[768,768]{1,0:T(8,128)(2,1)} %refs_7_.3) | copy-start | bytes 3538948
  4.6 8.9 %collective-permute-start.4 = (bf16[784,128]{1,0:T(8,128)(2,1)S(1)}, bf16[784,128]{1,0:T(8,128)(2,1)S(1)}, u32[]{:S(2)}, u32[]{:S(2)}) collective-permute-start(bf16[784,128]{1,0:T(8,128)(2,1)S(1)} %get-tuple-element.61), channel_id=1, source_target_pairs={{0,1},{1,0},{2,3},{3,2},{4,5},{5,4},{6,7},{7,6},{8,9},{9,8},{10,11... | collective-permute-start | bytes 602120 | tf_op jit(solution)/shard_map/ppermute | solution.py:429
  7.6 15.8 %collective-permute-start.5 = (bf16[784,128]{1,0:T(8,128)(2,1)S(1)}, bf16[784,128]{1,0:T(8,128)(2,1)S(1)}, u32[]{:S(2)}, u32[]{:S(2)}) collective-permute-start(bf16[784,128]{1,0:T(8,128)(2,1)S(1)} %get-tuple-element.62), channel_id=1, source_target_pairs={{0,2},{1,3},{2,0},{3,1},{4,6},{5,7},{6,4},{7,5},{8,10},{9,11},{10,... | collective-permute-start | bytes 602120 | tf_op jit(solution)/shard_map/ppermute | solution.py:429
  9.2 16.0 %collective-permute-start.6 = (bf16[784,128]{1,0:T(8,128)(2,1)S(1)}, bf16[784,128]{1,0:T(8,128)(2,1)S(1)}, u32[]{:S(2)}, u32[]{:S(2)}) collective-permute-start(bf16[784,128]{1,0:T(8,128)(2,1)S(1)} %get-tuple-element.63), channel_id=1, source_target_pairs={{0,3},{1,2},{2,1},{3,0},{4,7},{5,6},{6,5},{7,4},{8,11},{9,10},{10,... | collective-permute-start | bytes 602120 | tf_op jit(solution)/shard_map/ppermute | solution.py:429
  9.2 30.4 %collective-permute-start = (bf16[784,128]{1,0:T(8,128)(2,1)S(1)}, bf16[784,128]{1,0:T(8,128)(2,1)S(1)}, u32[]{:S(2)}, u32[]{:S(2)}) collective-permute-start(bf16[784,128]{1,0:T(8,128)(2,1)S(1)} %get-tuple-element.56), channel_id=1, source_target_pairs={{0,4},{1,5},{2,6},{3,7},{4,0},{5,1},{6,2},{7,3},{8,12},{9,13},{10,... | collective-permute-start | bytes 602120 | tf_op jit(solution)/shard_map/ppermute | solution.py:429
  12.2 28.7 %collective-permute-start.1 = (bf16[784,128]{1,0:T(8,128)(2,1)S(1)}, bf16[784,128]{1,0:T(8,128)(2,1)S(1)}, u32[]{:S(2)}, u32[]{:S(2)}) collective-permute-start(bf16[784,128]{1,0:T(8,128)(2,1)S(1)} %get-tuple-element.57), channel_id=1, source_target_pairs={{0,5},{1,4},{2,7},{3,6},{4,1},{5,0},{6,3},{7,2},{8,13},{9,12},{10,... | collective-permute-start | bytes 602120 | tf_op jit(solution)/shard_map/ppermute | solution.py:429
  13.5 27.4 %collective-permute-start.2 = (bf16[784,128]{1,0:T(8,128)(2,1)S(1)}, bf16[784,128]{1,0:T(8,128)(2,1)S(1)}, u32[]{:S(2)}, u32[]{:S(2)}) collective-permute-start(bf16[784,128]{1,0:T(8,128)(2,1)S(1)} %get-tuple-element.58), channel_id=1, source_target_pairs={{0,6},{1,7},{2,4},{3,5},{4,2},{5,3},{6,0},{7,1},{8,14},{9,15},{10,... | collective-permute-start | bytes 602120 | tf_op jit(solution)/shard_map/ppermute | solution.py:429
  23.4 17.5 %collective-permute-start.3 = (bf16[784,128]{1,0:T(8,128)(2,1)S(1)}, bf16[784,128]{1,0:T(8,128)(2,1)S(1)}, u32[]{:S(2)}, u32[]{:S(2)}) collective-permute-start(bf16[784,128]{1,0:T(8,128)(2,1)S(1)} %get-tuple-element.59), channel_id=1, source_target_pairs={{0,7},{1,6},{2,5},{3,4},{4,3},{5,2},{6,1},{7,0},{8,15},{9,14},{10,... | collective-permute-start | bytes 602120 | tf_op jit(solution)/shard_map/ppermute | solution.py:429
  25.2 1.3 %copy-start.5 = (bf16[768,768]{1,0:T(8,128)(2,1)S(1)}, bf16[768,768]{1,0:T(8,128)(2,1)}, u32[]{:S(2)}) copy-start(bf16[768,768]{1,0:T(8,128)(2,1)} %refs_8_.3) | copy-start | bytes 3538948
  26.4 1.3 %copy-start.6 = (bf16[768,768]{1,0:T(8,128)(2,1)S(1)}, bf16[768,768]{1,0:T(8,128)(2,1)}, u32[]{:S(2)}) copy-start(bf16[768,768]{1,0:T(8,128)(2,1)} %refs_9_.3) | copy-start | bytes 3538948
  27.7 1.3 %copy-start.7 = (bf16[768,768]{1,0:T(8,128)(2,1)S(1)}, bf16[768,768]{1,0:T(8,128)(2,1)}, u32[]{:S(2)}) copy-start(bf16[768,768]{1,0:T(8,128)(2,1)} %refs_10_.5) | copy-start | bytes 3538948
  29.0 1.3 %copy-start.8 = (bf16[768,768]{1,0:T(8,128)(2,1)S(1)}, bf16[768,768]{1,0:T(8,128)(2,1)}, u32[]{:S(2)}) copy-start(bf16[768,768]{1,0:T(8,128)(2,1)} %refs_11_.1) | copy-start | bytes 3538948
  30.2 1.3 %copy-start.9 = (bf16[768,768]{1,0:T(8,128)(2,1)S(1)}, bf16[768,768]{1,0:T(8,128)(2,1)}, u32[]{:S(2)}) copy-start(bf16[768,768]{1,0:T(8,128)(2,1)} %refs_12_.1) | copy-start | bytes 3538948
  31.5 1.3 %copy-start.10 = (bf16[768,768]{1,0:T(8,128)(2,1)S(1)}, bf16[768,768]{1,0:T(8,128)(2,1)}, u32[]{:S(2)}) copy-start(bf16[768,768]{1,0:T(8,128)(2,1)} %refs_13_.1) | copy-start | bytes 3538948
  32.8 8.1 %copy-start.11 = (bf16[768,768]{1,0:T(8,128)(2,1)S(1)}, bf16[768,768]{1,0:T(8,128)(2,1)}, u32[]{:S(2)}) copy-start(bf16[768,768]{1,0:T(8,128)(2,1)} %refs_13_.1) | copy-start | bytes 3538948
  40.9 9.6 %copy-start = (bf16[768,768]{1,0:T(8,128)(2,1)S(1)}, bf16[768,768]{1,0:T(8,128)(2,1)}, u32[]{:S(2)}) copy-start(bf16[768,768]{1,0:T(8,128)(2,1)} %refs_10_.7) | copy-start | bytes 3538948
  53.2 0.6 copy-start.2
  53.9 19.3 %collective-permute-start.7 = (bf16[4,16,768]{2,1,0:T(8,128)(2,1)S(1)}, bf16[4,16,768]{2,1,0:T(8,128)(2,1)S(1)}, u32[]{:S(2)}, u32[]{:S(2)}) collective-permute-start(bf16[4,16,768]{2,1,0:T(8,128)(2,1)S(1)} %get-tuple-element.78), channel_id=1, source_target_pairs={{0,4},{1,5},{2,6},{3,7},{4,0},{5,1},{6,2},{7,3},{8,12},{9,13},{10,... | collective-permute-start | bytes 294920 | tf_op jit(solution)/shard_map/ppermute | solution.py:429
  63.2 12.3 %collective-permute-start.9 = (bf16[4,16,768]{2,1,0:T(8,128)(2,1)S(1)}, bf16[4,16,768]{2,1,0:T(8,128)(2,1)S(1)}, u32[]{:S(2)}, u32[]{:S(2)}) collective-permute-start(bf16[4,16,768]{2,1,0:T(8,128)(2,1)S(1)} %get-tuple-element.81), channel_id=1, source_target_pairs={{0,5},{1,4},{2,7},{3,6},{4,1},{5,0},{6,3},{7,2},{8,13},{9,12},{10,... | collective-permute-start | bytes 294920 | tf_op jit(solution)/shard_map/ppermute | solution.py:429
  63.2 12.3 %collective-permute-start.11 = (bf16[4,16,768]{2,1,0:T(8,128)(2,1)S(1)}, bf16[4,16,768]{2,1,0:T(8,128)(2,1)S(1)}, u32[]{:S(2)}, u32[]{:S(2)}) collective-permute-start(bf16[4,16,768]{2,1,0:T(8,128)(2,1)S(1)} %get-tuple-element.84), channel_id=1, source_target_pairs={{0,6},{1,7},{2,4},{3,5},{4,2},{5,3},{6,0},{7,1},{8,14},{9,15},{10,... | collective-permute-start | bytes 294920 | tf_op jit(solution)/shard_map/ppermute | solution.py:429
  63.6 15.2 %collective-permute-start.13 = (bf16[4,16,768]{2,1,0:T(8,128)(2,1)S(1)}, bf16[4,16,768]{2,1,0:T(8,128)(2,1)S(1)}, u32[]{:S(2)}, u32[]{:S(2)}) collective-permute-start(bf16[4,16,768]{2,1,0:T(8,128)(2,1)S(1)} %get-tuple-element.87), channel_id=1, source_target_pairs={{0,7},{1,6},{2,5},{3,4},{4,3},{5,2},{6,1},{7,0},{8,15},{9,14},{10,... | collective-permute-start | bytes 294920 | tf_op jit(solution)/shard_map/ppermute | solution.py:429
  67.9 14.2 %collective-permute-start.15 = (bf16[4,16,768]{2,1,0:T(8,128)(2,1)S(1)}, bf16[4,16,768]{2,1,0:T(8,128)(2,1)S(1)}, u32[]{:S(2)}, u32[]{:S(2)}) collective-permute-start(bf16[4,16,768]{2,1,0:T(8,128)(2,1)S(1)} %get-tuple-element.90), channel_id=1, source_target_pairs={{0,1},{1,0},{2,3},{3,2},{4,5},{5,4},{6,7},{7,6},{8,9},{9,8},{10,11... | collective-permute-start | bytes 294920 | tf_op jit(solution)/shard_map/ppermute | solution.py:429
  71.2 0.6 copy-start.3
  73.2 19.4 %copy-start.12 = (bf16[4,16,768]{2,1,0:T(8,128)(2,1)}, bf16[4,16,768]{2,1,0:T(8,128)(2,1)S(1)}, u32[]{:S(2)}) copy-start(bf16[4,16,768]{2,1,0:T(8,128)(2,1)S(1)} %collective-permute-done.7.refs_0_) | copy-start | bytes 294916
  73.2 10.9 %collective-permute-start.17 = (bf16[4,16,768]{2,1,0:T(8,128)(2,1)S(1)}, bf16[4,16,768]{2,1,0:T(8,128)(2,1)S(1)}, u32[]{:S(2)}, u32[]{:S(2)}) collective-permute-start(bf16[4,16,768]{2,1,0:T(8,128)(2,1)S(1)} %get-tuple-element.93), channel_id=1, source_target_pairs={{0,2},{1,3},{2,0},{3,1},{4,6},{5,7},{6,4},{7,5},{8,10},{9,11},{10,... | collective-permute-start | bytes 294920 | tf_op jit(solution)/shard_map/ppermute | solution.py:429
  75.5 17.2 %copy-start.13 = (bf16[4,16,768]{2,1,0:T(8,128)(2,1)}, bf16[4,16,768]{2,1,0:T(8,128)(2,1)S(1)}, u32[]{:S(2)}) copy-start(bf16[4,16,768]{2,1,0:T(8,128)(2,1)S(1)} %collective-permute-done.9.refs_1_) | copy-start | bytes 294916
  75.5 10.4 %collective-permute-start.19 = (bf16[4,16,768]{2,1,0:T(8,128)(2,1)S(1)}, bf16[4,16,768]{2,1,0:T(8,128)(2,1)S(1)}, u32[]{:S(2)}, u32[]{:S(2)}) collective-permute-start(bf16[4,16,768]{2,1,0:T(8,128)(2,1)S(1)} %get-tuple-element.96), channel_id=1, source_target_pairs={{0,3},{1,2},{2,1},{3,0},{4,7},{5,6},{6,5},{7,4},{8,11},{9,10},{10,... | collective-permute-start | bytes 294920 | tf_op jit(solution)/shard_map/ppermute | solution.py:429
  75.5 17.2 %copy-start.14 = (bf16[4,16,768]{2,1,0:T(8,128)(2,1)}, bf16[4,16,768]{2,1,0:T(8,128)(2,1)S(1)}, u32[]{:S(2)}) copy-start(bf16[4,16,768]{2,1,0:T(8,128)(2,1)S(1)} %collective-permute-done.11.refs_2_) | copy-start | bytes 294916
  75.5 13.8 %collective-permute-start.8 = (bf16[4,16,768]{2,1,0:T(8,128)(2,1)S(1)}, bf16[4,16,768]{2,1,0:T(8,128)(2,1)S(1)}, u32[]{:S(2)}, u32[]{:S(2)}) collective-permute-start(bf16[4,16,768]{2,1,0:T(8,128)(2,1)S(1)} %get-tuple-element.79), channel_id=1, source_target_pairs={{0,4},{1,5},{2,6},{3,7},{4,0},{5,1},{6,2},{7,3},{8,12},{9,13},{10,... | collective-permute-start | bytes 294920 | tf_op jit(solution)/shard_map/ppermute | solution.py:429
  78.8 13.9 %copy-start.15 = (bf16[4,16,768]{2,1,0:T(8,128)(2,1)}, bf16[4,16,768]{2,1,0:T(8,128)(2,1)S(1)}, u32[]{:S(2)}) copy-start(bf16[4,16,768]{2,1,0:T(8,128)(2,1)S(1)} %collective-permute-done.13.refs_3_) | copy-start | bytes 294916
  78.8 13.8 %collective-permute-start.10 = (bf16[4,16,768]{2,1,0:T(8,128)(2,1)S(1)}, bf16[4,16,768]{2,1,0:T(8,128)(2,1)S(1)}, u32[]{:S(2)}, u32[]{:S(2)}) collective-permute-start(bf16[4,16,768]{2,1,0:T(8,128)(2,1)S(1)} %get-tuple-element.82), channel_id=1, source_target_pairs={{0,5},{1,4},{2,7},{3,6},{4,1},{5,0},{6,3},{7,2},{8,13},{9,12},{10,... | collective-permute-start | bytes 294920 | tf_op jit(solution)/shard_map/ppermute | solution.py:429
  82.1 10.6 %copy-start.16 = (bf16[4,16,768]{2,1,0:T(8,128)(2,1)}, bf16[4,16,768]{2,1,0:T(8,128)(2,1)S(1)}, u32[]{:S(2)}) copy-start(bf16[4,16,768]{2,1,0:T(8,128)(2,1)S(1)} %collective-permute-done.15.refs_4_) | copy-start | bytes 294916
  82.1 12.8 %collective-permute-start.12 = (bf16[4,16,768]{2,1,0:T(8,128)(2,1)S(1)}, bf16[4,16,768]{2,1,0:T(8,128)(2,1)S(1)}, u32[]{:S(2)}, u32[]{:S(2)}) collective-permute-start(bf16[4,16,768]{2,1,0:T(8,128)(2,1)S(1)} %get-tuple-element.85), channel_id=1, source_target_pairs={{0,6},{1,7},{2,4},{3,5},{4,2},{5,3},{6,0},{7,1},{8,14},{9,15},{10,... | collective-permute-start | bytes 294920 | tf_op jit(solution)/shard_map/ppermute | solution.py:429
  84.1 8.5 %copy-start.17 = (bf16[4,16,768]{2,1,0:T(8,128)(2,1)}, bf16[4,16,768]{2,1,0:T(8,128)(2,1)S(1)}, u32[]{:S(2)}) copy-start(bf16[4,16,768]{2,1,0:T(8,128)(2,1)S(1)} %collective-permute-done.17.refs_5_) | copy-start | bytes 294916
  84.1 10.8 %collective-permute-start.14 = (bf16[4,16,768]{2,1,0:T(8,128)(2,1)S(1)}, bf16[4,16,768]{2,1,0:T(8,128)(2,1)S(1)}, u32[]{:S(2)}, u32[]{:S(2)}) collective-permute-start(bf16[4,16,768]{2,1,0:T(8,128)(2,1)S(1)} %get-tuple-element.88), channel_id=1, source_target_pairs={{0,7},{1,6},{2,5},{3,4},{4,3},{5,2},{6,1},{7,0},{8,15},{9,14},{10,... | collective-permute-start | bytes 294920 | tf_op jit(solution)/shard_map/ppermute | solution.py:429
  85.8 6.8 %copy-start.18 = (bf16[4,16,768]{2,1,0:T(8,128)(2,1)}, bf16[4,16,768]{2,1,0:T(8,128)(2,1)S(1)}, u32[]{:S(2)}) copy-start(bf16[4,16,768]{2,1,0:T(8,128)(2,1)S(1)} %collective-permute-done.19.refs_6_) | copy-start | bytes 294916
  85.8 9.1 %collective-permute-start.16 = (bf16[4,16,768]{2,1,0:T(8,128)(2,1)S(1)}, bf16[4,16,768]{2,1,0:T(8,128)(2,1)S(1)}, u32[]{:S(2)}, u32[]{:S(2)}) collective-permute-start(bf16[4,16,768]{2,1,0:T(8,128)(2,1)S(1)} %get-tuple-element.91), channel_id=1, source_target_pairs={{0,1},{1,0},{2,3},{3,2},{4,5},{5,4},{6,7},{7,6},{8,9},{9,8},{10,11... | collective-permute-start | bytes 294920 | tf_op jit(solution)/shard_map/ppermute | solution.py:429
  89.3 5.5 %copy-start.19 = (bf16[4,16,768]{2,1,0:T(8,128)(2,1)}, bf16[4,16,768]{2,1,0:T(8,128)(2,1)S(1)}, u32[]{:S(2)}) copy-start(bf16[4,16,768]{2,1,0:T(8,128)(2,1)S(1)} %collective-permute-done.8.refs_0_) | copy-start | bytes 294916
  89.3 5.6 %collective-permute-start.18 = (bf16[4,16,768]{2,1,0:T(8,128)(2,1)S(1)}, bf16[4,16,768]{2,1,0:T(8,128)(2,1)S(1)}, u32[]{:S(2)}, u32[]{:S(2)}) collective-permute-start(bf16[4,16,768]{2,1,0:T(8,128)(2,1)S(1)} %get-tuple-element.94), channel_id=1, source_target_pairs={{0,2},{1,3},{2,0},{3,1},{4,6},{5,7},{6,4},{7,5},{8,10},{9,11},{10,... | collective-permute-start | bytes 294920 | tf_op jit(solution)/shard_map/ppermute | solution.py:429
  92.6 2.2 %copy-start.20 = (bf16[4,16,768]{2,1,0:T(8,128)(2,1)}, bf16[4,16,768]{2,1,0:T(8,128)(2,1)S(1)}, u32[]{:S(2)}) copy-start(bf16[4,16,768]{2,1,0:T(8,128)(2,1)S(1)} %collective-permute-done.10.refs_1_) | copy-start | bytes 294916
  92.6 5.5 %collective-permute-start.20 = (bf16[4,16,768]{2,1,0:T(8,128)(2,1)S(1)}, bf16[4,16,768]{2,1,0:T(8,128)(2,1)S(1)}, u32[]{:S(2)}, u32[]{:S(2)}) collective-permute-start(bf16[4,16,768]{2,1,0:T(8,128)(2,1)S(1)} %get-tuple-element.97), channel_id=1, source_target_pairs={{0,3},{1,2},{2,1},{3,0},{4,7},{5,6},{6,5},{7,4},{8,11},{9,10},{10,... | collective-permute-start | bytes 294920 | tf_op jit(solution)/shard_map/ppermute | solution.py:429
  94.9 3.3 %copy-start.21 = (bf16[4,16,768]{2,1,0:T(8,128)(2,1)}, bf16[4,16,768]{2,1,0:T(8,128)(2,1)S(1)}, u32[]{:S(2)}) copy-start(bf16[4,16,768]{2,1,0:T(8,128)(2,1)S(1)} %collective-permute-done.12.refs_2_) | copy-start | bytes 294916
  94.9 3.2 %copy-start.22 = (bf16[4,16,768]{2,1,0:T(8,128)(2,1)}, bf16[4,16,768]{2,1,0:T(8,128)(2,1)S(1)}, u32[]{:S(2)}) copy-start(bf16[4,16,768]{2,1,0:T(8,128)(2,1)S(1)} %collective-permute-done.14.refs_3_) | copy-start | bytes 294916
  94.9 3.2 %copy-start.23 = (bf16[4,16,768]{2,1,0:T(8,128)(2,1)}, bf16[4,16,768]{2,1,0:T(8,128)(2,1)S(1)}, u32[]{:S(2)}) copy-start(bf16[4,16,768]{2,1,0:T(8,128)(2,1)S(1)} %collective-permute-done.16.refs_4_) | copy-start | bytes 294916
  94.9 3.2 %copy-start.24 = (bf16[4,16,768]{2,1,0:T(8,128)(2,1)}, bf16[4,16,768]{2,1,0:T(8,128)(2,1)S(1)}, u32[]{:S(2)}) copy-start(bf16[4,16,768]{2,1,0:T(8,128)(2,1)S(1)} %collective-permute-done.18.refs_5_) | copy-start | bytes 294916
  98.1 0.6 copy-start.25

commit v4 on v3

--- a/solution.py
+++ b/solution.py
@@ -144,10 +144,6 @@
     return jnp.dot(a, b, preferred_element_type=jnp.float32)
 
 
-def diagonal(n, m):
-    return lax.broadcasted_iota(jnp.int32, (n, m), 0) == lax.broadcasted_iota(jnp.int32, (n, m), 1)
-
-
 def low_columns(shape, axis):
     return lax.broadcasted_iota(jnp.int32, shape, axis) % 8 < 4
 
@@ -176,71 +172,89 @@
 ORDER = (4, 5, 6, 7, 1, 2, 3, 0)
 
 
-def pack_kernel(distances, me_ref, marks_ref, fields_ref, *refs):
-    outs, (held, sems) = refs[: len(distances)], refs[len(distances) :]
+def pack_kernel(distances, me_ref, marks_ref, fields_ref, *outs):
     me = me_ref[0]
     tiles = fields_ref.shape[-1] // 128
-    copies = []
+    marks = marks_ref[...].astype(jnp.float32)
+    marks = jnp.concatenate([marks, jnp.zeros((16, 128 - marks.shape[1]), jnp.float32)], 1).astype(jnp.bfloat16)
     for i, d in enumerate(distances):
         there = jnp.bitwise_xor(me, d)
-        copies.append(pltpu.make_async_copy(fields_ref.at[pl.ds(there * 8, 8)], held.at[i], sems.at[i]))
-        copies[-1].start()
-    for i, d in enumerate(distances):
-        there = jnp.bitwise_xor(me, d)
-        row = marks_ref[pl.ds(there, 1), :]
-        outs[i][128 * tiles :, :] = jnp.broadcast_to(row, (16, 128)).astype(jnp.bfloat16)
-        copies[i].wait()
-        piece = held[i].reshape(128, 128 * tiles)
+        piece = fields_ref[pl.ds(there * 8, 8)].reshape(128, 128 * tiles)
         for t in range(tiles):
             outs[i][128 * t : 128 * t + 128, :] = piece[:, 128 * t : 128 * t + 128]
+        outs[i][128 * tiles :, :] = marks
 
 
 def pack(distances, me, marks, fields):
-    cols, width = fields.shape[1:]
+    width = fields.shape[-1]
     vmem = pl.BlockSpec(memory_space=pltpu.VMEM)
     piece = jax.ShapeDtypeStruct((width + 16, 128), jnp.bfloat16)
     n = len(distances)
     return pl.pallas_call(
         functools.partial(pack_kernel, distances),
         out_shape=(piece,) * n,
-        in_specs=[pl.BlockSpec(memory_space=pltpu.SMEM), vmem, pl.BlockSpec(memory_space=pltpu.HBM)],
+        in_specs=[pl.BlockSpec(memory_space=pltpu.SMEM), vmem, vmem],
         out_specs=(vmem,) * n,
-        scratch_shapes=[pltpu.VMEM((n, 8, cols, width), jnp.bfloat16), pltpu.SemaphoreType.DMA((n,))],
         compiler_params=pltpu.CompilerParams(vmem_limit_bytes=16 * 1024 * 1024),
         cost_estimate=pl.CostEstimate(flops=n * 200000, bytes_accessed=n * 400000, transcendentals=0),
         name="pack",
     )(me, marks, fields)
 
 
-def unpacked(piece):
+def hold_kernel(*refs):
+    *weights, out_ref, sems = refs
+    copies = [pltpu.make_async_copy(w, out_ref.at[i], sems.at[i]) for i, w in enumerate(weights)]
+    for copy in copies:
+        copy.start()
+    for copy in copies:
+        copy.wait()
+
+
+def hold(weights):
+    width = weights[0].shape[0]
+    return pl.pallas_call(
+        hold_kernel,
+        out_shape=jax.ShapeDtypeStruct((len(weights), width, width), jnp.bfloat16),
+        in_specs=[pl.BlockSpec(memory_space=pl.ANY)] * len(weights),
+        out_specs=pl.BlockSpec(memory_space=pltpu.VMEM),
+        scratch_shapes=[pltpu.SemaphoreType.DMA((len(weights),))],
+        compiler_params=pltpu.CompilerParams(vmem_limit_bytes=16 * 1024 * 1024),
+        cost_estimate=pl.CostEstimate(flops=0, bytes_accessed=32 << 20, transcendentals=0),
+        name="hold",
+    )(*weights)
+
+
+def unpacked(me, piece):
     tiles = (piece.shape[0] - 16) // 128
     lanes = [piece[128 * t : 128 * t + 128] for t in range(tiles)]
-    row = piece[128 * tiles :].astype(jnp.float32)[:1]
-    marks = jnp.sum(jnp.where(diagonal(128, 128), row, 0.0), 1, keepdims=True)
-    marks = jnp.broadcast_to(marks, (128, 128)).astype(jnp.bfloat16)
-    whole = jnp.concatenate(lanes + [marks], 1).astype(jnp.float32).reshape(8, 2, 8, 128 * tiles + 128)
+    marks = pltpu.roll(piece[128 * tiles :].astype(jnp.float32), jnp.bitwise_and(128 - 8 * me, 127), 1)
+    marks = jnp.concatenate([jnp.broadcast_to(marks[:, r : r + 1], (16, 128)) for r in range(8)], 0)
+    whole = jnp.concatenate(lanes + [marks.astype(jnp.bfloat16)], 1).astype(jnp.float32)
+    whole = whole.reshape(8, 2, 8, 128 * tiles + 128)
     return whole[:, 0], whole[:, 1]
 
 
+STAGES = ((3, 2), (8, 8), (5, 6))
+
+
 def window_kernel(stage, me_ref, *refs):
-    if stage == 0:
-        pieces, refs = refs[:4], refs[4:]
-    else:
-        (*pieces, edge0_ref, edge3_ref, tail_ref), refs = refs[:7], refs[7:]
-    wq, wk, wv, wo, wq2, wk2, wv2 = refs[:7]
-    if stage == 0:
-        y_ref, q2_ref, k2_ref, v2_ref, m_ref, edge0_ref, edge3_ref, tail_ref = refs[7:15]
-        refs = refs[15:]
-    else:
-        y_ref, q2_ref, k2_ref, v2_ref, m_ref = refs[7:12]
-        refs = refs[12:]
-    placed, q_s, k_s, v_s, o_s, rows_s = refs
+    pieces = refs[: (2, 4, 2)[stage]]
+    refs = refs[len(pieces) :]
+    carried = refs[: (0, 2, 5)[stage]]
+    refs = refs[len(carried) :]
+    weights, y_ref, q2_ref, k2_ref, v2_ref, m_ref = refs[:6]
+    wq, wk, wv, wo, wq2, wk2, wv2 = (weights.at[i] for i in range(7))
+    refs = refs[6:]
+    passed = refs[: (3, 2, 0)[stage]]
+    placed, q_s, k_s, v_s, o_s, rows_s = refs[len(passed) :]
     width = wq.shape[0]
     scale = (width // HEADS) ** (-0.5)
-    low = jnp.bitwise_and(me_ref[0], 3)
-    for d in range(4):
-        placed[jnp.bitwise_xor(low, d)] = pieces[d][...]
-    columns = [unpacked(placed[l]) for l in range(4)]
+    me = me_ref[0]
+    upper = jnp.bitwise_and(me, 2) > 0
+    low = jnp.bitwise_and(me, len(pieces) - 1)
+    for d, piece in enumerate(pieces):
+        placed[jnp.bitwise_xor(low, d)] = piece[...]
+    columns = [unpacked(me, placed[l]) for l in range(len(pieces))]
     mask = low_columns((8, 8, width + 128), 1)
     full = (64, width + 128)
 
@@ -250,17 +264,26 @@
     def straddling_window(left, right):
         return jnp.where(mask, right, left).reshape(full)
 
+    def either(if_upper, if_lower):
+        return jnp.where(upper, if_upper, if_lower)
+
     windows = [whole_window(0)]
-    for l in range(1, 4):
+    for l in range(1, len(pieces)):
         windows += [straddling_window(columns[l - 1][1], columns[l][0]), whole_window(l)]
-    if stage == 0:
-        edge0_ref[...] = columns[0][0].reshape(full)
-        edge3_ref[...] = columns[3][1].reshape(full)
-    else:
+    first, last = columns[0][0], columns[-1][1]
+    edges = [a[...].reshape(8, 8, width + 128) for a in carried[:4]]
+    if stage < 2:
+        passed[0][...] = first.reshape(full)
+        passed[1][...] = last.reshape(full)
+    if stage == 1:
+        second_first, second_last = edges
+        windows.append(straddling_window(either(second_last, last), either(first, second_first)))
+    if stage == 2:
+        second_first, second_last, own_first, own_last = edges
         windows = (
-            [straddling_window(edge3_ref[...].reshape(8, 8, -1), columns[0][0])]
+            [straddling_window(either(last, second_last), either(second_first, first))]
             + windows
-            + [straddling_window(columns[3][1], edge0_ref[...].reshape(8, 8, -1))]
+            + [straddling_window(either(own_last, last), either(first, own_first))]
         )
     count = len(windows)
     x = jnp.concatenate([w[:, :width] for w in windows], 0)
@@ -275,17 +298,17 @@
         for lanes, out in zip(PAIRS, outs):
             o_s[here, lanes] = out
     y = (x + dot_f32(o_s[...], wo[...])).astype(jnp.bfloat16).astype(jnp.float32)
-    first = 0
-    if stage == 1:
-        first = 1
-        rows_s[:, :8, :] = tail_ref[...]
+    skip = 0
+    if stage == 2:
+        skip = 1
+        rows_s[:, :8, :] = carried[4][...]
     for w in range(count):
         for r in range(8):
             at = 64 * w + 8 * r
-            to = 8 * (w + first)
+            to = 8 * (w + skip)
             if stage == 0 and w == count - 1:
-                tail_ref[r, :, :width] = y[at : at + 8]
-                tail_ref[r, :, width:] = marks[w][8 * r : 8 * r + 8]
+                passed[2][r, :, :width] = y[at : at + 8]
+                passed[2][r, :, width:] = marks[w][8 * r : 8 * r + 8]
             else:
                 rows_s[r, to : to + 8, :width] = y[at : at + 8]
                 rows_s[r, to : to + 8, width:] = marks[w][8 * r : 8 * r + 8]
@@ -300,24 +323,24 @@
 
 
 def window_layer(stage, me, pieces, carried, weights):
-    width = weights[0].shape[0]
-    tokens = 64 * (7, 9)[stage]
-    columns = 8 * (6, 10)[stage]
-    half = jax.ShapeDtypeStruct((8, columns, width), jnp.bfloat16)
+    width = weights.shape[1]
+    tokens = 64 * STAGES[stage][0]
+    columns = 8 * STAGES[stage][1]
+    part = jax.ShapeDtypeStruct((8, columns, width), jnp.bfloat16)
     marks = jax.ShapeDtypeStruct((8, columns, 128), jnp.bfloat16)
     edge = jax.ShapeDtypeStruct((64, width + 128), jnp.float32)
     tail = jax.ShapeDtypeStruct((8, 8, width + 128), jnp.float32)
-    outs = (half,) * 4 + (marks,) + ((edge, edge, tail) if stage == 0 else ())
+    outs = (part,) * 4 + (marks,) + ((edge, edge, tail), (edge, edge), ())[stage]
     vmem = pl.BlockSpec(memory_space=pltpu.VMEM)
     work = pltpu.VMEM((tokens, width), jnp.bfloat16)
-    inputs = [*pieces, *carried, *weights]
+    inputs = [*pieces, *carried, weights]
     return pl.pallas_call(
         functools.partial(window_kernel, stage),
         out_shape=outs,
         in_specs=[pl.BlockSpec(memory_space=pltpu.SMEM)] + [vmem] * len(inputs),
         out_specs=(vmem,) * len(outs),
         scratch_shapes=[
-            pltpu.VMEM((4, width + 16, 128), jnp.bfloat16),
+            pltpu.VMEM((len(pieces), width + 16, 128), jnp.bfloat16),
             work, work, work, work,
             pltpu.VMEM((8, columns, width + 128), jnp.float32),
         ],
@@ -329,70 +352,68 @@
     )(me, *inputs)
 
 
-def row_kernel(rows, me_ref, *refs):
-    (yb, qb, kb, vb, mb, ya, qa, ka, va, ma, wo), refs = refs[:11], refs[11:]
+def row_kernel(start, rows, me_ref, *refs):
+    parts, wo, refs = (refs[:5], refs[5:10], refs[10:15]), refs[15].at[7], refs[16:]
     outs, (o_s, placed) = refs[:8], refs[8:]
     width = wo.shape[0]
-    length = ya.shape[1] + yb.shape[1]
+    length = 128
+
+    def row(i, r, lanes=slice(None)):
+        return jnp.concatenate([part[i][start + r, :, lanes] for part in parts], 0)
+
     for r in range(rows):
         here = slice(length * r, length * r + length)
-        marks = jnp.concatenate([ma[r], mb[r]], 0).astype(jnp.float32)
-        heads = attend(
-            *(
-                [jnp.concatenate([a[r, :, lanes], b[r, :, lanes]], 0) for lanes in PAIRS]
-                for a, b in ((qa, qb), (ka, kb), (va, vb))
-            ),
-            marks,
-        )
+        heads = attend(*([row(i, r, lanes) for lanes in PAIRS] for i in (1, 2, 3)), row(4, r).astype(jnp.float32))
         for lanes, out in zip(PAIRS, heads):
             o_s[here, lanes] = out
     added = dot_f32(o_s[...], wo[...])
     mask = low_columns((8, width), 0)
+    me = me_ref[0]
+    upper = jnp.bitwise_and(me, 2) > 0
     for r in range(rows):
-        before = jnp.concatenate([ya[r], yb[r]], 0).astype(jnp.float32)
-        f = before + added[length * r : length * r + length]
+        f = row(0, r).astype(jnp.float32) + added[length * r : length * r + length]
         tiles = [f[8 * w : 8 * w + 8] for w in range(16)]
+        own = tiles[2:9]
+        second, third = (tiles[0], tiles[1], tiles[10]), tiles[12:15]
+        at_second, middle, at_third = tiles[9], tiles[11], tiles[15]
+        after_own = jnp.where(upper, at_third, at_second)
+        before_own = jnp.where(upper, at_second, at_third)
+        whole = [before_own, *own, after_own]
+        whole += [jnp.where(upper, middle, after_own), *second, jnp.where(upper, before_own, middle)]
+        whole += [jnp.where(upper, after_own, middle), *third, jnp.where(upper, middle, before_own)]
         for l in range(8):
-            placed[l, r] = jnp.concatenate(
-                [
-                    jnp.where(mask, tiles[(2 * l - 1) % 16], tiles[2 * l]),
-                    jnp.where(mask, tiles[2 * l], tiles[2 * l + 1]),
-                ],
-                0,
-            ).astype(jnp.bfloat16)
-    low = jnp.bitwise_and(me_ref[0], 3)
+            at = 2 * l if l < 4 else (9, 11, 14, 16)[l - 4]
+            before, a, after = whole[at : at + 3]
+            piece = jnp.concatenate([jnp.where(mask, before, a), jnp.where(mask, a, after)], 0)
+            placed[l, r] = piece.astype(jnp.bfloat16)
     for i, d in enumerate(ORDER):
-        outs[i][...] = placed[jnp.bitwise_xor(low, d)]
-
-
-def row_layer(start, rows, me, halves, w_out):
-    width = w_out.shape[0]
-    step = start // rows
+        if d < 4:
+            outs[i][...] = placed[jnp.bitwise_xor(jnp.bitwise_and(me, 3), d)]
+        else:
+            outs[i][...] = placed[jnp.bitwise_xor(jnp.bitwise_and(me, 1), d)]
+
+
+def row_layer(start, rows, me, parts, weights):
+    width = weights.shape[1]
     length = 128
-
-    def block(a):
-        return pl.BlockSpec((rows,) + a.shape[1:], lambda i: (step, 0, 0))
-
     piece = jax.ShapeDtypeStruct((rows, 16, width), jnp.bfloat16)
+    vmem = pl.BlockSpec(memory_space=pltpu.VMEM)
     return pl.pallas_call(
-        functools.partial(row_kernel, rows),
+        functools.partial(row_kernel, start, rows),
         out_shape=(piece,) * 8,
-        grid=(1,),
-        in_specs=[pl.BlockSpec(memory_space=pltpu.SMEM)]
-        + [block(a) for a in halves]
-        + [pl.BlockSpec((width, width), lambda i: (0, 0))],
-        out_specs=(pl.BlockSpec(piece.shape, lambda i: (0, 0, 0)),) * 8,
+        in_specs=[pl.BlockSpec(memory_space=pltpu.SMEM)] + [vmem] * (len(parts) + 1),
+        out_specs=(vmem,) * 8,
         scratch_shapes=[
             pltpu.VMEM((rows * length, width), jnp.bfloat16),
             pltpu.VMEM((8, rows, 16, width), jnp.bfloat16),
         ],
-        compiler_params=pltpu.CompilerParams(vmem_limit_bytes=32 * 1024 * 1024),
+        compiler_params=pltpu.CompilerParams(vmem_limit_bytes=36 * 1024 * 1024),
         cost_estimate=pl.CostEstimate(
             flops=2 * rows * length * width * (width + 1024), bytes_accessed=8 << 20,
             transcendentals=rows * length * length * HEADS,
         ),
         name="row_layer",
-    )(me, *halves, w_out)
+    )(me, *parts, weights)
 
 
 def place_kernel(start, rows, me_ref, *refs):
@@ -433,24 +454,24 @@
     fields, ocean, w_query1, w_key1, w_value1, w_out1, w_query2, w_key2, w_value2, w_out2
 ):
     me = lax.axis_index("lon").astype(jnp.int32).reshape(1)
-    marks = ocean.reshape(8, 128).astype(jnp.float32)
-    weights = (w_query1, w_key1, w_value1, w_out1, w_query2, w_key2, w_value2)
-
-    packed = dict(zip(ORDER, pack(ORDER, me, marks, fields)))
+    weights = hold((w_query1, w_key1, w_value1, w_out1, w_query2, w_key2, w_value2, w_out2))
+
+    packed = dict(zip(ORDER, pack(ORDER, me, ocean.T, fields)))
     got = {d: exchanged(packed[d], d) if d else packed[d] for d in ORDER}
-    own = window_layer(0, me, [got[d] for d in range(4)], (), weights)
-    other = window_layer(1, me, [got[d] for d in range(4, 8)], own[5:], weights)
-    halves = (*other, *own[:5])
+    second = window_layer(0, me, [got[4], got[5]], (), weights)
+    own = window_layer(1, me, [got[d] for d in range(4)], second[5:7], weights)
+    third = window_layer(2, me, [got[6], got[7]], (*second[5:7], *own[5:], second[7]), weights)
+    parts = (*second[:5], *own[:5], *third)
     start, out, back = 0, None, None
     for size in GROUPS:
-        sent = list(row_layer(start, size, me, halves, w_out2))
+        sent = list(row_layer(start, size, me, parts, weights))
         if back is not None:
             for i in range(7):
                 sent[i], back[i] = lax.optimization_barrier((sent[i], back[i]))
-            out = place(start - size, size, me, back, out, fields.shape)
+            out = place(start - before, before, me, back, out, fields.shape)
         back = [exchanged(piece, d) if d else piece for d, piece in zip(ORDER, sent)]
-        start += size
-    return place(start - size, size, me, back, out, fields.shape)
+        start, before = start + size, size
+    return place(start - before, before, me, back, out, fields.shape)
 
 
 def on_device(fields, *rest):

time: 102 us -> 94.6 us (0.927)
  waiting for transfers between devices: 20.6 us -> 11.7 us
  local copies, waits for them, and re-layouts: 11.1 us -> 12.9 us
    ppermute x21, waiting for transfers between devices: 20.6 us -> 11.7 us  [exchanged(): return lax.ppermute(piece, 'lon', [(s, s ^ distance) for s in range(count)])]
    pallas_call x1, Pallas kernels: 2.3 us -> 0.21 us  [pack(): pl.pallas_call(functools.partial(pack_kernel, distances), out_shape=(piec...]
    pallas_call x2 -> x3, Pallas kernels: 5.45 us -> 7.48 us  [the longest x2 5.48 us: row_layer(): pl.pallas_call(functools.partial(row_kernel, start, rows), out_shape=(pie...]
    unnamed x52, local copies, waits for them, and re-layouts: 11 us -> 12.9 us
    pallas_call x2 -> x3, Pallas kernels: 16.4 us -> 17.4 us  [window_layer(): pl.pallas_call(functools.partial(window_kernel, stage), out_shape=outs, i...]
  transfers between devices with their start and end apart: 21 -> 21, of which waited for: 8 -> 7; matrix products, arithmetic and copies ran while one was open for 0% -> 0% of each run, Pallas kernels for 12% -> 20%
where the time goes in v4:
time: 94.6 us; the launch traced here: 94.1 us
  starting transfers between devices  39.6 us (42%)
  Pallas kernels  29.4 us (31%)
  local copies, waits for them, and re-layouts  12.9 us (14%)
  waiting for transfers between devices  11.7 us (12%)
    ppermute x21, starting transfers between devices, exchanged(): return lax.ppermute(piece, 'lon', [(s, s ^ distance) for s in range(count)])  39.6 us
    pallas_call x3, Pallas kernels, window_layer(): pl.pallas_call(functools.partial(window_kernel, stage), out_shape=outs, i...  17.4 us
    unnamed x52, local copies, waits for them, and re-layouts  12.9 us
    ppermute x21, waiting for transfers between devices, exchanged(): return lax.ppermute(piece, 'lon', [(s, s ^ distance) for s in range(count)])  11.7 us
    pallas_call x2, Pallas kernels, row_layer(): pl.pallas_call(functools.partial(row_kernel, start, rows), out_shape=(pie...  5.48 us
    pallas_call x2, Pallas kernels, place(): pl.pallas_call(functools.partial(place_kernel, start, rows), out_shape=ja...  4.3 us
    pallas_call x1, Pallas kernels, hold(): pl.pallas_call(hold_kernel, out_shape=jax.ShapeDtypeStruct((len(weights),...  2 us
  transfers between devices with their start and end apart: 21, of which 7 were waited for; matrix products, arithmetic and copies ran while one was open for 0% of the time, Pallas kernels for 20%

profile of v4, /device:TPU:0, one launch (start us, length us, event | category | flops | bytes accessed | tf_op | source)
XLA Modules:
  0.0 94.1 jit_solution(14831471651279591431)
XLA Ops:
  0.0 1.4 %copy-done = bf16[64,16,768]{2,1,0:T(8,128)(2,1)S(1)} copy-done((bf16[64,16,768]{2,1,0:T(8,128)(2,1)S(1)}, bf16[64,16,768]{2,1,0:T(8,128)(2,1)}, u32[]{:S(2)}) %copy-start) | copy-done | bytes 1572888
  1.4 0.7 copy-done.11
  2.1 0.2 pack.1
  2.3 4.1 %collective-permute-start = (bf16[784,128]{1,0:T(8,128)(2,1)S(1)}, bf16[784,128]{1,0:T(8,128)(2,1)S(1)}, u32[]{:S(2)}, u32[]{:S(2)}) collective-permute-start(bf16[784,128]{1,0:T(8,128)(2,1)S(1)} %get-tuple-element.63), channel_id=1, source_target_pairs={{0,4},{1,5},{2,6},{3,7},{4,0},{5,1},{6,2},{7,3},{8,12},{9,13},{10,... | collective-permute-start | bytes 602120 | tf_op jit(solution)/shard_map/ppermute | solution.py:450
  6.4 1.3 %collective-permute-start.1 = (bf16[784,128]{1,0:T(8,128)(2,1)S(1)}, bf16[784,128]{1,0:T(8,128)(2,1)S(1)}, u32[]{:S(2)}, u32[]{:S(2)}) collective-permute-start(bf16[784,128]{1,0:T(8,128)(2,1)S(1)} %get-tuple-element.64), channel_id=1, source_target_pairs={{0,5},{1,4},{2,7},{3,6},{4,1},{5,0},{6,3},{7,2},{8,13},{9,12},{10,... | collective-permute-start | bytes 602120 | tf_op jit(solution)/shard_map/ppermute | solution.py:450
  7.7 0.2 collective-permute-start.2
  8.0 1.8 %collective-permute-start.3 = (bf16[784,128]{1,0:T(8,128)(2,1)S(1)}, bf16[784,128]{1,0:T(8,128)(2,1)S(1)}, u32[]{:S(2)}, u32[]{:S(2)}) collective-permute-start(bf16[784,128]{1,0:T(8,128)(2,1)S(1)} %get-tuple-element.72), channel_id=1, source_target_pairs={{0,2},{1,3},{2,0},{3,1},{4,6},{5,7},{6,4},{7,5},{8,10},{9,11},{10,... | collective-permute-start | bytes 602120 | tf_op jit(solution)/shard_map/ppermute | solution.py:450
  9.8 1.4 %collective-permute-start.4 = (bf16[784,128]{1,0:T(8,128)(2,1)S(1)}, bf16[784,128]{1,0:T(8,128)(2,1)S(1)}, u32[]{:S(2)}, u32[]{:S(2)}) collective-permute-start(bf16[784,128]{1,0:T(8,128)(2,1)S(1)} %get-tuple-element.73), channel_id=1, source_target_pairs={{0,3},{1,2},{2,1},{3,0},{4,7},{5,6},{6,5},{7,4},{8,11},{9,10},{10,... | collective-permute-start | bytes 602120 | tf_op jit(solution)/shard_map/ppermute | solution.py:450
  11.2 1.3 %copy-done.2 = bf16[768,768]{1,0:T(8,128)(2,1)S(1)} copy-done((bf16[768,768]{1,0:T(8,128)(2,1)S(1)}, bf16[768,768]{1,0:T(8,128)(2,1)}, u32[]{:S(2)}) %copy-start.2) | copy-done | bytes 1179672
  12.5 1.3 %copy-done.3 = bf16[768,768]{1,0:T(8,128)(2,1)S(1)} copy-done((bf16[768,768]{1,0:T(8,128)(2,1)S(1)}, bf16[768,768]{1,0:T(8,128)(2,1)}, u32[]{:S(2)}) %copy-start.3) | copy-done | bytes 1179672
  13.8 1.3 %copy-done.4 = bf16[768,768]{1,0:T(8,128)(2,1)S(1)} copy-done((bf16[768,768]{1,0:T(8,128)(2,1)S(1)}, bf16[768,768]{1,0:T(8,128)(2,1)}, u32[]{:S(2)}) %copy-start.4) | copy-done | bytes 1179672
  15.0 1.3 %copy-done.5 = bf16[768,768]{1,0:T(8,128)(2,1)S(1)} copy-done((bf16[768,768]{1,0:T(8,128)(2,1)S(1)}, bf16[768,768]{1,0:T(8,128)(2,1)}, u32[]{:S(2)}) %copy-start.5) | copy-done | bytes 1179672
  16.3 1.3 %copy-done.6 = bf16[768,768]{1,0:T(8,128)(2,1)S(1)} copy-done((bf16[768,768]{1,0:T(8,128)(2,1)S(1)}, bf16[768,768]{1,0:T(8,128)(2,1)}, u32[]{:S(2)}) %copy-start.6) | copy-done | bytes 1179672
  17.6 1.3 %copy-done.7 = bf16[768,768]{1,0:T(8,128)(2,1)S(1)} copy-done((bf16[768,768]{1,0:T(8,128)(2,1)S(1)}, bf16[768,768]{1,0:T(8,128)(2,1)}, u32[]{:S(2)}) %copy-start.7) | copy-done | bytes 1179672
  18.8 1.3 %copy-done.8 = bf16[768,768]{1,0:T(8,128)(2,1)S(1)} copy-done((bf16[768,768]{1,0:T(8,128)(2,1)S(1)}, bf16[768,768]{1,0:T(8,128)(2,1)}, u32[]{:S(2)}) %copy-start.8) | copy-done | bytes 1179672
  20.1 2.0 %hold.1.refs_2_.refs_6_.refs_7_.refs_15_ = bf16[8,768,768]{2,1,0:T(8,128)(2,1)S(1)} custom-call(bf16[768,768]{1,0:T(8,128)(2,1)S(1)} %copy-done.1, bf16[768,768]{1,0:T(8,128)(2,1)S(1)} %copy-done.2, bf16[768,768]{1,0:T(8,128)(2,1)S(1)} %copy-done.3, bf16[768,768]{1,0:T(8,128)(2,1)S(1)} %copy-done.4, bf16[768,768]{1,0:T(8,128)(2,1)S(1)} %copy-done.5, ...), custom_call_target="tpu_custom_call" | custom-call | bytes 33554432 | tf_op jit(solution)/shard_map/hold/pallas_call | solution.py:215
  22.1 0.0 collective-permute-done.refs_0_
  22.1 3.7 %collective-permute-start.5 = (bf16[784,128]{1,0:T(8,128)(2,1)S(1)}, bf16[784,128]{1,0:T(8,128)(2,1)S(1)}, u32[]{:S(2)}, u32[]{:S(2)}) collective-permute-start(bf16[784,128]{1,0:T(8,128)(2,1)S(1)} %get-tuple-element.81), channel_id=1, source_target_pairs={{0,6},{1,7},{2,4},{3,5},{4,2},{5,3},{6,0},{7,1},{8,14},{9,15},{10,... | collective-permute-start | bytes 602120 | tf_op jit(solution)/shard_map/ppermute | solution.py:450
  25.8 1.6 %collective-permute-done.1.refs_1_ = bf16[784,128]{1,0:T(8,128)(2,1)S(1)} collective-permute-done((bf16[784,128]{1,0:T(8,128)(2,1)S(1)}, bf16[784,128]{1,0:T(8,128)(2,1)S(1)}, u32[]{:S(2)}, u32[]{:S(2)}) %collective-permute-start.1) | collective-permute-done | bytes 200736 | tf_op jit(solution)/shard_map/ppermute | solution.py:450
  27.4 1.5 %collective-permute-start.6 = (bf16[784,128]{1,0:T(8,128)(2,1)S(1)}, bf16[784,128]{1,0:T(8,128)(2,1)S(1)}, u32[]{:S(2)}, u32[]{:S(2)}) collective-permute-start(bf16[784,128]{1,0:T(8,128)(2,1)S(1)} %get-tuple-element.82), channel_id=1, source_target_pairs={{0,7},{1,6},{2,5},{3,4},{4,3},{5,2},{6,1},{7,0},{8,15},{9,14},{10,... | collective-permute-start | bytes 602120 | tf_op jit(solution)/shard_map/ppermute | solution.py:450
  28.9 3.2 %window_layer.3 = (bf16[8,16,768]{2,1,0:T(8,128)(2,1)S(1)}, bf16[8,16,768]{2,1,0:T(8,128)(2,1)S(1)}, bf16[8,16,768]{2,1,0:T(8,128)(2,1)S(1)}, bf16[8,16,768]{2,1...) custom-call(s32[1]{0:T(128)} %bitcast.me_ref, ...), custom_call_target="tpu_custom_call" | custom-call | flops 1736441856 | bytes 16777216 | tf_op jit(solution)/shard_map/window_layer/pallas_call | solution.py:337
  32.1 0.0 collective-permute-done.2.refs_1_
  32.1 0.0 collective-permute-done.3.refs_2_
  32.1 1.2 %collective-permute-done.4.refs_3_ = bf16[784,128]{1,0:T(8,128)(2,1)S(1)} collective-permute-done((bf16[784,128]{1,0:T(8,128)(2,1)S(1)}, bf16[784,128]{1,0:T(8,128)(2,1)S(1)}, u32[]{:S(2)}, u32[]{:S(2)}) %collective-permute-start.4) | collective-permute-done | bytes 200736 | tf_op jit(solution)/shard_map/ppermute | solution.py:450
  33.3 8.3 %window_layer.4 = (bf16[8,64,768]{2,1,0:T(8,128)(2,1)S(1)}, bf16[8,64,768]{2,1,0:T(8,128)(2,1)S(1)}, bf16[8,64,768]{2,1,0:T(8,128)(2,1)S(1)}, bf16[8,64,768]{2,1...) custom-call(s32[1]{0:T(128)} %bitcast.me_ref, ...), custom_call_target="tpu_custom_call" | custom-call | flops 4630511616 | bytes 16777216 | tf_op jit(solution)/shard_map/window_layer/pallas_call | solution.py:337
  41.7 0.0 collective-permute-done.5.refs_0_
  41.7 0.0 collective-permute-done.6.refs_1_
  41.7 5.9 %window_layer.5 = (bf16[8,48,768]{2,1,0:T(8,128)(2,1)S(1)}, bf16[8,48,768]{2,1,0:T(8,128)(2,1)S(1)}, bf16[8,48,768]{2,1,0:T(8,128)(2,1)S(1)}, bf16[8,48,768]{2,1,0:T(8,128)(2,1)S(1)}, bf16[8,48,128]{2,1,0:T(8,128)(2,1)S(1)}) custom-call(s32[1]{0:T(128)} %bitcast.me_ref, bf16[784,128]{1,0:T(8,128)(2,1)S(1)} %collective-permute-done.5.refs_0_, ...), custom_call_target="tpu_custom_call" | custom-call | flops 2894069760 | bytes 16777216 | tf_op jit(solution)/shard_map/window_layer/pallas_call | solution.py:337
  47.6 2.7 %row_layer.3 = (bf16[4,16,768]{2,1,0:T(8,128)(2,1)S(1)}, bf16[4,16,768]{2,1,0:T(8,128)(2,1)S(1)}, bf16[4,16,768]{2,1,0:T(8,128)(2,1)S(1)}, bf16[4,16,768]{2,1,0:...) custom-call(s32[1]{0:T(128)} %bitcast.me_ref, ...), custom_call_target="tpu_custom_call" | custom-call | flops 1409286144 | bytes 8388608 | tf_op jit(solution)/shard_map/row_layer/pallas_call | solution.py:401
  50.3 0.6 copy-done.9
  51.0 3.9 %collective-permute-start.7 = (bf16[4,16,768]{2,1,0:T(8,128)(2,1)S(1)}, bf16[4,16,768]{2,1,0:T(8,128)(2,1)S(1)}, u32[]{:S(2)}, u32[]{:S(2)}) collective-permute-start(bf16[4,16,768]{2,1,0:T(8,128)(2,1)S(1)} %get-tuple-element.92), channel_id=1, source_target_pairs={{0,4},{1,5},{2,6},{3,7},{4,0},{5,1},{6,2},{7,3},{8,12},{9,13},{10,... | collective-permute-start | bytes 294920 | tf_op jit(solution)/shard_map/ppermute | solution.py:450
  54.8 1.1 %collective-permute-start.9 = (bf16[4,16,768]{2,1,0:T(8,128)(2,1)S(1)}, bf16[4,16,768]{2,1,0:T(8,128)(2,1)S(1)}, u32[]{:S(2)}, u32[]{:S(2)}) collective-permute-start(bf16[4,16,768]{2,1,0:T(8,128)(2,1)S(1)} %get-tuple-element.95), channel_id=1, source_target_pairs={{0,5},{1,4},{2,7},{3,6},{4,1},{5,0},{6,3},{7,2},{8,13},{9,12},{10,... | collective-permute-start | bytes 294920 | tf_op jit(solution)/shard_map/ppermute | solution.py:450
  55.9 4.6 %collective-permute-start.11 = (bf16[4,16,768]{2,1,0:T(8,128)(2,1)S(1)}, bf16[4,16,768]{2,1,0:T(8,128)(2,1)S(1)}, u32[]{:S(2)}, u32[]{:S(2)}) collective-permute-start(bf16[4,16,768]{2,1,0:T(8,128)(2,1)S(1)} %get-tuple-element.98), channel_id=1, source_target_pairs={{0,6},{1,7},{2,4},{3,5},{4,2},{5,3},{6,0},{7,1},{8,14},{9,15},{10,... | collective-permute-start | bytes 294920 | tf_op jit(solution)/shard_map/ppermute | solution.py:450
  60.6 0.9 %collective-permute-start.13 = (bf16[4,16,768]{2,1,0:T(8,128)(2,1)S(1)}, bf16[4,16,768]{2,1,0:T(8,128)(2,1)S(1)}, u32[]{:S(2)}, u32[]{:S(2)}) collective-permute-start(bf16[4,16,768]{2,1,0:T(8,128)(2,1)S(1)} %get-tuple-element.101), channel_id=1, source_target_pairs={{0,7},{1,6},{2,5},{3,4},{4,3},{5,2},{6,1},{7,0},{8,15},{9,14},{10,... | collective-permute-start | bytes 294920 | tf_op jit(solution)/shard_map/ppermute | solution.py:450
  61.5 0.6 collective-permute-start.15
  62.1 2.7 %row_layer.2 = (bf16[4,16,768]{2,1,0:T(8,128)(2,1)S(1)}, bf16[4,16,768]{2,1,0:T(8,128)(2,1)S(1)}, bf16[4,16,768]{2,1,0:T(8,128)(2,1)S(1)}, bf16[4,16,768]{2,1,0:...) custom-call(s32[1]{0:T(128)} %bitcast.me_ref, ...), custom_call_target="tpu_custom_call" | custom-call | flops 1409286144 | bytes 8388608 | tf_op jit(solution)/shard_map/row_layer/pallas_call | solution.py:401
  64.8 0.0 copy-start.10
  64.8 0.6 copy-done.10
  65.5 0.0 collective-permute-done.7.refs_0_
  65.5 0.2 collective-permute-start.17
  65.7 1.0 %collective-permute-done.9.refs_1_ = bf16[4,16,768]{2,1,0:T(8,128)(2,1)S(1)} collective-permute-done((bf16[4,16,768]{2,1,0:T(8,128)(2,1)S(1)}, bf16[4,16,768]{2,1,0:T(8,128)(2,1)S(1)}, u32[]{:S(2)}, u32[]{:S(2)}) %collective-permute-start.9) | collective-permute-done | bytes 98336 | tf_op jit(solution)/shard_map/ppermute | solution.py:450
  66.7 1.7 %collective-permute-start.19 = (bf16[4,16,768]{2,1,0:T(8,128)(2,1)S(1)}, bf16[4,16,768]{2,1,0:T(8,128)(2,1)S(1)}, u32[]{:S(2)}, u32[]{:S(2)}) collective-permute-start(bf16[4,16,768]{2,1,0:T(8,128)(2,1)S(1)} %get-tuple-element.110), channel_id=1, source_target_pairs={{0,3},{1,2},{2,1},{3,0},{4,7},{5,6},{6,5},{7,4},{8,11},{9,10},{10,... | collective-permute-start | bytes 294920 | tf_op jit(solution)/shard_map/ppermute | solution.py:450
  68.4 0.0 collective-permute-done.11.refs_2_
  68.4 4.6 %collective-permute-start.8 = (bf16[4,16,768]{2,1,0:T(8,128)(2,1)S(1)}, bf16[4,16,768]{2,1,0:T(8,128)(2,1)S(1)}, u32[]{:S(2)}, u32[]{:S(2)}) collective-permute-start(bf16[4,16,768]{2,1,0:T(8,128)(2,1)S(1)} %get-tuple-element.93), channel_id=1, source_target_pairs={{0,4},{1,5},{2,6},{3,7},{4,0},{5,1},{6,2},{7,3},{8,12},{9,13},{10,... | collective-permute-start | bytes 294920 | tf_op jit(solution)/shard_map/ppermute | solution.py:450
  73.0 0.0 collective-permute-done.13.refs_3_
  73.0 2.8 %collective-permute-start.10 = (bf16[4,16,768]{2,1,0:T(8,128)(2,1)S(1)}, bf16[4,16,768]{2,1,0:T(8,128)(2,1)S(1)}, u32[]{:S(2)}, u32[]{:S(2)}) collective-permute-start(bf16[4,16,768]{2,1,0:T(8,128)(2,1)S(1)} %get-tuple-element.96), channel_id=1, source_target_pairs={{0,5},{1,4},{2,7},{3,6},{4,1},{5,0},{6,3},{7,2},{8,13},{9,12},{10,... | collective-permute-start | bytes 294920 | tf_op jit(solution)/shard_map/ppermute | solution.py:450
  75.8 0.0 collective-permute-done.15.refs_4_
  75.8 0.0 collective-permute-start.12
  75.8 0.0 collective-permute-done.17.refs_5_
  75.8 4.0 %collective-permute-start.14 = (bf16[4,16,768]{2,1,0:T(8,128)(2,1)S(1)}, bf16[4,16,768]{2,1,0:T(8,128)(2,1)S(1)}, u32[]{:S(2)}, u32[]{:S(2)}) collective-permute-start(bf16[4,16,768]{2,1,0:T(8,128)(2,1)S(1)} %get-tuple-element.102), channel_id=1, source_target_pairs={{0,7},{1,6},{2,5},{3,4},{4,3},{5,2},{6,1},{7,0},{8,15},{9,14},{10,... | collective-permute-start | bytes 294920 | tf_op jit(solution)/shard_map/ppermute | solution.py:450
  79.8 0.0 collective-permute-done.19.refs_6_
  79.8 1.2 %collective-permute-start.16 = (bf16[4,16,768]{2,1,0:T(8,128)(2,1)S(1)}, bf16[4,16,768]{2,1,0:T(8,128)(2,1)S(1)}, u32[]{:S(2)}, u32[]{:S(2)}) collective-permute-start(bf16[4,16,768]{2,1,0:T(8,128)(2,1)S(1)} %get-tuple-element.105), channel_id=1, source_target_pairs={{0,1},{1,0},{2,3},{3,2},{4,5},{5,4},{6,7},{7,6},{8,9},{9,8},{10,11... | collective-permute-start | bytes 294920 | tf_op jit(solution)/shard_map/ppermute | solution.py:450
  81.1 3.1 %collective-permute-done.8.refs_0_ = bf16[4,16,768]{2,1,0:T(8,128)(2,1)S(1)} collective-permute-done((bf16[4,16,768]{2,1,0:T(8,128)(2,1)S(1)}, bf16[4,16,768]{2,1,0:T(8,128)(2,1)S(1)}, u32[]{:S(2)}, u32[]{:S(2)}) %collective-permute-start.8) | collective-permute-done | bytes 98336 | tf_op jit(solution)/shard_map/ppermute | solution.py:450
  84.1 0.0 collective-permute-start.18
  84.1 1.5 %collective-permute-done.10.refs_1_ = bf16[4,16,768]{2,1,0:T(8,128)(2,1)S(1)} collective-permute-done((bf16[4,16,768]{2,1,0:T(8,128)(2,1)S(1)}, bf16[4,16,768]{2,1,0:T(8,128)(2,1)S(1)}, u32[]{:S(2)}, u32[]{:S(2)}) %collective-permute-start.10) | collective-permute-done | bytes 98336 | tf_op jit(solution)/shard_map/ppermute | solution.py:450
  85.7 0.0 collective-permute-start.20
  85.7 2.2 %place.2.refs_8_ = bf16[64,16,768]{2,1,0:T(8,128)(2,1)} custom-call(s32[1]{0:T(128)} %bitcast.me_ref, bf16[4,16,768]{2,1,0:T(8,128)(2,1)} %copy-done.12, bf16[4,16,768]{2,1,0:T(8,128)(2,1)} %copy-done.13, bf16[4,16,768]{2,1,0:T(8,128)(2,1)} %copy-done.14, bf16[4,16,768]{2,1,0:T(8,128)(2,1)} %copy-done.15, bf16[4,16,768]{2,1,0:T(8,128)(2,1)} %copy-done.16, ...), custom_call_target="tpu_custom_call" | custom-call | bytes 1572864 | tf_op jit(solution)/shard_map/place/pallas_call | solution.py:436
  87.9 0.0 collective-permute-done.12.refs_2_
  87.9 0.0 collective-permute-done.14.refs_3_
  87.9 0.0 collective-permute-done.16.refs_4_
  88.0 0.8 collective-permute-done.18.refs_5_
  88.7 2.4 %collective-permute-done.20.refs_6_ = bf16[4,16,768]{2,1,0:T(8,128)(2,1)S(1)} collective-permute-done((bf16[4,16,768]{2,1,0:T(8,128)(2,1)S(1)}, bf16[4,16,768]{2,1,0:T(8,128)(2,1)S(1)}, u32[]{:S(2)}, u32[]{:S(2)}) %collective-permute-start.20) | collective-permute-done | bytes 98336 | tf_op jit(solution)/shard_map/ppermute | solution.py:450
  91.2 0.6 copy-done.25
  91.8 2.1 %place.3 = bf16[64,16,768]{2,1,0:T(8,128)(2,1)} custom-call(s32[1]{0:T(128)} %bitcast.me_ref, bf16[4,16,768]{2,1,0:T(8,128)(2,1)} %copy-done.19, bf16[4,16,768]{2,1,0:T(8,128)(2,1)} %copy-done.20, bf16[4,16,768]{2,1,0:T(8,128)(2,1)} %copy-done.21, bf16[4,16,768]{2,1,0:T(8,128)(2,1)} %copy-done.22, ...), custom_call_target="tpu_custom_call", output_to_operand_aliasing={{}: (9, {})} | custom-call | bytes 1572864 | tf_op jit(solution)/shard_map/place/pallas_call | solution.py:436
  (39 shorter events, 0.1 us)
Async XLA Ops:
  0.0 1.4 %copy-start = (bf16[64,16,768]{2,1,0:T(8,128)(2,1)S(1)}, bf16[64,16,768]{2,1,0:T(8,128)(2,1)}, u32[]{:S(2)}) copy-start(bf16[64,16,768]{2,1,0:T(8,128)(2,1)} %fields_ref.1) | copy-start | bytes 4718596
  1.4 0.7 copy-start.11
  2.1 9.1 %copy-start.1 = (bf16[768,768]{1,0:T(8,128)(2,1)S(1)}, bf16[768,768]{1,0:T(8,128)(2,1)}, u32[]{:S(2)}) copy-start(bf16[768,768]{1,0:T(8,128)(2,1)} %refs_0_.1) | copy-start | bytes 3538948
  2.3 19.8 %collective-permute-start = (bf16[784,128]{1,0:T(8,128)(2,1)S(1)}, bf16[784,128]{1,0:T(8,128)(2,1)S(1)}, u32[]{:S(2)}, u32[]{:S(2)}) collective-permute-start(bf16[784,128]{1,0:T(8,128)(2,1)S(1)} %get-tuple-element.63), channel_id=1, source_target_pairs={{0,4},{1,5},{2,6},{3,7},{4,0},{5,1},{6,2},{7,3},{8,12},{9,13},{10,... | collective-permute-start | bytes 602120 | tf_op jit(solution)/shard_map/ppermute | solution.py:450
  6.4 21.0 %collective-permute-start.1 = (bf16[784,128]{1,0:T(8,128)(2,1)S(1)}, bf16[784,128]{1,0:T(8,128)(2,1)S(1)}, u32[]{:S(2)}, u32[]{:S(2)}) collective-permute-start(bf16[784,128]{1,0:T(8,128)(2,1)S(1)} %get-tuple-element.64), channel_id=1, source_target_pairs={{0,5},{1,4},{2,7},{3,6},{4,1},{5,0},{6,3},{7,2},{8,13},{9,12},{10,... | collective-permute-start | bytes 602120 | tf_op jit(solution)/shard_map/ppermute | solution.py:450
  7.7 24.4 %collective-permute-start.2 = (bf16[784,128]{1,0:T(8,128)(2,1)S(1)}, bf16[784,128]{1,0:T(8,128)(2,1)S(1)}, u32[]{:S(2)}, u32[]{:S(2)}) collective-permute-start(bf16[784,128]{1,0:T(8,128)(2,1)S(1)} %get-tuple-element.71), channel_id=1, source_target_pairs={{0,1},{1,0},{2,3},{3,2},{4,5},{5,4},{6,7},{7,6},{8,9},{9,8},{10,11... | collective-permute-start | bytes 602120 | tf_op jit(solution)/shard_map/ppermute | solution.py:450
  8.0 24.2 %collective-permute-start.3 = (bf16[784,128]{1,0:T(8,128)(2,1)S(1)}, bf16[784,128]{1,0:T(8,128)(2,1)S(1)}, u32[]{:S(2)}, u32[]{:S(2)}) collective-permute-start(bf16[784,128]{1,0:T(8,128)(2,1)S(1)} %get-tuple-element.72), channel_id=1, source_target_pairs={{0,2},{1,3},{2,0},{3,1},{4,6},{5,7},{6,4},{7,5},{8,10},{9,11},{10,... | collective-permute-start | bytes 602120 | tf_op jit(solution)/shard_map/ppermute | solution.py:450
  9.8 23.5 %collective-permute-start.4 = (bf16[784,128]{1,0:T(8,128)(2,1)S(1)}, bf16[784,128]{1,0:T(8,128)(2,1)S(1)}, u32[]{:S(2)}, u32[]{:S(2)}) collective-permute-start(bf16[784,128]{1,0:T(8,128)(2,1)S(1)} %get-tuple-element.73), channel_id=1, source_target_pairs={{0,3},{1,2},{2,1},{3,0},{4,7},{5,6},{6,5},{7,4},{8,11},{9,10},{10,... | collective-permute-start | bytes 602120 | tf_op jit(solution)/shard_map/ppermute | solution.py:450
  11.2 1.3 %copy-start.2 = (bf16[768,768]{1,0:T(8,128)(2,1)S(1)}, bf16[768,768]{1,0:T(8,128)(2,1)}, u32[]{:S(2)}) copy-start(bf16[768,768]{1,0:T(8,128)(2,1)} %refs_1_.1) | copy-start | bytes 3538948
  12.5 1.3 %copy-start.3 = (bf16[768,768]{1,0:T(8,128)(2,1)S(1)}, bf16[768,768]{1,0:T(8,128)(2,1)}, u32[]{:S(2)}) copy-start(bf16[768,768]{1,0:T(8,128)(2,1)} %refs_2_.1) | copy-start | bytes 3538948
  13.7 1.3 %copy-start.4 = (bf16[768,768]{1,0:T(8,128)(2,1)S(1)}, bf16[768,768]{1,0:T(8,128)(2,1)}, u32[]{:S(2)}) copy-start(bf16[768,768]{1,0:T(8,128)(2,1)} %refs_3_.1) | copy-start | bytes 3538948
  15.0 1.3 %copy-start.5 = (bf16[768,768]{1,0:T(8,128)(2,1)S(1)}, bf16[768,768]{1,0:T(8,128)(2,1)}, u32[]{:S(2)}) copy-start(bf16[768,768]{1,0:T(8,128)(2,1)} %refs_4_.1) | copy-start | bytes 3538948
  16.3 1.3 %copy-start.6 = (bf16[768,768]{1,0:T(8,128)(2,1)S(1)}, bf16[768,768]{1,0:T(8,128)(2,1)}, u32[]{:S(2)}) copy-start(bf16[768,768]{1,0:T(8,128)(2,1)} %refs_5_.1) | copy-start | bytes 3538948
  17.6 1.3 %copy-start.7 = (bf16[768,768]{1,0:T(8,128)(2,1)S(1)}, bf16[768,768]{1,0:T(8,128)(2,1)}, u32[]{:S(2)}) copy-start(bf16[768,768]{1,0:T(8,128)(2,1)} %refs_6_.1) | copy-start | bytes 3538948
  18.8 1.3 %copy-start.8 = (bf16[768,768]{1,0:T(8,128)(2,1)S(1)}, bf16[768,768]{1,0:T(8,128)(2,1)}, u32[]{:S(2)}) copy-start(bf16[768,768]{1,0:T(8,128)(2,1)} %refs_7_.1) | copy-start | bytes 3538948
  22.1 19.6 %collective-permute-start.5 = (bf16[784,128]{1,0:T(8,128)(2,1)S(1)}, bf16[784,128]{1,0:T(8,128)(2,1)S(1)}, u32[]{:S(2)}, u32[]{:S(2)}) collective-permute-start(bf16[784,128]{1,0:T(8,128)(2,1)S(1)} %get-tuple-element.81), channel_id=1, source_target_pairs={{0,6},{1,7},{2,4},{3,5},{4,2},{5,3},{6,0},{7,1},{8,14},{9,15},{10,... | collective-permute-start | bytes 602120 | tf_op jit(solution)/shard_map/ppermute | solution.py:450
  27.4 14.3 %collective-permute-start.6 = (bf16[784,128]{1,0:T(8,128)(2,1)S(1)}, bf16[784,128]{1,0:T(8,128)(2,1)S(1)}, u32[]{:S(2)}, u32[]{:S(2)}) collective-permute-start(bf16[784,128]{1,0:T(8,128)(2,1)S(1)} %get-tuple-element.82), channel_id=1, source_target_pairs={{0,7},{1,6},{2,5},{3,4},{4,3},{5,2},{6,1},{7,0},{8,15},{9,14},{10,... | collective-permute-start | bytes 602120 | tf_op jit(solution)/shard_map/ppermute | solution.py:450
  50.3 0.6 copy-start.9
  51.0 14.5 %collective-permute-start.7 = (bf16[4,16,768]{2,1,0:T(8,128)(2,1)S(1)}, bf16[4,16,768]{2,1,0:T(8,128)(2,1)S(1)}, u32[]{:S(2)}, u32[]{:S(2)}) collective-permute-start(bf16[4,16,768]{2,1,0:T(8,128)(2,1)S(1)} %get-tuple-element.92), channel_id=1, source_target_pairs={{0,4},{1,5},{2,6},{3,7},{4,0},{5,1},{6,2},{7,3},{8,12},{9,13},{10,... | collective-permute-start | bytes 294920 | tf_op jit(solution)/shard_map/ppermute | solution.py:450
  54.8 11.9 %collective-permute-start.9 = (bf16[4,16,768]{2,1,0:T(8,128)(2,1)S(1)}, bf16[4,16,768]{2,1,0:T(8,128)(2,1)S(1)}, u32[]{:S(2)}, u32[]{:S(2)}) collective-permute-start(bf16[4,16,768]{2,1,0:T(8,128)(2,1)S(1)} %get-tuple-element.95), channel_id=1, source_target_pairs={{0,5},{1,4},{2,7},{3,6},{4,1},{5,0},{6,3},{7,2},{8,13},{9,12},{10,... | collective-permute-start | bytes 294920 | tf_op jit(solution)/shard_map/ppermute | solution.py:450
  55.9 12.5 %collective-permute-start.11 = (bf16[4,16,768]{2,1,0:T(8,128)(2,1)S(1)}, bf16[4,16,768]{2,1,0:T(8,128)(2,1)S(1)}, u32[]{:S(2)}, u32[]{:S(2)}) collective-permute-start(bf16[4,16,768]{2,1,0:T(8,128)(2,1)S(1)} %get-tuple-element.98), channel_id=1, source_target_pairs={{0,6},{1,7},{2,4},{3,5},{4,2},{5,3},{6,0},{7,1},{8,14},{9,15},{10,... | collective-permute-start | bytes 294920 | tf_op jit(solution)/shard_map/ppermute | solution.py:450
  60.6 12.4 %collective-permute-start.13 = (bf16[4,16,768]{2,1,0:T(8,128)(2,1)S(1)}, bf16[4,16,768]{2,1,0:T(8,128)(2,1)S(1)}, u32[]{:S(2)}, u32[]{:S(2)}) collective-permute-start(bf16[4,16,768]{2,1,0:T(8,128)(2,1)S(1)} %get-tuple-element.101), channel_id=1, source_target_pairs={{0,7},{1,6},{2,5},{3,4},{4,3},{5,2},{6,1},{7,0},{8,15},{9,14},{10,... | collective-permute-start | bytes 294920 | tf_op jit(solution)/shard_map/ppermute | solution.py:450
  61.5 14.2 %collective-permute-start.15 = (bf16[4,16,768]{2,1,0:T(8,128)(2,1)S(1)}, bf16[4,16,768]{2,1,0:T(8,128)(2,1)S(1)}, u32[]{:S(2)}, u32[]{:S(2)}) collective-permute-start(bf16[4,16,768]{2,1,0:T(8,128)(2,1)S(1)} %get-tuple-element.104), channel_id=1, source_target_pairs={{0,1},{1,0},{2,3},{3,2},{4,5},{5,4},{6,7},{7,6},{8,9},{9,8},{10,11... | collective-permute-start | bytes 294920 | tf_op jit(solution)/shard_map/ppermute | solution.py:450
  64.8 0.6 copy-start.10
  65.5 20.2 %copy-start.12 = (bf16[4,16,768]{2,1,0:T(8,128)(2,1)}, bf16[4,16,768]{2,1,0:T(8,128)(2,1)S(1)}, u32[]{:S(2)}) copy-start(bf16[4,16,768]{2,1,0:T(8,128)(2,1)S(1)} %collective-permute-done.7.refs_0_) | copy-start | bytes 294916
  65.5 10.3 %collective-permute-start.17 = (bf16[4,16,768]{2,1,0:T(8,128)(2,1)S(1)}, bf16[4,16,768]{2,1,0:T(8,128)(2,1)S(1)}, u32[]{:S(2)}, u32[]{:S(2)}) collective-permute-start(bf16[4,16,768]{2,1,0:T(8,128)(2,1)S(1)} %get-tuple-element.107), channel_id=1, source_target_pairs={{0,2},{1,3},{2,0},{3,1},{4,6},{5,7},{6,4},{7,5},{8,10},{9,11},{10,... | collective-permute-start | bytes 294920 | tf_op jit(solution)/shard_map/ppermute | solution.py:450
  66.7 18.9 %copy-start.13 = (bf16[4,16,768]{2,1,0:T(8,128)(2,1)}, bf16[4,16,768]{2,1,0:T(8,128)(2,1)S(1)}, u32[]{:S(2)}) copy-start(bf16[4,16,768]{2,1,0:T(8,128)(2,1)S(1)} %collective-permute-done.9.refs_1_) | copy-start | bytes 294916
  66.7 13.1 %collective-permute-start.19 = (bf16[4,16,768]{2,1,0:T(8,128)(2,1)S(1)}, bf16[4,16,768]{2,1,0:T(8,128)(2,1)S(1)}, u32[]{:S(2)}, u32[]{:S(2)}) collective-permute-start(bf16[4,16,768]{2,1,0:T(8,128)(2,1)S(1)} %get-tuple-element.110), channel_id=1, source_target_pairs={{0,3},{1,2},{2,1},{3,0},{4,7},{5,6},{6,5},{7,4},{8,11},{9,10},{10,... | collective-permute-start | bytes 294920 | tf_op jit(solution)/shard_map/ppermute | solution.py:450
  68.4 17.3 %copy-start.14 = (bf16[4,16,768]{2,1,0:T(8,128)(2,1)}, bf16[4,16,768]{2,1,0:T(8,128)(2,1)S(1)}, u32[]{:S(2)}) copy-start(bf16[4,16,768]{2,1,0:T(8,128)(2,1)S(1)} %collective-permute-done.11.refs_2_) | copy-start | bytes 294916
  68.4 15.7 %collective-permute-start.8 = (bf16[4,16,768]{2,1,0:T(8,128)(2,1)S(1)}, bf16[4,16,768]{2,1,0:T(8,128)(2,1)S(1)}, u32[]{:S(2)}, u32[]{:S(2)}) collective-permute-start(bf16[4,16,768]{2,1,0:T(8,128)(2,1)S(1)} %get-tuple-element.93), channel_id=1, source_target_pairs={{0,4},{1,5},{2,6},{3,7},{4,0},{5,1},{6,2},{7,3},{8,12},{9,13},{10,... | collective-permute-start | bytes 294920 | tf_op jit(solution)/shard_map/ppermute | solution.py:450
  73.0 12.7 %copy-start.15 = (bf16[4,16,768]{2,1,0:T(8,128)(2,1)}, bf16[4,16,768]{2,1,0:T(8,128)(2,1)S(1)}, u32[]{:S(2)}) copy-start(bf16[4,16,768]{2,1,0:T(8,128)(2,1)S(1)} %collective-permute-done.13.refs_3_) | copy-start | bytes 294916
  73.0 12.7 %collective-permute-start.10 = (bf16[4,16,768]{2,1,0:T(8,128)(2,1)S(1)}, bf16[4,16,768]{2,1,0:T(8,128)(2,1)S(1)}, u32[]{:S(2)}, u32[]{:S(2)}) collective-permute-start(bf16[4,16,768]{2,1,0:T(8,128)(2,1)S(1)} %get-tuple-element.96), channel_id=1, source_target_pairs={{0,5},{1,4},{2,7},{3,6},{4,1},{5,0},{6,3},{7,2},{8,13},{9,12},{10,... | collective-permute-start | bytes 294920 | tf_op jit(solution)/shard_map/ppermute | solution.py:450
  75.8 9.9 %copy-start.16 = (bf16[4,16,768]{2,1,0:T(8,128)(2,1)}, bf16[4,16,768]{2,1,0:T(8,128)(2,1)S(1)}, u32[]{:S(2)}) copy-start(bf16[4,16,768]{2,1,0:T(8,128)(2,1)S(1)} %collective-permute-done.15.refs_4_) | copy-start | bytes 294916
  75.8 12.2 %collective-permute-start.12 = (bf16[4,16,768]{2,1,0:T(8,128)(2,1)S(1)}, bf16[4,16,768]{2,1,0:T(8,128)(2,1)S(1)}, u32[]{:S(2)}, u32[]{:S(2)}) collective-permute-start(bf16[4,16,768]{2,1,0:T(8,128)(2,1)S(1)} %get-tuple-element.99), channel_id=1, source_target_pairs={{0,6},{1,7},{2,4},{3,5},{4,2},{5,3},{6,0},{7,1},{8,14},{9,15},{10,... | collective-permute-start | bytes 294920 | tf_op jit(solution)/shard_map/ppermute | solution.py:450
  75.8 9.9 %copy-start.17 = (bf16[4,16,768]{2,1,0:T(8,128)(2,1)}, bf16[4,16,768]{2,1,0:T(8,128)(2,1)S(1)}, u32[]{:S(2)}) copy-start(bf16[4,16,768]{2,1,0:T(8,128)(2,1)S(1)} %collective-permute-done.17.refs_5_) | copy-start | bytes 294916
  75.8 12.1 %collective-permute-start.14 = (bf16[4,16,768]{2,1,0:T(8,128)(2,1)S(1)}, bf16[4,16,768]{2,1,0:T(8,128)(2,1)S(1)}, u32[]{:S(2)}, u32[]{:S(2)}) collective-permute-start(bf16[4,16,768]{2,1,0:T(8,128)(2,1)S(1)} %get-tuple-element.102), channel_id=1, source_target_pairs={{0,7},{1,6},{2,5},{3,4},{4,3},{5,2},{6,1},{7,0},{8,15},{9,14},{10,... | collective-permute-start | bytes 294920 | tf_op jit(solution)/shard_map/ppermute | solution.py:450
  79.8 5.9 %copy-start.18 = (bf16[4,16,768]{2,1,0:T(8,128)(2,1)}, bf16[4,16,768]{2,1,0:T(8,128)(2,1)S(1)}, u32[]{:S(2)}) copy-start(bf16[4,16,768]{2,1,0:T(8,128)(2,1)S(1)} %collective-permute-done.19.refs_6_) | copy-start | bytes 294916
  79.8 8.1 %collective-permute-start.16 = (bf16[4,16,768]{2,1,0:T(8,128)(2,1)S(1)}, bf16[4,16,768]{2,1,0:T(8,128)(2,1)S(1)}, u32[]{:S(2)}, u32[]{:S(2)}) collective-permute-start(bf16[4,16,768]{2,1,0:T(8,128)(2,1)S(1)} %get-tuple-element.105), channel_id=1, source_target_pairs={{0,1},{1,0},{2,3},{3,2},{4,5},{5,4},{6,7},{7,6},{8,9},{9,8},{10,11... | collective-permute-start | bytes 294920 | tf_op jit(solution)/shard_map/ppermute | solution.py:450
  84.1 3.8 %copy-start.19 = (bf16[4,16,768]{2,1,0:T(8,128)(2,1)}, bf16[4,16,768]{2,1,0:T(8,128)(2,1)S(1)}, u32[]{:S(2)}) copy-start(bf16[4,16,768]{2,1,0:T(8,128)(2,1)S(1)} %collective-permute-done.8.refs_0_) | copy-start | bytes 294916
  84.1 4.6 %collective-permute-start.18 = (bf16[4,16,768]{2,1,0:T(8,128)(2,1)S(1)}, bf16[4,16,768]{2,1,0:T(8,128)(2,1)S(1)}, u32[]{:S(2)}, u32[]{:S(2)}) collective-permute-start(bf16[4,16,768]{2,1,0:T(8,128)(2,1)S(1)} %get-tuple-element.108), channel_id=1, source_target_pairs={{0,2},{1,3},{2,0},{3,1},{4,6},{5,7},{6,4},{7,5},{8,10},{9,11},{10,... | collective-permute-start | bytes 294920 | tf_op jit(solution)/shard_map/ppermute | solution.py:450
  85.7 2.2 %copy-start.20 = (bf16[4,16,768]{2,1,0:T(8,128)(2,1)}, bf16[4,16,768]{2,1,0:T(8,128)(2,1)S(1)}, u32[]{:S(2)}) copy-start(bf16[4,16,768]{2,1,0:T(8,128)(2,1)S(1)} %collective-permute-done.10.refs_1_) | copy-start | bytes 294916
  85.7 5.5 %collective-permute-start.20 = (bf16[4,16,768]{2,1,0:T(8,128)(2,1)S(1)}, bf16[4,16,768]{2,1,0:T(8,128)(2,1)S(1)}, u32[]{:S(2)}, u32[]{:S(2)}) collective-permute-start(bf16[4,16,768]{2,1,0:T(8,128)(2,1)S(1)} %get-tuple-element.111), channel_id=1, source_target_pairs={{0,3},{1,2},{2,1},{3,0},{4,7},{5,6},{6,5},{7,4},{8,11},{9,10},{10,... | collective-permute-start | bytes 294920 | tf_op jit(solution)/shard_map/ppermute | solution.py:450
  87.9 3.3 %copy-start.21 = (bf16[4,16,768]{2,1,0:T(8,128)(2,1)}, bf16[4,16,768]{2,1,0:T(8,128)(2,1)S(1)}, u32[]{:S(2)}) copy-start(bf16[4,16,768]{2,1,0:T(8,128)(2,1)S(1)} %collective-permute-done.12.refs_2_) | copy-start | bytes 294916
  87.9 3.2 %copy-start.22 = (bf16[4,16,768]{2,1,0:T(8,128)(2,1)}, bf16[4,16,768]{2,1,0:T(8,128)(2,1)S(1)}, u32[]{:S(2)}) copy-start(bf16[4,16,768]{2,1,0:T(8,128)(2,1)S(1)} %collective-permute-done.14.refs_3_) | copy-start | bytes 294916
  88.0 3.2 %copy-start.23 = (bf16[4,16,768]{2,1,0:T(8,128)(2,1)}, bf16[4,16,768]{2,1,0:T(8,128)(2,1)S(1)}, u32[]{:S(2)}) copy-start(bf16[4,16,768]{2,1,0:T(8,128)(2,1)S(1)} %collective-permute-done.16.refs_4_) | copy-start | bytes 294916
  88.7 2.5 %copy-start.24 = (bf16[4,16,768]{2,1,0:T(8,128)(2,1)}, bf16[4,16,768]{2,1,0:T(8,128)(2,1)S(1)}, u32[]{:S(2)}) copy-start(bf16[4,16,768]{2,1,0:T(8,128)(2,1)S(1)} %collective-permute-done.18.refs_5_) | copy-start | bytes 294916
  91.2 0.6 copy-start.25

commit v5 on v4

--- a/solution.py
+++ b/solution.py
@@ -13,7 +13,9 @@
 EPS = 1e-05
 NEG = -1e30
 
-GROUPS = (4, 4)
+ROWS_FIRST = 4
+
+PACK_VMEM = 52 * 1024 * 1024
 
 PAIRS = [slice(128 * p, 128 * p + 128) for p in range(HEADS // 2)]
 
@@ -172,55 +174,63 @@
 ORDER = (4, 5, 6, 7, 1, 2, 3, 0)
 
 
-def pack_kernel(distances, me_ref, marks_ref, fields_ref, *outs):
+def pack_kernel(distances, me_ref, marks_ref, fields_ref, *refs):
+    outs, (held, held_marks, sems) = refs[: len(distances)], refs[len(distances) :]
     me = me_ref[0]
     tiles = fields_ref.shape[-1] // 128
-    marks = marks_ref[...].astype(jnp.float32)
-    marks = jnp.concatenate([marks, jnp.zeros((16, 128 - marks.shape[1]), jnp.float32)], 1).astype(jnp.bfloat16)
+    copies = [pltpu.make_async_copy(marks_ref, held_marks, sems.at[len(distances)])]
     for i, d in enumerate(distances):
         there = jnp.bitwise_xor(me, d)
-        piece = fields_ref[pl.ds(there * 8, 8)].reshape(128, 128 * tiles)
+        copies.append(pltpu.make_async_copy(fields_ref.at[pl.ds(there * 8, 8)], held.at[i], sems.at[i]))
+    for copy in copies:
+        copy.start()
+    copies[0].wait()
+    marks = held_marks[...].astype(jnp.float32)
+    marks = jnp.concatenate([marks, jnp.zeros((16, 128 - marks.shape[1]), jnp.float32)], 1).astype(jnp.bfloat16)
+    for i in range(len(distances)):
+        copies[i + 1].wait()
+        piece = held[i].reshape(128, 128 * tiles)
         for t in range(tiles):
             outs[i][128 * t : 128 * t + 128, :] = piece[:, 128 * t : 128 * t + 128]
         outs[i][128 * tiles :, :] = marks
 
 
 def pack(distances, me, marks, fields):
-    width = fields.shape[-1]
+    cols, width = fields.shape[1:]
     vmem = pl.BlockSpec(memory_space=pltpu.VMEM)
+    anywhere = pl.BlockSpec(memory_space=pl.ANY)
     piece = jax.ShapeDtypeStruct((width + 16, 128), jnp.bfloat16)
     n = len(distances)
     return pl.pallas_call(
         functools.partial(pack_kernel, distances),
         out_shape=(piece,) * n,
-        in_specs=[pl.BlockSpec(memory_space=pltpu.SMEM), vmem, vmem],
+        in_specs=[pl.BlockSpec(memory_space=pltpu.SMEM), anywhere, anywhere],
         out_specs=(vmem,) * n,
-        compiler_params=pltpu.CompilerParams(vmem_limit_bytes=16 * 1024 * 1024),
+        scratch_shapes=[
+            pltpu.VMEM((n, 8, cols, width), jnp.bfloat16),
+            pltpu.VMEM(marks.shape, marks.dtype),
+            pltpu.SemaphoreType.DMA((n + 1,)),
+        ],
+        compiler_params=pltpu.CompilerParams(vmem_limit_bytes=PACK_VMEM),
         cost_estimate=pl.CostEstimate(flops=n * 200000, bytes_accessed=n * 400000, transcendentals=0),
         name="pack",
     )(me, marks, fields)
 
 
-def hold_kernel(*refs):
-    *weights, out_ref, sems = refs
-    copies = [pltpu.make_async_copy(w, out_ref.at[i], sems.at[i]) for i, w in enumerate(weights)]
-    for copy in copies:
-        copy.start()
-    for copy in copies:
-        copy.wait()
-
-
-def hold(weights):
-    width = weights[0].shape[0]
+def ready_kernel(*refs):
+    refs[-1][...] = jnp.zeros_like(refs[-1])
+
+
+def ready(weights):
+    vmem = pl.BlockSpec(memory_space=pltpu.VMEM)
     return pl.pallas_call(
-        hold_kernel,
-        out_shape=jax.ShapeDtypeStruct((len(weights), width, width), jnp.bfloat16),
-        in_specs=[pl.BlockSpec(memory_space=pl.ANY)] * len(weights),
-        out_specs=pl.BlockSpec(memory_space=pltpu.VMEM),
-        scratch_shapes=[pltpu.SemaphoreType.DMA((len(weights),))],
+        ready_kernel,
+        out_shape=jax.ShapeDtypeStruct((8, 128), jnp.float32),
+        in_specs=[vmem] * len(weights),
+        out_specs=vmem,
         compiler_params=pltpu.CompilerParams(vmem_limit_bytes=16 * 1024 * 1024),
         cost_estimate=pl.CostEstimate(flops=0, bytes_accessed=32 << 20, transcendentals=0),
-        name="hold",
+        name="ready",
     )(*weights)
 
 
@@ -234,18 +244,17 @@
     return whole[:, 0], whole[:, 1]
 
 
-STAGES = ((3, 2), (8, 8), (5, 6))
+STAGES = ((7, 6), (4, 4), (5, 6))
 
 
 def window_kernel(stage, me_ref, *refs):
-    pieces = refs[: (2, 4, 2)[stage]]
+    pieces = refs[: (4, 2, 2)[stage]]
     refs = refs[len(pieces) :]
-    carried = refs[: (0, 2, 5)[stage]]
+    carried = refs[: (0, 3, 5)[stage]]
     refs = refs[len(carried) :]
-    weights, y_ref, q2_ref, k2_ref, v2_ref, m_ref = refs[:6]
-    wq, wk, wv, wo, wq2, wk2, wv2 = (weights.at[i] for i in range(7))
-    refs = refs[6:]
-    passed = refs[: (3, 2, 0)[stage]]
+    _, wq, wk, wv, wo, wq2, wk2, wv2, y_ref, q2_ref, k2_ref, v2_ref, m_ref = refs[:13]
+    refs = refs[13:]
+    passed = refs[: (3, 3, 0)[stage]]
     placed, q_s, k_s, v_s, o_s, rows_s = refs[len(passed) :]
     width = wq.shape[0]
     scale = (width // HEADS) ** (-0.5)
@@ -271,15 +280,15 @@
     for l in range(1, len(pieces)):
         windows += [straddling_window(columns[l - 1][1], columns[l][0]), whole_window(l)]
     first, last = columns[0][0], columns[-1][1]
-    edges = [a[...].reshape(8, 8, width + 128) for a in carried[:4]]
     if stage < 2:
         passed[0][...] = first.reshape(full)
         passed[1][...] = last.reshape(full)
+    edges = [a[...].reshape(8, 8, width + 128) for a in carried[:-1]]
     if stage == 1:
-        second_first, second_last = edges
-        windows.append(straddling_window(either(second_last, last), either(first, second_first)))
+        own_first, own_last = edges
+        windows = [straddling_window(either(last, own_last), either(own_first, first))] + windows
     if stage == 2:
-        second_first, second_last, own_first, own_last = edges
+        own_first, own_last, second_first, second_last = edges
         windows = (
             [straddling_window(either(last, second_last), either(second_first, first))]
             + windows
@@ -299,14 +308,14 @@
             o_s[here, lanes] = out
     y = (x + dot_f32(o_s[...], wo[...])).astype(jnp.bfloat16).astype(jnp.float32)
     skip = 0
-    if stage == 2:
+    if stage > 0:
         skip = 1
-        rows_s[:, :8, :] = carried[4][...]
+        rows_s[:, :8, :] = carried[-1][...]
     for w in range(count):
         for r in range(8):
             at = 64 * w + 8 * r
             to = 8 * (w + skip)
-            if stage == 0 and w == count - 1:
+            if stage < 2 and w == count - 1:
                 passed[2][r, :, :width] = y[at : at + 8]
                 passed[2][r, :, width:] = marks[w][8 * r : 8 * r + 8]
             else:
@@ -323,17 +332,17 @@
 
 
 def window_layer(stage, me, pieces, carried, weights):
-    width = weights.shape[1]
+    width = weights[1].shape[0]
     tokens = 64 * STAGES[stage][0]
     columns = 8 * STAGES[stage][1]
     part = jax.ShapeDtypeStruct((8, columns, width), jnp.bfloat16)
     marks = jax.ShapeDtypeStruct((8, columns, 128), jnp.bfloat16)
     edge = jax.ShapeDtypeStruct((64, width + 128), jnp.float32)
     tail = jax.ShapeDtypeStruct((8, 8, width + 128), jnp.float32)
-    outs = (part,) * 4 + (marks,) + ((edge, edge, tail), (edge, edge), ())[stage]
+    outs = (part,) * 4 + (marks,) + ((edge, edge, tail), (edge, edge, tail), ())[stage]
     vmem = pl.BlockSpec(memory_space=pltpu.VMEM)
     work = pltpu.VMEM((tokens, width), jnp.bfloat16)
-    inputs = [*pieces, *carried, weights]
+    inputs = [*pieces, *carried, *weights]
     return pl.pallas_call(
         functools.partial(window_kernel, stage),
         out_shape=outs,
@@ -353,7 +362,8 @@
 
 
 def row_kernel(start, rows, me_ref, *refs):
-    parts, wo, refs = (refs[:5], refs[5:10], refs[10:15]), refs[15].at[7], refs[16:]
+    parts, wo, refs = (refs[:5], refs[5:10], refs[10:15]), refs[15], refs[16:]
+    earlier, refs = (refs[:4], refs[4:]) if start else ((), refs)
     outs, (o_s, placed) = refs[:8], refs[8:]
     width = wo.shape[0]
     length = 128
@@ -373,11 +383,10 @@
     for r in range(rows):
         f = row(0, r).astype(jnp.float32) + added[length * r : length * r + length]
         tiles = [f[8 * w : 8 * w + 8] for w in range(16)]
-        own = tiles[2:9]
-        second, third = (tiles[0], tiles[1], tiles[10]), tiles[12:15]
-        at_second, middle, at_third = tiles[9], tiles[11], tiles[15]
-        after_own = jnp.where(upper, at_third, at_second)
-        before_own = jnp.where(upper, at_second, at_third)
+        own, second, third = tiles[:7], tiles[8:11], tiles[12:15]
+        own_second, middle, third_own = tiles[7], tiles[11], tiles[15]
+        after_own = jnp.where(upper, third_own, own_second)
+        before_own = jnp.where(upper, own_second, third_own)
         whole = [before_own, *own, after_own]
         whole += [jnp.where(upper, middle, after_own), *second, jnp.where(upper, before_own, middle)]
         whole += [jnp.where(upper, after_own, middle), *third, jnp.where(upper, middle, before_own)]
@@ -388,20 +397,24 @@
             placed[l, r] = piece.astype(jnp.bfloat16)
     for i, d in enumerate(ORDER):
         if d < 4:
-            outs[i][...] = placed[jnp.bitwise_xor(jnp.bitwise_and(me, 3), d)]
+            if start:
+                outs[i][:start] = earlier[i - 4][...]
+            outs[i][start:] = placed[jnp.bitwise_xor(jnp.bitwise_and(me, 3), d)]
         else:
-            outs[i][...] = placed[jnp.bitwise_xor(jnp.bitwise_and(me, 1), d)]
-
-
-def row_layer(start, rows, me, parts, weights):
-    width = weights.shape[1]
+            outs[i][...] = placed[d // 2 * 2 + jnp.bitwise_xor(jnp.bitwise_and(me, 1), d % 2)]
+
+
+def row_layer(start, rows, me, parts, w_out, earlier):
+    width = w_out.shape[0]
     length = 128
-    piece = jax.ShapeDtypeStruct((rows, 16, width), jnp.bfloat16)
+    far = jax.ShapeDtypeStruct((rows, 16, width), jnp.bfloat16)
+    near = jax.ShapeDtypeStruct((start + rows, 16, width), jnp.bfloat16)
     vmem = pl.BlockSpec(memory_space=pltpu.VMEM)
+    inputs = [*parts, w_out, *earlier]
     return pl.pallas_call(
         functools.partial(row_kernel, start, rows),
-        out_shape=(piece,) * 8,
-        in_specs=[pl.BlockSpec(memory_space=pltpu.SMEM)] + [vmem] * (len(parts) + 1),
+        out_shape=(far,) * 4 + (near,) * 4,
+        in_specs=[pl.BlockSpec(memory_space=pltpu.SMEM)] + [vmem] * len(inputs),
         out_specs=(vmem,) * 8,
         scratch_shapes=[
             pltpu.VMEM((rows * length, width), jnp.bfloat16),
@@ -409,38 +422,37 @@
         ],
         compiler_params=pltpu.CompilerParams(vmem_limit_bytes=36 * 1024 * 1024),
         cost_estimate=pl.CostEstimate(
-            flops=2 * rows * length * width * (width + 1024), bytes_accessed=8 << 20,
-            transcendentals=rows * length * length * HEADS,
+            flops=0, bytes_accessed=1 << 16, transcendentals=0
         ),
         name="row_layer",
-    )(me, *parts, weights)
-
-
-def place_kernel(start, rows, me_ref, *refs):
-    pieces, out_ref, sems = refs[:8], refs[-2], refs[-1]
+    )(me, *inputs)
+
+
+def place_kernel(spots, me_ref, *refs):
+    pieces, out_ref, sems = refs[: len(spots)], refs[-2], refs[-1]
     copies = []
-    for i, d in enumerate(ORDER):
-        there = jnp.bitwise_xor(me_ref[0], d)
-        copies.append(
-            pltpu.make_async_copy(pieces[i], out_ref.at[pl.ds(there * 8 + start, rows)], sems.at[i])
-        )
+    for i, (d, start) in enumerate(spots):
+        at = jnp.bitwise_xor(me_ref[0], d) * 8 + start
+        copies.append(pltpu.make_async_copy(pieces[i], out_ref.at[pl.ds(at, pieces[i].shape[0])], sems.at[i]))
         copies[-1].start()
     for copy in copies:
         copy.wait()
 
 
-def place(start, rows, me, pieces, so_far, shape):
+def place(spots, me, pieces, so_far, shape):
     vmem = pl.BlockSpec(memory_space=pltpu.VMEM)
     hbm = pl.BlockSpec(memory_space=pltpu.HBM)
+    n = len(pieces)
     more = () if so_far is None else (so_far,)
     return pl.pallas_call(
-        functools.partial(place_kernel, start, rows),
+        functools.partial(place_kernel, spots),
         out_shape=jax.ShapeDtypeStruct(shape, jnp.bfloat16),
-        in_specs=[pl.BlockSpec(memory_space=pltpu.SMEM)] + [vmem] * 8 + [hbm] * len(more),
+        in_specs=[pl.BlockSpec(memory_space=pltpu.SMEM)] + [vmem] * n + [hbm] * len(more),
         out_specs=hbm,
-        scratch_shapes=[pltpu.SemaphoreType.DMA((8,))],
-        input_output_aliases={9: 0} if more else {},
-        cost_estimate=pl.CostEstimate(flops=0, bytes_accessed=16 * rows * shape[1] * shape[2] * 2, transcendentals=0),
+        scratch_shapes=[pltpu.SemaphoreType.DMA((n,))],
+        input_output_aliases={n + 1: 0} if more else {},
+        compiler_params=pltpu.CompilerParams(vmem_limit_bytes=8 * 1024 * 1024),
+        cost_estimate=pl.CostEstimate(flops=0, bytes_accessed=4 << 20, transcendentals=0),
         name="place",
     )(me, *pieces, *more)
 
@@ -454,24 +466,27 @@
     fields, ocean, w_query1, w_key1, w_value1, w_out1, w_query2, w_key2, w_value2, w_out2
 ):
     me = lax.axis_index("lon").astype(jnp.int32).reshape(1)
-    weights = hold((w_query1, w_key1, w_value1, w_out1, w_query2, w_key2, w_value2, w_out2))
+    weights = (w_query1, w_key1, w_value1, w_out1, w_query2, w_key2, w_value2)
+    weights = (ready(weights), *weights)
 
     packed = dict(zip(ORDER, pack(ORDER, me, ocean.T, fields)))
     got = {d: exchanged(packed[d], d) if d else packed[d] for d in ORDER}
-    second = window_layer(0, me, [got[4], got[5]], (), weights)
-    own = window_layer(1, me, [got[d] for d in range(4)], second[5:7], weights)
-    third = window_layer(2, me, [got[6], got[7]], (*second[5:7], *own[5:], second[7]), weights)
-    parts = (*second[:5], *own[:5], *third)
-    start, out, back = 0, None, None
-    for size in GROUPS:
-        sent = list(row_layer(start, size, me, parts, weights))
-        if back is not None:
-            for i in range(7):
-                sent[i], back[i] = lax.optimization_barrier((sent[i], back[i]))
-            out = place(start - before, before, me, back, out, fields.shape)
-        back = [exchanged(piece, d) if d else piece for d, piece in zip(ORDER, sent)]
-        start, before = start + size, size
-    return place(start - before, before, me, back, out, fields.shape)
+    got[4], *near = lax.optimization_barrier((got[4], got[2], got[3], got[1]))
+    got[2], got[3], got[1] = near
+    own = window_layer(0, me, [got[d] for d in range(4)], (), weights)
+    second = window_layer(1, me, [got[4], got[5]], own[5:], weights)
+    third = window_layer(2, me, [got[6], got[7]], (*own[5:7], *second[5:]), weights)
+    parts = (*own[:5], *second[:5], *third)
+    first = row_layer(0, ROWS_FIRST, me, parts, w_out2, ())
+    last = row_layer(ROWS_FIRST, 8 - ROWS_FIRST, me, parts, w_out2, first[4:])
+    far = [exchanged(piece, d) for d, piece in zip(ORDER[:4], first)]
+    last = list(last)
+    for i in range(4):
+        last[i], last[4 + i], far[i] = lax.optimization_barrier((last[i], last[4 + i], far[i]))
+    far_last = [exchanged(piece, d) for d, piece in zip(ORDER[:4], last)]
+    near = [exchanged(piece, d) if d else piece for d, piece in zip(ORDER[4:], last[4:])]
+    out = place([(d, 0) for d in ORDER], me, far + near, None, fields.shape)
+    return place([(d, ROWS_FIRST) for d in ORDER[:4]], me, far_last, out, fields.shape)
 
 
 def on_device(fields, *rest):

time: 94.6 us -> 88.9 us (0.940); the launches traced: 94.1 us -> 87.2 us
  waiting for transfers between devices: 11.7 us -> 17 us
  local copies, waits for them, and re-layouts: 12.9 us -> 8.45 us
  starting transfers between devices: 39.6 us -> 35.3 us
  Pallas kernels: 29.4 us -> 26.1 us
    ppermute x21 -> x18, waiting for transfers between devices: 11.7 us -> 17 us  [exchanged(): return lax.ppermute(piece, 'lon', [(s, s ^ distance) for s in range(count)])]
    pallas_call x5, Pallas kernels: 11.8 us -> 7.27 us  [the longest x2 5.42 us: row_layer(): pl.pallas_call(functools.partial(row_kernel, start, rows), out_shape=(far...]
    unnamed x52 -> x30, local copies, waits for them, and re-layouts: 12.9 us -> 8.45 us
    ppermute x21 -> x18, starting transfers between devices: 39.6 us -> 35.3 us  [exchanged(): return lax.ppermute(piece, 'lon', [(s, s ^ distance) for s in range(count)])]
    pallas_call x1, Pallas kernels: 0.21 us -> 1.56 us  [pack(): pl.pallas_call(functools.partial(pack_kernel, distances), out_shape=(piec...]
  transfers between devices with their start and end apart: 21 -> 18, of which waited for: 7 -> 4; matrix products, arithmetic and copies ran while one was open for 0% -> 0% of each run, Pallas kernels for 20% -> 17%
where the time goes in v5:
time: 88.9 us; the launch traced here: 87.2 us
  starting transfers between devices  35.3 us (40%)
  Pallas kernels  26.1 us (29%)
  waiting for transfers between devices  17 us (19%)
  local copies, waits for them, and re-layouts  8.45 us (10%)
    ppermute x18, starting transfers between devices, exchanged(): return lax.ppermute(piece, 'lon', [(s, s ^ distance) for s in range(count)])  35.3 us
    pallas_call x3, Pallas kernels, window_layer(): pl.pallas_call(functools.partial(window_kernel, stage), out_shape=outs, i...  17.3 us
    ppermute x18, waiting for transfers between devices, exchanged(): return lax.ppermute(piece, 'lon', [(s, s ^ distance) for s in range(count)])  17 us
    unnamed x30, local copies, waits for them, and re-layouts  8.45 us
    pallas_call x2, Pallas kernels, row_layer(): pl.pallas_call(functools.partial(row_kernel, start, rows), out_shape=(far...  5.42 us
    pallas_call x2, Pallas kernels, place(): pl.pallas_call(functools.partial(place_kernel, spots), out_shape=jax.Shap...  1.84 us
  transfers between devices with their start and end apart: 18, of which 4 were waited for; matrix products, arithmetic and copies ran while one was open for 0% of the time, Pallas kernels for 17%

profile of v5, /device:TPU:0, one launch (start us, length us, event | category | flops | bytes accessed | tf_op | source)
XLA Modules:
  0.0 87.2 jit_solution(15944292162748619570)
XLA Ops:
  0.0 0.0 copy-start
  0.0 0.0 copy-start.14
  0.0 0.8 copy-done.14
  0.8 1.6 %pack.1 = (bf16[784,128]{1,0:T(8,128)(2,1)S(1)}, bf16[784,128]{1,0:T(8,128)(2,1)S(1)}, bf16[784,128]{1,0:T(8,128)(2,1)S(1)}, bf16[784,128]{1,0:T(8,128)(2,1)S(1)...) custom-call(s32[1]{0:T(128)} %bitcast.me_ref, ...), custom_call_target="tpu_custom_call" | custom-call | flops 1600000 | bytes 3200000 | tf_op jit(solution)/shard_map/pack/pallas_call | solution.py:204
  2.4 4.1 %collective-permute-start = (bf16[784,128]{1,0:T(8,128)(2,1)S(1)}, bf16[784,128]{1,0:T(8,128)(2,1)S(1)}, u32[]{:S(2)}, u32[]{:S(2)}) collective-permute-start(bf16[784,128]{1,0:T(8,128)(2,1)S(1)} %get-tuple-element.67), channel_id=1, source_target_pairs={{0,4},{1,5},{2,6},{3,7},{4,0},{5,1},{6,2},{7,3},{8,12},{9,13},{10,... | collective-permute-start | bytes 602120 | tf_op jit(solution)/shard_map/ppermute | solution.py:462
  6.5 1.6 %collective-permute-start.1 = (bf16[784,128]{1,0:T(8,128)(2,1)S(1)}, bf16[784,128]{1,0:T(8,128)(2,1)S(1)}, u32[]{:S(2)}, u32[]{:S(2)}) collective-permute-start(bf16[784,128]{1,0:T(8,128)(2,1)S(1)} %get-tuple-element.68), channel_id=1, source_target_pairs={{0,2},{1,3},{2,0},{3,1},{4,6},{5,7},{6,4},{7,5},{8,10},{9,11},{10,... | collective-permute-start | bytes 602120 | tf_op jit(solution)/shard_map/ppermute | solution.py:462
  8.0 1.4 %collective-permute-start.2 = (bf16[784,128]{1,0:T(8,128)(2,1)S(1)}, bf16[784,128]{1,0:T(8,128)(2,1)S(1)}, u32[]{:S(2)}, u32[]{:S(2)}) collective-permute-start(bf16[784,128]{1,0:T(8,128)(2,1)S(1)} %get-tuple-element.69), channel_id=1, source_target_pairs={{0,3},{1,2},{2,1},{3,0},{4,7},{5,6},{6,5},{7,4},{8,11},{9,10},{10,... | collective-permute-start | bytes 602120 | tf_op jit(solution)/shard_map/ppermute | solution.py:462
  9.4 0.5 collective-permute-start.3
  10.0 1.3 %collective-permute-start.4 = (bf16[784,128]{1,0:T(8,128)(2,1)S(1)}, bf16[784,128]{1,0:T(8,128)(2,1)S(1)}, u32[]{:S(2)}, u32[]{:S(2)}) collective-permute-start(bf16[784,128]{1,0:T(8,128)(2,1)S(1)} %get-tuple-element.80), channel_id=1, source_target_pairs={{0,5},{1,4},{2,7},{3,6},{4,1},{5,0},{6,3},{7,2},{8,13},{9,12},{10,... | collective-permute-start | bytes 602120 | tf_op jit(solution)/shard_map/ppermute | solution.py:462
  11.2 0.0 copy-done
  11.3 1.3 %copy-done.1 = bf16[768,768]{1,0:T(8,128)(2,1)S(1)} copy-done((bf16[768,768]{1,0:T(8,128)(2,1)S(1)}, bf16[768,768]{1,0:T(8,128)(2,1)}, u32[]{:S(2)}) %copy-start.1) | copy-done | bytes 1179672
  12.5 1.3 %copy-done.3 = bf16[768,768]{1,0:T(8,128)(2,1)S(1)} copy-done((bf16[768,768]{1,0:T(8,128)(2,1)S(1)}, bf16[768,768]{1,0:T(8,128)(2,1)}, u32[]{:S(2)}) %copy-start.3) | copy-done | bytes 1179672
  13.8 1.3 %copy-done.5 = bf16[768,768]{1,0:T(8,128)(2,1)S(1)} copy-done((bf16[768,768]{1,0:T(8,128)(2,1)S(1)}, bf16[768,768]{1,0:T(8,128)(2,1)}, u32[]{:S(2)}) %copy-start.5) | copy-done | bytes 1179672
  15.1 1.3 %copy-done.7 = bf16[768,768]{1,0:T(8,128)(2,1)S(1)} copy-done((bf16[768,768]{1,0:T(8,128)(2,1)S(1)}, bf16[768,768]{1,0:T(8,128)(2,1)}, u32[]{:S(2)}) %copy-start.7) | copy-done | bytes 1179672
  16.3 1.3 %copy-done.9 = bf16[768,768]{1,0:T(8,128)(2,1)S(1)} copy-done((bf16[768,768]{1,0:T(8,128)(2,1)S(1)}, bf16[768,768]{1,0:T(8,128)(2,1)}, u32[]{:S(2)}) %copy-start.9) | copy-done | bytes 1179672
  17.6 1.3 %copy-done.11 = bf16[768,768]{1,0:T(8,128)(2,1)S(1)} copy-done((bf16[768,768]{1,0:T(8,128)(2,1)S(1)}, bf16[768,768]{1,0:T(8,128)(2,1)}, u32[]{:S(2)}) %copy-start.11) | copy-done | bytes 1179672
  18.9 0.0 copy-start.10
  18.9 0.0 copy-start.12
  18.9 0.0 collective-permute-done.refs_0_
  18.9 3.7 %collective-permute-start.5 = (bf16[784,128]{1,0:T(8,128)(2,1)S(1)}, bf16[784,128]{1,0:T(8,128)(2,1)S(1)}, u32[]{:S(2)}, u32[]{:S(2)}) collective-permute-start(bf16[784,128]{1,0:T(8,128)(2,1)S(1)} %get-tuple-element.89), channel_id=1, source_target_pairs={{0,6},{1,7},{2,4},{3,5},{4,2},{5,3},{6,0},{7,1},{8,14},{9,15},{10,... | collective-permute-start | bytes 602120 | tf_op jit(solution)/shard_map/ppermute | solution.py:462
  22.6 0.0 collective-permute-done.1.refs_2_
  22.6 2.1 %collective-permute-start.6 = (bf16[784,128]{1,0:T(8,128)(2,1)S(1)}, bf16[784,128]{1,0:T(8,128)(2,1)S(1)}, u32[]{:S(2)}, u32[]{:S(2)}) collective-permute-start(bf16[784,128]{1,0:T(8,128)(2,1)S(1)} %get-tuple-element.90), channel_id=1, source_target_pairs={{0,7},{1,6},{2,5},{3,4},{4,3},{5,2},{6,1},{7,0},{8,15},{9,14},{10,... | collective-permute-start | bytes 602120 | tf_op jit(solution)/shard_map/ppermute | solution.py:462
  24.7 1.2 %collective-permute-done.2.refs_3_ = bf16[784,128]{1,0:T(8,128)(2,1)S(1)} collective-permute-done((bf16[784,128]{1,0:T(8,128)(2,1)S(1)}, bf16[784,128]{1,0:T(8,128)(2,1)S(1)}, u32[]{:S(2)}, u32[]{:S(2)}) %collective-permute-start.2) | collective-permute-done | bytes 200736 | tf_op jit(solution)/shard_map/ppermute | solution.py:462
  25.9 0.0 collective-permute-done.3.refs_1_
  25.9 0.0 copy-done.2
  25.9 0.0 copy-done.4
  25.9 0.0 copy-done.6
  25.9 0.0 copy-done.8
  25.9 0.0 copy-done.10
  25.9 0.0 copy-done.12
  26.0 6.9 %window_layer.3 = (bf16[8,48,768]{2,1,0:T(8,128)(2,1)S(1)}, bf16[8,48,768]{2,1,0:T(8,128)(2,1)S(1)}, bf16[8,48,768]{2,1,0:T(8,128)(2,1)S(1)}, bf16[8,48,768]{2,1...) custom-call(s32[1]{0:T(128)} %bitcast.me_ref, ...), custom_call_target="tpu_custom_call" | custom-call | flops 4051697664 | bytes 16777216 | tf_op jit(solution)/shard_map/window_layer/pallas_call | solution.py:346
  32.9 0.0 collective-permute-done.4.refs_1_
  32.9 4.5 %window_layer.4 = (bf16[8,32,768]{2,1,0:T(8,128)(2,1)S(1)}, bf16[8,32,768]{2,1,0:T(8,128)(2,1)S(1)}, bf16[8,32,768]{2,1,0:T(8,128)(2,1)S(1)}, bf16[8,32,768]{2,1...) custom-call(s32[1]{0:T(128)} %bitcast.me_ref, ...), custom_call_target="tpu_custom_call" | custom-call | flops 2315255808 | bytes 16777216 | tf_op jit(solution)/shard_map/window_layer/pallas_call | solution.py:346
  37.4 0.0 collective-permute-done.5.refs_0_
  37.4 0.0 collective-permute-done.6.refs_1_
  37.4 0.0 copy-start.13
  37.4 5.9 %window_layer.5 = (bf16[8,48,768]{2,1,0:T(8,128)(2,1)S(1)}, bf16[8,48,768]{2,1,0:T(8,128)(2,1)S(1)}, bf16[8,48,768]{2,1,0:T(8,128)(2,1)S(1)}, bf16[8,48,768]{2,1,0:T(8,128)(2,1)S(1)}, bf16[8,48,128]{2,1,0:T(8,128)(2,1)S(1)}) custom-call(s32[1]{0:T(128)} %bitcast.me_ref, bf16[784,128]{1,0:T(8,128)(2,1)S(1)} %collective-permute-done.5.refs_0_, ...), custom_call_target="tpu_custom_call" | custom-call | flops 2894069760 | bytes 16777216 | tf_op jit(solution)/shard_map/window_layer/pallas_call | solution.py:346
  43.3 0.0 copy-done.13
  43.3 2.7 %row_layer.2 = (bf16[4,16,768]{2,1,0:T(8,128)(2,1)S(1)}, bf16[4,16,768]{2,1,0:T(8,128)(2,1)S(1)}, bf16[4,16,768]{2,1,0:T(8,128)(2,1)S(1)}, bf16[4,16,768]{2,1,0:...) custom-call(s32[1]{0:T(128)} %bitcast.me_ref, ...), custom_call_target="tpu_custom_call" | custom-call | bytes 65536 | tf_op jit(solution)/shard_map/row_layer/pallas_call | solution.py:414
  46.0 2.6 %collective-permute-start.11 = (bf16[4,16,768]{2,1,0:T(8,128)(2,1)S(1)}, bf16[4,16,768]{2,1,0:T(8,128)(2,1)S(1)}, u32[]{:S(2)}, u32[]{:S(2)}) collective-permute-start(bf16[4,16,768]{2,1,0:T(8,128)(2,1)S(1)} %get-tuple-element.113), channel_id=1, source_target_pairs={{0,6},{1,7},{2,4},{3,5},{4,2},{5,3},{6,0},{7,1},{8,14},{9,15},{10,... | collective-permute-start | bytes 294920 | tf_op jit(solution)/shard_map/ppermute | solution.py:462
  48.6 5.3 %collective-permute-start.9 = (bf16[4,16,768]{2,1,0:T(8,128)(2,1)S(1)}, bf16[4,16,768]{2,1,0:T(8,128)(2,1)S(1)}, u32[]{:S(2)}, u32[]{:S(2)}) collective-permute-start(bf16[4,16,768]{2,1,0:T(8,128)(2,1)S(1)} %get-tuple-element.109), channel_id=1, source_target_pairs={{0,5},{1,4},{2,7},{3,6},{4,1},{5,0},{6,3},{7,2},{8,13},{9,12},{10,... | collective-permute-start | bytes 294920 | tf_op jit(solution)/shard_map/ppermute | solution.py:462
  53.9 0.1 collective-permute-start.7
  54.0 2.7 %row_layer.3 = (bf16[4,16,768]{2,1,0:T(8,128)(2,1)S(1)}, bf16[4,16,768]{2,1,0:T(8,128)(2,1)S(1)}, bf16[4,16,768]{2,1,0:T(8,128)(2,1)S(1)}, bf16[4,16,768]{2,1,0:...) custom-call(s32[1]{0:T(128)} %bitcast.me_ref, ...), custom_call_target="tpu_custom_call" | custom-call | bytes 65536 | tf_op jit(solution)/shard_map/row_layer/pallas_call | solution.py:414
  56.7 0.0 collective-permute-done.11.refs_2_
  56.7 5.0 %collective-permute-start.17 = (bf16[8,16,768]{2,1,0:T(8,128)(2,1)S(1)}, bf16[8,16,768]{2,1,0:T(8,128)(2,1)S(1)}, u32[]{:S(2)}, u32[]{:S(2)}) collective-permute-start(bf16[8,16,768]{2,1,0:T(8,128)(2,1)S(1)} %get-tuple-element.125), channel_id=1, source_target_pairs={{0,3},{1,2},{2,1},{3,0},{4,7},{5,6},{6,5},{7,4},{8,11},{9,10},{10,... | collective-permute-start | bytes 589832 | tf_op jit(solution)/shard_map/ppermute | solution.py:462
  61.8 2.1 %collective-permute-done.9.refs_1_ = bf16[4,16,768]{2,1,0:T(8,128)(2,1)S(1)} collective-permute-done((bf16[4,16,768]{2,1,0:T(8,128)(2,1)S(1)}, bf16[4,16,768]{2,1,0:T(8,128)(2,1)S(1)}, u32[]{:S(2)}, u32[]{:S(2)}) %collective-permute-start.9) | collective-permute-done | bytes 98336 | tf_op jit(solution)/shard_map/ppermute | solution.py:462
  63.8 0.1 collective-permute-start.16
  64.0 3.8 %collective-permute-start.13 = (bf16[4,16,768]{2,1,0:T(8,128)(2,1)S(1)}, bf16[4,16,768]{2,1,0:T(8,128)(2,1)S(1)}, u32[]{:S(2)}, u32[]{:S(2)}) collective-permute-start(bf16[4,16,768]{2,1,0:T(8,128)(2,1)S(1)} %get-tuple-element.117), channel_id=1, source_target_pairs={{0,7},{1,6},{2,5},{3,4},{4,3},{5,2},{6,1},{7,0},{8,15},{9,14},{10,... | collective-permute-start | bytes 294920 | tf_op jit(solution)/shard_map/ppermute | solution.py:462
  67.7 0.0 collective-permute-done.7.refs_0_
  67.7 0.5 collective-permute-start.15
  68.2 0.6 collective-permute-start.8
  68.9 8.8 %collective-permute-done.13.refs_3_ = bf16[4,16,768]{2,1,0:T(8,128)(2,1)S(1)} collective-permute-done((bf16[4,16,768]{2,1,0:T(8,128)(2,1)S(1)}, bf16[4,16,768]{2,1,0:T(8,128)(2,1)S(1)}, u32[]{:S(2)}, u32[]{:S(2)}) %collective-permute-start.13) | collective-permute-done | bytes 98336 | tf_op jit(solution)/shard_map/ppermute | solution.py:462
  77.7 0.0 collective-permute-start.10
  77.7 0.0 collective-permute-done.17.refs_6_
  77.7 1.0 %collective-permute-start.12 = (bf16[4,16,768]{2,1,0:T(8,128)(2,1)S(1)}, bf16[4,16,768]{2,1,0:T(8,128)(2,1)S(1)}, u32[]{:S(2)}, u32[]{:S(2)}) collective-permute-start(bf16[4,16,768]{2,1,0:T(8,128)(2,1)S(1)} %get-tuple-element.114), channel_id=1, source_target_pairs={{0,6},{1,7},{2,4},{3,5},{4,2},{5,3},{6,0},{7,1},{8,14},{9,15},{10,... | collective-permute-start | bytes 294920 | tf_op jit(solution)/shard_map/ppermute | solution.py:462
  78.6 0.0 collective-permute-done.16.refs_5_
  78.6 1.6 %collective-permute-start.14 = (bf16[4,16,768]{2,1,0:T(8,128)(2,1)S(1)}, bf16[4,16,768]{2,1,0:T(8,128)(2,1)S(1)}, u32[]{:S(2)}, u32[]{:S(2)}) collective-permute-start(bf16[4,16,768]{2,1,0:T(8,128)(2,1)S(1)} %get-tuple-element.118), channel_id=1, source_target_pairs={{0,7},{1,6},{2,5},{3,4},{4,3},{5,2},{6,1},{7,0},{8,15},{9,14},{10,... | collective-permute-start | bytes 294920 | tf_op jit(solution)/shard_map/ppermute | solution.py:462
  80.3 0.0 collective-permute-done.15.refs_4_
  80.3 1.1 %place.2.refs_4_ = bf16[64,16,768]{2,1,0:T(8,128)(2,1)} custom-call(s32[1]{0:T(128)} %bitcast.me_ref, bf16[4,16,768]{2,1,0:T(8,128)(2,1)S(1)} %collective-permute-done.7.refs_0_, bf16[4,16,768]{2,1,0:T(8,128)(2,1)S(1)} %collective-permute-done.9.refs_1_, bf16[4,16,768]{2,1,0:T(8,128)(2,1)S(1)} %collective-permute-done.11.refs_2_, ...), custom_call_target="tpu_custom_call" | custom-call | bytes 4194304 | tf_op jit(solution)/shard_map/place/pallas_call | solution.py:447
  81.3 0.0 collective-permute-done.8.refs_0_
  81.4 4.9 %collective-permute-done.10.refs_1_ = bf16[4,16,768]{2,1,0:T(8,128)(2,1)S(1)} collective-permute-done((bf16[4,16,768]{2,1,0:T(8,128)(2,1)S(1)}, bf16[4,16,768]{2,1,0:T(8,128)(2,1)S(1)}, u32[]{:S(2)}, u32[]{:S(2)}) %collective-permute-start.10) | collective-permute-done | bytes 98336 | tf_op jit(solution)/shard_map/ppermute | solution.py:462
  86.2 0.0 collective-permute-done.12.refs_2_
  86.2 0.0 collective-permute-done.14.refs_3_
  86.3 0.8 place.3
  (11 shorter events, 0.0 us)
Async XLA Ops:
  0.0 11.2 %copy-start = (bf16[768,768]{1,0:T(8,128)(2,1)S(1)}, bf16[768,768]{1,0:T(8,128)(2,1)}, u32[]{:S(2)}) copy-start(bf16[768,768]{1,0:T(8,128)(2,1)} %refs_8_.5) | copy-start | bytes 3538948
  0.0 0.8 copy-start.14
  2.4 16.6 %collective-permute-start = (bf16[784,128]{1,0:T(8,128)(2,1)S(1)}, bf16[784,128]{1,0:T(8,128)(2,1)S(1)}, u32[]{:S(2)}, u32[]{:S(2)}) collective-permute-start(bf16[784,128]{1,0:T(8,128)(2,1)S(1)} %get-tuple-element.67), channel_id=1, source_target_pairs={{0,4},{1,5},{2,6},{3,7},{4,0},{5,1},{6,2},{7,3},{8,12},{9,13},{10,... | collective-permute-start | bytes 602120 | tf_op jit(solution)/shard_map/ppermute | solution.py:462
  6.5 16.1 %collective-permute-start.1 = (bf16[784,128]{1,0:T(8,128)(2,1)S(1)}, bf16[784,128]{1,0:T(8,128)(2,1)S(1)}, u32[]{:S(2)}, u32[]{:S(2)}) collective-permute-start(bf16[784,128]{1,0:T(8,128)(2,1)S(1)} %get-tuple-element.68), channel_id=1, source_target_pairs={{0,2},{1,3},{2,0},{3,1},{4,6},{5,7},{6,4},{7,5},{8,10},{9,11},{10,... | collective-permute-start | bytes 602120 | tf_op jit(solution)/shard_map/ppermute | solution.py:462
  8.0 17.9 %collective-permute-start.2 = (bf16[784,128]{1,0:T(8,128)(2,1)S(1)}, bf16[784,128]{1,0:T(8,128)(2,1)S(1)}, u32[]{:S(2)}, u32[]{:S(2)}) collective-permute-start(bf16[784,128]{1,0:T(8,128)(2,1)S(1)} %get-tuple-element.69), channel_id=1, source_target_pairs={{0,3},{1,2},{2,1},{3,0},{4,7},{5,6},{6,5},{7,4},{8,11},{9,10},{10,... | collective-permute-start | bytes 602120 | tf_op jit(solution)/shard_map/ppermute | solution.py:462
  9.4 16.5 %collective-permute-start.3 = (bf16[784,128]{1,0:T(8,128)(2,1)S(1)}, bf16[784,128]{1,0:T(8,128)(2,1)S(1)}, u32[]{:S(2)}, u32[]{:S(2)}) collective-permute-start(bf16[784,128]{1,0:T(8,128)(2,1)S(1)} %get-tuple-element.70), channel_id=1, source_target_pairs={{0,1},{1,0},{2,3},{3,2},{4,5},{5,4},{6,7},{7,6},{8,9},{9,8},{10,11... | collective-permute-start | bytes 602120 | tf_op jit(solution)/shard_map/ppermute | solution.py:462
  10.0 22.9 %collective-permute-start.4 = (bf16[784,128]{1,0:T(8,128)(2,1)S(1)}, bf16[784,128]{1,0:T(8,128)(2,1)S(1)}, u32[]{:S(2)}, u32[]{:S(2)}) collective-permute-start(bf16[784,128]{1,0:T(8,128)(2,1)S(1)} %get-tuple-element.80), channel_id=1, source_target_pairs={{0,5},{1,4},{2,7},{3,6},{4,1},{5,0},{6,3},{7,2},{8,13},{9,12},{10,... | collective-permute-start | bytes 602120 | tf_op jit(solution)/shard_map/ppermute | solution.py:462
  11.3 1.3 %copy-start.1 = (bf16[768,768]{1,0:T(8,128)(2,1)S(1)}, bf16[768,768]{1,0:T(8,128)(2,1)}, u32[]{:S(2)}) copy-start(bf16[768,768]{1,0:T(8,128)(2,1)} %refs_9_.5) | copy-start | bytes 3538948
  12.5 1.3 %copy-start.3 = (bf16[768,768]{1,0:T(8,128)(2,1)S(1)}, bf16[768,768]{1,0:T(8,128)(2,1)}, u32[]{:S(2)}) copy-start(bf16[768,768]{1,0:T(8,128)(2,1)} %refs_10_.5) | copy-start | bytes 3538948
  13.8 1.3 %copy-start.5 = (bf16[768,768]{1,0:T(8,128)(2,1)S(1)}, bf16[768,768]{1,0:T(8,128)(2,1)}, u32[]{:S(2)}) copy-start(bf16[768,768]{1,0:T(8,128)(2,1)} %refs_11_.5) | copy-start | bytes 3538948
  15.1 1.3 %copy-start.7 = (bf16[768,768]{1,0:T(8,128)(2,1)S(1)}, bf16[768,768]{1,0:T(8,128)(2,1)}, u32[]{:S(2)}) copy-start(bf16[768,768]{1,0:T(8,128)(2,1)} %refs_12_.3) | copy-start | bytes 3538948
  16.3 1.3 %copy-start.9 = (bf16[768,768]{1,0:T(8,128)(2,1)S(1)}, bf16[768,768]{1,0:T(8,128)(2,1)}, u32[]{:S(2)}) copy-start(bf16[768,768]{1,0:T(8,128)(2,1)} %refs_13_.1) | copy-start | bytes 3538948
  17.6 1.3 %copy-start.11 = (bf16[768,768]{1,0:T(8,128)(2,1)S(1)}, bf16[768,768]{1,0:T(8,128)(2,1)}, u32[]{:S(2)}) copy-start(bf16[768,768]{1,0:T(8,128)(2,1)} %refs_14_.1) | copy-start | bytes 3538948
  18.9 7.0 %copy-start.2 = (bf16[768,768]{1,0:T(8,128)(2,1)S(1)}, bf16[768,768]{1,0:T(8,128)(2,1)}, u32[]{:S(2)}) copy-start(bf16[768,768]{1,0:T(8,128)(2,1)} %refs_9_.5) | copy-start | bytes 3538948
  18.9 7.0 %copy-start.4 = (bf16[768,768]{1,0:T(8,128)(2,1)S(1)}, bf16[768,768]{1,0:T(8,128)(2,1)}, u32[]{:S(2)}) copy-start(bf16[768,768]{1,0:T(8,128)(2,1)} %refs_10_.5) | copy-start | bytes 3538948
  18.9 7.0 %copy-start.6 = (bf16[768,768]{1,0:T(8,128)(2,1)S(1)}, bf16[768,768]{1,0:T(8,128)(2,1)}, u32[]{:S(2)}) copy-start(bf16[768,768]{1,0:T(8,128)(2,1)} %refs_11_.5) | copy-start | bytes 3538948
  18.9 7.0 %copy-start.8 = (bf16[768,768]{1,0:T(8,128)(2,1)S(1)}, bf16[768,768]{1,0:T(8,128)(2,1)}, u32[]{:S(2)}) copy-start(bf16[768,768]{1,0:T(8,128)(2,1)} %refs_12_.3) | copy-start | bytes 3538948
  18.9 7.0 %copy-start.10 = (bf16[768,768]{1,0:T(8,128)(2,1)S(1)}, bf16[768,768]{1,0:T(8,128)(2,1)}, u32[]{:S(2)}) copy-start(bf16[768,768]{1,0:T(8,128)(2,1)} %refs_13_.1) | copy-start | bytes 3538948
  18.9 7.0 %copy-start.12 = (bf16[768,768]{1,0:T(8,128)(2,1)S(1)}, bf16[768,768]{1,0:T(8,128)(2,1)}, u32[]{:S(2)}) copy-start(bf16[768,768]{1,0:T(8,128)(2,1)} %refs_14_.1) | copy-start | bytes 3538948
  18.9 18.4 %collective-permute-start.5 = (bf16[784,128]{1,0:T(8,128)(2,1)S(1)}, bf16[784,128]{1,0:T(8,128)(2,1)S(1)}, u32[]{:S(2)}, u32[]{:S(2)}) collective-permute-start(bf16[784,128]{1,0:T(8,128)(2,1)S(1)} %get-tuple-element.89), channel_id=1, source_target_pairs={{0,6},{1,7},{2,4},{3,5},{4,2},{5,3},{6,0},{7,1},{8,14},{9,15},{10,... | collective-permute-start | bytes 602120 | tf_op jit(solution)/shard_map/ppermute | solution.py:462
  22.6 14.8 %collective-permute-start.6 = (bf16[784,128]{1,0:T(8,128)(2,1)S(1)}, bf16[784,128]{1,0:T(8,128)(2,1)S(1)}, u32[]{:S(2)}, u32[]{:S(2)}) collective-permute-start(bf16[784,128]{1,0:T(8,128)(2,1)S(1)} %get-tuple-element.90), channel_id=1, source_target_pairs={{0,7},{1,6},{2,5},{3,4},{4,3},{5,2},{6,1},{7,0},{8,15},{9,14},{10,... | collective-permute-start | bytes 602120 | tf_op jit(solution)/shard_map/ppermute | solution.py:462
  37.4 5.9 %copy-start.13 = (bf16[768,768]{1,0:T(8,128)(2,1)S(1)}, bf16[768,768]{1,0:T(8,128)(2,1)}, u32[]{:S(2)}) copy-start(bf16[768,768]{1,0:T(8,128)(2,1)} %refs_15_.3) | copy-start | bytes 3538948
  46.0 10.7 %collective-permute-start.11 = (bf16[4,16,768]{2,1,0:T(8,128)(2,1)S(1)}, bf16[4,16,768]{2,1,0:T(8,128)(2,1)S(1)}, u32[]{:S(2)}, u32[]{:S(2)}) collective-permute-start(bf16[4,16,768]{2,1,0:T(8,128)(2,1)S(1)} %get-tuple-element.113), channel_id=1, source_target_pairs={{0,6},{1,7},{2,4},{3,5},{4,2},{5,3},{6,0},{7,1},{8,14},{9,15},{10,... | collective-permute-start | bytes 294920 | tf_op jit(solution)/shard_map/ppermute | solution.py:462
  48.6 15.2 %collective-permute-start.9 = (bf16[4,16,768]{2,1,0:T(8,128)(2,1)S(1)}, bf16[4,16,768]{2,1,0:T(8,128)(2,1)S(1)}, u32[]{:S(2)}, u32[]{:S(2)}) collective-permute-start(bf16[4,16,768]{2,1,0:T(8,128)(2,1)S(1)} %get-tuple-element.109), channel_id=1, source_target_pairs={{0,5},{1,4},{2,7},{3,6},{4,1},{5,0},{6,3},{7,2},{8,13},{9,12},{10,... | collective-permute-start | bytes 294920 | tf_op jit(solution)/shard_map/ppermute | solution.py:462
  53.9 13.9 %collective-permute-start.7 = (bf16[4,16,768]{2,1,0:T(8,128)(2,1)S(1)}, bf16[4,16,768]{2,1,0:T(8,128)(2,1)S(1)}, u32[]{:S(2)}, u32[]{:S(2)}) collective-permute-start(bf16[4,16,768]{2,1,0:T(8,128)(2,1)S(1)} %get-tuple-element.105), channel_id=1, source_target_pairs={{0,4},{1,5},{2,6},{3,7},{4,0},{5,1},{6,2},{7,3},{8,12},{9,13},{10,... | collective-permute-start | bytes 294920 | tf_op jit(solution)/shard_map/ppermute | solution.py:462
  56.7 20.9 %collective-permute-start.17 = (bf16[8,16,768]{2,1,0:T(8,128)(2,1)S(1)}, bf16[8,16,768]{2,1,0:T(8,128)(2,1)S(1)}, u32[]{:S(2)}, u32[]{:S(2)}) collective-permute-start(bf16[8,16,768]{2,1,0:T(8,128)(2,1)S(1)} %get-tuple-element.125), channel_id=1, source_target_pairs={{0,3},{1,2},{2,1},{3,0},{4,7},{5,6},{6,5},{7,4},{8,11},{9,10},{10,... | collective-permute-start | bytes 589832 | tf_op jit(solution)/shard_map/ppermute | solution.py:462
  63.8 14.8 %collective-permute-start.16 = (bf16[8,16,768]{2,1,0:T(8,128)(2,1)S(1)}, bf16[8,16,768]{2,1,0:T(8,128)(2,1)S(1)}, u32[]{:S(2)}, u32[]{:S(2)}) collective-permute-start(bf16[8,16,768]{2,1,0:T(8,128)(2,1)S(1)} %get-tuple-element.124), channel_id=1, source_target_pairs={{0,2},{1,3},{2,0},{3,1},{4,6},{5,7},{6,4},{7,5},{8,10},{9,11},{10,... | collective-permute-start | bytes 589832 | tf_op jit(solution)/shard_map/ppermute | solution.py:462
  64.0 13.7 %collective-permute-start.13 = (bf16[4,16,768]{2,1,0:T(8,128)(2,1)S(1)}, bf16[4,16,768]{2,1,0:T(8,128)(2,1)S(1)}, u32[]{:S(2)}, u32[]{:S(2)}) collective-permute-start(bf16[4,16,768]{2,1,0:T(8,128)(2,1)S(1)} %get-tuple-element.117), channel_id=1, source_target_pairs={{0,7},{1,6},{2,5},{3,4},{4,3},{5,2},{6,1},{7,0},{8,15},{9,14},{10,... | collective-permute-start | bytes 294920 | tf_op jit(solution)/shard_map/ppermute | solution.py:462
  67.7 12.5 %collective-permute-start.15 = (bf16[8,16,768]{2,1,0:T(8,128)(2,1)S(1)}, bf16[8,16,768]{2,1,0:T(8,128)(2,1)S(1)}, u32[]{:S(2)}, u32[]{:S(2)}) collective-permute-start(bf16[8,16,768]{2,1,0:T(8,128)(2,1)S(1)} %get-tuple-element.123), channel_id=1, source_target_pairs={{0,1},{1,0},{2,3},{3,2},{4,5},{5,4},{6,7},{7,6},{8,9},{9,8},{10,11... | collective-permute-start | bytes 589832 | tf_op jit(solution)/shard_map/ppermute | solution.py:462
  68.2 13.1 %collective-permute-start.8 = (bf16[4,16,768]{2,1,0:T(8,128)(2,1)S(1)}, bf16[4,16,768]{2,1,0:T(8,128)(2,1)S(1)}, u32[]{:S(2)}, u32[]{:S(2)}) collective-permute-start(bf16[4,16,768]{2,1,0:T(8,128)(2,1)S(1)} %get-tuple-element.106), channel_id=1, source_target_pairs={{0,4},{1,5},{2,6},{3,7},{4,0},{5,1},{6,2},{7,3},{8,12},{9,13},{10,... | collective-permute-start | bytes 294920 | tf_op jit(solution)/shard_map/ppermute | solution.py:462
  77.7 8.6 %collective-permute-start.10 = (bf16[4,16,768]{2,1,0:T(8,128)(2,1)S(1)}, bf16[4,16,768]{2,1,0:T(8,128)(2,1)S(1)}, u32[]{:S(2)}, u32[]{:S(2)}) collective-permute-start(bf16[4,16,768]{2,1,0:T(8,128)(2,1)S(1)} %get-tuple-element.110), channel_id=1, source_target_pairs={{0,5},{1,4},{2,7},{3,6},{4,1},{5,0},{6,3},{7,2},{8,13},{9,12},{10,... | collective-permute-start | bytes 294920 | tf_op jit(solution)/shard_map/ppermute | solution.py:462
  77.7 8.6 %collective-permute-start.12 = (bf16[4,16,768]{2,1,0:T(8,128)(2,1)S(1)}, bf16[4,16,768]{2,1,0:T(8,128)(2,1)S(1)}, u32[]{:S(2)}, u32[]{:S(2)}) collective-permute-start(bf16[4,16,768]{2,1,0:T(8,128)(2,1)S(1)} %get-tuple-element.114), channel_id=1, source_target_pairs={{0,6},{1,7},{2,4},{3,5},{4,2},{5,3},{6,0},{7,1},{8,14},{9,15},{10,... | collective-permute-start | bytes 294920 | tf_op jit(solution)/shard_map/ppermute | solution.py:462
  78.6 7.6 %collective-permute-start.14 = (bf16[4,16,768]{2,1,0:T(8,128)(2,1)S(1)}, bf16[4,16,768]{2,1,0:T(8,128)(2,1)S(1)}, u32[]{:S(2)}, u32[]{:S(2)}) collective-permute-start(bf16[4,16,768]{2,1,0:T(8,128)(2,1)S(1)} %get-tuple-element.118), channel_id=1, source_target_pairs={{0,7},{1,6},{2,5},{3,4},{4,3},{5,2},{6,1},{7,0},{8,15},{9,14},{10,... | collective-permute-start | bytes 294920 | tf_op jit(solution)/shard_map/ppermute | solution.py:462

commit v6 on v5

--- a/solution.py
+++ b/solution.py
@@ -12,8 +12,6 @@
 
 EPS = 1e-05
 NEG = -1e30
-
-ROWS_FIRST = 4
 
 PACK_VMEM = 52 * 1024 * 1024
 
@@ -150,11 +148,11 @@
     return lax.broadcasted_iota(jnp.int32, shape, axis) % 8 < 4
 
 
-def attend(queries, keys, values, marks):
-    n = marks.shape[0]
+def attend(queries, keys, values, query_marks, key_marks):
+    n = query_marks.shape[0]
     low = lax.broadcasted_iota(jnp.int32, (n, 128), 1) < 64
-    land = 1.0 - marks
-    bias = jnp.concatenate([land * NEG] * (2 * n // 128), 1)
+    land = 1.0 - query_marks
+    bias = (1.0 - key_marks) * NEG
     scores = []
     for q, k in zip(queries, keys):
         zero = jnp.zeros_like(q)
@@ -167,11 +165,11 @@
         sums = lax.dot_general(expo, wide, (((0,), (0,)), ((), ())), preferred_element_type=jnp.float32)
         upper = jnp.where(low, sums[:n, :128], sums[n:, :128])
         total = jnp.where(low, sums[:n, 128:], sums[n:, 128:]) + land
-        outs.append((upper / total * marks).astype(jnp.bfloat16))
+        outs.append((upper / total * query_marks).astype(jnp.bfloat16))
     return outs
 
 
-ORDER = (4, 5, 6, 7, 1, 2, 3, 0)
+ORDER = (4, 5, 6, 7, 2, 3, 1, 0)
 
 
 def pack_kernel(distances, me_ref, marks_ref, fields_ref, *refs):
@@ -303,24 +301,28 @@
     v_s[...] = dot_f32(h, wv[...]).astype(jnp.bfloat16)
     for w in range(count):
         here = slice(64 * w, 64 * w + 64)
-        outs = attend(*([a[here, lanes] for lanes in PAIRS] for a in (q_s, k_s, v_s)), marks[w])
+        outs = attend(*([a[here, lanes] for lanes in PAIRS] for a in (q_s, k_s, v_s)), marks[w], marks[w])
         for lanes, out in zip(PAIRS, outs):
             o_s[here, lanes] = out
     y = (x + dot_f32(o_s[...], wo[...])).astype(jnp.bfloat16).astype(jnp.float32)
-    skip = 0
-    if stage > 0:
-        skip = 1
-        rows_s[:, :8, :] = carried[-1][...]
-    for w in range(count):
-        for r in range(8):
-            at = 64 * w + 8 * r
-            to = 8 * (w + skip)
-            if stage < 2 and w == count - 1:
-                passed[2][r, :, :width] = y[at : at + 8]
-                passed[2][r, :, width:] = marks[w][8 * r : 8 * r + 8]
-            else:
-                rows_s[r, to : to + 8, :width] = y[at : at + 8]
-                rows_s[r, to : to + 8, width:] = marks[w][8 * r : 8 * r + 8]
+    for r in range(8):
+        tiles = [
+            jnp.concatenate([y[64 * w + 8 * r : 64 * w + 8 * r + 8], marks[w][8 * r : 8 * r + 8]], 1)
+            for w in range(count)
+        ]
+        if stage == 0:
+            *tiles, passed[2][r] = tiles
+        if stage == 1:
+            passed[2][r] = tiles[0]
+            tiles = [tiles[1], tiles[2], carried[-1][r], tiles[3]]
+        if stage == 2:
+            one, other = carried[-1][r], tiles.pop()
+            tiles += [
+                jnp.where(mask[0], either(one, other), either(other, one)),
+                jnp.where(mask[0], either(other, one), either(one, other)),
+            ]
+        for w, tile in enumerate(tiles):
+            rows_s[r, 8 * w : 8 * w + 8, :] = tile
     tokens = rows_s.shape[0] * rows_s.shape[1]
     y = rows_s[:, :, :width].reshape(tokens, width)
     m_ref[...] = rows_s[:, :, width:].astype(jnp.bfloat16)
@@ -361,91 +363,93 @@
     )(me, *inputs)
 
 
-def row_kernel(start, rows, me_ref, *refs):
+def row_kernel(far, me_ref, *refs):
     parts, wo, refs = (refs[:5], refs[5:10], refs[10:15]), refs[15], refs[16:]
-    earlier, refs = (refs[:4], refs[4:]) if start else ((), refs)
-    outs, (o_s, placed) = refs[:8], refs[8:]
+    (*outs, o_s, placed) = refs if far else refs[1:]
     width = wo.shape[0]
-    length = 128
-
-    def row(i, r, lanes=slice(None)):
-        return jnp.concatenate([part[i][start + r, :, lanes] for part in parts], 0)
-
-    for r in range(rows):
-        here = slice(length * r, length * r + length)
-        heads = attend(*([row(i, r, lanes) for lanes in PAIRS] for i in (1, 2, 3)), row(4, r).astype(jnp.float32))
+    count = 64
+
+    def keys(i, r, lanes=slice(None)):
+        return jnp.concatenate([part[i][r, :, lanes] for part in parts], 0)
+
+    def queries(i, r, lanes=slice(None)):
+        mixed = [parts[1][i][r, 16:, lanes], parts[2][i][r, 32:, lanes]]
+        mixed = [a.astype(jnp.float32)[8:] if far else a.astype(jnp.float32)[:8] for a in mixed]
+        mixed = jnp.concatenate(mixed, 0).astype(jnp.bfloat16)
+        whole = [parts[1][i][r, :16, lanes], parts[2][i][r, :32, lanes]] if far else [parts[0][i][r, :, lanes]]
+        return jnp.concatenate([*whole, mixed], 0)
+
+    for r in range(8):
+        heads = attend(
+            [queries(1, r, lanes) for lanes in PAIRS],
+            [keys(2, r, lanes) for lanes in PAIRS],
+            [keys(3, r, lanes) for lanes in PAIRS],
+            queries(4, r).astype(jnp.float32),
+            keys(4, r).astype(jnp.float32),
+        )
         for lanes, out in zip(PAIRS, heads):
-            o_s[here, lanes] = out
+            o_s[count * r : count * r + count, lanes] = out
     added = dot_f32(o_s[...], wo[...])
     mask = low_columns((8, width), 0)
     me = me_ref[0]
     upper = jnp.bitwise_and(me, 2) > 0
-    for r in range(rows):
-        f = row(0, r).astype(jnp.float32) + added[length * r : length * r + length]
-        tiles = [f[8 * w : 8 * w + 8] for w in range(16)]
-        own, second, third = tiles[:7], tiles[8:11], tiles[12:15]
-        own_second, middle, third_own = tiles[7], tiles[11], tiles[15]
-        after_own = jnp.where(upper, third_own, own_second)
-        before_own = jnp.where(upper, own_second, third_own)
-        whole = [before_own, *own, after_own]
-        whole += [jnp.where(upper, middle, after_own), *second, jnp.where(upper, before_own, middle)]
-        whole += [jnp.where(upper, after_own, middle), *third, jnp.where(upper, middle, before_own)]
-        for l in range(8):
-            at = 2 * l if l < 4 else (9, 11, 14, 16)[l - 4]
-            before, a, after = whole[at : at + 3]
+    for r in range(8):
+        f = queries(0, r).astype(jnp.float32) + added[count * r : count * r + count]
+        tiles = [f[8 * w : 8 * w + 8] for w in range(8)]
+        if far:
+            second, middle, third, edge = (tiles[0], tiles[1], tiles[6]), tiles[2], tiles[3:6], tiles[7]
+            start, end = jnp.where(upper, middle, edge), jnp.where(upper, edge, middle)
+            whole = ((start, *second, end), (end, *third, start))
+            pieces = [side[at : at + 3] for side in whole for at in (0, 2)]
+        else:
+            whole = (tiles[7], *tiles[:7], tiles[7])
+            pieces = [whole[at : at + 3] for at in (0, 2, 4, 6)]
+        for l, (before, a, after) in enumerate(pieces):
             piece = jnp.concatenate([jnp.where(mask, before, a), jnp.where(mask, a, after)], 0)
             placed[l, r] = piece.astype(jnp.bfloat16)
-    for i, d in enumerate(ORDER):
-        if d < 4:
-            if start:
-                outs[i][:start] = earlier[i - 4][...]
-            outs[i][start:] = placed[jnp.bitwise_xor(jnp.bitwise_and(me, 3), d)]
+    for out, d in zip(outs, ORDER[:4] if far else ORDER[4:]):
+        if far:
+            out[...] = placed[(d - 4) // 2 * 2 + jnp.bitwise_xor(jnp.bitwise_and(me, 1), d % 2)]
         else:
-            outs[i][...] = placed[d // 2 * 2 + jnp.bitwise_xor(jnp.bitwise_and(me, 1), d % 2)]
-
-
-def row_layer(start, rows, me, parts, w_out, earlier):
+            out[...] = placed[jnp.bitwise_xor(jnp.bitwise_and(me, 3), d)]
+
+
+def row_layer(far, me, parts, w_out, after=()):
     width = w_out.shape[0]
-    length = 128
-    far = jax.ShapeDtypeStruct((rows, 16, width), jnp.bfloat16)
-    near = jax.ShapeDtypeStruct((start + rows, 16, width), jnp.bfloat16)
+    piece = jax.ShapeDtypeStruct((8, 16, width), jnp.bfloat16)
     vmem = pl.BlockSpec(memory_space=pltpu.VMEM)
-    inputs = [*parts, w_out, *earlier]
     return pl.pallas_call(
-        functools.partial(row_kernel, start, rows),
-        out_shape=(far,) * 4 + (near,) * 4,
-        in_specs=[pl.BlockSpec(memory_space=pltpu.SMEM)] + [vmem] * len(inputs),
-        out_specs=(vmem,) * 8,
-        scratch_shapes=[
-            pltpu.VMEM((rows * length, width), jnp.bfloat16),
-            pltpu.VMEM((8, rows, 16, width), jnp.bfloat16),
-        ],
+        functools.partial(row_kernel, far),
+        out_shape=(piece,) * 4,
+        in_specs=[pl.BlockSpec(memory_space=pltpu.SMEM)] + [vmem] * (len(parts) + 1) + [pl.BlockSpec(memory_space=pl.ANY)] * len(after),
+        out_specs=(vmem,) * 4,
+        scratch_shapes=[pltpu.VMEM((8 * 64, width), jnp.bfloat16), pltpu.VMEM((4, 8, 16, width), jnp.bfloat16)],
         compiler_params=pltpu.CompilerParams(vmem_limit_bytes=36 * 1024 * 1024),
         cost_estimate=pl.CostEstimate(
-            flops=0, bytes_accessed=1 << 16, transcendentals=0
+            flops=0, bytes_accessed=1 << 10, transcendentals=0
         ),
         name="row_layer",
-    )(me, *inputs)
-
-
-def place_kernel(spots, me_ref, *refs):
-    pieces, out_ref, sems = refs[: len(spots)], refs[-2], refs[-1]
+    )(me, *parts, w_out, *after)
+
+
+def place_kernel(distances, me_ref, *refs):
+    pieces, out_ref, sems = refs[: len(distances)], refs[-2], refs[-1]
     copies = []
-    for i, (d, start) in enumerate(spots):
-        at = jnp.bitwise_xor(me_ref[0], d) * 8 + start
-        copies.append(pltpu.make_async_copy(pieces[i], out_ref.at[pl.ds(at, pieces[i].shape[0])], sems.at[i]))
+    for i, d in enumerate(distances):
+        at = jnp.bitwise_xor(me_ref[0], d) * 8
+        copies.append(pltpu.make_async_copy(pieces[i], out_ref.at[pl.ds(at, 8)], sems.at[i]))
         copies[-1].start()
     for copy in copies:
         copy.wait()
 
 
-def place(spots, me, pieces, so_far, shape):
+def place(distances, me, pieces, so_far, shape):
     vmem = pl.BlockSpec(memory_space=pltpu.VMEM)
     hbm = pl.BlockSpec(memory_space=pltpu.HBM)
     n = len(pieces)
     more = () if so_far is None else (so_far,)
     return pl.pallas_call(
-        functools.partial(place_kernel, spots),
+        functools.partial(place_kernel, distances),
         out_shape=jax.ShapeDtypeStruct(shape, jnp.bfloat16),
         in_specs=[pl.BlockSpec(memory_space=pltpu.SMEM)] + [vmem] * n + [hbm] * len(more),
         out_specs=hbm,
@@ -471,22 +475,18 @@
 
     packed = dict(zip(ORDER, pack(ORDER, me, ocean.T, fields)))
     got = {d: exchanged(packed[d], d) if d else packed[d] for d in ORDER}
-    got[4], *near = lax.optimization_barrier((got[4], got[2], got[3], got[1]))
-    got[2], got[3], got[1] = near
+    early = (4, 2, 5, 3, 1)
+    got.update(zip(early, lax.optimization_barrier(tuple(got[d] for d in early))))
     own = window_layer(0, me, [got[d] for d in range(4)], (), weights)
     second = window_layer(1, me, [got[4], got[5]], own[5:], weights)
     third = window_layer(2, me, [got[6], got[7]], (*own[5:7], *second[5:]), weights)
     parts = (*own[:5], *second[:5], *third)
-    first = row_layer(0, ROWS_FIRST, me, parts, w_out2, ())
-    last = row_layer(ROWS_FIRST, 8 - ROWS_FIRST, me, parts, w_out2, first[4:])
-    far = [exchanged(piece, d) for d, piece in zip(ORDER[:4], first)]
-    last = list(last)
-    for i in range(4):
-        last[i], last[4 + i], far[i] = lax.optimization_barrier((last[i], last[4 + i], far[i]))
-    far_last = [exchanged(piece, d) for d, piece in zip(ORDER[:4], last)]
-    near = [exchanged(piece, d) if d else piece for d, piece in zip(ORDER[4:], last[4:])]
-    out = place([(d, 0) for d in ORDER], me, far + near, None, fields.shape)
-    return place([(d, ROWS_FIRST) for d in ORDER[:4]], me, far_last, out, fields.shape)
+    far = row_layer(True, me, parts, w_out2)
+    near = row_layer(False, me, parts, w_out2, far[:1])
+    far = [exchanged(piece, d) for d, piece in zip(ORDER[:4], far)]
+    near = [exchanged(piece, d) if d else piece for d, piece in zip(ORDER[4:], near)]
+    out = place(ORDER[:4], me, far, None, fields.shape)
+    return place(ORDER[4:], me, near, out, fields.shape)
 
 
 def on_device(fields, *rest):

time: 88.9 us -> 91.5 us (1.029)
  the two profiles are of different devices: /device:TPU:0 before, /device:TPU:8 now
where the time goes in v6:
time: 91.5 us; the launch traced here: 91.1 us
  waiting for transfers between devices  29.5 us (32%)
  Pallas kernels  27.9 us (30%)
  starting transfers between devices  24.9 us (27%)
  local copies, waits for them, and re-layouts  8.44 us (9%)
    ppermute x14, waiting for transfers between devices, exchanged(): return lax.ppermute(piece, 'lon', [(s, s ^ distance) for s in range(count)])  29.5 us
    ppermute x14, starting transfers between devices, exchanged(): return lax.ppermute(piece, 'lon', [(s, s ^ distance) for s in range(count)])  24.9 us
    pallas_call x3, Pallas kernels, window_layer(): pl.pallas_call(functools.partial(window_kernel, stage), out_shape=outs, i...  17.3 us
    unnamed x30, local copies, waits for them, and re-layouts  8.44 us
    pallas_call x2, Pallas kernels, row_layer(): pl.pallas_call(functools.partial(row_kernel, far), out_shape=(piece,) * 4...  7.24 us
  transfers between devices with their start and end apart: 14, of which 7 were waited for; matrix products, arithmetic and copies ran while one was open for 0% of the time, Pallas kernels for 18%

profile of v6, /device:TPU:8, one launch (start us, length us, event | category | flops | bytes accessed | tf_op | source)
XLA Modules:
  0.0 91.1 jit_solution(3347905157080309447)
XLA Ops:
  0.0 0.0 copy-start
  0.0 0.0 copy-start.14
  0.0 0.8 copy-done.14
  0.8 1.6 %pack.1 = (bf16[784,128]{1,0:T(8,128)(2,1)S(1)}, bf16[784,128]{1,0:T(8,128)(2,1)S(1)}, bf16[784,128]{1,0:T(8,128)(2,1)S(1)}, bf16[784,128]{1,0:T(8,128)(2,1)S(1)...) custom-call(s32[1]{0:T(128)} %bitcast.me_ref, ...), custom_call_target="tpu_custom_call" | custom-call | flops 1600000 | bytes 3200000 | tf_op jit(solution)/shard_map/pack/pallas_call | solution.py:202
  2.4 2.7 %collective-permute-start = (bf16[784,128]{1,0:T(8,128)(2,1)S(1)}, bf16[784,128]{1,0:T(8,128)(2,1)S(1)}, u32[]{:S(2)}, u32[]{:S(2)}) collective-permute-start(bf16[784,128]{1,0:T(8,128)(2,1)S(1)} %get-tuple-element.48), channel_id=1, source_target_pairs={{0,4},{1,5},{2,6},{3,7},{4,0},{5,1},{6,2},{7,3},{8,12},{9,13},{10,... | collective-permute-start | bytes 602120 | tf_op jit(solution)/shard_map/ppermute | solution.py:466
  5.0 0.4 collective-permute-start.1
  5.5 1.3 %collective-permute-start.2 = (bf16[784,128]{1,0:T(8,128)(2,1)S(1)}, bf16[784,128]{1,0:T(8,128)(2,1)S(1)}, u32[]{:S(2)}, u32[]{:S(2)}) collective-permute-start(bf16[784,128]{1,0:T(8,128)(2,1)S(1)} %get-tuple-element.50), channel_id=1, source_target_pairs={{0,5},{1,4},{2,7},{3,6},{4,1},{5,0},{6,3},{7,2},{8,13},{9,12},{10,... | collective-permute-start | bytes 602120 | tf_op jit(solution)/shard_map/ppermute | solution.py:466
  6.8 1.5 %collective-permute-start.3 = (bf16[784,128]{1,0:T(8,128)(2,1)S(1)}, bf16[784,128]{1,0:T(8,128)(2,1)S(1)}, u32[]{:S(2)}, u32[]{:S(2)}) collective-permute-start(bf16[784,128]{1,0:T(8,128)(2,1)S(1)} %get-tuple-element.51), channel_id=1, source_target_pairs={{0,3},{1,2},{2,1},{3,0},{4,7},{5,6},{6,5},{7,4},{8,11},{9,10},{10,... | collective-permute-start | bytes 602120 | tf_op jit(solution)/shard_map/ppermute | solution.py:466
  8.3 1.5 %collective-permute-start.4 = (bf16[784,128]{1,0:T(8,128)(2,1)S(1)}, bf16[784,128]{1,0:T(8,128)(2,1)S(1)}, u32[]{:S(2)}, u32[]{:S(2)}) collective-permute-start(bf16[784,128]{1,0:T(8,128)(2,1)S(1)} %get-tuple-element.52), channel_id=1, source_target_pairs={{0,1},{1,0},{2,3},{3,2},{4,5},{5,4},{6,7},{7,6},{8,9},{9,8},{10,11... | collective-permute-start | bytes 602120 | tf_op jit(solution)/shard_map/ppermute | solution.py:466
  9.8 0.0 copy-done
  9.8 0.0 copy-start.1
  9.8 1.3 %copy-done.1 = bf16[768,768]{1,0:T(8,128)(2,1)S(1)} copy-done((bf16[768,768]{1,0:T(8,128)(2,1)S(1)}, bf16[768,768]{1,0:T(8,128)(2,1)}, u32[]{:S(2)}) %copy-start.1) | copy-done | bytes 1179672
  11.1 0.0 copy-start.3
  11.1 1.3 %copy-done.3 = bf16[768,768]{1,0:T(8,128)(2,1)S(1)} copy-done((bf16[768,768]{1,0:T(8,128)(2,1)S(1)}, bf16[768,768]{1,0:T(8,128)(2,1)}, u32[]{:S(2)}) %copy-start.3) | copy-done | bytes 1179672
  12.3 0.0 copy-start.5
  12.3 1.3 %copy-done.5 = bf16[768,768]{1,0:T(8,128)(2,1)S(1)} copy-done((bf16[768,768]{1,0:T(8,128)(2,1)S(1)}, bf16[768,768]{1,0:T(8,128)(2,1)}, u32[]{:S(2)}) %copy-start.5) | copy-done | bytes 1179672
  13.6 0.0 copy-start.7
  13.6 1.3 %copy-done.7 = bf16[768,768]{1,0:T(8,128)(2,1)S(1)} copy-done((bf16[768,768]{1,0:T(8,128)(2,1)S(1)}, bf16[768,768]{1,0:T(8,128)(2,1)}, u32[]{:S(2)}) %copy-start.7) | copy-done | bytes 1179672
  14.9 1.3 %copy-done.9 = bf16[768,768]{1,0:T(8,128)(2,1)S(1)} copy-done((bf16[768,768]{1,0:T(8,128)(2,1)S(1)}, bf16[768,768]{1,0:T(8,128)(2,1)}, u32[]{:S(2)}) %copy-start.9) | copy-done | bytes 1179672
  16.2 0.0 copy-start.11
  16.2 1.3 %copy-done.11 = bf16[768,768]{1,0:T(8,128)(2,1)S(1)} copy-done((bf16[768,768]{1,0:T(8,128)(2,1)S(1)}, bf16[768,768]{1,0:T(8,128)(2,1)}, u32[]{:S(2)}) %copy-start.11) | copy-done | bytes 1179672
  17.4 0.0 copy-start.2
  17.4 0.0 copy-start.4
  17.4 0.0 copy-start.6
  17.4 0.0 copy-start.8
  17.4 0.0 copy-start.10
  17.5 0.0 copy-start.12
  17.5 0.0 collective-permute-done.refs_0_
  17.5 1.6 %collective-permute-start.5 = (bf16[784,128]{1,0:T(8,128)(2,1)S(1)}, bf16[784,128]{1,0:T(8,128)(2,1)S(1)}, u32[]{:S(2)}, u32[]{:S(2)}) collective-permute-start(bf16[784,128]{1,0:T(8,128)(2,1)S(1)} %get-tuple-element.71), channel_id=1, source_target_pairs={{0,6},{1,7},{2,4},{3,5},{4,2},{5,3},{6,0},{7,1},{8,14},{9,15},{10,... | collective-permute-start | bytes 602120 | tf_op jit(solution)/shard_map/ppermute | solution.py:466
  19.1 0.0 collective-permute-done.1.refs_2_
  19.1 0.4 collective-permute-start.6
  19.5 3.5 %collective-permute-done.2.refs_1_ = bf16[784,128]{1,0:T(8,128)(2,1)S(1)} collective-permute-done((bf16[784,128]{1,0:T(8,128)(2,1)S(1)}, bf16[784,128]{1,0:T(8,128)(2,1)S(1)}, u32[]{:S(2)}, u32[]{:S(2)}) %collective-permute-start.2) | collective-permute-done | bytes 200736 | tf_op jit(solution)/shard_map/ppermute | solution.py:466
  23.1 2.2 %collective-permute-done.3.refs_3_ = bf16[784,128]{1,0:T(8,128)(2,1)S(1)} collective-permute-done((bf16[784,128]{1,0:T(8,128)(2,1)S(1)}, bf16[784,128]{1,0:T(8,128)(2,1)S(1)}, u32[]{:S(2)}, u32[]{:S(2)}) %collective-permute-start.3) | collective-permute-done | bytes 200736 | tf_op jit(solution)/shard_map/ppermute | solution.py:466
  25.3 0.0 collective-permute-done.4.refs_1_
  25.3 0.0 copy-done.2
  25.3 0.0 copy-done.4
  25.3 0.0 copy-done.6
  25.3 0.0 copy-done.8
  25.3 0.0 copy-done.10
  25.3 0.0 copy-done.12
  25.3 6.9 %window_layer.3 = (bf16[8,48,768]{2,1,0:T(8,128)(2,1)S(1)}, bf16[8,48,768]{2,1,0:T(8,128)(2,1)S(1)}, bf16[8,48,768]{2,1,0:T(8,128)(2,1)S(1)}, bf16[8,48,768]{2,1...) custom-call(s32[1]{0:T(128)} %bitcast.me_ref, ...), custom_call_target="tpu_custom_call" | custom-call | flops 4051697664 | bytes 16777216 | tf_op jit(solution)/shard_map/window_layer/pallas_call | solution.py:348
  32.3 4.5 %window_layer.4 = (bf16[8,32,768]{2,1,0:T(8,128)(2,1)S(1)}, bf16[8,32,768]{2,1,0:T(8,128)(2,1)S(1)}, bf16[8,32,768]{2,1,0:T(8,128)(2,1)S(1)}, bf16[8,32,768]{2,1...) custom-call(s32[1]{0:T(128)} %bitcast.me_ref, ...), custom_call_target="tpu_custom_call" | custom-call | flops 2315255808 | bytes 16777216 | tf_op jit(solution)/shard_map/window_layer/pallas_call | solution.py:348
  36.8 0.0 collective-permute-done.5.refs_0_
  36.8 3.4 %collective-permute-done.6.refs_1_ = bf16[784,128]{1,0:T(8,128)(2,1)S(1)} collective-permute-done((bf16[784,128]{1,0:T(8,128)(2,1)S(1)}, bf16[784,128]{1,0:T(8,128)(2,1)S(1)}, u32[]{:S(2)}, u32[]{:S(2)}) %collective-permute-start.6) | collective-permute-done | bytes 200736 | tf_op jit(solution)/shard_map/ppermute | solution.py:466
  40.2 5.9 %window_layer.5 = (bf16[8,48,768]{2,1,0:T(8,128)(2,1)S(1)}, bf16[8,48,768]{2,1,0:T(8,128)(2,1)S(1)}, bf16[8,48,768]{2,1,0:T(8,128)(2,1)S(1)}, bf16[8,48,768]{2,1,0:T(8,128)(2,1)S(1)}, bf16[8,48,128]{2,1,0:T(8,128)(2,1)S(1)}) custom-call(s32[1]{0:T(128)} %bitcast.me_ref, bf16[784,128]{1,0:T(8,128)(2,1)S(1)} %collective-permute-done.5.refs_0_, ...), custom_call_target="tpu_custom_call" | custom-call | flops 2894069760 | bytes 16777216 | tf_op jit(solution)/shard_map/window_layer/pallas_call | solution.py:348
  46.1 0.0 copy-done.13
  46.1 3.6 %row_layer.2 = (bf16[8,16,768]{2,1,0:T(8,128)(2,1)S(1)}, bf16[8,16,768]{2,1,0:T(8,128)(2,1)S(1)}, bf16[8,16,768]{2,1,0:T(8,128)(2,1)S(1)}, bf16[8,16,768]{2,1,0:T(8,128)(2,1)S(1)}) custom-call(s32[1]{0:T(128)} %bitcast.me_ref, bf16[8,48,768]{2,1,0:T(8,128)(2,1)S(1)} %get-tuple-element.56.refs_0_, bf16[8,48,768]{2,1,0:T(8,128)(2,1)S(1)} %get-tuple-element.57.refs_1_, ...), custom_call_target="tpu_custom_call" | custom-call | bytes 1024 | tf_op jit(solution)/shard_map/row_layer/pallas_call | solution.py:421
  49.7 0.1 collective-permute-start.11
  49.8 2.6 %collective-permute-start.12 = (bf16[8,16,768]{2,1,0:T(8,128)(2,1)S(1)}, bf16[8,16,768]{2,1,0:T(8,128)(2,1)S(1)}, u32[]{:S(2)}, u32[]{:S(2)}) collective-permute-start(bf16[8,16,768]{2,1,0:T(8,128)(2,1)S(1)} %get-tuple-element.87), channel_id=1, source_target_pairs={{0,6},{1,7},{2,4},{3,5},{4,2},{5,3},{6,0},{7,1},{8,14},{9,15},{10,... | collective-permute-start | bytes 589832 | tf_op jit(solution)/shard_map/ppermute | solution.py:466
  52.4 3.6 %row_layer.3 = (bf16[8,16,768]{2,1,0:T(8,128)(2,1)S(1)}, bf16[8,16,768]{2,1,0:T(8,128)(2,1)S(1)}, bf16[8,16,768]{2,1,0:T(8,128)(2,1)S(1)}, bf16[8,16,768]{2,1,0:T(8,128)(2,1)S(1)}) custom-call(s32[1]{0:T(128)} %bitcast.me_ref, bf16[8,48,768]{2,1,0:T(8,128)(2,1)S(1)} %get-tuple-element.56.refs_0_, bf16[8,48,768]{2,1,0:T(8,128)(2,1)S(1)} %get-tuple-element.57.refs_1_, ...), custom_call_target="tpu_custom_call" | custom-call | bytes 1024 | tf_op jit(solution)/shard_map/row_layer/pallas_call | solution.py:421
  56.0 3.8 %collective-permute-start.10 = (bf16[8,16,768]{2,1,0:T(8,128)(2,1)S(1)}, bf16[8,16,768]{2,1,0:T(8,128)(2,1)S(1)}, u32[]{:S(2)}, u32[]{:S(2)}) collective-permute-start(bf16[8,16,768]{2,1,0:T(8,128)(2,1)S(1)} %get-tuple-element.81.refs_16_), channel_id=1, source_target_pairs={{0,4},{1,5},{2,6},{3,7},{4,0},{5,1},{6,2},{7,3},{8,12},{9,13},{10,... | collective-permute-start | bytes 589832 | tf_op jit(solution)/shard_map/ppermute | solution.py:466
  59.8 0.4 collective-permute-start.13
  60.2 2.1 %collective-permute-start.7 = (bf16[8,16,768]{2,1,0:T(8,128)(2,1)S(1)}, bf16[8,16,768]{2,1,0:T(8,128)(2,1)S(1)}, u32[]{:S(2)}, u32[]{:S(2)}) collective-permute-start(bf16[8,16,768]{2,1,0:T(8,128)(2,1)S(1)} %get-tuple-element.82), channel_id=1, source_target_pairs={{0,2},{1,3},{2,0},{3,1},{4,6},{5,7},{6,4},{7,5},{8,10},{9,11},{10,... | collective-permute-start | bytes 589832 | tf_op jit(solution)/shard_map/ppermute | solution.py:466
  62.3 8.6 %collective-permute-done.11.refs_1_ = bf16[8,16,768]{2,1,0:T(8,128)(2,1)S(1)} collective-permute-done((bf16[8,16,768]{2,1,0:T(8,128)(2,1)S(1)}, bf16[8,16,768]{2,1,0:T(8,128)(2,1)S(1)}, u32[]{:S(2)}, u32[]{:S(2)}) %collective-permute-start.11) | collective-permute-done | bytes 196640 | tf_op jit(solution)/shard_map/ppermute | solution.py:466
  70.9 6.0 %collective-permute-start.8 = (bf16[8,16,768]{2,1,0:T(8,128)(2,1)S(1)}, bf16[8,16,768]{2,1,0:T(8,128)(2,1)S(1)}, u32[]{:S(2)}, u32[]{:S(2)}) collective-permute-start(bf16[8,16,768]{2,1,0:T(8,128)(2,1)S(1)} %get-tuple-element.83), channel_id=1, source_target_pairs={{0,3},{1,2},{2,1},{3,0},{4,7},{5,6},{6,5},{7,4},{8,11},{9,10},{10,... | collective-permute-start | bytes 589832 | tf_op jit(solution)/shard_map/ppermute | solution.py:466
  76.9 1.9 %collective-permute-done.12.refs_2_ = bf16[8,16,768]{2,1,0:T(8,128)(2,1)S(1)} collective-permute-done((bf16[8,16,768]{2,1,0:T(8,128)(2,1)S(1)}, bf16[8,16,768]{2,1,0:T(8,128)(2,1)S(1)}, u32[]{:S(2)}, u32[]{:S(2)}) %collective-permute-start.12) | collective-permute-done | bytes 196640 | tf_op jit(solution)/shard_map/ppermute | solution.py:466
  78.8 0.5 collective-permute-start.9
  79.3 7.8 %collective-permute-done.13.refs_3_ = bf16[8,16,768]{2,1,0:T(8,128)(2,1)S(1)} collective-permute-done((bf16[8,16,768]{2,1,0:T(8,128)(2,1)S(1)}, bf16[8,16,768]{2,1,0:T(8,128)(2,1)S(1)}, u32[]{:S(2)}, u32[]{:S(2)}) %collective-permute-start.13) | collective-permute-done | bytes 196640 | tf_op jit(solution)/shard_map/ppermute | solution.py:466
  87.1 0.0 collective-permute-done.10.refs_0_
  87.1 0.9 place.2.refs_4_
  88.0 0.0 collective-permute-done.7.refs_0_
  88.0 0.0 collective-permute-done.8.refs_1_
  88.0 2.0 %collective-permute-done.9.refs_2_ = bf16[8,16,768]{2,1,0:T(8,128)(2,1)S(1)} collective-permute-done((bf16[8,16,768]{2,1,0:T(8,128)(2,1)S(1)}, bf16[8,16,768]{2,1,0:T(8,128)(2,1)S(1)}, u32[]{:S(2)}, u32[]{:S(2)}) %collective-permute-start.9) | collective-permute-done | bytes 196640 | tf_op jit(solution)/shard_map/ppermute | solution.py:466
  90.0 0.9 place.3
  (3 shorter events, 0.0 us)
Async XLA Ops:
  0.0 9.8 %copy-start = (bf16[768,768]{1,0:T(8,128)(2,1)S(1)}, bf16[768,768]{1,0:T(8,128)(2,1)}, u32[]{:S(2)}) copy-start(bf16[768,768]{1,0:T(8,128)(2,1)} %refs_8_.5) | copy-start | bytes 3538948
  0.0 0.8 copy-start.14
  2.4 15.1 %collective-permute-start = (bf16[784,128]{1,0:T(8,128)(2,1)S(1)}, bf16[784,128]{1,0:T(8,128)(2,1)S(1)}, u32[]{:S(2)}, u32[]{:S(2)}) collective-permute-start(bf16[784,128]{1,0:T(8,128)(2,1)S(1)} %get-tuple-element.48), channel_id=1, source_target_pairs={{0,4},{1,5},{2,6},{3,7},{4,0},{5,1},{6,2},{7,3},{8,12},{9,13},{10,... | collective-permute-start | bytes 602120 | tf_op jit(solution)/shard_map/ppermute | solution.py:466
  5.0 14.1 %collective-permute-start.1 = (bf16[784,128]{1,0:T(8,128)(2,1)S(1)}, bf16[784,128]{1,0:T(8,128)(2,1)S(1)}, u32[]{:S(2)}, u32[]{:S(2)}) collective-permute-start(bf16[784,128]{1,0:T(8,128)(2,1)S(1)} %get-tuple-element.49), channel_id=1, source_target_pairs={{0,2},{1,3},{2,0},{3,1},{4,6},{5,7},{6,4},{7,5},{8,10},{9,11},{10,... | collective-permute-start | bytes 602120 | tf_op jit(solution)/shard_map/ppermute | solution.py:466
  5.5 17.6 %collective-permute-start.2 = (bf16[784,128]{1,0:T(8,128)(2,1)S(1)}, bf16[784,128]{1,0:T(8,128)(2,1)S(1)}, u32[]{:S(2)}, u32[]{:S(2)}) collective-permute-start(bf16[784,128]{1,0:T(8,128)(2,1)S(1)} %get-tuple-element.50), channel_id=1, source_target_pairs={{0,5},{1,4},{2,7},{3,6},{4,1},{5,0},{6,3},{7,2},{8,13},{9,12},{10,... | collective-permute-start | bytes 602120 | tf_op jit(solution)/shard_map/ppermute | solution.py:466
  6.8 18.5 %collective-permute-start.3 = (bf16[784,128]{1,0:T(8,128)(2,1)S(1)}, bf16[784,128]{1,0:T(8,128)(2,1)S(1)}, u32[]{:S(2)}, u32[]{:S(2)}) collective-permute-start(bf16[784,128]{1,0:T(8,128)(2,1)S(1)} %get-tuple-element.51), channel_id=1, source_target_pairs={{0,3},{1,2},{2,1},{3,0},{4,7},{5,6},{6,5},{7,4},{8,11},{9,10},{10,... | collective-permute-start | bytes 602120 | tf_op jit(solution)/shard_map/ppermute | solution.py:466
  8.3 17.0 %collective-permute-start.4 = (bf16[784,128]{1,0:T(8,128)(2,1)S(1)}, bf16[784,128]{1,0:T(8,128)(2,1)S(1)}, u32[]{:S(2)}, u32[]{:S(2)}) collective-permute-start(bf16[784,128]{1,0:T(8,128)(2,1)S(1)} %get-tuple-element.52), channel_id=1, source_target_pairs={{0,1},{1,0},{2,3},{3,2},{4,5},{5,4},{6,7},{7,6},{8,9},{9,8},{10,11... | collective-permute-start | bytes 602120 | tf_op jit(solution)/shard_map/ppermute | solution.py:466
  9.8 1.3 %copy-start.1 = (bf16[768,768]{1,0:T(8,128)(2,1)S(1)}, bf16[768,768]{1,0:T(8,128)(2,1)}, u32[]{:S(2)}) copy-start(bf16[768,768]{1,0:T(8,128)(2,1)} %refs_9_.5) | copy-start | bytes 3538948
  11.1 1.3 %copy-start.3 = (bf16[768,768]{1,0:T(8,128)(2,1)S(1)}, bf16[768,768]{1,0:T(8,128)(2,1)}, u32[]{:S(2)}) copy-start(bf16[768,768]{1,0:T(8,128)(2,1)} %refs_10_.5) | copy-start | bytes 3538948
  12.3 1.3 %copy-start.5 = (bf16[768,768]{1,0:T(8,128)(2,1)S(1)}, bf16[768,768]{1,0:T(8,128)(2,1)}, u32[]{:S(2)}) copy-start(bf16[768,768]{1,0:T(8,128)(2,1)} %refs_11_.5) | copy-start | bytes 3538948
  13.6 1.3 %copy-start.7 = (bf16[768,768]{1,0:T(8,128)(2,1)S(1)}, bf16[768,768]{1,0:T(8,128)(2,1)}, u32[]{:S(2)}) copy-start(bf16[768,768]{1,0:T(8,128)(2,1)} %refs_12_.3) | copy-start | bytes 3538948
  14.9 1.3 %copy-start.9 = (bf16[768,768]{1,0:T(8,128)(2,1)S(1)}, bf16[768,768]{1,0:T(8,128)(2,1)}, u32[]{:S(2)}) copy-start(bf16[768,768]{1,0:T(8,128)(2,1)} %refs_13_.1) | copy-start | bytes 3538948
  16.2 1.3 %copy-start.11 = (bf16[768,768]{1,0:T(8,128)(2,1)S(1)}, bf16[768,768]{1,0:T(8,128)(2,1)}, u32[]{:S(2)}) copy-start(bf16[768,768]{1,0:T(8,128)(2,1)} %refs_14_.1) | copy-start | bytes 3538948
  17.4 7.8 %copy-start.2 = (bf16[768,768]{1,0:T(8,128)(2,1)S(1)}, bf16[768,768]{1,0:T(8,128)(2,1)}, u32[]{:S(2)}) copy-start(bf16[768,768]{1,0:T(8,128)(2,1)} %refs_9_.5) | copy-start | bytes 3538948
  17.4 7.8 %copy-start.4 = (bf16[768,768]{1,0:T(8,128)(2,1)S(1)}, bf16[768,768]{1,0:T(8,128)(2,1)}, u32[]{:S(2)}) copy-start(bf16[768,768]{1,0:T(8,128)(2,1)} %refs_10_.5) | copy-start | bytes 3538948
  17.4 7.8 %copy-start.6 = (bf16[768,768]{1,0:T(8,128)(2,1)S(1)}, bf16[768,768]{1,0:T(8,128)(2,1)}, u32[]{:S(2)}) copy-start(bf16[768,768]{1,0:T(8,128)(2,1)} %refs_11_.5) | copy-start | bytes 3538948
  17.4 7.9 %copy-start.8 = (bf16[768,768]{1,0:T(8,128)(2,1)S(1)}, bf16[768,768]{1,0:T(8,128)(2,1)}, u32[]{:S(2)}) copy-start(bf16[768,768]{1,0:T(8,128)(2,1)} %refs_12_.3) | copy-start | bytes 3538948
  17.4 7.9 %copy-start.10 = (bf16[768,768]{1,0:T(8,128)(2,1)S(1)}, bf16[768,768]{1,0:T(8,128)(2,1)}, u32[]{:S(2)}) copy-start(bf16[768,768]{1,0:T(8,128)(2,1)} %refs_13_.1) | copy-start | bytes 3538948
  17.5 7.9 %copy-start.12 = (bf16[768,768]{1,0:T(8,128)(2,1)S(1)}, bf16[768,768]{1,0:T(8,128)(2,1)}, u32[]{:S(2)}) copy-start(bf16[768,768]{1,0:T(8,128)(2,1)} %refs_14_.1) | copy-start | bytes 3538948
  17.5 19.3 %collective-permute-start.5 = (bf16[784,128]{1,0:T(8,128)(2,1)S(1)}, bf16[784,128]{1,0:T(8,128)(2,1)S(1)}, u32[]{:S(2)}, u32[]{:S(2)}) collective-permute-start(bf16[784,128]{1,0:T(8,128)(2,1)S(1)} %get-tuple-element.71), channel_id=1, source_target_pairs={{0,6},{1,7},{2,4},{3,5},{4,2},{5,3},{6,0},{7,1},{8,14},{9,15},{10,... | collective-permute-start | bytes 602120 | tf_op jit(solution)/shard_map/ppermute | solution.py:466
  19.1 21.1 %collective-permute-start.6 = (bf16[784,128]{1,0:T(8,128)(2,1)S(1)}, bf16[784,128]{1,0:T(8,128)(2,1)S(1)}, u32[]{:S(2)}, u32[]{:S(2)}) collective-permute-start(bf16[784,128]{1,0:T(8,128)(2,1)S(1)} %get-tuple-element.72), channel_id=1, source_target_pairs={{0,7},{1,6},{2,5},{3,4},{4,3},{5,2},{6,1},{7,0},{8,15},{9,14},{10,... | collective-permute-start | bytes 602120 | tf_op jit(solution)/shard_map/ppermute | solution.py:466
  40.2 5.9 %copy-start.13 = (bf16[768,768]{1,0:T(8,128)(2,1)S(1)}, bf16[768,768]{1,0:T(8,128)(2,1)}, u32[]{:S(2)}) copy-start(bf16[768,768]{1,0:T(8,128)(2,1)} %refs_15_.3) | copy-start | bytes 3538948
  49.7 21.2 %collective-permute-start.11 = (bf16[8,16,768]{2,1,0:T(8,128)(2,1)S(1)}, bf16[8,16,768]{2,1,0:T(8,128)(2,1)S(1)}, u32[]{:S(2)}, u32[]{:S(2)}) collective-permute-start(bf16[8,16,768]{2,1,0:T(8,128)(2,1)S(1)} %get-tuple-element.86), channel_id=1, source_target_pairs={{0,5},{1,4},{2,7},{3,6},{4,1},{5,0},{6,3},{7,2},{8,13},{9,12},{10,... | collective-permute-start | bytes 589832 | tf_op jit(solution)/shard_map/ppermute | solution.py:466
  49.8 29.0 %collective-permute-start.12 = (bf16[8,16,768]{2,1,0:T(8,128)(2,1)S(1)}, bf16[8,16,768]{2,1,0:T(8,128)(2,1)S(1)}, u32[]{:S(2)}, u32[]{:S(2)}) collective-permute-start(bf16[8,16,768]{2,1,0:T(8,128)(2,1)S(1)} %get-tuple-element.87), channel_id=1, source_target_pairs={{0,6},{1,7},{2,4},{3,5},{4,2},{5,3},{6,0},{7,1},{8,14},{9,15},{10,... | collective-permute-start | bytes 589832 | tf_op jit(solution)/shard_map/ppermute | solution.py:466
  56.0 31.0 %collective-permute-start.10 = (bf16[8,16,768]{2,1,0:T(8,128)(2,1)S(1)}, bf16[8,16,768]{2,1,0:T(8,128)(2,1)S(1)}, u32[]{:S(2)}, u32[]{:S(2)}) collective-permute-start(bf16[8,16,768]{2,1,0:T(8,128)(2,1)S(1)} %get-tuple-element.81.refs_16_), channel_id=1, source_target_pairs={{0,4},{1,5},{2,6},{3,7},{4,0},{5,1},{6,2},{7,3},{8,12},{9,13},{10,... | collective-permute-start | bytes 589832 | tf_op jit(solution)/shard_map/ppermute | solution.py:466
  59.8 27.3 %collective-permute-start.13 = (bf16[8,16,768]{2,1,0:T(8,128)(2,1)S(1)}, bf16[8,16,768]{2,1,0:T(8,128)(2,1)S(1)}, u32[]{:S(2)}, u32[]{:S(2)}) collective-permute-start(bf16[8,16,768]{2,1,0:T(8,128)(2,1)S(1)} %get-tuple-element.88), channel_id=1, source_target_pairs={{0,7},{1,6},{2,5},{3,4},{4,3},{5,2},{6,1},{7,0},{8,15},{9,14},{10,... | collective-permute-start | bytes 589832 | tf_op jit(solution)/shard_map/ppermute | solution.py:466
  60.2 27.8 %collective-permute-start.7 = (bf16[8,16,768]{2,1,0:T(8,128)(2,1)S(1)}, bf16[8,16,768]{2,1,0:T(8,128)(2,1)S(1)}, u32[]{:S(2)}, u32[]{:S(2)}) collective-permute-start(bf16[8,16,768]{2,1,0:T(8,128)(2,1)S(1)} %get-tuple-element.82), channel_id=1, source_target_pairs={{0,2},{1,3},{2,0},{3,1},{4,6},{5,7},{6,4},{7,5},{8,10},{9,11},{10,... | collective-permute-start | bytes 589832 | tf_op jit(solution)/shard_map/ppermute | solution.py:466
  70.9 17.1 %collective-permute-start.8 = (bf16[8,16,768]{2,1,0:T(8,128)(2,1)S(1)}, bf16[8,16,768]{2,1,0:T(8,128)(2,1)S(1)}, u32[]{:S(2)}, u32[]{:S(2)}) collective-permute-start(bf16[8,16,768]{2,1,0:T(8,128)(2,1)S(1)} %get-tuple-element.83), channel_id=1, source_target_pairs={{0,3},{1,2},{2,1},{3,0},{4,7},{5,6},{6,5},{7,4},{8,11},{9,10},{10,... | collective-permute-start | bytes 589832 | tf_op jit(solution)/shard_map/ppermute | solution.py:466
  78.8 11.3 %collective-permute-start.9 = (bf16[8,16,768]{2,1,0:T(8,128)(2,1)S(1)}, bf16[8,16,768]{2,1,0:T(8,128)(2,1)S(1)}, u32[]{:S(2)}, u32[]{:S(2)}) collective-permute-start(bf16[8,16,768]{2,1,0:T(8,128)(2,1)S(1)} %get-tuple-element.84), channel_id=1, source_target_pairs={{0,1},{1,0},{2,3},{3,2},{4,5},{5,4},{6,7},{7,6},{8,9},{9,8},{10,11... | collective-permute-start | bytes 589832 | tf_op jit(solution)/shard_map/ppermute | solution.py:466

commit v7 on v5

--- a/solution.py
+++ b/solution.py
@@ -467,12 +467,12 @@
 ):
     me = lax.axis_index("lon").astype(jnp.int32).reshape(1)
     weights = (w_query1, w_key1, w_value1, w_out1, w_query2, w_key2, w_value2)
-    weights = (ready(weights), *weights)
+    weights = (ready(weights[:3]), *weights)
 
     packed = dict(zip(ORDER, pack(ORDER, me, ocean.T, fields)))
     got = {d: exchanged(packed[d], d) if d else packed[d] for d in ORDER}
-    got[4], *near = lax.optimization_barrier((got[4], got[2], got[3], got[1]))
-    got[2], got[3], got[1] = near
+    early = (2, 4, 3, 5, 1)
+    got.update(zip(early, lax.optimization_barrier(tuple(got[d] for d in early))))
     own = window_layer(0, me, [got[d] for d in range(4)], (), weights)
     second = window_layer(1, me, [got[4], got[5]], own[5:], weights)
     third = window_layer(2, me, [got[6], got[7]], (*own[5:7], *second[5:]), weights)

time: 88.9 us -> 97.1 us (1.092); the launches traced: 87.2 us -> 96.8 us
  waiting for transfers between devices: 17 us -> 30.4 us
  starting transfers between devices: 35.3 us -> 32.8 us
  local copies, waits for them, and re-layouts: 8.45 us -> 7.17 us
    ppermute x18, waiting for transfers between devices: 17 us -> 30.4 us  [exchanged(): return lax.ppermute(piece, 'lon', [(s, s ^ distance) for s in range(count)])]
    ppermute x18, starting transfers between devices: 35.3 us -> 32.8 us  [exchanged(): return lax.ppermute(piece, 'lon', [(s, s ^ distance) for s in range(count)])]
    unnamed x30 -> x28, local copies, waits for them, and re-layouts: 8.45 us -> 7.17 us
  transfers between devices with their start and end apart: 18 -> 18, of which waited for: 4 -> 8; matrix products, arithmetic and copies ran while one was open for 0% -> 0% of each run, Pallas kernels for 17% -> 16%
where the time goes in v7:
time: 97.1 us; the launch traced here: 96.8 us
  starting transfers between devices  32.8 us (34%)
  waiting for transfers between devices  30.4 us (31%)
  Pallas kernels  26 us (27%)
  local copies, waits for them, and re-layouts  7.17 us (7%)
    ppermute x18, starting transfers between devices, exchanged(): return lax.ppermute(piece, 'lon', [(s, s ^ distance) for s in range(count)])  32.8 us
    ppermute x18, waiting for transfers between devices, exchanged(): return lax.ppermute(piece, 'lon', [(s, s ^ distance) for s in range(count)])  30.4 us
    pallas_call x3, Pallas kernels, window_layer(): pl.pallas_call(functools.partial(window_kernel, stage), out_shape=outs, i...  17.2 us
    unnamed x28, local copies, waits for them, and re-layouts  7.17 us
    pallas_call x2, Pallas kernels, row_layer(): pl.pallas_call(functools.partial(row_kernel, start, rows), out_shape=(far...  5.44 us
  transfers between devices with their start and end apart: 18, of which 8 were waited for; matrix products, arithmetic and copies ran while one was open for 0% of the time, Pallas kernels for 16%

profile of v7, /device:TPU:0, one launch (start us, length us, event | category | flops | bytes accessed | tf_op | source)
XLA Modules:
  0.0 96.8 jit_solution(10919655111069599694)
XLA Ops:
  0.0 0.0 copy-start
  0.0 0.0 copy-start.13
  0.0 0.8 copy-done.13
  0.8 1.6 %pack.1 = (bf16[784,128]{1,0:T(8,128)(2,1)S(1)}, bf16[784,128]{1,0:T(8,128)(2,1)S(1)}, bf16[784,128]{1,0:T(8,128)(2,1)S(1)}, bf16[784,128]{1,0:T(8,128)(2,1)S(1)...) custom-call(s32[1]{0:T(128)} %bitcast.me_ref, ...), custom_call_target="tpu_custom_call" | custom-call | flops 1600000 | bytes 3200000 | tf_op jit(solution)/shard_map/pack/pallas_call | solution.py:204
  2.4 3.1 %collective-permute-start = (bf16[784,128]{1,0:T(8,128)(2,1)S(1)}, bf16[784,128]{1,0:T(8,128)(2,1)S(1)}, u32[]{:S(2)}, u32[]{:S(2)}) collective-permute-start(bf16[784,128]{1,0:T(8,128)(2,1)S(1)} %get-tuple-element.68), channel_id=1, source_target_pairs={{0,2},{1,3},{2,0},{3,1},{4,6},{5,7},{6,4},{7,5},{8,10},{9,11},{10,... | collective-permute-start | bytes 602120 | tf_op jit(solution)/shard_map/ppermute | solution.py:462
  5.5 2.6 %collective-permute-start.1 = (bf16[784,128]{1,0:T(8,128)(2,1)S(1)}, bf16[784,128]{1,0:T(8,128)(2,1)S(1)}, u32[]{:S(2)}, u32[]{:S(2)}) collective-permute-start(bf16[784,128]{1,0:T(8,128)(2,1)S(1)} %get-tuple-element.69), channel_id=1, source_target_pairs={{0,4},{1,5},{2,6},{3,7},{4,0},{5,1},{6,2},{7,3},{8,12},{9,13},{10,... | collective-permute-start | bytes 602120 | tf_op jit(solution)/shard_map/ppermute | solution.py:462
  8.0 1.4 %collective-permute-start.2 = (bf16[784,128]{1,0:T(8,128)(2,1)S(1)}, bf16[784,128]{1,0:T(8,128)(2,1)S(1)}, u32[]{:S(2)}, u32[]{:S(2)}) collective-permute-start(bf16[784,128]{1,0:T(8,128)(2,1)S(1)} %get-tuple-element.70), channel_id=1, source_target_pairs={{0,3},{1,2},{2,1},{3,0},{4,7},{5,6},{6,5},{7,4},{8,11},{9,10},{10,... | collective-permute-start | bytes 602120 | tf_op jit(solution)/shard_map/ppermute | solution.py:462
  9.4 0.0 collective-permute-start.3
  9.5 1.8 %collective-permute-start.4 = (bf16[784,128]{1,0:T(8,128)(2,1)S(1)}, bf16[784,128]{1,0:T(8,128)(2,1)S(1)}, u32[]{:S(2)}, u32[]{:S(2)}) collective-permute-start(bf16[784,128]{1,0:T(8,128)(2,1)S(1)} %get-tuple-element.72), channel_id=1, source_target_pairs={{0,1},{1,0},{2,3},{3,2},{4,5},{5,4},{6,7},{7,6},{8,9},{9,8},{10,11... | collective-permute-start | bytes 602120 | tf_op jit(solution)/shard_map/ppermute | solution.py:462
  11.2 0.0 copy-done
  11.3 0.0 copy-start.1
  11.3 1.3 %copy-done.1 = bf16[768,768]{1,0:T(8,128)(2,1)S(1)} copy-done((bf16[768,768]{1,0:T(8,128)(2,1)S(1)}, bf16[768,768]{1,0:T(8,128)(2,1)}, u32[]{:S(2)}) %copy-start.1) | copy-done | bytes 1179672
  12.5 1.3 %copy-done.3 = bf16[768,768]{1,0:T(8,128)(2,1)S(1)} copy-done((bf16[768,768]{1,0:T(8,128)(2,1)S(1)}, bf16[768,768]{1,0:T(8,128)(2,1)}, u32[]{:S(2)}) %copy-start.3) | copy-done | bytes 1179672
  13.8 1.7 %collective-permute-done.refs_2_ = bf16[784,128]{1,0:T(8,128)(2,1)S(1)} collective-permute-done((bf16[784,128]{1,0:T(8,128)(2,1)S(1)}, bf16[784,128]{1,0:T(8,128)(2,1)S(1)}, u32[]{:S(2)}, u32[]{:S(2)}) %collective-permute-start) | collective-permute-done | bytes 200736 | tf_op jit(solution)/shard_map/ppermute | solution.py:462
  15.5 4.1 %collective-permute-start.5 = (bf16[784,128]{1,0:T(8,128)(2,1)S(1)}, bf16[784,128]{1,0:T(8,128)(2,1)S(1)}, u32[]{:S(2)}, u32[]{:S(2)}) collective-permute-start(bf16[784,128]{1,0:T(8,128)(2,1)S(1)} %get-tuple-element.91), channel_id=1, source_target_pairs={{0,6},{1,7},{2,4},{3,5},{4,2},{5,3},{6,0},{7,1},{8,14},{9,15},{10,... | collective-permute-start | bytes 602120 | tf_op jit(solution)/shard_map/ppermute | solution.py:462
  19.5 0.0 collective-permute-done.1.refs_0_
  19.5 2.6 %collective-permute-start.6 = (bf16[784,128]{1,0:T(8,128)(2,1)S(1)}, bf16[784,128]{1,0:T(8,128)(2,1)S(1)}, u32[]{:S(2)}, u32[]{:S(2)}) collective-permute-start(bf16[784,128]{1,0:T(8,128)(2,1)S(1)} %get-tuple-element.92), channel_id=1, source_target_pairs={{0,7},{1,6},{2,5},{3,4},{4,3},{5,2},{6,1},{7,0},{8,15},{9,14},{10,... | collective-permute-start | bytes 602120 | tf_op jit(solution)/shard_map/ppermute | solution.py:462
  22.1 1.8 %collective-permute-done.2.refs_3_ = bf16[784,128]{1,0:T(8,128)(2,1)S(1)} collective-permute-done((bf16[784,128]{1,0:T(8,128)(2,1)S(1)}, bf16[784,128]{1,0:T(8,128)(2,1)S(1)}, u32[]{:S(2)}, u32[]{:S(2)}) %collective-permute-start.2) | collective-permute-done | bytes 200736 | tf_op jit(solution)/shard_map/ppermute | solution.py:462
  23.9 12.6 %collective-permute-done.3.refs_1_ = bf16[784,128]{1,0:T(8,128)(2,1)S(1)} collective-permute-done((bf16[784,128]{1,0:T(8,128)(2,1)S(1)}, bf16[784,128]{1,0:T(8,128)(2,1)S(1)}, u32[]{:S(2)}, u32[]{:S(2)}) %collective-permute-start.3) | collective-permute-done | bytes 200736 | tf_op jit(solution)/shard_map/ppermute | solution.py:462
  36.5 0.0 collective-permute-done.4.refs_1_
  36.5 0.0 copy-done.2
  36.5 0.0 copy-done.4
  36.5 0.0 copy-done.6
  36.5 0.0 copy-start.7
  36.5 1.3 %copy-done.7 = bf16[768,768]{1,0:T(8,128)(2,1)S(1)} copy-done((bf16[768,768]{1,0:T(8,128)(2,1)S(1)}, bf16[768,768]{1,0:T(8,128)(2,1)}, u32[]{:S(2)}) %copy-start.7) | copy-done | bytes 1179672
  37.7 1.3 %copy-done.9 = bf16[768,768]{1,0:T(8,128)(2,1)S(1)} copy-done((bf16[768,768]{1,0:T(8,128)(2,1)S(1)}, bf16[768,768]{1,0:T(8,128)(2,1)}, u32[]{:S(2)}) %copy-start.9) | copy-done | bytes 1179672
  39.0 1.3 %copy-done.11 = bf16[768,768]{1,0:T(8,128)(2,1)S(1)} copy-done((bf16[768,768]{1,0:T(8,128)(2,1)S(1)}, bf16[768,768]{1,0:T(8,128)(2,1)}, u32[]{:S(2)}) %copy-start.11) | copy-done | bytes 1179672
  40.3 6.9 %window_layer.3 = (bf16[8,48,768]{2,1,0:T(8,128)(2,1)S(1)}, bf16[8,48,768]{2,1,0:T(8,128)(2,1)S(1)}, bf16[8,48,768]{2,1,0:T(8,128)(2,1)S(1)}, bf16[8,48,768]{2,1...) custom-call(s32[1]{0:T(128)} %bitcast.me_ref, ...), custom_call_target="tpu_custom_call" | custom-call | flops 4051697664 | bytes 16777216 | tf_op jit(solution)/shard_map/window_layer/pallas_call | solution.py:346
  47.2 0.0 copy-done.10
  47.2 0.0 copy-done.12
  47.2 0.0 copy-start.8
  47.2 4.4 %window_layer.4 = (bf16[8,32,768]{2,1,0:T(8,128)(2,1)S(1)}, bf16[8,32,768]{2,1,0:T(8,128)(2,1)S(1)}, bf16[8,32,768]{2,1,0:T(8,128)(2,1)S(1)}, bf16[8,32,768]{2,1...) custom-call(s32[1]{0:T(128)} %bitcast.me_ref, ...), custom_call_target="tpu_custom_call" | custom-call | flops 2315255808 | bytes 16777216 | tf_op jit(solution)/shard_map/window_layer/pallas_call | solution.py:346
  51.7 0.0 collective-permute-done.5.refs_0_
  51.7 0.0 collective-permute-done.6.refs_1_
  51.7 0.0 copy-done.8
  51.7 0.0 copy-start.5
  51.7 5.8 %window_layer.5 = (bf16[8,48,768]{2,1,0:T(8,128)(2,1)S(1)}, bf16[8,48,768]{2,1,0:T(8,128)(2,1)S(1)}, bf16[8,48,768]{2,1,0:T(8,128)(2,1)S(1)}, bf16[8,48,768]{2,1,0:T(8,128)(2,1)S(1)}, bf16[8,48,128]{2,1,0:T(8,128)(2,1)S(1)}) custom-call(s32[1]{0:T(128)} %bitcast.me_ref, bf16[784,128]{1,0:T(8,128)(2,1)S(1)} %collective-permute-done.5.refs_0_, ...), custom_call_target="tpu_custom_call" | custom-call | flops 2894069760 | bytes 16777216 | tf_op jit(solution)/shard_map/window_layer/pallas_call | solution.py:346
  57.6 0.0 copy-done.5
  57.6 2.7 %row_layer.2 = (bf16[4,16,768]{2,1,0:T(8,128)(2,1)S(1)}, bf16[4,16,768]{2,1,0:T(8,128)(2,1)S(1)}, bf16[4,16,768]{2,1,0:T(8,128)(2,1)S(1)}, bf16[4,16,768]{2,1,0:...) custom-call(s32[1]{0:T(128)} %bitcast.me_ref, ...), custom_call_target="tpu_custom_call" | custom-call | bytes 65536 | tf_op jit(solution)/shard_map/row_layer/pallas_call | solution.py:414
  60.3 2.9 %collective-permute-start.11 = (bf16[4,16,768]{2,1,0:T(8,128)(2,1)S(1)}, bf16[4,16,768]{2,1,0:T(8,128)(2,1)S(1)}, u32[]{:S(2)}, u32[]{:S(2)}) collective-permute-start(bf16[4,16,768]{2,1,0:T(8,128)(2,1)S(1)} %get-tuple-element.115), channel_id=1, source_target_pairs={{0,6},{1,7},{2,4},{3,5},{4,2},{5,3},{6,0},{7,1},{8,14},{9,15},{10,... | collective-permute-start | bytes 294920 | tf_op jit(solution)/shard_map/ppermute | solution.py:462
  63.1 0.0 collective-permute-start.9
  63.2 2.9 %collective-permute-start.7 = (bf16[4,16,768]{2,1,0:T(8,128)(2,1)S(1)}, bf16[4,16,768]{2,1,0:T(8,128)(2,1)S(1)}, u32[]{:S(2)}, u32[]{:S(2)}) collective-permute-start(bf16[4,16,768]{2,1,0:T(8,128)(2,1)S(1)} %get-tuple-element.107), channel_id=1, source_target_pairs={{0,4},{1,5},{2,6},{3,7},{4,0},{5,1},{6,2},{7,3},{8,12},{9,13},{10,... | collective-permute-start | bytes 294920 | tf_op jit(solution)/shard_map/ppermute | solution.py:462
  66.0 2.7 %row_layer.3 = (bf16[4,16,768]{2,1,0:T(8,128)(2,1)S(1)}, bf16[4,16,768]{2,1,0:T(8,128)(2,1)S(1)}, bf16[4,16,768]{2,1,0:T(8,128)(2,1)S(1)}, bf16[4,16,768]{2,1,0:...) custom-call(s32[1]{0:T(128)} %bitcast.me_ref, ...), custom_call_target="tpu_custom_call" | custom-call | bytes 65536 | tf_op jit(solution)/shard_map/row_layer/pallas_call | solution.py:414
  68.7 0.0 collective-permute-done.11.refs_2_
  68.8 0.1 collective-permute-start.17
  68.8 6.7 %collective-permute-done.9.refs_1_ = bf16[4,16,768]{2,1,0:T(8,128)(2,1)S(1)} collective-permute-done((bf16[4,16,768]{2,1,0:T(8,128)(2,1)S(1)}, bf16[4,16,768]{2,1,0:T(8,128)(2,1)S(1)}, u32[]{:S(2)}, u32[]{:S(2)}) %collective-permute-start.9) | collective-permute-done | bytes 98336 | tf_op jit(solution)/shard_map/ppermute | solution.py:462
  75.5 0.0 collective-permute-start.16
  75.5 4.0 %collective-permute-start.13 = (bf16[4,16,768]{2,1,0:T(8,128)(2,1)S(1)}, bf16[4,16,768]{2,1,0:T(8,128)(2,1)S(1)}, u32[]{:S(2)}, u32[]{:S(2)}) collective-permute-start(bf16[4,16,768]{2,1,0:T(8,128)(2,1)S(1)} %get-tuple-element.119), channel_id=1, source_target_pairs={{0,7},{1,6},{2,5},{3,4},{4,3},{5,2},{6,1},{7,0},{8,15},{9,14},{10,... | collective-permute-start | bytes 294920 | tf_op jit(solution)/shard_map/ppermute | solution.py:462
  79.5 0.0 collective-permute-done.7.refs_0_
  79.5 0.5 collective-permute-start.15
  80.0 0.8 collective-permute-start.8
  80.8 3.5 %collective-permute-done.13.refs_3_ = bf16[4,16,768]{2,1,0:T(8,128)(2,1)S(1)} collective-permute-done((bf16[4,16,768]{2,1,0:T(8,128)(2,1)S(1)}, bf16[4,16,768]{2,1,0:T(8,128)(2,1)S(1)}, u32[]{:S(2)}, u32[]{:S(2)}) %collective-permute-start.13) | collective-permute-done | bytes 98336 | tf_op jit(solution)/shard_map/ppermute | solution.py:462
  84.3 3.4 %collective-permute-start.10 = (bf16[4,16,768]{2,1,0:T(8,128)(2,1)S(1)}, bf16[4,16,768]{2,1,0:T(8,128)(2,1)S(1)}, u32[]{:S(2)}, u32[]{:S(2)}) collective-permute-start(bf16[4,16,768]{2,1,0:T(8,128)(2,1)S(1)} %get-tuple-element.112), channel_id=1, source_target_pairs={{0,5},{1,4},{2,7},{3,6},{4,1},{5,0},{6,3},{7,2},{8,13},{9,12},{10,... | collective-permute-start | bytes 294920 | tf_op jit(solution)/shard_map/ppermute | solution.py:462
  87.7 0.0 collective-permute-done.17.refs_6_
  87.7 0.7 collective-permute-start.12
  88.4 0.0 collective-permute-done.16.refs_5_
  88.4 2.1 %collective-permute-start.14 = (bf16[4,16,768]{2,1,0:T(8,128)(2,1)S(1)}, bf16[4,16,768]{2,1,0:T(8,128)(2,1)S(1)}, u32[]{:S(2)}, u32[]{:S(2)}) collective-permute-start(bf16[4,16,768]{2,1,0:T(8,128)(2,1)S(1)} %get-tuple-element.120), channel_id=1, source_target_pairs={{0,7},{1,6},{2,5},{3,4},{4,3},{5,2},{6,1},{7,0},{8,15},{9,14},{10,... | collective-permute-start | bytes 294920 | tf_op jit(solution)/shard_map/ppermute | solution.py:462
  90.5 0.0 collective-permute-done.15.refs_4_
  90.5 1.1 %place.2.refs_4_ = bf16[64,16,768]{2,1,0:T(8,128)(2,1)} custom-call(s32[1]{0:T(128)} %bitcast.me_ref, bf16[4,16,768]{2,1,0:T(8,128)(2,1)S(1)} %collective-permute-done.7.refs_0_, bf16[4,16,768]{2,1,0:T(8,128)(2,1)S(1)} %collective-permute-done.9.refs_1_, bf16[4,16,768]{2,1,0:T(8,128)(2,1)S(1)} %collective-permute-done.11.refs_2_, ...), custom_call_target="tpu_custom_call" | custom-call | bytes 4194304 | tf_op jit(solution)/shard_map/place/pallas_call | solution.py:447
  91.6 0.0 collective-permute-done.8.refs_0_
  91.6 0.2 collective-permute-done.10.refs_1_
  91.8 2.4 %collective-permute-done.12.refs_2_ = bf16[4,16,768]{2,1,0:T(8,128)(2,1)S(1)} collective-permute-done((bf16[4,16,768]{2,1,0:T(8,128)(2,1)S(1)}, bf16[4,16,768]{2,1,0:T(8,128)(2,1)S(1)}, u32[]{:S(2)}, u32[]{:S(2)}) %collective-permute-start.12) | collective-permute-done | bytes 98336 | tf_op jit(solution)/shard_map/ppermute | solution.py:462
  94.2 1.6 %collective-permute-done.14.refs_3_ = bf16[4,16,768]{2,1,0:T(8,128)(2,1)S(1)} collective-permute-done((bf16[4,16,768]{2,1,0:T(8,128)(2,1)S(1)}, bf16[4,16,768]{2,1,0:T(8,128)(2,1)S(1)}, u32[]{:S(2)}, u32[]{:S(2)}) %collective-permute-start.14) | collective-permute-done | bytes 98336 | tf_op jit(solution)/shard_map/ppermute | solution.py:462
  95.8 0.8 place.3
  (9 shorter events, 0.0 us)
Async XLA Ops:
  0.0 11.3 %copy-start = (bf16[768,768]{1,0:T(8,128)(2,1)S(1)}, bf16[768,768]{1,0:T(8,128)(2,1)}, u32[]{:S(2)}) copy-start(bf16[768,768]{1,0:T(8,128)(2,1)} %refs_8_.5) | copy-start | bytes 3538948
  0.0 0.8 copy-start.13
  2.4 13.1 %collective-permute-start = (bf16[784,128]{1,0:T(8,128)(2,1)S(1)}, bf16[784,128]{1,0:T(8,128)(2,1)S(1)}, u32[]{:S(2)}, u32[]{:S(2)}) collective-permute-start(bf16[784,128]{1,0:T(8,128)(2,1)S(1)} %get-tuple-element.68), channel_id=1, source_target_pairs={{0,2},{1,3},{2,0},{3,1},{4,6},{5,7},{6,4},{7,5},{8,10},{9,11},{10,... | collective-permute-start | bytes 602120 | tf_op jit(solution)/shard_map/ppermute | solution.py:462
  5.5 14.1 %collective-permute-start.1 = (bf16[784,128]{1,0:T(8,128)(2,1)S(1)}, bf16[784,128]{1,0:T(8,128)(2,1)S(1)}, u32[]{:S(2)}, u32[]{:S(2)}) collective-permute-start(bf16[784,128]{1,0:T(8,128)(2,1)S(1)} %get-tuple-element.69), channel_id=1, source_target_pairs={{0,4},{1,5},{2,6},{3,7},{4,0},{5,1},{6,2},{7,3},{8,12},{9,13},{10,... | collective-permute-start | bytes 602120 | tf_op jit(solution)/shard_map/ppermute | solution.py:462
  8.0 15.8 %collective-permute-start.2 = (bf16[784,128]{1,0:T(8,128)(2,1)S(1)}, bf16[784,128]{1,0:T(8,128)(2,1)S(1)}, u32[]{:S(2)}, u32[]{:S(2)}) collective-permute-start(bf16[784,128]{1,0:T(8,128)(2,1)S(1)} %get-tuple-element.70), channel_id=1, source_target_pairs={{0,3},{1,2},{2,1},{3,0},{4,7},{5,6},{6,5},{7,4},{8,11},{9,10},{10,... | collective-permute-start | bytes 602120 | tf_op jit(solution)/shard_map/ppermute | solution.py:462
  9.4 27.0 %collective-permute-start.3 = (bf16[784,128]{1,0:T(8,128)(2,1)S(1)}, bf16[784,128]{1,0:T(8,128)(2,1)S(1)}, u32[]{:S(2)}, u32[]{:S(2)}) collective-permute-start(bf16[784,128]{1,0:T(8,128)(2,1)S(1)} %get-tuple-element.71), channel_id=1, source_target_pairs={{0,5},{1,4},{2,7},{3,6},{4,1},{5,0},{6,3},{7,2},{8,13},{9,12},{10,... | collective-permute-start | bytes 602120 | tf_op jit(solution)/shard_map/ppermute | solution.py:462
  9.5 27.0 %collective-permute-start.4 = (bf16[784,128]{1,0:T(8,128)(2,1)S(1)}, bf16[784,128]{1,0:T(8,128)(2,1)S(1)}, u32[]{:S(2)}, u32[]{:S(2)}) collective-permute-start(bf16[784,128]{1,0:T(8,128)(2,1)S(1)} %get-tuple-element.72), channel_id=1, source_target_pairs={{0,1},{1,0},{2,3},{3,2},{4,5},{5,4},{6,7},{7,6},{8,9},{9,8},{10,11... | collective-permute-start | bytes 602120 | tf_op jit(solution)/shard_map/ppermute | solution.py:462
  11.3 1.3 %copy-start.1 = (bf16[768,768]{1,0:T(8,128)(2,1)S(1)}, bf16[768,768]{1,0:T(8,128)(2,1)}, u32[]{:S(2)}) copy-start(bf16[768,768]{1,0:T(8,128)(2,1)} %refs_9_.5) | copy-start | bytes 3538948
  12.5 1.3 %copy-start.3 = (bf16[768,768]{1,0:T(8,128)(2,1)S(1)}, bf16[768,768]{1,0:T(8,128)(2,1)}, u32[]{:S(2)}) copy-start(bf16[768,768]{1,0:T(8,128)(2,1)} %refs_10_.5) | copy-start | bytes 3538948
  13.8 22.7 %copy-start.2 = (bf16[768,768]{1,0:T(8,128)(2,1)S(1)}, bf16[768,768]{1,0:T(8,128)(2,1)}, u32[]{:S(2)}) copy-start(bf16[768,768]{1,0:T(8,128)(2,1)} %refs_9_.5) | copy-start | bytes 3538948
  13.8 22.7 %copy-start.4 = (bf16[768,768]{1,0:T(8,128)(2,1)S(1)}, bf16[768,768]{1,0:T(8,128)(2,1)}, u32[]{:S(2)}) copy-start(bf16[768,768]{1,0:T(8,128)(2,1)} %refs_10_.5) | copy-start | bytes 3538948
  13.8 22.7 %copy-start.6 = (bf16[768,768]{1,0:T(8,128)(2,1)S(1)}, bf16[768,768]{1,0:T(8,128)(2,1)}, u32[]{:S(2)}) copy-start(bf16[768,768]{1,0:T(8,128)(2,1)} %refs_11_.5) | copy-start | bytes 3538948
  15.5 36.2 %collective-permute-start.5 = (bf16[784,128]{1,0:T(8,128)(2,1)S(1)}, bf16[784,128]{1,0:T(8,128)(2,1)S(1)}, u32[]{:S(2)}, u32[]{:S(2)}) collective-permute-start(bf16[784,128]{1,0:T(8,128)(2,1)S(1)} %get-tuple-element.91), channel_id=1, source_target_pairs={{0,6},{1,7},{2,4},{3,5},{4,2},{5,3},{6,0},{7,1},{8,14},{9,15},{10,... | collective-permute-start | bytes 602120 | tf_op jit(solution)/shard_map/ppermute | solution.py:462
  19.5 32.2 %collective-permute-start.6 = (bf16[784,128]{1,0:T(8,128)(2,1)S(1)}, bf16[784,128]{1,0:T(8,128)(2,1)S(1)}, u32[]{:S(2)}, u32[]{:S(2)}) collective-permute-start(bf16[784,128]{1,0:T(8,128)(2,1)S(1)} %get-tuple-element.92), channel_id=1, source_target_pairs={{0,7},{1,6},{2,5},{3,4},{4,3},{5,2},{6,1},{7,0},{8,15},{9,14},{10,... | collective-permute-start | bytes 602120 | tf_op jit(solution)/shard_map/ppermute | solution.py:462
  36.5 1.3 %copy-start.7 = (bf16[768,768]{1,0:T(8,128)(2,1)S(1)}, bf16[768,768]{1,0:T(8,128)(2,1)}, u32[]{:S(2)}) copy-start(bf16[768,768]{1,0:T(8,128)(2,1)} %refs_12_.3) | copy-start | bytes 3538948
  37.7 1.3 %copy-start.9 = (bf16[768,768]{1,0:T(8,128)(2,1)S(1)}, bf16[768,768]{1,0:T(8,128)(2,1)}, u32[]{:S(2)}) copy-start(bf16[768,768]{1,0:T(8,128)(2,1)} %refs_13_.1) | copy-start | bytes 3538948
  39.0 1.3 %copy-start.11 = (bf16[768,768]{1,0:T(8,128)(2,1)S(1)}, bf16[768,768]{1,0:T(8,128)(2,1)}, u32[]{:S(2)}) copy-start(bf16[768,768]{1,0:T(8,128)(2,1)} %refs_14_.1) | copy-start | bytes 3538948
  40.3 6.9 %copy-start.10 = (bf16[768,768]{1,0:T(8,128)(2,1)S(1)}, bf16[768,768]{1,0:T(8,128)(2,1)}, u32[]{:S(2)}) copy-start(bf16[768,768]{1,0:T(8,128)(2,1)} %refs_13_.1) | copy-start | bytes 3538948
  40.3 6.9 %copy-start.12 = (bf16[768,768]{1,0:T(8,128)(2,1)S(1)}, bf16[768,768]{1,0:T(8,128)(2,1)}, u32[]{:S(2)}) copy-start(bf16[768,768]{1,0:T(8,128)(2,1)} %refs_14_.1) | copy-start | bytes 3538948
  47.2 4.5 %copy-start.8 = (bf16[768,768]{1,0:T(8,128)(2,1)S(1)}, bf16[768,768]{1,0:T(8,128)(2,1)}, u32[]{:S(2)}) copy-start(bf16[768,768]{1,0:T(8,128)(2,1)} %refs_12_.3) | copy-start | bytes 3538948
  51.7 5.9 %copy-start.5 = (bf16[768,768]{1,0:T(8,128)(2,1)S(1)}, bf16[768,768]{1,0:T(8,128)(2,1)}, u32[]{:S(2)}) copy-start(bf16[768,768]{1,0:T(8,128)(2,1)} %refs_15_.3) | copy-start | bytes 3538948
  60.3 8.5 %collective-permute-start.11 = (bf16[4,16,768]{2,1,0:T(8,128)(2,1)S(1)}, bf16[4,16,768]{2,1,0:T(8,128)(2,1)S(1)}, u32[]{:S(2)}, u32[]{:S(2)}) collective-permute-start(bf16[4,16,768]{2,1,0:T(8,128)(2,1)S(1)} %get-tuple-element.115), channel_id=1, source_target_pairs={{0,6},{1,7},{2,4},{3,5},{4,2},{5,3},{6,0},{7,1},{8,14},{9,15},{10,... | collective-permute-start | bytes 294920 | tf_op jit(solution)/shard_map/ppermute | solution.py:462
  63.1 12.4 %collective-permute-start.9 = (bf16[4,16,768]{2,1,0:T(8,128)(2,1)S(1)}, bf16[4,16,768]{2,1,0:T(8,128)(2,1)S(1)}, u32[]{:S(2)}, u32[]{:S(2)}) collective-permute-start(bf16[4,16,768]{2,1,0:T(8,128)(2,1)S(1)} %get-tuple-element.111), channel_id=1, source_target_pairs={{0,5},{1,4},{2,7},{3,6},{4,1},{5,0},{6,3},{7,2},{8,13},{9,12},{10,... | collective-permute-start | bytes 294920 | tf_op jit(solution)/shard_map/ppermute | solution.py:462
  63.2 16.3 %collective-permute-start.7 = (bf16[4,16,768]{2,1,0:T(8,128)(2,1)S(1)}, bf16[4,16,768]{2,1,0:T(8,128)(2,1)S(1)}, u32[]{:S(2)}, u32[]{:S(2)}) collective-permute-start(bf16[4,16,768]{2,1,0:T(8,128)(2,1)S(1)} %get-tuple-element.107), channel_id=1, source_target_pairs={{0,4},{1,5},{2,6},{3,7},{4,0},{5,1},{6,2},{7,3},{8,12},{9,13},{10,... | collective-permute-start | bytes 294920 | tf_op jit(solution)/shard_map/ppermute | solution.py:462
  68.8 18.9 %collective-permute-start.17 = (bf16[8,16,768]{2,1,0:T(8,128)(2,1)S(1)}, bf16[8,16,768]{2,1,0:T(8,128)(2,1)S(1)}, u32[]{:S(2)}, u32[]{:S(2)}) collective-permute-start(bf16[8,16,768]{2,1,0:T(8,128)(2,1)S(1)} %get-tuple-element.127), channel_id=1, source_target_pairs={{0,3},{1,2},{2,1},{3,0},{4,7},{5,6},{6,5},{7,4},{8,11},{9,10},{10,... | collective-permute-start | bytes 589832 | tf_op jit(solution)/shard_map/ppermute | solution.py:462
  75.5 12.9 %collective-permute-start.16 = (bf16[8,16,768]{2,1,0:T(8,128)(2,1)S(1)}, bf16[8,16,768]{2,1,0:T(8,128)(2,1)S(1)}, u32[]{:S(2)}, u32[]{:S(2)}) collective-permute-start(bf16[8,16,768]{2,1,0:T(8,128)(2,1)S(1)} %get-tuple-element.126), channel_id=1, source_target_pairs={{0,2},{1,3},{2,0},{3,1},{4,6},{5,7},{6,4},{7,5},{8,10},{9,11},{10,... | collective-permute-start | bytes 589832 | tf_op jit(solution)/shard_map/ppermute | solution.py:462
  75.5 8.8 %collective-permute-start.13 = (bf16[4,16,768]{2,1,0:T(8,128)(2,1)S(1)}, bf16[4,16,768]{2,1,0:T(8,128)(2,1)S(1)}, u32[]{:S(2)}, u32[]{:S(2)}) collective-permute-start(bf16[4,16,768]{2,1,0:T(8,128)(2,1)S(1)} %get-tuple-element.119), channel_id=1, source_target_pairs={{0,7},{1,6},{2,5},{3,4},{4,3},{5,2},{6,1},{7,0},{8,15},{9,14},{10,... | collective-permute-start | bytes 294920 | tf_op jit(solution)/shard_map/ppermute | solution.py:462
  79.5 11.0 %collective-permute-start.15 = (bf16[8,16,768]{2,1,0:T(8,128)(2,1)S(1)}, bf16[8,16,768]{2,1,0:T(8,128)(2,1)S(1)}, u32[]{:S(2)}, u32[]{:S(2)}) collective-permute-start(bf16[8,16,768]{2,1,0:T(8,128)(2,1)S(1)} %get-tuple-element.125), channel_id=1, source_target_pairs={{0,1},{1,0},{2,3},{3,2},{4,5},{5,4},{6,7},{7,6},{8,9},{9,8},{10,11... | collective-permute-start | bytes 589832 | tf_op jit(solution)/shard_map/ppermute | solution.py:462
  80.0 11.6 %collective-permute-start.8 = (bf16[4,16,768]{2,1,0:T(8,128)(2,1)S(1)}, bf16[4,16,768]{2,1,0:T(8,128)(2,1)S(1)}, u32[]{:S(2)}, u32[]{:S(2)}) collective-permute-start(bf16[4,16,768]{2,1,0:T(8,128)(2,1)S(1)} %get-tuple-element.108), channel_id=1, source_target_pairs={{0,4},{1,5},{2,6},{3,7},{4,0},{5,1},{6,2},{7,3},{8,12},{9,13},{10,... | collective-permute-start | bytes 294920 | tf_op jit(solution)/shard_map/ppermute | solution.py:462
  84.3 7.5 %collective-permute-start.10 = (bf16[4,16,768]{2,1,0:T(8,128)(2,1)S(1)}, bf16[4,16,768]{2,1,0:T(8,128)(2,1)S(1)}, u32[]{:S(2)}, u32[]{:S(2)}) collective-permute-start(bf16[4,16,768]{2,1,0:T(8,128)(2,1)S(1)} %get-tuple-element.112), channel_id=1, source_target_pairs={{0,5},{1,4},{2,7},{3,6},{4,1},{5,0},{6,3},{7,2},{8,13},{9,12},{10,... | collective-permute-start | bytes 294920 | tf_op jit(solution)/shard_map/ppermute | solution.py:462
  87.7 6.5 %collective-permute-start.12 = (bf16[4,16,768]{2,1,0:T(8,128)(2,1)S(1)}, bf16[4,16,768]{2,1,0:T(8,128)(2,1)S(1)}, u32[]{:S(2)}, u32[]{:S(2)}) collective-permute-start(bf16[4,16,768]{2,1,0:T(8,128)(2,1)S(1)} %get-tuple-element.116), channel_id=1, source_target_pairs={{0,6},{1,7},{2,4},{3,5},{4,2},{5,3},{6,0},{7,1},{8,14},{9,15},{10,... | collective-permute-start | bytes 294920 | tf_op jit(solution)/shard_map/ppermute | solution.py:462
  88.4 7.4 %collective-permute-start.14 = (bf16[4,16,768]{2,1,0:T(8,128)(2,1)S(1)}, bf16[4,16,768]{2,1,0:T(8,128)(2,1)S(1)}, u32[]{:S(2)}, u32[]{:S(2)}) collective-permute-start(bf16[4,16,768]{2,1,0:T(8,128)(2,1)S(1)} %get-tuple-element.120), channel_id=1, source_target_pairs={{0,7},{1,6},{2,5},{3,4},{4,3},{5,2},{6,1},{7,0},{8,15},{9,14},{10,... | collective-permute-start | bytes 294920 | tf_op jit(solution)/shard_map/ppermute | solution.py:462

commit v8 on v5

--- a/solution.py
+++ b/solution.py
@@ -250,6 +250,8 @@
 def window_kernel(stage, me_ref, *refs):
     pieces = refs[: (4, 2, 2)[stage]]
     refs = refs[len(pieces) :]
+    if stage > 0:
+        others, refs = refs[:2], refs[2:]
     carried = refs[: (0, 3, 5)[stage]]
     refs = refs[len(carried) :]
     _, wq, wk, wv, wo, wq2, wk2, wv2, y_ref, q2_ref, k2_ref, v2_ref, m_ref = refs[:13]
@@ -262,7 +264,7 @@
     upper = jnp.bitwise_and(me, 2) > 0
     low = jnp.bitwise_and(me, len(pieces) - 1)
     for d, piece in enumerate(pieces):
-        placed[jnp.bitwise_xor(low, d)] = piece[...]
+        placed[jnp.bitwise_xor(low, d)] = piece[...] if stage == 0 else jnp.where(me_ref[1] > 0, piece[...], others[d][...])
     columns = [unpacked(me, placed[l]) for l in range(len(pieces))]
     mask = low_columns((8, 8, width + 128), 1)
     full = (64, width + 128)
@@ -331,7 +333,7 @@
     v2_ref[...] = dot_f32(h, wv2[...]).astype(jnp.bfloat16).reshape(v2_ref.shape)
 
 
-def window_layer(stage, me, pieces, carried, weights):
+def window_layer(stage, me, pieces, others, carried, weights):
     width = weights[1].shape[0]
     tokens = 64 * STAGES[stage][0]
     columns = 8 * STAGES[stage][1]
@@ -342,7 +344,7 @@
     outs = (part,) * 4 + (marks,) + ((edge, edge, tail), (edge, edge, tail), ())[stage]
     vmem = pl.BlockSpec(memory_space=pltpu.VMEM)
     work = pltpu.VMEM((tokens, width), jnp.bfloat16)
-    inputs = [*pieces, *carried, *weights]
+    inputs = [*pieces, *others, *carried, *weights]
     return pl.pallas_call(
         functools.partial(window_kernel, stage),
         out_shape=outs,
@@ -462,20 +464,32 @@
     return lax.ppermute(piece, "lon", [(s, s ^ distance) for s in range(count)])
 
 
+def exchanged_of(lat, piece, distance):
+    count = lax.axis_size("lon")
+    pairs = [(lat * count + s, lat * count + (s ^ distance)) for s in range(count)]
+    return lax.ppermute(piece, ("lat", "lon"), pairs)
+
+
 def gathered_bands(
     fields, ocean, w_query1, w_key1, w_value1, w_out1, w_query2, w_key2, w_value2, w_out2
 ):
-    me = lax.axis_index("lon").astype(jnp.int32).reshape(1)
+    me = jnp.stack([lax.axis_index("lon"), lax.axis_index("lat")]).astype(jnp.int32)
     weights = (w_query1, w_key1, w_value1, w_out1, w_query2, w_key2, w_value2)
     weights = (ready(weights), *weights)
 
     packed = dict(zip(ORDER, pack(ORDER, me, ocean.T, fields)))
-    got = {d: exchanged(packed[d], d) if d else packed[d] for d in ORDER}
-    got[4], *near = lax.optimization_barrier((got[4], got[2], got[3], got[1]))
-    got[2], got[3], got[1] = near
-    own = window_layer(0, me, [got[d] for d in range(4)], (), weights)
-    second = window_layer(1, me, [got[4], got[5]], own[5:], weights)
-    third = window_layer(2, me, [got[6], got[7]], (*own[5:7], *second[5:]), weights)
+    got = {0: packed[0], 2: exchanged(packed[2], 2), 3: exchanged(packed[3], 3)}
+    last, got[2] = lax.optimization_barrier((packed[7], got[2]))
+    packed[1], got[3] = lax.optimization_barrier((packed[1], got[3]))
+    got[1] = exchanged(packed[1], 1)
+    far = {d: exchanged_of(1, last if d == 7 else packed[d], d) for d in ORDER[:4]}
+    far_other = {}
+    for d in ORDER[:4]:
+        packed[d], far[d] = lax.optimization_barrier((packed[d], far[d]))
+        far_other[d] = exchanged_of(0, packed[d], d)
+    own = window_layer(0, me, [got[d] for d in range(4)], (), (), weights)
+    second = window_layer(1, me, [far[4], far[5]], [far_other[4], far_other[5]], own[5:], weights)
+    third = window_layer(2, me, [far[6], far[7]], [far_other[6], far_other[7]], (*own[5:7], *second[5:]), weights)
     parts = (*own[:5], *second[:5], *third)
     first = row_layer(0, ROWS_FIRST, me, parts, w_out2, ())
     last = row_layer(ROWS_FIRST, 8 - ROWS_FIRST, me, parts, w_out2, first[4:])

time: 88.9 us -> 104 us (1.17)
  starting transfers between devices: 35.3 us -> 41.6 us
  waiting for transfers between devices: 17 us -> 21.8 us
  Pallas kernels: 26.1 us -> 30.8 us
    ppermute x0 -> x8, starting transfers between devices: none -> 18.2 us  [exchanged_of(): return lax.ppermute(piece, ('lat', 'lon'), pairs)]
    ppermute x18 -> x14, starting transfers between devices: 35.3 us -> 23.4 us  [exchanged(): return lax.ppermute(piece, 'lon', [(s, s ^ distance) for s in range(count)])]
    ppermute x18 -> x14, waiting for transfers between devices: 17 us -> 21.8 us  [exchanged(): return lax.ppermute(piece, 'lon', [(s, s ^ distance) for s in range(count)])]
    pallas_call x3, Pallas kernels: 17.3 us -> 19.1 us  [window_layer(): pl.pallas_call(functools.partial(window_kernel, stage), out_shape=outs, i...]
    pallas_call x2, Pallas kernels: 5.42 us -> 6.6 us  [row_layer(): pl.pallas_call(functools.partial(row_kernel, start, rows), out_shape=(far...]
    pallas_call x2, Pallas kernels: 1.84 us -> 2.93 us  [place(): pl.pallas_call(functools.partial(place_kernel, spots), out_shape=jax.Shap...]
  transfers between devices with their start and end apart: 18 -> 22, of which waited for: 4 -> 6; matrix products, arithmetic and copies ran while one was open for 0% -> 0% of each run, Pallas kernels for 17% -> 17%
where the time goes in v8:
time: 104 us; the launch traced here: 103 us
  starting transfers between devices  41.6 us (40%)
  Pallas kernels  30.8 us (30%)
  waiting for transfers between devices  21.8 us (21%)
  local copies, waits for them, and re-layouts  8.43 us (8%)
    ppermute x14, starting transfers between devices, exchanged(): return lax.ppermute(piece, 'lon', [(s, s ^ distance) for s in range(count)])  23.4 us
    ppermute x14, waiting for transfers between devices, exchanged(): return lax.ppermute(piece, 'lon', [(s, s ^ distance) for s in range(count)])  21.8 us
    pallas_call x3, Pallas kernels, window_layer(): pl.pallas_call(functools.partial(window_kernel, stage), out_shape=outs, i...  19.1 us
    ppermute x8, starting transfers between devices, exchanged_of(): return lax.ppermute(piece, ('lat', 'lon'), pairs)  18.2 us
    unnamed x30, local copies, waits for them, and re-layouts  8.43 us
    pallas_call x2, Pallas kernels, row_layer(): pl.pallas_call(functools.partial(row_kernel, start, rows), out_shape=(far...  6.6 us
    pallas_call x2, Pallas kernels, place(): pl.pallas_call(functools.partial(place_kernel, spots), out_shape=jax.Shap...  2.93 us
    pallas_call x1, Pallas kernels, pack(): pl.pallas_call(functools.partial(pack_kernel, distances), out_shape=(piec...  2.11 us
  transfers between devices with their start and end apart: 22, of which 6 were waited for; matrix products, arithmetic and copies ran while one was open for 0% of the time, Pallas kernels for 17%

profile of v8, /device:TPU:0, one launch (start us, length us, event | category | flops | bytes accessed | tf_op | source)
XLA Modules:
  0.0 103.2 jit_solution(7646089718452458002)
XLA Ops:
  0.0 0.1 pad_add_fusion.me_ref
  0.1 0.8 copy-done.14
  0.9 2.1 %pack.1 = (bf16[784,128]{1,0:T(8,128)(2,1)S(1)}, bf16[784,128]{1,0:T(8,128)(2,1)S(1)}, bf16[784,128]{1,0:T(8,128)(2,1)S(1)}, bf16[784,128]{1,0:T(8,128)(2,1)S(1)...) custom-call(s32[2]{0:T(128)S(1)} %pad_add_fusion.me_ref, ...), custom_call_target="tpu_custom_call" | custom-call | flops 1600000 | bytes 3200000 | tf_op jit(solution)/shard_map/pack/pallas_call | solution.py:204
  3.0 3.1 %collective-permute-start.2 = (bf16[784,128]{1,0:T(8,128)(2,1)S(1)}, bf16[784,128]{1,0:T(8,128)(2,1)S(1)}, u32[]{:S(2)}, u32[]{:S(2)}) collective-permute-start(bf16[784,128]{1,0:T(8,128)(2,1)S(1)} %get-tuple-element.79), channel_id=1, source_target_pairs={{0,2},{1,3},{2,0},{3,1},{4,6},{5,7},{6,4},{7,5},{8,10},{9,11},{10,... | collective-permute-start | bytes 602120 | tf_op jit(solution)/shard_map/ppermute | solution.py:464
  6.1 1.4 %collective-permute-start = (bf16[784,128]{1,0:T(8,128)(2,1)S(1)}, bf16[784,128]{1,0:T(8,128)(2,1)S(1)}, u32[]{:S(2)}, u32[]{:S(2)}) collective-permute-start(bf16[784,128]{1,0:T(8,128)(2,1)S(1)} %get-tuple-element.76), channel_id=1, source_target_pairs={{0,3},{1,2},{2,1},{3,0},{4,7},{5,6},{6,5},{7,4},{8,11},{9,10},{10,... | collective-permute-start | bytes 602120 | tf_op jit(solution)/shard_map/ppermute | solution.py:464
  7.5 0.7 collective-permute-start.3
  8.1 0.7 collective-permute-start.4
  8.8 0.7 collective-permute-start.7
  9.5 2.4 %collective-permute-done.2.refs_2_ = bf16[784,128]{1,0:T(8,128)(2,1)S(1)} collective-permute-done((bf16[784,128]{1,0:T(8,128)(2,1)S(1)}, bf16[784,128]{1,0:T(8,128)(2,1)S(1)}, u32[]{:S(2)}, u32[]{:S(2)}) %collective-permute-start.2) | collective-permute-done | bytes 200736 | tf_op jit(solution)/shard_map/ppermute | solution.py:464
  11.9 0.7 collective-permute-start.8
  12.6 7.4 %collective-permute-done.refs_3_ = bf16[784,128]{1,0:T(8,128)(2,1)S(1)} collective-permute-done((bf16[784,128]{1,0:T(8,128)(2,1)S(1)}, bf16[784,128]{1,0:T(8,128)(2,1)S(1)}, u32[]{:S(2)}, u32[]{:S(2)}) %collective-permute-start) | collective-permute-done | bytes 200736 | tf_op jit(solution)/shard_map/ppermute | solution.py:464
  20.0 0.3 collective-permute-start.1
  20.3 0.0 copy-done
  20.3 1.3 %copy-done.1 = bf16[768,768]{1,0:T(8,128)(2,1)S(1)} copy-done((bf16[768,768]{1,0:T(8,128)(2,1)S(1)}, bf16[768,768]{1,0:T(8,128)(2,1)}, u32[]{:S(2)}) %copy-start.1) | copy-done | bytes 1179672
  21.6 1.3 %copy-done.3 = bf16[768,768]{1,0:T(8,128)(2,1)S(1)} copy-done((bf16[768,768]{1,0:T(8,128)(2,1)S(1)}, bf16[768,768]{1,0:T(8,128)(2,1)}, u32[]{:S(2)}) %copy-start.3) | copy-done | bytes 1179672
  22.9 1.3 %copy-done.5 = bf16[768,768]{1,0:T(8,128)(2,1)S(1)} copy-done((bf16[768,768]{1,0:T(8,128)(2,1)S(1)}, bf16[768,768]{1,0:T(8,128)(2,1)}, u32[]{:S(2)}) %copy-start.5) | copy-done | bytes 1179672
  24.1 1.3 %copy-done.7 = bf16[768,768]{1,0:T(8,128)(2,1)S(1)} copy-done((bf16[768,768]{1,0:T(8,128)(2,1)S(1)}, bf16[768,768]{1,0:T(8,128)(2,1)}, u32[]{:S(2)}) %copy-start.7) | copy-done | bytes 1179672
  25.4 1.3 %copy-done.9 = bf16[768,768]{1,0:T(8,128)(2,1)S(1)} copy-done((bf16[768,768]{1,0:T(8,128)(2,1)S(1)}, bf16[768,768]{1,0:T(8,128)(2,1)}, u32[]{:S(2)}) %copy-start.9) | copy-done | bytes 1179672
  26.7 1.3 %copy-done.11 = bf16[768,768]{1,0:T(8,128)(2,1)S(1)} copy-done((bf16[768,768]{1,0:T(8,128)(2,1)S(1)}, bf16[768,768]{1,0:T(8,128)(2,1)}, u32[]{:S(2)}) %copy-start.11) | copy-done | bytes 1179672
  28.0 0.0 copy-start.10
  28.0 0.0 collective-permute-done.3.refs_0_
  28.0 4.1 %collective-permute-start.5 = (bf16[784,128]{1,0:T(8,128)(2,1)S(1)}, bf16[784,128]{1,0:T(8,128)(2,1)S(1)}, u32[]{:S(2)}, u32[]{:S(2)}) collective-permute-start(bf16[784,128]{1,0:T(8,128)(2,1)S(1)} %get-tuple-element.91), channel_id=1, source_target_pairs={{0,4},{1,5},{2,6},{3,7},{4,0},{5,1},{6,2},{7,3},{16,20},{17,21},{1... | collective-permute-start | bytes 602120 | tf_op jit(solution)/shard_map/ppermute | solution.py:470
  32.1 0.0 collective-permute-done.4.refs_1_
  32.1 4.0 %collective-permute-start.6 = (bf16[784,128]{1,0:T(8,128)(2,1)S(1)}, bf16[784,128]{1,0:T(8,128)(2,1)S(1)}, u32[]{:S(2)}, u32[]{:S(2)}) collective-permute-start(bf16[784,128]{1,0:T(8,128)(2,1)S(1)} %get-tuple-element.92), channel_id=1, source_target_pairs={{0,5},{1,4},{2,7},{3,6},{4,1},{5,0},{6,3},{7,2},{16,21},{17,20},{1... | collective-permute-start | bytes 602120 | tf_op jit(solution)/shard_map/ppermute | solution.py:470
  36.2 0.0 collective-permute-done.7.refs_0_
  36.2 5.5 %collective-permute-start.9 = (bf16[784,128]{1,0:T(8,128)(2,1)S(1)}, bf16[784,128]{1,0:T(8,128)(2,1)S(1)}, u32[]{:S(2)}, u32[]{:S(2)}) collective-permute-start(bf16[784,128]{1,0:T(8,128)(2,1)S(1)} %get-tuple-element.105), channel_id=1, source_target_pairs={{0,6},{1,7},{2,4},{3,5},{4,2},{5,3},{6,0},{7,1},{16,22},{17,23},{1... | collective-permute-start | bytes 602120 | tf_op jit(solution)/shard_map/ppermute | solution.py:470
  41.7 0.0 collective-permute-done.8.refs_1_
  41.7 1.9 %collective-permute-start.10 = (bf16[784,128]{1,0:T(8,128)(2,1)S(1)}, bf16[784,128]{1,0:T(8,128)(2,1)S(1)}, u32[]{:S(2)}, u32[]{:S(2)}) collective-permute-start(bf16[784,128]{1,0:T(8,128)(2,1)S(1)} %get-tuple-element.106), channel_id=1, source_target_pairs={{0,7},{1,6},{2,5},{3,4},{4,3},{5,2},{6,1},{7,0},{16,23},{17,22},{1... | collective-permute-start | bytes 602120 | tf_op jit(solution)/shard_map/ppermute | solution.py:470
  43.6 0.0 collective-permute-done.1.refs_1_
  43.7 7.5 %window_layer.3 = (bf16[8,48,768]{2,1,0:T(8,128)(2,1)S(1)}, bf16[8,48,768]{2,1,0:T(8,128)(2,1)S(1)}, bf16[8,48,768]{2,1,0:T(8,128)(2,1)S(1)}, bf16[8,48,768]{2,1...) custom-call(s32[2]{0:T(128)S(1)} %pad_add_fusion.me_ref, ...), custom_call_target="tpu_custom_call" | custom-call | flops 4051697664 | bytes 16777216 | tf_op jit(solution)/shard_map/window_layer/pallas_call | solution.py:348
  51.2 0.0 collective-permute-done.5.refs_2_
  51.2 0.0 collective-permute-done.6.refs_3_
  51.2 5.1 %window_layer.4 = (bf16[8,32,768]{2,1,0:T(8,128)(2,1)S(1)}, bf16[8,32,768]{2,1,0:T(8,128)(2,1)S(1)}, bf16[8,32,768]{2,1,0:T(8,128)(2,1)S(1)}, bf16[8,32,768]{2,1...) custom-call(s32[2]{0:T(128)S(1)} %pad_add_fusion.me_ref, ...), custom_call_target="tpu_custom_call" | custom-call | flops 2315255808 | bytes 16777216 | tf_op jit(solution)/shard_map/window_layer/pallas_call | solution.py:348
  56.4 0.0 collective-permute-done.9.refs_2_
  56.4 0.0 collective-permute-done.10.refs_3_
  56.4 0.0 copy-start.13
  56.4 6.5 %window_layer.5 = (bf16[8,48,768]{2,1,0:T(8,128)(2,1)S(1)}, bf16[8,48,768]{2,1,0:T(8,128)(2,1)S(1)}, bf16[8,48,768]{2,1,0:T(8,128)(2,1)S(1)}, bf16[8,48,768]{2,1,0:T(8,128)(2,1)S(1)}, bf16[8,48,128]{2,1,0:T(8,128)(2,1)S(1)}) custom-call(s32[2]{0:T(128)S(1)} %pad_add_fusion.me_ref, bf16[784,128]{1,0:T(8,128)(2,1)S(1)} %collective-permute-done.7.refs_0_, ...), custom_call_target="tpu_custom_call" | custom-call | flops 2894069760 | bytes 16777216 | tf_op jit(solution)/shard_map/window_layer/pallas_call | solution.py:348
  62.9 0.0 copy-done.13
  62.9 3.3 %row_layer.2 = (bf16[4,16,768]{2,1,0:T(8,128)(2,1)S(1)}, bf16[4,16,768]{2,1,0:T(8,128)(2,1)S(1)}, bf16[4,16,768]{2,1,0:T(8,128)(2,1)S(1)}, bf16[4,16,768]{2,1,0:...) custom-call(s32[2]{0:T(128)S(1)} %pad_add_fusion.me_ref, ...), custom_call_target="tpu_custom_call" | custom-call | bytes 65536 | tf_op jit(solution)/shard_map/row_layer/pallas_call | solution.py:416
  66.2 3.5 %collective-permute-start.15 = (bf16[4,16,768]{2,1,0:T(8,128)(2,1)S(1)}, bf16[4,16,768]{2,1,0:T(8,128)(2,1)S(1)}, u32[]{:S(2)}, u32[]{:S(2)}) collective-permute-start(bf16[4,16,768]{2,1,0:T(8,128)(2,1)S(1)} %get-tuple-element.129), channel_id=1, source_target_pairs={{0,6},{1,7},{2,4},{3,5},{4,2},{5,3},{6,0},{7,1},{8,14},{9,15},{10,... | collective-permute-start | bytes 294920 | tf_op jit(solution)/shard_map/ppermute | solution.py:464
  69.8 0.0 collective-permute-start.13
  69.8 4.2 %collective-permute-start.11 = (bf16[4,16,768]{2,1,0:T(8,128)(2,1)S(1)}, bf16[4,16,768]{2,1,0:T(8,128)(2,1)S(1)}, u32[]{:S(2)}, u32[]{:S(2)}) collective-permute-start(bf16[4,16,768]{2,1,0:T(8,128)(2,1)S(1)} %get-tuple-element.121), channel_id=1, source_target_pairs={{0,4},{1,5},{2,6},{3,7},{4,0},{5,1},{6,2},{7,3},{8,12},{9,13},{10,... | collective-permute-start | bytes 294920 | tf_op jit(solution)/shard_map/ppermute | solution.py:464
  73.9 3.3 %row_layer.3 = (bf16[4,16,768]{2,1,0:T(8,128)(2,1)S(1)}, bf16[4,16,768]{2,1,0:T(8,128)(2,1)S(1)}, bf16[4,16,768]{2,1,0:T(8,128)(2,1)S(1)}, bf16[4,16,768]{2,1,0:...) custom-call(s32[2]{0:T(128)S(1)} %pad_add_fusion.me_ref, ...), custom_call_target="tpu_custom_call" | custom-call | bytes 65536 | tf_op jit(solution)/shard_map/row_layer/pallas_call | solution.py:416
  77.2 0.0 collective-permute-done.15.refs_2_
  77.3 0.1 collective-permute-start.21
  77.3 5.7 %collective-permute-done.13.refs_1_ = bf16[4,16,768]{2,1,0:T(8,128)(2,1)S(1)} collective-permute-done((bf16[4,16,768]{2,1,0:T(8,128)(2,1)S(1)}, bf16[4,16,768]{2,1,0:T(8,128)(2,1)S(1)}, u32[]{:S(2)}, u32[]{:S(2)}) %collective-permute-start.13) | collective-permute-done | bytes 98336 | tf_op jit(solution)/shard_map/ppermute | solution.py:464
  83.0 0.0 collective-permute-start.20
  83.1 2.3 %collective-permute-start.17 = (bf16[4,16,768]{2,1,0:T(8,128)(2,1)S(1)}, bf16[4,16,768]{2,1,0:T(8,128)(2,1)S(1)}, u32[]{:S(2)}, u32[]{:S(2)}) collective-permute-start(bf16[4,16,768]{2,1,0:T(8,128)(2,1)S(1)} %get-tuple-element.133), channel_id=1, source_target_pairs={{0,7},{1,6},{2,5},{3,4},{4,3},{5,2},{6,1},{7,0},{8,15},{9,14},{10,... | collective-permute-start | bytes 294920 | tf_op jit(solution)/shard_map/ppermute | solution.py:464
  85.3 0.0 collective-permute-done.11.refs_0_
  85.3 0.6 collective-permute-start.19
  85.9 2.1 %collective-permute-start.12 = (bf16[4,16,768]{2,1,0:T(8,128)(2,1)S(1)}, bf16[4,16,768]{2,1,0:T(8,128)(2,1)S(1)}, u32[]{:S(2)}, u32[]{:S(2)}) collective-permute-start(bf16[4,16,768]{2,1,0:T(8,128)(2,1)S(1)} %get-tuple-element.122), channel_id=1, source_target_pairs={{0,4},{1,5},{2,6},{3,7},{4,0},{5,1},{6,2},{7,3},{8,12},{9,13},{10,... | collective-permute-start | bytes 294920 | tf_op jit(solution)/shard_map/ppermute | solution.py:464
  88.0 2.5 %collective-permute-done.17.refs_3_ = bf16[4,16,768]{2,1,0:T(8,128)(2,1)S(1)} collective-permute-done((bf16[4,16,768]{2,1,0:T(8,128)(2,1)S(1)}, bf16[4,16,768]{2,1,0:T(8,128)(2,1)S(1)}, u32[]{:S(2)}, u32[]{:S(2)}) %collective-permute-start.17) | collective-permute-done | bytes 98336 | tf_op jit(solution)/shard_map/ppermute | solution.py:464
  90.5 2.0 %collective-permute-start.14 = (bf16[4,16,768]{2,1,0:T(8,128)(2,1)S(1)}, bf16[4,16,768]{2,1,0:T(8,128)(2,1)S(1)}, u32[]{:S(2)}, u32[]{:S(2)}) collective-permute-start(bf16[4,16,768]{2,1,0:T(8,128)(2,1)S(1)} %get-tuple-element.126), channel_id=1, source_target_pairs={{0,5},{1,4},{2,7},{3,6},{4,1},{5,0},{6,3},{7,2},{8,13},{9,12},{10,... | collective-permute-start | bytes 294920 | tf_op jit(solution)/shard_map/ppermute | solution.py:464
  92.5 0.0 collective-permute-done.21.refs_6_
  92.5 1.8 %collective-permute-start.16 = (bf16[4,16,768]{2,1,0:T(8,128)(2,1)S(1)}, bf16[4,16,768]{2,1,0:T(8,128)(2,1)S(1)}, u32[]{:S(2)}, u32[]{:S(2)}) collective-permute-start(bf16[4,16,768]{2,1,0:T(8,128)(2,1)S(1)} %get-tuple-element.130), channel_id=1, source_target_pairs={{0,6},{1,7},{2,4},{3,5},{4,2},{5,3},{6,0},{7,1},{8,14},{9,15},{10,... | collective-permute-start | bytes 294920 | tf_op jit(solution)/shard_map/ppermute | solution.py:464
  94.3 0.0 collective-permute-done.20.refs_5_
  94.3 2.0 %collective-permute-start.18 = (bf16[4,16,768]{2,1,0:T(8,128)(2,1)S(1)}, bf16[4,16,768]{2,1,0:T(8,128)(2,1)S(1)}, u32[]{:S(2)}, u32[]{:S(2)}) collective-permute-start(bf16[4,16,768]{2,1,0:T(8,128)(2,1)S(1)} %get-tuple-element.134), channel_id=1, source_target_pairs={{0,7},{1,6},{2,5},{3,4},{4,3},{5,2},{6,1},{7,0},{8,15},{9,14},{10,... | collective-permute-start | bytes 294920 | tf_op jit(solution)/shard_map/ppermute | solution.py:464
  96.4 0.0 collective-permute-done.19.refs_4_
  96.4 1.6 %place.2.refs_4_ = bf16[64,16,768]{2,1,0:T(8,128)(2,1)} custom-call(s32[2]{0:T(128)S(1)} %pad_add_fusion.me_ref, bf16[4,16,768]{2,1,0:T(8,128)(2,1)S(1)} %collective-permute-done.11.refs_0_, bf16[4,16,768]{2,1,0:T(8,128)(2,1)S(1)} %collective-permute-done.13.refs_1_, bf16[4,16,768]{2,1,0:T(8,128)(2,1)S(1)} %collective-permute-done.15.refs_2_, ...), custom_call_target="tpu_custom_call" | custom-call | bytes 4194304 | tf_op jit(solution)/shard_map/place/pallas_call | solution.py:449
  98.0 0.0 collective-permute-done.12.refs_0_
  98.0 1.0 collective-permute-done.14.refs_1_
  99.0 0.0 collective-permute-done.16.refs_2_
  99.1 2.7 %collective-permute-done.18.refs_3_ = bf16[4,16,768]{2,1,0:T(8,128)(2,1)S(1)} collective-permute-done((bf16[4,16,768]{2,1,0:T(8,128)(2,1)S(1)}, bf16[4,16,768]{2,1,0:T(8,128)(2,1)S(1)}, u32[]{:S(2)}, u32[]{:S(2)}) %collective-permute-start.18) | collective-permute-done | bytes 98336 | tf_op jit(solution)/shard_map/ppermute | solution.py:464
  101.8 1.3 %place.3 = bf16[64,16,768]{2,1,0:T(8,128)(2,1)} custom-call(s32[2]{0:T(128)S(1)} %pad_add_fusion.me_ref, bf16[4,16,768]{2,1,0:T(8,128)(2,1)S(1)} %collective-permute-done.12.refs_0_, bf16[4,16,768]{2,1,0:T(8,128)(2,1)S(1)} %collective-permute-done.14.refs_1_, ...), custom_call_target="tpu_custom_call", output_to_operand_aliasing={{}: (5, {})} | custom-call | bytes 4194304 | tf_op jit(solution)/shard_map/place/pallas_call | solution.py:449
  (20 shorter events, 0.0 us)
Async XLA Ops:
  0.0 20.3 %copy-start = (bf16[768,768]{1,0:T(8,128)(2,1)S(1)}, bf16[768,768]{1,0:T(8,128)(2,1)}, u32[]{:S(2)}) copy-start(bf16[768,768]{1,0:T(8,128)(2,1)} %refs_10_.5) | copy-start | bytes 3538948
  0.1 0.8 copy-start.14
  3.0 8.9 %collective-permute-start.2 = (bf16[784,128]{1,0:T(8,128)(2,1)S(1)}, bf16[784,128]{1,0:T(8,128)(2,1)S(1)}, u32[]{:S(2)}, u32[]{:S(2)}) collective-permute-start(bf16[784,128]{1,0:T(8,128)(2,1)S(1)} %get-tuple-element.79), channel_id=1, source_target_pairs={{0,2},{1,3},{2,0},{3,1},{4,6},{5,7},{6,4},{7,5},{8,10},{9,11},{10,... | collective-permute-start | bytes 602120 | tf_op jit(solution)/shard_map/ppermute | solution.py:464
  6.1 13.9 %collective-permute-start = (bf16[784,128]{1,0:T(8,128)(2,1)S(1)}, bf16[784,128]{1,0:T(8,128)(2,1)S(1)}, u32[]{:S(2)}, u32[]{:S(2)}) collective-permute-start(bf16[784,128]{1,0:T(8,128)(2,1)S(1)} %get-tuple-element.76), channel_id=1, source_target_pairs={{0,3},{1,2},{2,1},{3,0},{4,7},{5,6},{6,5},{7,4},{8,11},{9,10},{10,... | collective-permute-start | bytes 602120 | tf_op jit(solution)/shard_map/ppermute | solution.py:464
  7.5 20.5 %collective-permute-start.3 = (bf16[784,128]{1,0:T(8,128)(2,1)S(1)}, bf16[784,128]{1,0:T(8,128)(2,1)S(1)}, u32[]{:S(2)}, u32[]{:S(2)}) collective-permute-start(bf16[784,128]{1,0:T(8,128)(2,1)S(1)} %get-tuple-element.91), channel_id=1, source_target_pairs={{8,12},{9,13},{10,14},{11,15},{12,8},{13,9},{14,10},{15,11},{24,28... | collective-permute-start | bytes 602120 | tf_op jit(solution)/shard_map/ppermute | solution.py:470
  8.1 24.0 %collective-permute-start.4 = (bf16[784,128]{1,0:T(8,128)(2,1)S(1)}, bf16[784,128]{1,0:T(8,128)(2,1)S(1)}, u32[]{:S(2)}, u32[]{:S(2)}) collective-permute-start(bf16[784,128]{1,0:T(8,128)(2,1)S(1)} %get-tuple-element.92), channel_id=1, source_target_pairs={{8,13},{9,12},{10,15},{11,14},{12,9},{13,8},{14,11},{15,10},{24,29... | collective-permute-start | bytes 602120 | tf_op jit(solution)/shard_map/ppermute | solution.py:470
  8.8 27.3 %collective-permute-start.7 = (bf16[784,128]{1,0:T(8,128)(2,1)S(1)}, bf16[784,128]{1,0:T(8,128)(2,1)S(1)}, u32[]{:S(2)}, u32[]{:S(2)}) collective-permute-start(bf16[784,128]{1,0:T(8,128)(2,1)S(1)} %get-tuple-element.105), channel_id=1, source_target_pairs={{8,14},{9,15},{10,12},{11,13},{12,10},{13,11},{14,8},{15,9},{24,30... | collective-permute-start | bytes 602120 | tf_op jit(solution)/shard_map/ppermute | solution.py:470
  11.9 29.8 %collective-permute-start.8 = (bf16[784,128]{1,0:T(8,128)(2,1)S(1)}, bf16[784,128]{1,0:T(8,128)(2,1)S(1)}, u32[]{:S(2)}, u32[]{:S(2)}) collective-permute-start(bf16[784,128]{1,0:T(8,128)(2,1)S(1)} %get-tuple-element.106), channel_id=1, source_target_pairs={{8,15},{9,14},{10,13},{11,12},{12,11},{13,10},{14,9},{15,8},{24,31... | collective-permute-start | bytes 602120 | tf_op jit(solution)/shard_map/ppermute | solution.py:470
  20.0 23.7 %collective-permute-start.1 = (bf16[784,128]{1,0:T(8,128)(2,1)S(1)}, bf16[784,128]{1,0:T(8,128)(2,1)S(1)}, u32[]{:S(2)}, u32[]{:S(2)}) collective-permute-start(bf16[784,128]{1,0:T(8,128)(2,1)S(1)} %get-tuple-element.77), channel_id=1, source_target_pairs={{0,1},{1,0},{2,3},{3,2},{4,5},{5,4},{6,7},{7,6},{8,9},{9,8},{10,11... | collective-permute-start | bytes 602120 | tf_op jit(solution)/shard_map/ppermute | solution.py:464
  20.3 1.3 %copy-start.1 = (bf16[768,768]{1,0:T(8,128)(2,1)S(1)}, bf16[768,768]{1,0:T(8,128)(2,1)}, u32[]{:S(2)}) copy-start(bf16[768,768]{1,0:T(8,128)(2,1)} %refs_11_.5) | copy-start | bytes 3538948
  21.6 1.3 %copy-start.3 = (bf16[768,768]{1,0:T(8,128)(2,1)S(1)}, bf16[768,768]{1,0:T(8,128)(2,1)}, u32[]{:S(2)}) copy-start(bf16[768,768]{1,0:T(8,128)(2,1)} %refs_12_.3) | copy-start | bytes 3538948
  22.9 1.3 %copy-start.5 = (bf16[768,768]{1,0:T(8,128)(2,1)S(1)}, bf16[768,768]{1,0:T(8,128)(2,1)}, u32[]{:S(2)}) copy-start(bf16[768,768]{1,0:T(8,128)(2,1)} %refs_13_.3) | copy-start | bytes 3538948
  24.1 1.3 %copy-start.7 = (bf16[768,768]{1,0:T(8,128)(2,1)S(1)}, bf16[768,768]{1,0:T(8,128)(2,1)}, u32[]{:S(2)}) copy-start(bf16[768,768]{1,0:T(8,128)(2,1)} %refs_14_.3) | copy-start | bytes 3538948
  25.4 1.3 %copy-start.9 = (bf16[768,768]{1,0:T(8,128)(2,1)S(1)}, bf16[768,768]{1,0:T(8,128)(2,1)}, u32[]{:S(2)}) copy-start(bf16[768,768]{1,0:T(8,128)(2,1)} %refs_15_.3) | copy-start | bytes 3538948
  26.7 1.3 %copy-start.11 = (bf16[768,768]{1,0:T(8,128)(2,1)S(1)}, bf16[768,768]{1,0:T(8,128)(2,1)}, u32[]{:S(2)}) copy-start(bf16[768,768]{1,0:T(8,128)(2,1)} %refs_16_.1) | copy-start | bytes 3538948
  28.0 15.7 %copy-start.2 = (bf16[768,768]{1,0:T(8,128)(2,1)S(1)}, bf16[768,768]{1,0:T(8,128)(2,1)}, u32[]{:S(2)}) copy-start(bf16[768,768]{1,0:T(8,128)(2,1)} %refs_11_.5) | copy-start | bytes 3538948
  28.0 15.7 %copy-start.4 = (bf16[768,768]{1,0:T(8,128)(2,1)S(1)}, bf16[768,768]{1,0:T(8,128)(2,1)}, u32[]{:S(2)}) copy-start(bf16[768,768]{1,0:T(8,128)(2,1)} %refs_12_.3) | copy-start | bytes 3538948
  28.0 15.7 %copy-start.6 = (bf16[768,768]{1,0:T(8,128)(2,1)S(1)}, bf16[768,768]{1,0:T(8,128)(2,1)}, u32[]{:S(2)}) copy-start(bf16[768,768]{1,0:T(8,128)(2,1)} %refs_13_.3) | copy-start | bytes 3538948
  28.0 15.7 %copy-start.8 = (bf16[768,768]{1,0:T(8,128)(2,1)S(1)}, bf16[768,768]{1,0:T(8,128)(2,1)}, u32[]{:S(2)}) copy-start(bf16[768,768]{1,0:T(8,128)(2,1)} %refs_14_.3) | copy-start | bytes 3538948
  28.0 15.7 %copy-start.10 = (bf16[768,768]{1,0:T(8,128)(2,1)S(1)}, bf16[768,768]{1,0:T(8,128)(2,1)}, u32[]{:S(2)}) copy-start(bf16[768,768]{1,0:T(8,128)(2,1)} %refs_15_.3) | copy-start | bytes 3538948
  28.0 15.7 %copy-start.12 = (bf16[768,768]{1,0:T(8,128)(2,1)S(1)}, bf16[768,768]{1,0:T(8,128)(2,1)}, u32[]{:S(2)}) copy-start(bf16[768,768]{1,0:T(8,128)(2,1)} %refs_16_.1) | copy-start | bytes 3538948
  28.0 23.2 %collective-permute-start.5 = (bf16[784,128]{1,0:T(8,128)(2,1)S(1)}, bf16[784,128]{1,0:T(8,128)(2,1)S(1)}, u32[]{:S(2)}, u32[]{:S(2)}) collective-permute-start(bf16[784,128]{1,0:T(8,128)(2,1)S(1)} %get-tuple-element.91), channel_id=1, source_target_pairs={{0,4},{1,5},{2,6},{3,7},{4,0},{5,1},{6,2},{7,3},{16,20},{17,21},{1... | collective-permute-start | bytes 602120 | tf_op jit(solution)/shard_map/ppermute | solution.py:470
  32.1 19.1 %collective-permute-start.6 = (bf16[784,128]{1,0:T(8,128)(2,1)S(1)}, bf16[784,128]{1,0:T(8,128)(2,1)S(1)}, u32[]{:S(2)}, u32[]{:S(2)}) collective-permute-start(bf16[784,128]{1,0:T(8,128)(2,1)S(1)} %get-tuple-element.92), channel_id=1, source_target_pairs={{0,5},{1,4},{2,7},{3,6},{4,1},{5,0},{6,3},{7,2},{16,21},{17,20},{1... | collective-permute-start | bytes 602120 | tf_op jit(solution)/shard_map/ppermute | solution.py:470
  36.2 20.2 %collective-permute-start.9 = (bf16[784,128]{1,0:T(8,128)(2,1)S(1)}, bf16[784,128]{1,0:T(8,128)(2,1)S(1)}, u32[]{:S(2)}, u32[]{:S(2)}) collective-permute-start(bf16[784,128]{1,0:T(8,128)(2,1)S(1)} %get-tuple-element.105), channel_id=1, source_target_pairs={{0,6},{1,7},{2,4},{3,5},{4,2},{5,3},{6,0},{7,1},{16,22},{17,23},{1... | collective-permute-start | bytes 602120 | tf_op jit(solution)/shard_map/ppermute | solution.py:470
  41.7 14.7 %collective-permute-start.10 = (bf16[784,128]{1,0:T(8,128)(2,1)S(1)}, bf16[784,128]{1,0:T(8,128)(2,1)S(1)}, u32[]{:S(2)}, u32[]{:S(2)}) collective-permute-start(bf16[784,128]{1,0:T(8,128)(2,1)S(1)} %get-tuple-element.106), channel_id=1, source_target_pairs={{0,7},{1,6},{2,5},{3,4},{4,3},{5,2},{6,1},{7,0},{16,23},{17,22},{1... | collective-permute-start | bytes 602120 | tf_op jit(solution)/shard_map/ppermute | solution.py:470
  56.4 6.5 %copy-start.13 = (bf16[768,768]{1,0:T(8,128)(2,1)S(1)}, bf16[768,768]{1,0:T(8,128)(2,1)}, u32[]{:S(2)}) copy-start(bf16[768,768]{1,0:T(8,128)(2,1)} %refs_15_.5) | copy-start | bytes 3538948
  66.2 11.0 %collective-permute-start.15 = (bf16[4,16,768]{2,1,0:T(8,128)(2,1)S(1)}, bf16[4,16,768]{2,1,0:T(8,128)(2,1)S(1)}, u32[]{:S(2)}, u32[]{:S(2)}) collective-permute-start(bf16[4,16,768]{2,1,0:T(8,128)(2,1)S(1)} %get-tuple-element.129), channel_id=1, source_target_pairs={{0,6},{1,7},{2,4},{3,5},{4,2},{5,3},{6,0},{7,1},{8,14},{9,15},{10,... | collective-permute-start | bytes 294920 | tf_op jit(solution)/shard_map/ppermute | solution.py:464
  69.8 13.3 %collective-permute-start.13 = (bf16[4,16,768]{2,1,0:T(8,128)(2,1)S(1)}, bf16[4,16,768]{2,1,0:T(8,128)(2,1)S(1)}, u32[]{:S(2)}, u32[]{:S(2)}) collective-permute-start(bf16[4,16,768]{2,1,0:T(8,128)(2,1)S(1)} %get-tuple-element.125), channel_id=1, source_target_pairs={{0,5},{1,4},{2,7},{3,6},{4,1},{5,0},{6,3},{7,2},{8,13},{9,12},{10,... | collective-permute-start | bytes 294920 | tf_op jit(solution)/shard_map/ppermute | solution.py:464
  69.8 15.5 %collective-permute-start.11 = (bf16[4,16,768]{2,1,0:T(8,128)(2,1)S(1)}, bf16[4,16,768]{2,1,0:T(8,128)(2,1)S(1)}, u32[]{:S(2)}, u32[]{:S(2)}) collective-permute-start(bf16[4,16,768]{2,1,0:T(8,128)(2,1)S(1)} %get-tuple-element.121), channel_id=1, source_target_pairs={{0,4},{1,5},{2,6},{3,7},{4,0},{5,1},{6,2},{7,3},{8,12},{9,13},{10,... | collective-permute-start | bytes 294920 | tf_op jit(solution)/shard_map/ppermute | solution.py:464
  77.3 15.3 %collective-permute-start.21 = (bf16[8,16,768]{2,1,0:T(8,128)(2,1)S(1)}, bf16[8,16,768]{2,1,0:T(8,128)(2,1)S(1)}, u32[]{:S(2)}, u32[]{:S(2)}) collective-permute-start(bf16[8,16,768]{2,1,0:T(8,128)(2,1)S(1)} %get-tuple-element.141), channel_id=1, source_target_pairs={{0,3},{1,2},{2,1},{3,0},{4,7},{5,6},{6,5},{7,4},{8,11},{9,10},{10,... | collective-permute-start | bytes 589832 | tf_op jit(solution)/shard_map/ppermute | solution.py:464
  83.0 11.3 %collective-permute-start.20 = (bf16[8,16,768]{2,1,0:T(8,128)(2,1)S(1)}, bf16[8,16,768]{2,1,0:T(8,128)(2,1)S(1)}, u32[]{:S(2)}, u32[]{:S(2)}) collective-permute-start(bf16[8,16,768]{2,1,0:T(8,128)(2,1)S(1)} %get-tuple-element.140), channel_id=1, source_target_pairs={{0,2},{1,3},{2,0},{3,1},{4,6},{5,7},{6,4},{7,5},{8,10},{9,11},{10,... | collective-permute-start | bytes 589832 | tf_op jit(solution)/shard_map/ppermute | solution.py:464
  83.1 7.5 %collective-permute-start.17 = (bf16[4,16,768]{2,1,0:T(8,128)(2,1)S(1)}, bf16[4,16,768]{2,1,0:T(8,128)(2,1)S(1)}, u32[]{:S(2)}, u32[]{:S(2)}) collective-permute-start(bf16[4,16,768]{2,1,0:T(8,128)(2,1)S(1)} %get-tuple-element.133), channel_id=1, source_target_pairs={{0,7},{1,6},{2,5},{3,4},{4,3},{5,2},{6,1},{7,0},{8,15},{9,14},{10,... | collective-permute-start | bytes 294920 | tf_op jit(solution)/shard_map/ppermute | solution.py:464
  85.3 11.1 %collective-permute-start.19 = (bf16[8,16,768]{2,1,0:T(8,128)(2,1)S(1)}, bf16[8,16,768]{2,1,0:T(8,128)(2,1)S(1)}, u32[]{:S(2)}, u32[]{:S(2)}) collective-permute-start(bf16[8,16,768]{2,1,0:T(8,128)(2,1)S(1)} %get-tuple-element.139), channel_id=1, source_target_pairs={{0,1},{1,0},{2,3},{3,2},{4,5},{5,4},{6,7},{7,6},{8,9},{9,8},{10,11... | collective-permute-start | bytes 589832 | tf_op jit(solution)/shard_map/ppermute | solution.py:464
  85.9 12.1 %collective-permute-start.12 = (bf16[4,16,768]{2,1,0:T(8,128)(2,1)S(1)}, bf16[4,16,768]{2,1,0:T(8,128)(2,1)S(1)}, u32[]{:S(2)}, u32[]{:S(2)}) collective-permute-start(bf16[4,16,768]{2,1,0:T(8,128)(2,1)S(1)} %get-tuple-element.122), channel_id=1, source_target_pairs={{0,4},{1,5},{2,6},{3,7},{4,0},{5,1},{6,2},{7,3},{8,12},{9,13},{10,... | collective-permute-start | bytes 294920 | tf_op jit(solution)/shard_map/ppermute | solution.py:464
  90.5 8.5 %collective-permute-start.14 = (bf16[4,16,768]{2,1,0:T(8,128)(2,1)S(1)}, bf16[4,16,768]{2,1,0:T(8,128)(2,1)S(1)}, u32[]{:S(2)}, u32[]{:S(2)}) collective-permute-start(bf16[4,16,768]{2,1,0:T(8,128)(2,1)S(1)} %get-tuple-element.126), channel_id=1, source_target_pairs={{0,5},{1,4},{2,7},{3,6},{4,1},{5,0},{6,3},{7,2},{8,13},{9,12},{10,... | collective-permute-start | bytes 294920 | tf_op jit(solution)/shard_map/ppermute | solution.py:464
  92.5 6.5 %collective-permute-start.16 = (bf16[4,16,768]{2,1,0:T(8,128)(2,1)S(1)}, bf16[4,16,768]{2,1,0:T(8,128)(2,1)S(1)}, u32[]{:S(2)}, u32[]{:S(2)}) collective-permute-start(bf16[4,16,768]{2,1,0:T(8,128)(2,1)S(1)} %get-tuple-element.130), channel_id=1, source_target_pairs={{0,6},{1,7},{2,4},{3,5},{4,2},{5,3},{6,0},{7,1},{8,14},{9,15},{10,... | collective-permute-start | bytes 294920 | tf_op jit(solution)/shard_map/ppermute | solution.py:464
  94.3 7.4 %collective-permute-start.18 = (bf16[4,16,768]{2,1,0:T(8,128)(2,1)S(1)}, bf16[4,16,768]{2,1,0:T(8,128)(2,1)S(1)}, u32[]{:S(2)}, u32[]{:S(2)}) collective-permute-start(bf16[4,16,768]{2,1,0:T(8,128)(2,1)S(1)} %get-tuple-element.134), channel_id=1, source_target_pairs={{0,7},{1,6},{2,5},{3,4},{4,3},{5,2},{6,1},{7,0},{8,15},{9,14},{10,... | collective-permute-start | bytes 294920 | tf_op jit(solution)/shard_map/ppermute | solution.py:464

commit v9 on v5

--- a/solution.py
+++ b/solution.py
@@ -12,8 +12,6 @@
 
 EPS = 1e-05
 NEG = -1e30
-
-ROWS_FIRST = 4
 
 PACK_VMEM = 52 * 1024 * 1024
 
@@ -244,22 +242,25 @@
     return whole[:, 0], whole[:, 1]
 
 
-STAGES = ((7, 6), (4, 4), (5, 6))
+STAGES = ((7, 6), (4, 4), (2, 2), (3, 4))
+
+ROWS_FIRST = 4
 
 
 def window_kernel(stage, me_ref, *refs):
-    pieces = refs[: (4, 2, 2)[stage]]
+    pieces = refs[: (4, 2, 1, 1)[stage]]
     refs = refs[len(pieces) :]
-    carried = refs[: (0, 3, 5)[stage]]
+    carried = refs[: (0, 3, 5, 7)[stage]]
     refs = refs[len(carried) :]
     _, wq, wk, wv, wo, wq2, wk2, wv2, y_ref, q2_ref, k2_ref, v2_ref, m_ref = refs[:13]
     refs = refs[13:]
-    passed = refs[: (3, 3, 0)[stage]]
+    passed = refs[: 3 if stage < 3 else 0]
     placed, q_s, k_s, v_s, o_s, rows_s = refs[len(passed) :]
     width = wq.shape[0]
     scale = (width // HEADS) ** (-0.5)
     me = me_ref[0]
     upper = jnp.bitwise_and(me, 2) > 0
+    odd = jnp.bitwise_and(me, 1) > 0
     low = jnp.bitwise_and(me, len(pieces) - 1)
     for d, piece in enumerate(pieces):
         placed[jnp.bitwise_xor(low, d)] = piece[...]
@@ -280,20 +281,22 @@
     for l in range(1, len(pieces)):
         windows += [straddling_window(columns[l - 1][1], columns[l][0]), whole_window(l)]
     first, last = columns[0][0], columns[-1][1]
-    if stage < 2:
+    if stage < 3:
         passed[0][...] = first.reshape(full)
         passed[1][...] = last.reshape(full)
     edges = [a[...].reshape(8, 8, width + 128) for a in carried[:-1]]
     if stage == 1:
         own_first, own_last = edges
         windows = [straddling_window(either(last, own_last), either(own_first, first))] + windows
+    if stage >= 2:
+        own_first, own_last, second_first, second_last = edges[:4]
+        before, after = either(own_last, second_last), either(second_first, own_first)
     if stage == 2:
-        own_first, own_last, second_first, second_last = edges
-        windows = (
-            [straddling_window(either(last, second_last), either(second_first, first))]
-            + windows
-            + [straddling_window(either(own_last, last), either(first, own_first))]
-        )
+        windows.append(straddling_window(jnp.where(odd, last, before), jnp.where(odd, after, first)))
+    if stage == 3:
+        one_first, one_last = edges[4:]
+        windows.append(straddling_window(jnp.where(odd, last, one_last), jnp.where(odd, one_first, first)))
+        windows.append(straddling_window(jnp.where(odd, before, last), jnp.where(odd, first, after)))
     count = len(windows)
     x = jnp.concatenate([w[:, :width] for w in windows], 0)
     marks = [w[:, width:] for w in windows]
@@ -315,17 +318,16 @@
         for r in range(8):
             at = 64 * w + 8 * r
             to = 8 * (w + skip)
-            if stage < 2 and w == count - 1:
+            if stage < 3 and w == count - 1:
                 passed[2][r, :, :width] = y[at : at + 8]
                 passed[2][r, :, width:] = marks[w][8 * r : 8 * r + 8]
             else:
                 rows_s[r, to : to + 8, :width] = y[at : at + 8]
                 rows_s[r, to : to + 8, width:] = marks[w][8 * r : 8 * r + 8]
-    tokens = rows_s.shape[0] * rows_s.shape[1]
-    y = rows_s[:, :, :width].reshape(tokens, width)
     m_ref[...] = rows_s[:, :, width:].astype(jnp.bfloat16)
-    y_ref[...] = y.astype(jnp.bfloat16).reshape(y_ref.shape)
-    h = normed_f32(y)
+    y_ref[...] = rows_s[:, :, :width].astype(jnp.bfloat16)
+    rows = q2_ref.shape[0]
+    h = normed_f32(rows_s[:rows, :, :width].reshape(rows * rows_s.shape[1], width))
     q2_ref[...] = (dot_f32(h, wq2[...]) * scale).astype(jnp.bfloat16).reshape(q2_ref.shape)
     k2_ref[...] = dot_f32(h, wk2[...]).astype(jnp.bfloat16).reshape(k2_ref.shape)
     v2_ref[...] = dot_f32(h, wv2[...]).astype(jnp.bfloat16).reshape(v2_ref.shape)
@@ -339,7 +341,8 @@
     marks = jax.ShapeDtypeStruct((8, columns, 128), jnp.bfloat16)
     edge = jax.ShapeDtypeStruct((64, width + 128), jnp.float32)
     tail = jax.ShapeDtypeStruct((8, 8, width + 128), jnp.float32)
-    outs = (part,) * 4 + (marks,) + ((edge, edge, tail), (edge, edge, tail), ())[stage]
+    projected = part if stage < 3 else jax.ShapeDtypeStruct((ROWS_FIRST, columns, width), jnp.bfloat16)
+    outs = (part, projected, projected, projected, marks) + ((edge, edge, tail) if stage < 3 else ())
     vmem = pl.BlockSpec(memory_space=pltpu.VMEM)
     work = pltpu.VMEM((tokens, width), jnp.bfloat16)
     inputs = [*pieces, *carried, *weights]
@@ -362,14 +365,26 @@
 
 
 def row_kernel(start, rows, me_ref, *refs):
-    parts, wo, refs = (refs[:5], refs[5:10], refs[10:15]), refs[15], refs[16:]
-    earlier, refs = (refs[:4], refs[4:]) if start else ((), refs)
-    outs, (o_s, placed) = refs[:8], refs[8:]
+    parts, wo, refs = [refs[at : at + 5] for at in range(0, 20, 5)], refs[20], refs[21:]
     width = wo.shape[0]
     length = 128
+    earlier = ()
+    if start:
+        earlier, weights, refs = refs[:4], refs[4:7], refs[7:]
+        *refs, q_s, k_s, v_s = refs
+        y = parts[3][0][start:].astype(jnp.float32)
+        h = normed_f32(y.reshape(rows * y.shape[1], width))
+        for to, weight, factor in zip((q_s, k_s, v_s), weights, ((width // HEADS) ** (-0.5), 1.0, 1.0)):
+            to[...] = (dot_f32(h, weight[...]) * factor).astype(jnp.bfloat16).reshape(to.shape)
+    outs, (o_s, placed) = refs[:8], refs[8:]
 
     def row(i, r, lanes=slice(None)):
-        return jnp.concatenate([part[i][start + r, :, lanes] for part in parts], 0)
+        pieces = [part[i][start + r, :, lanes] for part in parts[:3]]
+        if 1 <= i <= 3:
+            pieces.append((q_s, k_s, v_s)[i - 1][r, :, lanes] if start else parts[3][i][r, :, lanes])
+        else:
+            pieces.append(parts[3][i][start + r, :, lanes])
+        return jnp.concatenate(pieces, 0)
 
     for r in range(rows):
         here = slice(length * r, length * r + length)
@@ -380,11 +395,14 @@
     mask = low_columns((8, width), 0)
     me = me_ref[0]
     upper = jnp.bitwise_and(me, 2) > 0
+    odd = jnp.bitwise_and(me, 1) > 0
+    same = upper == odd
     for r in range(rows):
         f = row(0, r).astype(jnp.float32) + added[length * r : length * r + length]
         tiles = [f[8 * w : 8 * w + 8] for w in range(16)]
-        own, second, third = tiles[:7], tiles[8:11], tiles[12:15]
-        own_second, middle, third_own = tiles[7], tiles[11], tiles[15]
+        own, own_second, second = tiles[:7], tiles[7], tiles[8:11]
+        third = (jnp.where(odd, tiles[13], tiles[11]), tiles[14], jnp.where(odd, tiles[11], tiles[13]))
+        middle, third_own = jnp.where(same, tiles[12], tiles[15]), jnp.where(same, tiles[15], tiles[12])
         after_own = jnp.where(upper, third_own, own_second)
         before_own = jnp.where(upper, own_second, third_own)
         whole = [before_own, *own, after_own]
@@ -411,6 +429,8 @@
     near = jax.ShapeDtypeStruct((start + rows, 16, width), jnp.bfloat16)
     vmem = pl.BlockSpec(memory_space=pltpu.VMEM)
     inputs = [*parts, w_out, *earlier]
+    rest = parts[15].shape[1]
+    work = pltpu.VMEM((rows, rest, width), jnp.bfloat16)
     return pl.pallas_call(
         functools.partial(row_kernel, start, rows),
         out_shape=(far,) * 4 + (near,) * 4,
@@ -419,7 +439,8 @@
         scratch_shapes=[
             pltpu.VMEM((rows * length, width), jnp.bfloat16),
             pltpu.VMEM((8, rows, 16, width), jnp.bfloat16),
-        ],
+        ]
+        + [work] * (3 if start else 0),
         compiler_params=pltpu.CompilerParams(vmem_limit_bytes=36 * 1024 * 1024),
         cost_estimate=pl.CostEstimate(
             flops=0, bytes_accessed=1 << 16, transcendentals=0
@@ -475,10 +496,12 @@
     got[2], got[3], got[1] = near
     own = window_layer(0, me, [got[d] for d in range(4)], (), weights)
     second = window_layer(1, me, [got[4], got[5]], own[5:], weights)
-    third = window_layer(2, me, [got[6], got[7]], (*own[5:7], *second[5:]), weights)
-    parts = (*own[:5], *second[:5], *third)
+    edges = (*own[5:7], *second[5:7])
+    third = window_layer(2, me, [got[6]], (*edges, second[7]), weights)
+    fourth = window_layer(3, me, [got[7]], (*edges, *third[5:]), weights)
+    parts = (*own[:5], *second[:5], *third[:5], *fourth)
     first = row_layer(0, ROWS_FIRST, me, parts, w_out2, ())
-    last = row_layer(ROWS_FIRST, 8 - ROWS_FIRST, me, parts, w_out2, first[4:])
+    last = row_layer(ROWS_FIRST, 8 - ROWS_FIRST, me, parts, w_out2, (*first[4:], w_query2, w_key2, w_value2))
     far = [exchanged(piece, d) for d, piece in zip(ORDER[:4], first)]
     last = list(last)
     for i in range(4):

time: 88.9 us -> 87.3 us (0.982)
  starting transfers between devices: 35.3 us -> 32 us
  waiting for transfers between devices: 17 us -> 18.5 us
  Pallas kernels: 26.1 us -> 27 us
    ppermute x18, starting transfers between devices: 35.3 us -> 32 us  [exchanged(): return lax.ppermute(piece, 'lon', [(s, s ^ distance) for s in range(count)])]
    ppermute x18, waiting for transfers between devices: 17 us -> 18.5 us  [exchanged(): return lax.ppermute(piece, 'lon', [(s, s ^ distance) for s in range(count)])]
    pallas_call x3 -> x4, Pallas kernels: 17.3 us -> 17.5 us  [window_layer(): pl.pallas_call(functools.partial(window_kernel, stage), out_shape=outs, i...]
  transfers between devices with their start and end apart: 18 -> 18, of which waited for: 4 -> 4; matrix products, arithmetic and copies ran while one was open for 0% -> 0% of each run, Pallas kernels for 17% -> 21%
where the time goes in v9:
time: 87.3 us; the launch traced here: 86.4 us
  starting transfers between devices  32 us (37%)
  Pallas kernels  27 us (31%)
  waiting for transfers between devices  18.5 us (21%)
  local copies, waits for them, and re-layouts  8.45 us (10%)
    ppermute x18, starting transfers between devices, exchanged(): return lax.ppermute(piece, 'lon', [(s, s ^ distance) for s in range(count)])  32 us
    ppermute x18, waiting for transfers between devices, exchanged(): return lax.ppermute(piece, 'lon', [(s, s ^ distance) for s in range(count)])  18.5 us
    pallas_call x4, Pallas kernels, window_layer(): pl.pallas_call(functools.partial(window_kernel, stage), out_shape=outs, i...  17.5 us
    unnamed x30, local copies, waits for them, and re-layouts  8.45 us
    pallas_call x2, Pallas kernels, row_layer(): pl.pallas_call(functools.partial(row_kernel, start, rows), out_shape=(far...  6.1 us
    pallas_call x2, Pallas kernels, place(): pl.pallas_call(functools.partial(place_kernel, spots), out_shape=jax.Shap...  1.84 us
  transfers between devices with their start and end apart: 18, of which 4 were waited for; matrix products, arithmetic and copies ran while one was open for 0% of the time, Pallas kernels for 21%

profile of v9, /device:TPU:0, one launch (start us, length us, event | category | flops | bytes accessed | tf_op | source)
XLA Modules:
  0.0 86.4 jit_solution(14270863270646264740)
XLA Ops:
  0.0 0.0 copy-start
  0.0 0.8 copy-done.14
  0.8 1.6 %pack.1 = (bf16[784,128]{1,0:T(8,128)(2,1)S(1)}, bf16[784,128]{1,0:T(8,128)(2,1)S(1)}, bf16[784,128]{1,0:T(8,128)(2,1)S(1)}, bf16[784,128]{1,0:T(8,128)(2,1)S(1)...) custom-call(s32[1]{0:T(128)} %bitcast.me_ref, ...), custom_call_target="tpu_custom_call" | custom-call | flops 1600000 | bytes 3200000 | tf_op jit(solution)/shard_map/pack/pallas_call | solution.py:202
  2.4 4.1 %collective-permute-start = (bf16[784,128]{1,0:T(8,128)(2,1)S(1)}, bf16[784,128]{1,0:T(8,128)(2,1)S(1)}, u32[]{:S(2)}, u32[]{:S(2)}) collective-permute-start(bf16[784,128]{1,0:T(8,128)(2,1)S(1)} %get-tuple-element.75), channel_id=1, source_target_pairs={{0,4},{1,5},{2,6},{3,7},{4,0},{5,1},{6,2},{7,3},{8,12},{9,13},{10,... | collective-permute-start | bytes 602120 | tf_op jit(solution)/shard_map/ppermute | solution.py:483
  6.5 1.6 %collective-permute-start.1 = (bf16[784,128]{1,0:T(8,128)(2,1)S(1)}, bf16[784,128]{1,0:T(8,128)(2,1)S(1)}, u32[]{:S(2)}, u32[]{:S(2)}) collective-permute-start(bf16[784,128]{1,0:T(8,128)(2,1)S(1)} %get-tuple-element.76), channel_id=1, source_target_pairs={{0,2},{1,3},{2,0},{3,1},{4,6},{5,7},{6,4},{7,5},{8,10},{9,11},{10,... | collective-permute-start | bytes 602120 | tf_op jit(solution)/shard_map/ppermute | solution.py:483
  8.0 1.4 %collective-permute-start.2 = (bf16[784,128]{1,0:T(8,128)(2,1)S(1)}, bf16[784,128]{1,0:T(8,128)(2,1)S(1)}, u32[]{:S(2)}, u32[]{:S(2)}) collective-permute-start(bf16[784,128]{1,0:T(8,128)(2,1)S(1)} %get-tuple-element.77), channel_id=1, source_target_pairs={{0,3},{1,2},{2,1},{3,0},{4,7},{5,6},{6,5},{7,4},{8,11},{9,10},{10,... | collective-permute-start | bytes 602120 | tf_op jit(solution)/shard_map/ppermute | solution.py:483
  9.4 0.5 collective-permute-start.3
  10.0 1.3 %collective-permute-start.4 = (bf16[784,128]{1,0:T(8,128)(2,1)S(1)}, bf16[784,128]{1,0:T(8,128)(2,1)S(1)}, u32[]{:S(2)}, u32[]{:S(2)}) collective-permute-start(bf16[784,128]{1,0:T(8,128)(2,1)S(1)} %get-tuple-element.88), channel_id=1, source_target_pairs={{0,5},{1,4},{2,7},{3,6},{4,1},{5,0},{6,3},{7,2},{8,13},{9,12},{10,... | collective-permute-start | bytes 602120 | tf_op jit(solution)/shard_map/ppermute | solution.py:483
  11.2 0.0 copy-done
  11.3 1.3 %copy-done.1 = bf16[768,768]{1,0:T(8,128)(2,1)S(1)} copy-done((bf16[768,768]{1,0:T(8,128)(2,1)S(1)}, bf16[768,768]{1,0:T(8,128)(2,1)}, u32[]{:S(2)}) %copy-start.1) | copy-done | bytes 1179672
  12.5 1.3 %copy-done.3 = bf16[768,768]{1,0:T(8,128)(2,1)S(1)} copy-done((bf16[768,768]{1,0:T(8,128)(2,1)S(1)}, bf16[768,768]{1,0:T(8,128)(2,1)}, u32[]{:S(2)}) %copy-start.3) | copy-done | bytes 1179672
  13.8 1.3 %copy-done.5 = bf16[768,768]{1,0:T(8,128)(2,1)S(1)} copy-done((bf16[768,768]{1,0:T(8,128)(2,1)S(1)}, bf16[768,768]{1,0:T(8,128)(2,1)}, u32[]{:S(2)}) %copy-start.5) | copy-done | bytes 1179672
  15.1 1.3 %copy-done.7 = bf16[768,768]{1,0:T(8,128)(2,1)S(1)} copy-done((bf16[768,768]{1,0:T(8,128)(2,1)S(1)}, bf16[768,768]{1,0:T(8,128)(2,1)}, u32[]{:S(2)}) %copy-start.7) | copy-done | bytes 1179672
  16.3 1.3 %copy-done.9 = bf16[768,768]{1,0:T(8,128)(2,1)S(1)} copy-done((bf16[768,768]{1,0:T(8,128)(2,1)S(1)}, bf16[768,768]{1,0:T(8,128)(2,1)}, u32[]{:S(2)}) %copy-start.9) | copy-done | bytes 1179672
  17.6 1.3 %copy-done.11 = bf16[768,768]{1,0:T(8,128)(2,1)S(1)} copy-done((bf16[768,768]{1,0:T(8,128)(2,1)S(1)}, bf16[768,768]{1,0:T(8,128)(2,1)}, u32[]{:S(2)}) %copy-start.11) | copy-done | bytes 1179672
  18.9 0.0 copy-start.10
  18.9 0.0 copy-start.12
  18.9 0.0 collective-permute-done.refs_0_
  18.9 3.7 %collective-permute-start.5 = (bf16[784,128]{1,0:T(8,128)(2,1)S(1)}, bf16[784,128]{1,0:T(8,128)(2,1)S(1)}, u32[]{:S(2)}, u32[]{:S(2)}) collective-permute-start(bf16[784,128]{1,0:T(8,128)(2,1)S(1)} %get-tuple-element.97), channel_id=1, source_target_pairs={{0,6},{1,7},{2,4},{3,5},{4,2},{5,3},{6,0},{7,1},{8,14},{9,15},{10,... | collective-permute-start | bytes 602120 | tf_op jit(solution)/shard_map/ppermute | solution.py:483
  22.6 0.0 collective-permute-done.1.refs_2_
  22.6 2.1 %collective-permute-start.6 = (bf16[784,128]{1,0:T(8,128)(2,1)S(1)}, bf16[784,128]{1,0:T(8,128)(2,1)S(1)}, u32[]{:S(2)}, u32[]{:S(2)}) collective-permute-start(bf16[784,128]{1,0:T(8,128)(2,1)S(1)} %get-tuple-element.106), channel_id=1, source_target_pairs={{0,7},{1,6},{2,5},{3,4},{4,3},{5,2},{6,1},{7,0},{8,15},{9,14},{10,... | collective-permute-start | bytes 602120 | tf_op jit(solution)/shard_map/ppermute | solution.py:483
  24.7 1.2 %collective-permute-done.2.refs_3_ = bf16[784,128]{1,0:T(8,128)(2,1)S(1)} collective-permute-done((bf16[784,128]{1,0:T(8,128)(2,1)S(1)}, bf16[784,128]{1,0:T(8,128)(2,1)S(1)}, u32[]{:S(2)}, u32[]{:S(2)}) %collective-permute-start.2) | collective-permute-done | bytes 200736 | tf_op jit(solution)/shard_map/ppermute | solution.py:483
  25.9 0.0 collective-permute-done.3.refs_1_
  25.9 0.0 copy-done.2
  25.9 0.0 copy-done.4
  25.9 0.0 copy-done.6
  25.9 0.0 copy-done.8
  25.9 0.0 copy-done.10
  25.9 0.0 copy-done.12
  26.0 7.0 %window_layer.4 = (bf16[8,48,768]{2,1,0:T(8,128)(2,1)S(1)}, bf16[8,48,768]{2,1,0:T(8,128)(2,1)S(1)}, bf16[8,48,768]{2,1,0:T(8,128)(2,1)S(1)}, bf16[8,48,768]{2,1...) custom-call(s32[1]{0:T(128)} %bitcast.me_ref, ...), custom_call_target="tpu_custom_call" | custom-call | flops 4051697664 | bytes 16777216 | tf_op jit(solution)/shard_map/window_layer/pallas_call | solution.py:349
  32.9 0.0 collective-permute-done.4.refs_1_
  32.9 4.5 %window_layer.5 = (bf16[8,32,768]{2,1,0:T(8,128)(2,1)S(1)}, bf16[8,32,768]{2,1,0:T(8,128)(2,1)S(1)}, bf16[8,32,768]{2,1,0:T(8,128)(2,1)S(1)}, bf16[8,32,768]{2,1...) custom-call(s32[1]{0:T(128)} %bitcast.me_ref, ...), custom_call_target="tpu_custom_call" | custom-call | flops 2315255808 | bytes 16777216 | tf_op jit(solution)/shard_map/window_layer/pallas_call | solution.py:349
  37.4 0.0 collective-permute-done.5.refs_0_
  37.4 2.6 %window_layer.6 = (bf16[8,16,768]{2,1,0:T(8,128)(2,1)S(1)}, bf16[8,16,768]{2,1,0:T(8,128)(2,1)S(1)}, bf16[8,16,768]{2,1,0:T(8,128)(2,1)S(1)}, bf16[8,16,768]{2,1...) custom-call(s32[1]{0:T(128)} %bitcast.me_ref, ...), custom_call_target="tpu_custom_call" | custom-call | flops 1157627904 | bytes 16777216 | tf_op jit(solution)/shard_map/window_layer/pallas_call | solution.py:349
  40.1 0.0 collective-permute-done.6.refs_0_
  40.1 0.0 copy-start.13
  40.1 3.4 %window_layer.7 = (bf16[8,32,768]{2,1,0:T(8,128)(2,1)S(1)}, bf16[4,32,768]{2,1,0:T(8,128)(2,1)S(1)}, bf16[4,32,768]{2,1,0:T(8,128)(2,1)S(1)}, bf16[4,32,768]{2,1,0:T(8,128)(2,1)S(1)}, bf16[8,32,128]{2,1,0:T(8,128)(2,1)S(1)}) custom-call(s32[1]{0:T(128)} %bitcast.me_ref, bf16[784,128]{1,0:T(8,128)(2,1)S(1)} %collective-permute-done.6.refs_0_, ...), custom_call_target="tpu_custom_call" | custom-call | flops 1736441856 | bytes 16777216 | tf_op jit(solution)/shard_map/window_layer/pallas_call | solution.py:349
  43.5 0.0 copy-done.13
  43.5 2.7 %row_layer.2 = (bf16[4,16,768]{2,1,0:T(8,128)(2,1)S(1)}, bf16[4,16,768]{2,1,0:T(8,128)(2,1)S(1)}, bf16[4,16,768]{2,1,0:T(8,128)(2,1)S(1)}, bf16[4,16,768]{2,1,0:...) custom-call(s32[1]{0:T(128)} %bitcast.me_ref, ...), custom_call_target="tpu_custom_call" | custom-call | bytes 65536 | tf_op jit(solution)/shard_map/row_layer/pallas_call | solution.py:434
  46.3 2.6 %collective-permute-start.11 = (bf16[4,16,768]{2,1,0:T(8,128)(2,1)S(1)}, bf16[4,16,768]{2,1,0:T(8,128)(2,1)S(1)}, u32[]{:S(2)}, u32[]{:S(2)}) collective-permute-start(bf16[4,16,768]{2,1,0:T(8,128)(2,1)S(1)} %get-tuple-element.129), channel_id=1, source_target_pairs={{0,6},{1,7},{2,4},{3,5},{4,2},{5,3},{6,0},{7,1},{8,14},{9,15},{10,... | collective-permute-start | bytes 294920 | tf_op jit(solution)/shard_map/ppermute | solution.py:483
  48.9 2.6 %collective-permute-start.9 = (bf16[4,16,768]{2,1,0:T(8,128)(2,1)S(1)}, bf16[4,16,768]{2,1,0:T(8,128)(2,1)S(1)}, u32[]{:S(2)}, u32[]{:S(2)}) collective-permute-start(bf16[4,16,768]{2,1,0:T(8,128)(2,1)S(1)} %get-tuple-element.125), channel_id=1, source_target_pairs={{0,5},{1,4},{2,7},{3,6},{4,1},{5,0},{6,3},{7,2},{8,13},{9,12},{10,... | collective-permute-start | bytes 294920 | tf_op jit(solution)/shard_map/ppermute | solution.py:483
  51.5 0.3 collective-permute-start.7
  51.8 3.4 %row_layer.3 = (bf16[4,16,768]{2,1,0:T(8,128)(2,1)S(1)}, bf16[4,16,768]{2,1,0:T(8,128)(2,1)S(1)}, bf16[4,16,768]{2,1,0:T(8,128)(2,1)S(1)}, bf16[4,16,768]{2,1,0:...) custom-call(s32[1]{0:T(128)} %bitcast.me_ref, ...), custom_call_target="tpu_custom_call" | custom-call | bytes 65536 | tf_op jit(solution)/shard_map/row_layer/pallas_call | solution.py:434
  55.1 0.0 collective-permute-done.11.refs_2_
  55.1 4.2 %collective-permute-start.17 = (bf16[8,16,768]{2,1,0:T(8,128)(2,1)S(1)}, bf16[8,16,768]{2,1,0:T(8,128)(2,1)S(1)}, u32[]{:S(2)}, u32[]{:S(2)}) collective-permute-start(bf16[8,16,768]{2,1,0:T(8,128)(2,1)S(1)} %get-tuple-element.141), channel_id=1, source_target_pairs={{0,3},{1,2},{2,1},{3,0},{4,7},{5,6},{6,5},{7,4},{8,11},{9,10},{10,... | collective-permute-start | bytes 589832 | tf_op jit(solution)/shard_map/ppermute | solution.py:483
  59.4 2.1 %collective-permute-done.9.refs_1_ = bf16[4,16,768]{2,1,0:T(8,128)(2,1)S(1)} collective-permute-done((bf16[4,16,768]{2,1,0:T(8,128)(2,1)S(1)}, bf16[4,16,768]{2,1,0:T(8,128)(2,1)S(1)}, u32[]{:S(2)}, u32[]{:S(2)}) %collective-permute-start.9) | collective-permute-done | bytes 98336 | tf_op jit(solution)/shard_map/ppermute | solution.py:483
  61.5 0.1 collective-permute-start.16
  61.6 3.8 %collective-permute-start.13 = (bf16[4,16,768]{2,1,0:T(8,128)(2,1)S(1)}, bf16[4,16,768]{2,1,0:T(8,128)(2,1)S(1)}, u32[]{:S(2)}, u32[]{:S(2)}) collective-permute-start(bf16[4,16,768]{2,1,0:T(8,128)(2,1)S(1)} %get-tuple-element.133), channel_id=1, source_target_pairs={{0,7},{1,6},{2,5},{3,4},{4,3},{5,2},{6,1},{7,0},{8,15},{9,14},{10,... | collective-permute-start | bytes 294920 | tf_op jit(solution)/shard_map/ppermute | solution.py:483
  65.3 0.0 collective-permute-done.7.refs_0_
  65.3 0.5 collective-permute-start.15
  65.9 0.6 collective-permute-start.8
  66.5 9.4 %collective-permute-done.13.refs_3_ = bf16[4,16,768]{2,1,0:T(8,128)(2,1)S(1)} collective-permute-done((bf16[4,16,768]{2,1,0:T(8,128)(2,1)S(1)}, bf16[4,16,768]{2,1,0:T(8,128)(2,1)S(1)}, u32[]{:S(2)}, u32[]{:S(2)}) %collective-permute-start.13) | collective-permute-done | bytes 98336 | tf_op jit(solution)/shard_map/ppermute | solution.py:483
  75.8 0.0 collective-permute-start.10
  75.8 0.0 collective-permute-done.17.refs_6_
  75.8 0.0 collective-permute-start.12
  75.8 0.0 collective-permute-done.16.refs_5_
  75.8 2.7 %collective-permute-start.14 = (bf16[4,16,768]{2,1,0:T(8,128)(2,1)S(1)}, bf16[4,16,768]{2,1,0:T(8,128)(2,1)S(1)}, u32[]{:S(2)}, u32[]{:S(2)}) collective-permute-start(bf16[4,16,768]{2,1,0:T(8,128)(2,1)S(1)} %get-tuple-element.134), channel_id=1, source_target_pairs={{0,7},{1,6},{2,5},{3,4},{4,3},{5,2},{6,1},{7,0},{8,15},{9,14},{10,... | collective-permute-start | bytes 294920 | tf_op jit(solution)/shard_map/ppermute | solution.py:483
  78.5 0.0 collective-permute-done.15.refs_4_
  78.5 1.1 %place.2.refs_4_ = bf16[64,16,768]{2,1,0:T(8,128)(2,1)} custom-call(s32[1]{0:T(128)} %bitcast.me_ref, bf16[4,16,768]{2,1,0:T(8,128)(2,1)S(1)} %collective-permute-done.7.refs_0_, bf16[4,16,768]{2,1,0:T(8,128)(2,1)S(1)} %collective-permute-done.9.refs_1_, bf16[4,16,768]{2,1,0:T(8,128)(2,1)S(1)} %collective-permute-done.11.refs_2_, ...), custom_call_target="tpu_custom_call" | custom-call | bytes 4194304 | tf_op jit(solution)/shard_map/place/pallas_call | solution.py:468
  79.6 0.0 collective-permute-done.8.refs_0_
  79.6 5.9 %collective-permute-done.10.refs_1_ = bf16[4,16,768]{2,1,0:T(8,128)(2,1)S(1)} collective-permute-done((bf16[4,16,768]{2,1,0:T(8,128)(2,1)S(1)}, bf16[4,16,768]{2,1,0:T(8,128)(2,1)S(1)}, u32[]{:S(2)}, u32[]{:S(2)}) %collective-permute-start.10) | collective-permute-done | bytes 98336 | tf_op jit(solution)/shard_map/ppermute | solution.py:483
  85.5 0.0 collective-permute-done.12.refs_2_
  85.5 0.0 collective-permute-done.14.refs_3_
  85.5 0.8 place.3
  (12 shorter events, 0.0 us)
Async XLA Ops:
  0.0 11.2 %copy-start = (bf16[768,768]{1,0:T(8,128)(2,1)S(1)}, bf16[768,768]{1,0:T(8,128)(2,1)}, u32[]{:S(2)}) copy-start(bf16[768,768]{1,0:T(8,128)(2,1)} %refs_25_.1) | copy-start | bytes 3538948
  0.0 0.8 copy-start.14
  2.4 16.6 %collective-permute-start = (bf16[784,128]{1,0:T(8,128)(2,1)S(1)}, bf16[784,128]{1,0:T(8,128)(2,1)S(1)}, u32[]{:S(2)}, u32[]{:S(2)}) collective-permute-start(bf16[784,128]{1,0:T(8,128)(2,1)S(1)} %get-tuple-element.75), channel_id=1, source_target_pairs={{0,4},{1,5},{2,6},{3,7},{4,0},{5,1},{6,2},{7,3},{8,12},{9,13},{10,... | collective-permute-start | bytes 602120 | tf_op jit(solution)/shard_map/ppermute | solution.py:483
  6.5 16.1 %collective-permute-start.1 = (bf16[784,128]{1,0:T(8,128)(2,1)S(1)}, bf16[784,128]{1,0:T(8,128)(2,1)S(1)}, u32[]{:S(2)}, u32[]{:S(2)}) collective-permute-start(bf16[784,128]{1,0:T(8,128)(2,1)S(1)} %get-tuple-element.76), channel_id=1, source_target_pairs={{0,2},{1,3},{2,0},{3,1},{4,6},{5,7},{6,4},{7,5},{8,10},{9,11},{10,... | collective-permute-start | bytes 602120 | tf_op jit(solution)/shard_map/ppermute | solution.py:483
  8.0 17.9 %collective-permute-start.2 = (bf16[784,128]{1,0:T(8,128)(2,1)S(1)}, bf16[784,128]{1,0:T(8,128)(2,1)S(1)}, u32[]{:S(2)}, u32[]{:S(2)}) collective-permute-start(bf16[784,128]{1,0:T(8,128)(2,1)S(1)} %get-tuple-element.77), channel_id=1, source_target_pairs={{0,3},{1,2},{2,1},{3,0},{4,7},{5,6},{6,5},{7,4},{8,11},{9,10},{10,... | collective-permute-start | bytes 602120 | tf_op jit(solution)/shard_map/ppermute | solution.py:483
  9.4 16.5 %collective-permute-start.3 = (bf16[784,128]{1,0:T(8,128)(2,1)S(1)}, bf16[784,128]{1,0:T(8,128)(2,1)S(1)}, u32[]{:S(2)}, u32[]{:S(2)}) collective-permute-start(bf16[784,128]{1,0:T(8,128)(2,1)S(1)} %get-tuple-element.78), channel_id=1, source_target_pairs={{0,1},{1,0},{2,3},{3,2},{4,5},{5,4},{6,7},{7,6},{8,9},{9,8},{10,11... | collective-permute-start | bytes 602120 | tf_op jit(solution)/shard_map/ppermute | solution.py:483
  10.0 23.0 %collective-permute-start.4 = (bf16[784,128]{1,0:T(8,128)(2,1)S(1)}, bf16[784,128]{1,0:T(8,128)(2,1)S(1)}, u32[]{:S(2)}, u32[]{:S(2)}) collective-permute-start(bf16[784,128]{1,0:T(8,128)(2,1)S(1)} %get-tuple-element.88), channel_id=1, source_target_pairs={{0,5},{1,4},{2,7},{3,6},{4,1},{5,0},{6,3},{7,2},{8,13},{9,12},{10,... | collective-permute-start | bytes 602120 | tf_op jit(solution)/shard_map/ppermute | solution.py:483
  11.3 1.3 %copy-start.1 = (bf16[768,768]{1,0:T(8,128)(2,1)S(1)}, bf16[768,768]{1,0:T(8,128)(2,1)}, u32[]{:S(2)}) copy-start(bf16[768,768]{1,0:T(8,128)(2,1)} %refs_26_.1) | copy-start | bytes 3538948
  12.5 1.3 %copy-start.3 = (bf16[768,768]{1,0:T(8,128)(2,1)S(1)}, bf16[768,768]{1,0:T(8,128)(2,1)}, u32[]{:S(2)}) copy-start(bf16[768,768]{1,0:T(8,128)(2,1)} %refs_27_.1) | copy-start | bytes 3538948
  13.8 1.3 %copy-start.5 = (bf16[768,768]{1,0:T(8,128)(2,1)S(1)}, bf16[768,768]{1,0:T(8,128)(2,1)}, u32[]{:S(2)}) copy-start(bf16[768,768]{1,0:T(8,128)(2,1)} %refs_9_.7) | copy-start | bytes 3538948
  15.1 1.3 %copy-start.7 = (bf16[768,768]{1,0:T(8,128)(2,1)S(1)}, bf16[768,768]{1,0:T(8,128)(2,1)}, u32[]{:S(2)}) copy-start(bf16[768,768]{1,0:T(8,128)(2,1)} %refs_10_.7) | copy-start | bytes 3538948
  16.3 1.3 %copy-start.9 = (bf16[768,768]{1,0:T(8,128)(2,1)S(1)}, bf16[768,768]{1,0:T(8,128)(2,1)}, u32[]{:S(2)}) copy-start(bf16[768,768]{1,0:T(8,128)(2,1)} %refs_11_.7) | copy-start | bytes 3538948
  17.6 1.3 %copy-start.11 = (bf16[768,768]{1,0:T(8,128)(2,1)S(1)}, bf16[768,768]{1,0:T(8,128)(2,1)}, u32[]{:S(2)}) copy-start(bf16[768,768]{1,0:T(8,128)(2,1)} %refs_12_.5) | copy-start | bytes 3538948
  18.9 7.0 %copy-start.2 = (bf16[768,768]{1,0:T(8,128)(2,1)S(1)}, bf16[768,768]{1,0:T(8,128)(2,1)}, u32[]{:S(2)}) copy-start(bf16[768,768]{1,0:T(8,128)(2,1)} %refs_26_.1) | copy-start | bytes 3538948
  18.9 7.0 %copy-start.4 = (bf16[768,768]{1,0:T(8,128)(2,1)S(1)}, bf16[768,768]{1,0:T(8,128)(2,1)}, u32[]{:S(2)}) copy-start(bf16[768,768]{1,0:T(8,128)(2,1)} %refs_27_.1) | copy-start | bytes 3538948
  18.9 7.0 %copy-start.6 = (bf16[768,768]{1,0:T(8,128)(2,1)S(1)}, bf16[768,768]{1,0:T(8,128)(2,1)}, u32[]{:S(2)}) copy-start(bf16[768,768]{1,0:T(8,128)(2,1)} %refs_9_.7) | copy-start | bytes 3538948
  18.9 7.0 %copy-start.8 = (bf16[768,768]{1,0:T(8,128)(2,1)S(1)}, bf16[768,768]{1,0:T(8,128)(2,1)}, u32[]{:S(2)}) copy-start(bf16[768,768]{1,0:T(8,128)(2,1)} %refs_10_.7) | copy-start | bytes 3538948
  18.9 7.0 %copy-start.10 = (bf16[768,768]{1,0:T(8,128)(2,1)S(1)}, bf16[768,768]{1,0:T(8,128)(2,1)}, u32[]{:S(2)}) copy-start(bf16[768,768]{1,0:T(8,128)(2,1)} %refs_11_.7) | copy-start | bytes 3538948
  18.9 7.0 %copy-start.12 = (bf16[768,768]{1,0:T(8,128)(2,1)S(1)}, bf16[768,768]{1,0:T(8,128)(2,1)}, u32[]{:S(2)}) copy-start(bf16[768,768]{1,0:T(8,128)(2,1)} %refs_12_.5) | copy-start | bytes 3538948
  18.9 18.5 %collective-permute-start.5 = (bf16[784,128]{1,0:T(8,128)(2,1)S(1)}, bf16[784,128]{1,0:T(8,128)(2,1)S(1)}, u32[]{:S(2)}, u32[]{:S(2)}) collective-permute-start(bf16[784,128]{1,0:T(8,128)(2,1)S(1)} %get-tuple-element.97), channel_id=1, source_target_pairs={{0,6},{1,7},{2,4},{3,5},{4,2},{5,3},{6,0},{7,1},{8,14},{9,15},{10,... | collective-permute-start | bytes 602120 | tf_op jit(solution)/shard_map/ppermute | solution.py:483
  22.6 17.5 %collective-permute-start.6 = (bf16[784,128]{1,0:T(8,128)(2,1)S(1)}, bf16[784,128]{1,0:T(8,128)(2,1)S(1)}, u32[]{:S(2)}, u32[]{:S(2)}) collective-permute-start(bf16[784,128]{1,0:T(8,128)(2,1)S(1)} %get-tuple-element.106), channel_id=1, source_target_pairs={{0,7},{1,6},{2,5},{3,4},{4,3},{5,2},{6,1},{7,0},{8,15},{9,14},{10,... | collective-permute-start | bytes 602120 | tf_op jit(solution)/shard_map/ppermute | solution.py:483
  40.1 3.5 %copy-start.13 = (bf16[768,768]{1,0:T(8,128)(2,1)S(1)}, bf16[768,768]{1,0:T(8,128)(2,1)}, u32[]{:S(2)}) copy-start(bf16[768,768]{1,0:T(8,128)(2,1)} %refs_20_.3) | copy-start | bytes 3538948
  46.3 8.8 %collective-permute-start.11 = (bf16[4,16,768]{2,1,0:T(8,128)(2,1)S(1)}, bf16[4,16,768]{2,1,0:T(8,128)(2,1)S(1)}, u32[]{:S(2)}, u32[]{:S(2)}) collective-permute-start(bf16[4,16,768]{2,1,0:T(8,128)(2,1)S(1)} %get-tuple-element.129), channel_id=1, source_target_pairs={{0,6},{1,7},{2,4},{3,5},{4,2},{5,3},{6,0},{7,1},{8,14},{9,15},{10,... | collective-permute-start | bytes 294920 | tf_op jit(solution)/shard_map/ppermute | solution.py:483
  48.9 12.6 %collective-permute-start.9 = (bf16[4,16,768]{2,1,0:T(8,128)(2,1)S(1)}, bf16[4,16,768]{2,1,0:T(8,128)(2,1)S(1)}, u32[]{:S(2)}, u32[]{:S(2)}) collective-permute-start(bf16[4,16,768]{2,1,0:T(8,128)(2,1)S(1)} %get-tuple-element.125), channel_id=1, source_target_pairs={{0,5},{1,4},{2,7},{3,6},{4,1},{5,0},{6,3},{7,2},{8,13},{9,12},{10,... | collective-permute-start | bytes 294920 | tf_op jit(solution)/shard_map/ppermute | solution.py:483
  51.5 13.9 %collective-permute-start.7 = (bf16[4,16,768]{2,1,0:T(8,128)(2,1)S(1)}, bf16[4,16,768]{2,1,0:T(8,128)(2,1)S(1)}, u32[]{:S(2)}, u32[]{:S(2)}) collective-permute-start(bf16[4,16,768]{2,1,0:T(8,128)(2,1)S(1)} %get-tuple-element.121), channel_id=1, source_target_pairs={{0,4},{1,5},{2,6},{3,7},{4,0},{5,1},{6,2},{7,3},{8,12},{9,13},{10,... | collective-permute-start | bytes 294920 | tf_op jit(solution)/shard_map/ppermute | solution.py:483
  55.1 20.7 %collective-permute-start.17 = (bf16[8,16,768]{2,1,0:T(8,128)(2,1)S(1)}, bf16[8,16,768]{2,1,0:T(8,128)(2,1)S(1)}, u32[]{:S(2)}, u32[]{:S(2)}) collective-permute-start(bf16[8,16,768]{2,1,0:T(8,128)(2,1)S(1)} %get-tuple-element.141), channel_id=1, source_target_pairs={{0,3},{1,2},{2,1},{3,0},{4,7},{5,6},{6,5},{7,4},{8,11},{9,10},{10,... | collective-permute-start | bytes 589832 | tf_op jit(solution)/shard_map/ppermute | solution.py:483
  61.5 14.4 %collective-permute-start.16 = (bf16[8,16,768]{2,1,0:T(8,128)(2,1)S(1)}, bf16[8,16,768]{2,1,0:T(8,128)(2,1)S(1)}, u32[]{:S(2)}, u32[]{:S(2)}) collective-permute-start(bf16[8,16,768]{2,1,0:T(8,128)(2,1)S(1)} %get-tuple-element.140), channel_id=1, source_target_pairs={{0,2},{1,3},{2,0},{3,1},{4,6},{5,7},{6,4},{7,5},{8,10},{9,11},{10,... | collective-permute-start | bytes 589832 | tf_op jit(solution)/shard_map/ppermute | solution.py:483
  61.6 14.3 %collective-permute-start.13 = (bf16[4,16,768]{2,1,0:T(8,128)(2,1)S(1)}, bf16[4,16,768]{2,1,0:T(8,128)(2,1)S(1)}, u32[]{:S(2)}, u32[]{:S(2)}) collective-permute-start(bf16[4,16,768]{2,1,0:T(8,128)(2,1)S(1)} %get-tuple-element.133), channel_id=1, source_target_pairs={{0,7},{1,6},{2,5},{3,4},{4,3},{5,2},{6,1},{7,0},{8,15},{9,14},{10,... | collective-permute-start | bytes 294920 | tf_op jit(solution)/shard_map/ppermute | solution.py:483
  65.3 13.2 %collective-permute-start.15 = (bf16[8,16,768]{2,1,0:T(8,128)(2,1)S(1)}, bf16[8,16,768]{2,1,0:T(8,128)(2,1)S(1)}, u32[]{:S(2)}, u32[]{:S(2)}) collective-permute-start(bf16[8,16,768]{2,1,0:T(8,128)(2,1)S(1)} %get-tuple-element.139), channel_id=1, source_target_pairs={{0,1},{1,0},{2,3},{3,2},{4,5},{5,4},{6,7},{7,6},{8,9},{9,8},{10,11... | collective-permute-start | bytes 589832 | tf_op jit(solution)/shard_map/ppermute | solution.py:483
  65.9 13.7 %collective-permute-start.8 = (bf16[4,16,768]{2,1,0:T(8,128)(2,1)S(1)}, bf16[4,16,768]{2,1,0:T(8,128)(2,1)S(1)}, u32[]{:S(2)}, u32[]{:S(2)}) collective-permute-start(bf16[4,16,768]{2,1,0:T(8,128)(2,1)S(1)} %get-tuple-element.122), channel_id=1, source_target_pairs={{0,4},{1,5},{2,6},{3,7},{4,0},{5,1},{6,2},{7,3},{8,12},{9,13},{10,... | collective-permute-start | bytes 294920 | tf_op jit(solution)/shard_map/ppermute | solution.py:483
  75.8 9.6 %collective-permute-start.10 = (bf16[4,16,768]{2,1,0:T(8,128)(2,1)S(1)}, bf16[4,16,768]{2,1,0:T(8,128)(2,1)S(1)}, u32[]{:S(2)}, u32[]{:S(2)}) collective-permute-start(bf16[4,16,768]{2,1,0:T(8,128)(2,1)S(1)} %get-tuple-element.126), channel_id=1, source_target_pairs={{0,5},{1,4},{2,7},{3,6},{4,1},{5,0},{6,3},{7,2},{8,13},{9,12},{10,... | collective-permute-start | bytes 294920 | tf_op jit(solution)/shard_map/ppermute | solution.py:483
  75.8 9.6 %collective-permute-start.12 = (bf16[4,16,768]{2,1,0:T(8,128)(2,1)S(1)}, bf16[4,16,768]{2,1,0:T(8,128)(2,1)S(1)}, u32[]{:S(2)}, u32[]{:S(2)}) collective-permute-start(bf16[4,16,768]{2,1,0:T(8,128)(2,1)S(1)} %get-tuple-element.130), channel_id=1, source_target_pairs={{0,6},{1,7},{2,4},{3,5},{4,2},{5,3},{6,0},{7,1},{8,14},{9,15},{10,... | collective-permute-start | bytes 294920 | tf_op jit(solution)/shard_map/ppermute | solution.py:483
  75.8 9.6 %collective-permute-start.14 = (bf16[4,16,768]{2,1,0:T(8,128)(2,1)S(1)}, bf16[4,16,768]{2,1,0:T(8,128)(2,1)S(1)}, u32[]{:S(2)}, u32[]{:S(2)}) collective-permute-start(bf16[4,16,768]{2,1,0:T(8,128)(2,1)S(1)} %get-tuple-element.134), channel_id=1, source_target_pairs={{0,7},{1,6},{2,5},{3,4},{4,3},{5,2},{6,1},{7,0},{8,15},{9,14},{10,... | collective-permute-start | bytes 294920 | tf_op jit(solution)/shard_map/ppermute | solution.py:483

commit v10 on v9

--- a/solution.py
+++ b/solution.py
@@ -505,9 +505,10 @@
     far = [exchanged(piece, d) for d, piece in zip(ORDER[:4], first)]
     last = list(last)
     for i in range(4):
-        last[i], last[4 + i], far[i] = lax.optimization_barrier((last[i], last[4 + i], far[i]))
+        last[i], far[i] = lax.optimization_barrier((last[i], far[i]))
     far_last = [exchanged(piece, d) for d, piece in zip(ORDER[:4], last)]
-    near = [exchanged(piece, d) if d else piece for d, piece in zip(ORDER[4:], last[4:])]
+    near = {d: exchanged(piece, d) if d else piece for d, piece in zip(ORDER[4:], last[4:])}
+    near = [near[d] for d in ORDER[4:]]
     out = place([(d, 0) for d in ORDER], me, far + near, None, fields.shape)
     return place([(d, ROWS_FIRST) for d in ORDER[:4]], me, far_last, out, fields.shape)
 

time: 87.3 us -> 86.1 us (0.986)
  transfers between devices with their start and end apart: 18 -> 18, of which waited for: 4 -> 5; matrix products, arithmetic and copies ran while one was open for 0% -> 0% of each run, Pallas kernels for 21% -> 22%
where the time goes in v10:
time: 86.1 us; the launch traced here: 85.7 us
  starting transfers between devices  32.1 us (37%)
  Pallas kernels  27 us (31%)
  waiting for transfers between devices  17.8 us (21%)
  local copies, waits for them, and re-layouts  8.45 us (10%)
    ppermute x18, starting transfers between devices, exchanged(): return lax.ppermute(piece, 'lon', [(s, s ^ distance) for s in range(count)])  32.1 us
    ppermute x18, waiting for transfers between devices, exchanged(): return lax.ppermute(piece, 'lon', [(s, s ^ distance) for s in range(count)])  17.8 us
    pallas_call x4, Pallas kernels, window_layer(): pl.pallas_call(functools.partial(window_kernel, stage), out_shape=outs, i...  17.5 us
    unnamed x30, local copies, waits for them, and re-layouts  8.45 us
    pallas_call x2, Pallas kernels, row_layer(): pl.pallas_call(functools.partial(row_kernel, start, rows), out_shape=(far...  6.1 us
    pallas_call x2, Pallas kernels, place(): pl.pallas_call(functools.partial(place_kernel, spots), out_shape=jax.Shap...  1.84 us
  transfers between devices with their start and end apart: 18, of which 5 were waited for; matrix products, arithmetic and copies ran while one was open for 0% of the time, Pallas kernels for 22%

profile of v10, /device:TPU:0, one launch (start us, length us, event | category | flops | bytes accessed | tf_op | source)
XLA Modules:
  0.0 85.7 jit_solution(11423900502701117083)
XLA Ops:
  0.0 0.0 copy-start
  0.0 0.8 copy-done.14
  0.8 1.6 %pack.1 = (bf16[784,128]{1,0:T(8,128)(2,1)S(1)}, bf16[784,128]{1,0:T(8,128)(2,1)S(1)}, bf16[784,128]{1,0:T(8,128)(2,1)S(1)}, bf16[784,128]{1,0:T(8,128)(2,1)S(1)...) custom-call(s32[1]{0:T(128)} %bitcast.me_ref, ...), custom_call_target="tpu_custom_call" | custom-call | flops 1600000 | bytes 3200000 | tf_op jit(solution)/shard_map/pack/pallas_call | solution.py:202
  2.4 4.1 %collective-permute-start = (bf16[784,128]{1,0:T(8,128)(2,1)S(1)}, bf16[784,128]{1,0:T(8,128)(2,1)S(1)}, u32[]{:S(2)}, u32[]{:S(2)}) collective-permute-start(bf16[784,128]{1,0:T(8,128)(2,1)S(1)} %get-tuple-element.71), channel_id=1, source_target_pairs={{0,4},{1,5},{2,6},{3,7},{4,0},{5,1},{6,2},{7,3},{8,12},{9,13},{10,... | collective-permute-start | bytes 602120 | tf_op jit(solution)/shard_map/ppermute | solution.py:483
  6.5 1.6 %collective-permute-start.1 = (bf16[784,128]{1,0:T(8,128)(2,1)S(1)}, bf16[784,128]{1,0:T(8,128)(2,1)S(1)}, u32[]{:S(2)}, u32[]{:S(2)}) collective-permute-start(bf16[784,128]{1,0:T(8,128)(2,1)S(1)} %get-tuple-element.72), channel_id=1, source_target_pairs={{0,2},{1,3},{2,0},{3,1},{4,6},{5,7},{6,4},{7,5},{8,10},{9,11},{10,... | collective-permute-start | bytes 602120 | tf_op jit(solution)/shard_map/ppermute | solution.py:483
  8.0 1.4 %collective-permute-start.2 = (bf16[784,128]{1,0:T(8,128)(2,1)S(1)}, bf16[784,128]{1,0:T(8,128)(2,1)S(1)}, u32[]{:S(2)}, u32[]{:S(2)}) collective-permute-start(bf16[784,128]{1,0:T(8,128)(2,1)S(1)} %get-tuple-element.73), channel_id=1, source_target_pairs={{0,3},{1,2},{2,1},{3,0},{4,7},{5,6},{6,5},{7,4},{8,11},{9,10},{10,... | collective-permute-start | bytes 602120 | tf_op jit(solution)/shard_map/ppermute | solution.py:483
  9.4 0.5 collective-permute-start.3
  10.0 1.3 %collective-permute-start.4 = (bf16[784,128]{1,0:T(8,128)(2,1)S(1)}, bf16[784,128]{1,0:T(8,128)(2,1)S(1)}, u32[]{:S(2)}, u32[]{:S(2)}) collective-permute-start(bf16[784,128]{1,0:T(8,128)(2,1)S(1)} %get-tuple-element.84), channel_id=1, source_target_pairs={{0,5},{1,4},{2,7},{3,6},{4,1},{5,0},{6,3},{7,2},{8,13},{9,12},{10,... | collective-permute-start | bytes 602120 | tf_op jit(solution)/shard_map/ppermute | solution.py:483
  11.2 0.0 copy-done
  11.3 1.3 %copy-done.1 = bf16[768,768]{1,0:T(8,128)(2,1)S(1)} copy-done((bf16[768,768]{1,0:T(8,128)(2,1)S(1)}, bf16[768,768]{1,0:T(8,128)(2,1)}, u32[]{:S(2)}) %copy-start.1) | copy-done | bytes 1179672
  12.5 1.3 %copy-done.3 = bf16[768,768]{1,0:T(8,128)(2,1)S(1)} copy-done((bf16[768,768]{1,0:T(8,128)(2,1)S(1)}, bf16[768,768]{1,0:T(8,128)(2,1)}, u32[]{:S(2)}) %copy-start.3) | copy-done | bytes 1179672
  13.8 1.3 %copy-done.5 = bf16[768,768]{1,0:T(8,128)(2,1)S(1)} copy-done((bf16[768,768]{1,0:T(8,128)(2,1)S(1)}, bf16[768,768]{1,0:T(8,128)(2,1)}, u32[]{:S(2)}) %copy-start.5) | copy-done | bytes 1179672
  15.1 1.3 %copy-done.7 = bf16[768,768]{1,0:T(8,128)(2,1)S(1)} copy-done((bf16[768,768]{1,0:T(8,128)(2,1)S(1)}, bf16[768,768]{1,0:T(8,128)(2,1)}, u32[]{:S(2)}) %copy-start.7) | copy-done | bytes 1179672
  16.3 1.3 %copy-done.9 = bf16[768,768]{1,0:T(8,128)(2,1)S(1)} copy-done((bf16[768,768]{1,0:T(8,128)(2,1)S(1)}, bf16[768,768]{1,0:T(8,128)(2,1)}, u32[]{:S(2)}) %copy-start.9) | copy-done | bytes 1179672
  17.6 1.3 %copy-done.11 = bf16[768,768]{1,0:T(8,128)(2,1)S(1)} copy-done((bf16[768,768]{1,0:T(8,128)(2,1)S(1)}, bf16[768,768]{1,0:T(8,128)(2,1)}, u32[]{:S(2)}) %copy-start.11) | copy-done | bytes 1179672
  18.9 0.0 copy-start.10
  18.9 0.0 copy-start.12
  18.9 0.0 collective-permute-done.refs_0_
  18.9 3.7 %collective-permute-start.5 = (bf16[784,128]{1,0:T(8,128)(2,1)S(1)}, bf16[784,128]{1,0:T(8,128)(2,1)S(1)}, u32[]{:S(2)}, u32[]{:S(2)}) collective-permute-start(bf16[784,128]{1,0:T(8,128)(2,1)S(1)} %get-tuple-element.93), channel_id=1, source_target_pairs={{0,6},{1,7},{2,4},{3,5},{4,2},{5,3},{6,0},{7,1},{8,14},{9,15},{10,... | collective-permute-start | bytes 602120 | tf_op jit(solution)/shard_map/ppermute | solution.py:483
  22.6 0.0 collective-permute-done.1.refs_2_
  22.6 2.1 %collective-permute-start.6 = (bf16[784,128]{1,0:T(8,128)(2,1)S(1)}, bf16[784,128]{1,0:T(8,128)(2,1)S(1)}, u32[]{:S(2)}, u32[]{:S(2)}) collective-permute-start(bf16[784,128]{1,0:T(8,128)(2,1)S(1)} %get-tuple-element.102), channel_id=1, source_target_pairs={{0,7},{1,6},{2,5},{3,4},{4,3},{5,2},{6,1},{7,0},{8,15},{9,14},{10,... | collective-permute-start | bytes 602120 | tf_op jit(solution)/shard_map/ppermute | solution.py:483
  24.7 1.2 %collective-permute-done.2.refs_3_ = bf16[784,128]{1,0:T(8,128)(2,1)S(1)} collective-permute-done((bf16[784,128]{1,0:T(8,128)(2,1)S(1)}, bf16[784,128]{1,0:T(8,128)(2,1)S(1)}, u32[]{:S(2)}, u32[]{:S(2)}) %collective-permute-start.2) | collective-permute-done | bytes 200736 | tf_op jit(solution)/shard_map/ppermute | solution.py:483
  25.9 0.0 collective-permute-done.3.refs_1_
  25.9 0.0 copy-done.2
  25.9 0.0 copy-done.4
  25.9 0.0 copy-done.6
  25.9 0.0 copy-done.8
  25.9 0.0 copy-done.10
  25.9 0.0 copy-done.12
  26.0 7.0 %window_layer.4 = (bf16[8,48,768]{2,1,0:T(8,128)(2,1)S(1)}, bf16[8,48,768]{2,1,0:T(8,128)(2,1)S(1)}, bf16[8,48,768]{2,1,0:T(8,128)(2,1)S(1)}, bf16[8,48,768]{2,1...) custom-call(s32[1]{0:T(128)} %bitcast.me_ref, ...), custom_call_target="tpu_custom_call" | custom-call | flops 4051697664 | bytes 16777216 | tf_op jit(solution)/shard_map/window_layer/pallas_call | solution.py:349
  32.9 0.0 collective-permute-done.4.refs_1_
  32.9 4.5 %window_layer.5 = (bf16[8,32,768]{2,1,0:T(8,128)(2,1)S(1)}, bf16[8,32,768]{2,1,0:T(8,128)(2,1)S(1)}, bf16[8,32,768]{2,1,0:T(8,128)(2,1)S(1)}, bf16[8,32,768]{2,1...) custom-call(s32[1]{0:T(128)} %bitcast.me_ref, ...), custom_call_target="tpu_custom_call" | custom-call | flops 2315255808 | bytes 16777216 | tf_op jit(solution)/shard_map/window_layer/pallas_call | solution.py:349
  37.4 0.0 collective-permute-done.5.refs_0_
  37.4 2.6 %window_layer.6 = (bf16[8,16,768]{2,1,0:T(8,128)(2,1)S(1)}, bf16[8,16,768]{2,1,0:T(8,128)(2,1)S(1)}, bf16[8,16,768]{2,1,0:T(8,128)(2,1)S(1)}, bf16[8,16,768]{2,1...) custom-call(s32[1]{0:T(128)} %bitcast.me_ref, ...), custom_call_target="tpu_custom_call" | custom-call | flops 1157627904 | bytes 16777216 | tf_op jit(solution)/shard_map/window_layer/pallas_call | solution.py:349
  40.1 0.0 collective-permute-done.6.refs_0_
  40.1 0.0 copy-start.13
  40.1 3.4 %window_layer.7 = (bf16[8,32,768]{2,1,0:T(8,128)(2,1)S(1)}, bf16[4,32,768]{2,1,0:T(8,128)(2,1)S(1)}, bf16[4,32,768]{2,1,0:T(8,128)(2,1)S(1)}, bf16[4,32,768]{2,1,0:T(8,128)(2,1)S(1)}, bf16[8,32,128]{2,1,0:T(8,128)(2,1)S(1)}) custom-call(s32[1]{0:T(128)} %bitcast.me_ref, bf16[784,128]{1,0:T(8,128)(2,1)S(1)} %collective-permute-done.6.refs_0_, ...), custom_call_target="tpu_custom_call" | custom-call | flops 1736441856 | bytes 16777216 | tf_op jit(solution)/shard_map/window_layer/pallas_call | solution.py:349
  43.5 0.0 copy-done.13
  43.5 2.7 %row_layer.2 = (bf16[4,16,768]{2,1,0:T(8,128)(2,1)S(1)}, bf16[4,16,768]{2,1,0:T(8,128)(2,1)S(1)}, bf16[4,16,768]{2,1,0:T(8,128)(2,1)S(1)}, bf16[4,16,768]{2,1,0:...) custom-call(s32[1]{0:T(128)} %bitcast.me_ref, ...), custom_call_target="tpu_custom_call" | custom-call | bytes 65536 | tf_op jit(solution)/shard_map/row_layer/pallas_call | solution.py:434
  46.3 5.2 %collective-permute-start.7 = (bf16[4,16,768]{2,1,0:T(8,128)(2,1)S(1)}, bf16[4,16,768]{2,1,0:T(8,128)(2,1)S(1)}, u32[]{:S(2)}, u32[]{:S(2)}) collective-permute-start(bf16[4,16,768]{2,1,0:T(8,128)(2,1)S(1)} %get-tuple-element.116), channel_id=1, source_target_pairs={{0,4},{1,5},{2,6},{3,7},{4,0},{5,1},{6,2},{7,3},{8,12},{9,13},{10,... | collective-permute-start | bytes 294920 | tf_op jit(solution)/shard_map/ppermute | solution.py:483
  51.5 0.0 collective-permute-start.9
  51.5 3.4 %row_layer.3 = (bf16[4,16,768]{2,1,0:T(8,128)(2,1)S(1)}, bf16[4,16,768]{2,1,0:T(8,128)(2,1)S(1)}, bf16[4,16,768]{2,1,0:T(8,128)(2,1)S(1)}, bf16[4,16,768]{2,1,0:...) custom-call(s32[1]{0:T(128)} %bitcast.me_ref, ...), custom_call_target="tpu_custom_call" | custom-call | bytes 65536 | tf_op jit(solution)/shard_map/row_layer/pallas_call | solution.py:434
  54.9 1.6 %collective-permute-start.15 = (bf16[8,16,768]{2,1,0:T(8,128)(2,1)S(1)}, bf16[8,16,768]{2,1,0:T(8,128)(2,1)S(1)}, u32[]{:S(2)}, u32[]{:S(2)}) collective-permute-start(bf16[8,16,768]{2,1,0:T(8,128)(2,1)S(1)} %get-tuple-element.131), channel_id=1, source_target_pairs={{0,1},{1,0},{2,3},{3,2},{4,5},{5,4},{6,7},{7,6},{8,9},{9,8},{10,11... | collective-permute-start | bytes 589832 | tf_op jit(solution)/shard_map/ppermute | solution.py:483
  56.4 0.8 collective-permute-start.16
  57.3 3.5 %collective-permute-start.11 = (bf16[4,16,768]{2,1,0:T(8,128)(2,1)S(1)}, bf16[4,16,768]{2,1,0:T(8,128)(2,1)S(1)}, u32[]{:S(2)}, u32[]{:S(2)}) collective-permute-start(bf16[4,16,768]{2,1,0:T(8,128)(2,1)S(1)} %get-tuple-element.122), channel_id=1, source_target_pairs={{0,6},{1,7},{2,4},{3,5},{4,2},{5,3},{6,0},{7,1},{8,14},{9,15},{10,... | collective-permute-start | bytes 294920 | tf_op jit(solution)/shard_map/ppermute | solution.py:483
  60.7 0.0 collective-permute-done.7.refs_0_
  60.7 0.7 collective-permute-start.13
  61.4 0.0 collective-permute-done.9.refs_1_
  61.5 0.0 collective-permute-start.17
  61.5 7.2 %collective-permute-done.11.refs_2_ = bf16[4,16,768]{2,1,0:T(8,128)(2,1)S(1)} collective-permute-done((bf16[4,16,768]{2,1,0:T(8,128)(2,1)S(1)}, bf16[4,16,768]{2,1,0:T(8,128)(2,1)S(1)}, u32[]{:S(2)}, u32[]{:S(2)}) %collective-permute-start.11) | collective-permute-done | bytes 98336 | tf_op jit(solution)/shard_map/ppermute | solution.py:483
  68.7 0.0 collective-permute-start.8
  68.7 2.0 %collective-permute-done.13.refs_3_ = bf16[4,16,768]{2,1,0:T(8,128)(2,1)S(1)} collective-permute-done((bf16[4,16,768]{2,1,0:T(8,128)(2,1)S(1)}, bf16[4,16,768]{2,1,0:T(8,128)(2,1)S(1)}, u32[]{:S(2)}, u32[]{:S(2)}) %collective-permute-start.13) | collective-permute-done | bytes 98336 | tf_op jit(solution)/shard_map/ppermute | solution.py:483
  70.7 0.8 collective-permute-start.10
  71.5 0.0 collective-permute-done.15.refs_4_
  71.5 0.0 collective-permute-start.12
  71.5 0.0 collective-permute-done.16.refs_5_
  71.5 4.8 %collective-permute-start.14 = (bf16[4,16,768]{2,1,0:T(8,128)(2,1)S(1)}, bf16[4,16,768]{2,1,0:T(8,128)(2,1)S(1)}, u32[]{:S(2)}, u32[]{:S(2)}) collective-permute-start(bf16[4,16,768]{2,1,0:T(8,128)(2,1)S(1)} %get-tuple-element.126), channel_id=1, source_target_pairs={{0,7},{1,6},{2,5},{3,4},{4,3},{5,2},{6,1},{7,0},{8,15},{9,14},{10,... | collective-permute-start | bytes 294920 | tf_op jit(solution)/shard_map/ppermute | solution.py:483
  76.3 0.0 collective-permute-done.17.refs_6_
  76.3 1.1 %place.2.refs_4_ = bf16[64,16,768]{2,1,0:T(8,128)(2,1)} custom-call(s32[1]{0:T(128)} %bitcast.me_ref, bf16[4,16,768]{2,1,0:T(8,128)(2,1)S(1)} %collective-permute-done.7.refs_0_, bf16[4,16,768]{2,1,0:T(8,128)(2,1)S(1)} %collective-permute-done.9.refs_1_, bf16[4,16,768]{2,1,0:T(8,128)(2,1)S(1)} %collective-permute-done.11.refs_2_, ...), custom_call_target="tpu_custom_call" | custom-call | bytes 4194304 | tf_op jit(solution)/shard_map/place/pallas_call | solution.py:468
  77.4 5.3 %collective-permute-done.8.refs_0_ = bf16[4,16,768]{2,1,0:T(8,128)(2,1)S(1)} collective-permute-done((bf16[4,16,768]{2,1,0:T(8,128)(2,1)S(1)}, bf16[4,16,768]{2,1,0:T(8,128)(2,1)S(1)}, u32[]{:S(2)}, u32[]{:S(2)}) %collective-permute-start.8) | collective-permute-done | bytes 98336 | tf_op jit(solution)/shard_map/ppermute | solution.py:483
  82.7 2.0 %collective-permute-done.10.refs_1_ = bf16[4,16,768]{2,1,0:T(8,128)(2,1)S(1)} collective-permute-done((bf16[4,16,768]{2,1,0:T(8,128)(2,1)S(1)}, bf16[4,16,768]{2,1,0:T(8,128)(2,1)S(1)}, u32[]{:S(2)}, u32[]{:S(2)}) %collective-permute-start.10) | collective-permute-done | bytes 98336 | tf_op jit(solution)/shard_map/ppermute | solution.py:483
  84.8 0.0 collective-permute-done.12.refs_2_
  84.8 0.0 collective-permute-done.14.refs_3_
  84.8 0.8 place.3
  (12 shorter events, 0.0 us)
Async XLA Ops:
  0.0 11.2 %copy-start = (bf16[768,768]{1,0:T(8,128)(2,1)S(1)}, bf16[768,768]{1,0:T(8,128)(2,1)}, u32[]{:S(2)}) copy-start(bf16[768,768]{1,0:T(8,128)(2,1)} %refs_25_.1) | copy-start | bytes 3538948
  0.0 0.8 copy-start.14
  2.4 16.6 %collective-permute-start = (bf16[784,128]{1,0:T(8,128)(2,1)S(1)}, bf16[784,128]{1,0:T(8,128)(2,1)S(1)}, u32[]{:S(2)}, u32[]{:S(2)}) collective-permute-start(bf16[784,128]{1,0:T(8,128)(2,1)S(1)} %get-tuple-element.71), channel_id=1, source_target_pairs={{0,4},{1,5},{2,6},{3,7},{4,0},{5,1},{6,2},{7,3},{8,12},{9,13},{10,... | collective-permute-start | bytes 602120 | tf_op jit(solution)/shard_map/ppermute | solution.py:483
  6.5 16.1 %collective-permute-start.1 = (bf16[784,128]{1,0:T(8,128)(2,1)S(1)}, bf16[784,128]{1,0:T(8,128)(2,1)S(1)}, u32[]{:S(2)}, u32[]{:S(2)}) collective-permute-start(bf16[784,128]{1,0:T(8,128)(2,1)S(1)} %get-tuple-element.72), channel_id=1, source_target_pairs={{0,2},{1,3},{2,0},{3,1},{4,6},{5,7},{6,4},{7,5},{8,10},{9,11},{10,... | collective-permute-start | bytes 602120 | tf_op jit(solution)/shard_map/ppermute | solution.py:483
  8.0 17.9 %collective-permute-start.2 = (bf16[784,128]{1,0:T(8,128)(2,1)S(1)}, bf16[784,128]{1,0:T(8,128)(2,1)S(1)}, u32[]{:S(2)}, u32[]{:S(2)}) collective-permute-start(bf16[784,128]{1,0:T(8,128)(2,1)S(1)} %get-tuple-element.73), channel_id=1, source_target_pairs={{0,3},{1,2},{2,1},{3,0},{4,7},{5,6},{6,5},{7,4},{8,11},{9,10},{10,... | collective-permute-start | bytes 602120 | tf_op jit(solution)/shard_map/ppermute | solution.py:483
  9.4 16.5 %collective-permute-start.3 = (bf16[784,128]{1,0:T(8,128)(2,1)S(1)}, bf16[784,128]{1,0:T(8,128)(2,1)S(1)}, u32[]{:S(2)}, u32[]{:S(2)}) collective-permute-start(bf16[784,128]{1,0:T(8,128)(2,1)S(1)} %get-tuple-element.74), channel_id=1, source_target_pairs={{0,1},{1,0},{2,3},{3,2},{4,5},{5,4},{6,7},{7,6},{8,9},{9,8},{10,11... | collective-permute-start | bytes 602120 | tf_op jit(solution)/shard_map/ppermute | solution.py:483
  10.0 23.0 %collective-permute-start.4 = (bf16[784,128]{1,0:T(8,128)(2,1)S(1)}, bf16[784,128]{1,0:T(8,128)(2,1)S(1)}, u32[]{:S(2)}, u32[]{:S(2)}) collective-permute-start(bf16[784,128]{1,0:T(8,128)(2,1)S(1)} %get-tuple-element.84), channel_id=1, source_target_pairs={{0,5},{1,4},{2,7},{3,6},{4,1},{5,0},{6,3},{7,2},{8,13},{9,12},{10,... | collective-permute-start | bytes 602120 | tf_op jit(solution)/shard_map/ppermute | solution.py:483
  11.3 1.3 %copy-start.1 = (bf16[768,768]{1,0:T(8,128)(2,1)S(1)}, bf16[768,768]{1,0:T(8,128)(2,1)}, u32[]{:S(2)}) copy-start(bf16[768,768]{1,0:T(8,128)(2,1)} %refs_26_.1) | copy-start | bytes 3538948
  12.5 1.3 %copy-start.3 = (bf16[768,768]{1,0:T(8,128)(2,1)S(1)}, bf16[768,768]{1,0:T(8,128)(2,1)}, u32[]{:S(2)}) copy-start(bf16[768,768]{1,0:T(8,128)(2,1)} %refs_27_.1) | copy-start | bytes 3538948
  13.8 1.3 %copy-start.5 = (bf16[768,768]{1,0:T(8,128)(2,1)S(1)}, bf16[768,768]{1,0:T(8,128)(2,1)}, u32[]{:S(2)}) copy-start(bf16[768,768]{1,0:T(8,128)(2,1)} %refs_9_.7) | copy-start | bytes 3538948
  15.1 1.3 %copy-start.7 = (bf16[768,768]{1,0:T(8,128)(2,1)S(1)}, bf16[768,768]{1,0:T(8,128)(2,1)}, u32[]{:S(2)}) copy-start(bf16[768,768]{1,0:T(8,128)(2,1)} %refs_10_.7) | copy-start | bytes 3538948
  16.3 1.3 %copy-start.9 = (bf16[768,768]{1,0:T(8,128)(2,1)S(1)}, bf16[768,768]{1,0:T(8,128)(2,1)}, u32[]{:S(2)}) copy-start(bf16[768,768]{1,0:T(8,128)(2,1)} %refs_11_.7) | copy-start | bytes 3538948
  17.6 1.3 %copy-start.11 = (bf16[768,768]{1,0:T(8,128)(2,1)S(1)}, bf16[768,768]{1,0:T(8,128)(2,1)}, u32[]{:S(2)}) copy-start(bf16[768,768]{1,0:T(8,128)(2,1)} %refs_12_.5) | copy-start | bytes 3538948
  18.9 7.0 %copy-start.2 = (bf16[768,768]{1,0:T(8,128)(2,1)S(1)}, bf16[768,768]{1,0:T(8,128)(2,1)}, u32[]{:S(2)}) copy-start(bf16[768,768]{1,0:T(8,128)(2,1)} %refs_26_.1) | copy-start | bytes 3538948
  18.9 7.0 %copy-start.4 = (bf16[768,768]{1,0:T(8,128)(2,1)S(1)}, bf16[768,768]{1,0:T(8,128)(2,1)}, u32[]{:S(2)}) copy-start(bf16[768,768]{1,0:T(8,128)(2,1)} %refs_27_.1) | copy-start | bytes 3538948
  18.9 7.0 %copy-start.6 = (bf16[768,768]{1,0:T(8,128)(2,1)S(1)}, bf16[768,768]{1,0:T(8,128)(2,1)}, u32[]{:S(2)}) copy-start(bf16[768,768]{1,0:T(8,128)(2,1)} %refs_9_.7) | copy-start | bytes 3538948
  18.9 7.0 %copy-start.8 = (bf16[768,768]{1,0:T(8,128)(2,1)S(1)}, bf16[768,768]{1,0:T(8,128)(2,1)}, u32[]{:S(2)}) copy-start(bf16[768,768]{1,0:T(8,128)(2,1)} %refs_10_.7) | copy-start | bytes 3538948
  18.9 7.0 %copy-start.10 = (bf16[768,768]{1,0:T(8,128)(2,1)S(1)}, bf16[768,768]{1,0:T(8,128)(2,1)}, u32[]{:S(2)}) copy-start(bf16[768,768]{1,0:T(8,128)(2,1)} %refs_11_.7) | copy-start | bytes 3538948
  18.9 7.0 %copy-start.12 = (bf16[768,768]{1,0:T(8,128)(2,1)S(1)}, bf16[768,768]{1,0:T(8,128)(2,1)}, u32[]{:S(2)}) copy-start(bf16[768,768]{1,0:T(8,128)(2,1)} %refs_12_.5) | copy-start | bytes 3538948
  18.9 18.5 %collective-permute-start.5 = (bf16[784,128]{1,0:T(8,128)(2,1)S(1)}, bf16[784,128]{1,0:T(8,128)(2,1)S(1)}, u32[]{:S(2)}, u32[]{:S(2)}) collective-permute-start(bf16[784,128]{1,0:T(8,128)(2,1)S(1)} %get-tuple-element.93), channel_id=1, source_target_pairs={{0,6},{1,7},{2,4},{3,5},{4,2},{5,3},{6,0},{7,1},{8,14},{9,15},{10,... | collective-permute-start | bytes 602120 | tf_op jit(solution)/shard_map/ppermute | solution.py:483
  22.6 17.5 %collective-permute-start.6 = (bf16[784,128]{1,0:T(8,128)(2,1)S(1)}, bf16[784,128]{1,0:T(8,128)(2,1)S(1)}, u32[]{:S(2)}, u32[]{:S(2)}) collective-permute-start(bf16[784,128]{1,0:T(8,128)(2,1)S(1)} %get-tuple-element.102), channel_id=1, source_target_pairs={{0,7},{1,6},{2,5},{3,4},{4,3},{5,2},{6,1},{7,0},{8,15},{9,14},{10,... | collective-permute-start | bytes 602120 | tf_op jit(solution)/shard_map/ppermute | solution.py:483
  40.1 3.5 %copy-start.13 = (bf16[768,768]{1,0:T(8,128)(2,1)S(1)}, bf16[768,768]{1,0:T(8,128)(2,1)}, u32[]{:S(2)}) copy-start(bf16[768,768]{1,0:T(8,128)(2,1)} %refs_20_.3) | copy-start | bytes 3538948
  46.3 14.5 %collective-permute-start.7 = (bf16[4,16,768]{2,1,0:T(8,128)(2,1)S(1)}, bf16[4,16,768]{2,1,0:T(8,128)(2,1)S(1)}, u32[]{:S(2)}, u32[]{:S(2)}) collective-permute-start(bf16[4,16,768]{2,1,0:T(8,128)(2,1)S(1)} %get-tuple-element.116), channel_id=1, source_target_pairs={{0,4},{1,5},{2,6},{3,7},{4,0},{5,1},{6,2},{7,3},{8,12},{9,13},{10,... | collective-permute-start | bytes 294920 | tf_op jit(solution)/shard_map/ppermute | solution.py:483
  51.5 10.0 %collective-permute-start.9 = (bf16[4,16,768]{2,1,0:T(8,128)(2,1)S(1)}, bf16[4,16,768]{2,1,0:T(8,128)(2,1)S(1)}, u32[]{:S(2)}, u32[]{:S(2)}) collective-permute-start(bf16[4,16,768]{2,1,0:T(8,128)(2,1)S(1)} %get-tuple-element.119), channel_id=1, source_target_pairs={{0,5},{1,4},{2,7},{3,6},{4,1},{5,0},{6,3},{7,2},{8,13},{9,12},{10,... | collective-permute-start | bytes 294920 | tf_op jit(solution)/shard_map/ppermute | solution.py:483
  54.9 16.7 %collective-permute-start.15 = (bf16[8,16,768]{2,1,0:T(8,128)(2,1)S(1)}, bf16[8,16,768]{2,1,0:T(8,128)(2,1)S(1)}, u32[]{:S(2)}, u32[]{:S(2)}) collective-permute-start(bf16[8,16,768]{2,1,0:T(8,128)(2,1)S(1)} %get-tuple-element.131), channel_id=1, source_target_pairs={{0,1},{1,0},{2,3},{3,2},{4,5},{5,4},{6,7},{7,6},{8,9},{9,8},{10,11... | collective-permute-start | bytes 589832 | tf_op jit(solution)/shard_map/ppermute | solution.py:483
  56.4 15.1 %collective-permute-start.16 = (bf16[8,16,768]{2,1,0:T(8,128)(2,1)S(1)}, bf16[8,16,768]{2,1,0:T(8,128)(2,1)S(1)}, u32[]{:S(2)}, u32[]{:S(2)}) collective-permute-start(bf16[8,16,768]{2,1,0:T(8,128)(2,1)S(1)} %get-tuple-element.132), channel_id=1, source_target_pairs={{0,2},{1,3},{2,0},{3,1},{4,6},{5,7},{6,4},{7,5},{8,10},{9,11},{10,... | collective-permute-start | bytes 589832 | tf_op jit(solution)/shard_map/ppermute | solution.py:483
  57.3 11.4 %collective-permute-start.11 = (bf16[4,16,768]{2,1,0:T(8,128)(2,1)S(1)}, bf16[4,16,768]{2,1,0:T(8,128)(2,1)S(1)}, u32[]{:S(2)}, u32[]{:S(2)}) collective-permute-start(bf16[4,16,768]{2,1,0:T(8,128)(2,1)S(1)} %get-tuple-element.122), channel_id=1, source_target_pairs={{0,6},{1,7},{2,4},{3,5},{4,2},{5,3},{6,0},{7,1},{8,14},{9,15},{10,... | collective-permute-start | bytes 294920 | tf_op jit(solution)/shard_map/ppermute | solution.py:483
  60.7 10.0 %collective-permute-start.13 = (bf16[4,16,768]{2,1,0:T(8,128)(2,1)S(1)}, bf16[4,16,768]{2,1,0:T(8,128)(2,1)S(1)}, u32[]{:S(2)}, u32[]{:S(2)}) collective-permute-start(bf16[4,16,768]{2,1,0:T(8,128)(2,1)S(1)} %get-tuple-element.125), channel_id=1, source_target_pairs={{0,7},{1,6},{2,5},{3,4},{4,3},{5,2},{6,1},{7,0},{8,15},{9,14},{10,... | collective-permute-start | bytes 294920 | tf_op jit(solution)/shard_map/ppermute | solution.py:483
  61.5 14.9 %collective-permute-start.17 = (bf16[8,16,768]{2,1,0:T(8,128)(2,1)S(1)}, bf16[8,16,768]{2,1,0:T(8,128)(2,1)S(1)}, u32[]{:S(2)}, u32[]{:S(2)}) collective-permute-start(bf16[8,16,768]{2,1,0:T(8,128)(2,1)S(1)} %get-tuple-element.133), channel_id=1, source_target_pairs={{0,3},{1,2},{2,1},{3,0},{4,7},{5,6},{6,5},{7,4},{8,11},{9,10},{10,... | collective-permute-start | bytes 589832 | tf_op jit(solution)/shard_map/ppermute | solution.py:483
  68.7 14.1 %collective-permute-start.8 = (bf16[4,16,768]{2,1,0:T(8,128)(2,1)S(1)}, bf16[4,16,768]{2,1,0:T(8,128)(2,1)S(1)}, u32[]{:S(2)}, u32[]{:S(2)}) collective-permute-start(bf16[4,16,768]{2,1,0:T(8,128)(2,1)S(1)} %get-tuple-element.117), channel_id=1, source_target_pairs={{0,4},{1,5},{2,6},{3,7},{4,0},{5,1},{6,2},{7,3},{8,12},{9,13},{10,... | collective-permute-start | bytes 294920 | tf_op jit(solution)/shard_map/ppermute | solution.py:483
  70.7 14.1 %collective-permute-start.10 = (bf16[4,16,768]{2,1,0:T(8,128)(2,1)S(1)}, bf16[4,16,768]{2,1,0:T(8,128)(2,1)S(1)}, u32[]{:S(2)}, u32[]{:S(2)}) collective-permute-start(bf16[4,16,768]{2,1,0:T(8,128)(2,1)S(1)} %get-tuple-element.120), channel_id=1, source_target_pairs={{0,5},{1,4},{2,7},{3,6},{4,1},{5,0},{6,3},{7,2},{8,13},{9,12},{10,... | collective-permute-start | bytes 294920 | tf_op jit(solution)/shard_map/ppermute | solution.py:483
  71.5 13.2 %collective-permute-start.12 = (bf16[4,16,768]{2,1,0:T(8,128)(2,1)S(1)}, bf16[4,16,768]{2,1,0:T(8,128)(2,1)S(1)}, u32[]{:S(2)}, u32[]{:S(2)}) collective-permute-start(bf16[4,16,768]{2,1,0:T(8,128)(2,1)S(1)} %get-tuple-element.123), channel_id=1, source_target_pairs={{0,6},{1,7},{2,4},{3,5},{4,2},{5,3},{6,0},{7,1},{8,14},{9,15},{10,... | collective-permute-start | bytes 294920 | tf_op jit(solution)/shard_map/ppermute | solution.py:483
  71.5 13.2 %collective-permute-start.14 = (bf16[4,16,768]{2,1,0:T(8,128)(2,1)S(1)}, bf16[4,16,768]{2,1,0:T(8,128)(2,1)S(1)}, u32[]{:S(2)}, u32[]{:S(2)}) collective-permute-start(bf16[4,16,768]{2,1,0:T(8,128)(2,1)S(1)} %get-tuple-element.126), channel_id=1, source_target_pairs={{0,7},{1,6},{2,5},{3,4},{4,3},{5,2},{6,1},{7,0},{8,15},{9,14},{10,... | collective-permute-start | bytes 294920 | tf_op jit(solution)/shard_map/ppermute | solution.py:483

commit v11 on v10

--- a/solution.py
+++ b/solution.py
@@ -488,7 +488,7 @@
 ):
     me = lax.axis_index("lon").astype(jnp.int32).reshape(1)
     weights = (w_query1, w_key1, w_value1, w_out1, w_query2, w_key2, w_value2)
-    weights = (ready(weights), *weights)
+    weights = (ready(weights[:3]), *weights)
 
     packed = dict(zip(ORDER, pack(ORDER, me, ocean.T, fields)))
     got = {d: exchanged(packed[d], d) if d else packed[d] for d in ORDER}

time: 86.1 us -> 86.1 us (level)
  waiting for transfers between devices: 17.8 us -> 21.7 us
  starting transfers between devices: 32.1 us -> 29.6 us
  local copies, waits for them, and re-layouts: 8.45 us -> 7.17 us
    ppermute x18, waiting for transfers between devices: 17.8 us -> 21.7 us  [exchanged(): return lax.ppermute(piece, 'lon', [(s, s ^ distance) for s in range(count)])]
    ppermute x18, starting transfers between devices: 32.1 us -> 29.6 us  [exchanged(): return lax.ppermute(piece, 'lon', [(s, s ^ distance) for s in range(count)])]
    unnamed x30 -> x26, local copies, waits for them, and re-layouts: 8.45 us -> 7.17 us
  transfers between devices with their start and end apart: 18 -> 18, of which waited for: 5 -> 7; matrix products, arithmetic and copies ran while one was open for 0% -> 0% of each run, Pallas kernels for 22% -> 22%
where the time goes in v11:
time: 86.1 us; the launch traced here: 85.8 us
  starting transfers between devices  29.6 us (34%)
  Pallas kernels  27 us (31%)
  waiting for transfers between devices  21.7 us (25%)
  local copies, waits for them, and re-layouts  7.17 us (8%)
    ppermute x18, starting transfers between devices, exchanged(): return lax.ppermute(piece, 'lon', [(s, s ^ distance) for s in range(count)])  29.6 us
    ppermute x18, waiting for transfers between devices, exchanged(): return lax.ppermute(piece, 'lon', [(s, s ^ distance) for s in range(count)])  21.7 us
    pallas_call x4, Pallas kernels, window_layer(): pl.pallas_call(functools.partial(window_kernel, stage), out_shape=outs, i...  17.5 us
    unnamed x26, local copies, waits for them, and re-layouts  7.17 us
    pallas_call x2, Pallas kernels, row_layer(): pl.pallas_call(functools.partial(row_kernel, start, rows), out_shape=(far...  6.09 us
    pallas_call x2, Pallas kernels, place(): pl.pallas_call(functools.partial(place_kernel, spots), out_shape=jax.Shap...  1.84 us
  transfers between devices with their start and end apart: 18, of which 7 were waited for; matrix products, arithmetic and copies ran while one was open for 0% of the time, Pallas kernels for 22%

profile of v11, /device:TPU:0, one launch (start us, length us, event | category | flops | bytes accessed | tf_op | source)
XLA Modules:
  0.0 85.8 jit_solution(6207739114811402164)
XLA Ops:
  0.0 0.0 copy-start
  0.0 0.0 copy-start.12
  0.0 0.8 copy-done.12
  0.8 1.6 %pack.1 = (bf16[784,128]{1,0:T(8,128)(2,1)S(1)}, bf16[784,128]{1,0:T(8,128)(2,1)S(1)}, bf16[784,128]{1,0:T(8,128)(2,1)S(1)}, bf16[784,128]{1,0:T(8,128)(2,1)S(1)...) custom-call(s32[1]{0:T(128)} %bitcast.me_ref, ...), custom_call_target="tpu_custom_call" | custom-call | flops 1600000 | bytes 3200000 | tf_op jit(solution)/shard_map/pack/pallas_call | solution.py:202
  2.4 4.1 %collective-permute-start = (bf16[784,128]{1,0:T(8,128)(2,1)S(1)}, bf16[784,128]{1,0:T(8,128)(2,1)S(1)}, u32[]{:S(2)}, u32[]{:S(2)}) collective-permute-start(bf16[784,128]{1,0:T(8,128)(2,1)S(1)} %get-tuple-element.71), channel_id=1, source_target_pairs={{0,4},{1,5},{2,6},{3,7},{4,0},{5,1},{6,2},{7,3},{8,12},{9,13},{10,... | collective-permute-start | bytes 602120 | tf_op jit(solution)/shard_map/ppermute | solution.py:483
  6.5 1.6 %collective-permute-start.1 = (bf16[784,128]{1,0:T(8,128)(2,1)S(1)}, bf16[784,128]{1,0:T(8,128)(2,1)S(1)}, u32[]{:S(2)}, u32[]{:S(2)}) collective-permute-start(bf16[784,128]{1,0:T(8,128)(2,1)S(1)} %get-tuple-element.72), channel_id=1, source_target_pairs={{0,2},{1,3},{2,0},{3,1},{4,6},{5,7},{6,4},{7,5},{8,10},{9,11},{10,... | collective-permute-start | bytes 602120 | tf_op jit(solution)/shard_map/ppermute | solution.py:483
  8.0 1.4 %collective-permute-start.2 = (bf16[784,128]{1,0:T(8,128)(2,1)S(1)}, bf16[784,128]{1,0:T(8,128)(2,1)S(1)}, u32[]{:S(2)}, u32[]{:S(2)}) collective-permute-start(bf16[784,128]{1,0:T(8,128)(2,1)S(1)} %get-tuple-element.73), channel_id=1, source_target_pairs={{0,3},{1,2},{2,1},{3,0},{4,7},{5,6},{6,5},{7,4},{8,11},{9,10},{10,... | collective-permute-start | bytes 602120 | tf_op jit(solution)/shard_map/ppermute | solution.py:483
  9.4 0.5 collective-permute-start.3
  10.0 1.3 %collective-permute-start.4 = (bf16[784,128]{1,0:T(8,128)(2,1)S(1)}, bf16[784,128]{1,0:T(8,128)(2,1)S(1)}, u32[]{:S(2)}, u32[]{:S(2)}) collective-permute-start(bf16[784,128]{1,0:T(8,128)(2,1)S(1)} %get-tuple-element.84), channel_id=1, source_target_pairs={{0,5},{1,4},{2,7},{3,6},{4,1},{5,0},{6,3},{7,2},{8,13},{9,12},{10,... | collective-permute-start | bytes 602120 | tf_op jit(solution)/shard_map/ppermute | solution.py:483
  11.2 0.0 copy-done
  11.3 0.0 copy-start.1
  11.3 1.3 %copy-done.1 = bf16[768,768]{1,0:T(8,128)(2,1)S(1)} copy-done((bf16[768,768]{1,0:T(8,128)(2,1)S(1)}, bf16[768,768]{1,0:T(8,128)(2,1)}, u32[]{:S(2)}) %copy-start.1) | copy-done | bytes 1179672
  12.5 1.3 %copy-done.3 = bf16[768,768]{1,0:T(8,128)(2,1)S(1)} copy-done((bf16[768,768]{1,0:T(8,128)(2,1)S(1)}, bf16[768,768]{1,0:T(8,128)(2,1)}, u32[]{:S(2)}) %copy-start.3) | copy-done | bytes 1179672
  13.8 2.9 %collective-permute-done.refs_0_ = bf16[784,128]{1,0:T(8,128)(2,1)S(1)} collective-permute-done((bf16[784,128]{1,0:T(8,128)(2,1)S(1)}, bf16[784,128]{1,0:T(8,128)(2,1)S(1)}, u32[]{:S(2)}, u32[]{:S(2)}) %collective-permute-start) | collective-permute-done | bytes 200736 | tf_op jit(solution)/shard_map/ppermute | solution.py:483
  16.7 2.8 %collective-permute-start.5 = (bf16[784,128]{1,0:T(8,128)(2,1)S(1)}, bf16[784,128]{1,0:T(8,128)(2,1)S(1)}, u32[]{:S(2)}, u32[]{:S(2)}) collective-permute-start(bf16[784,128]{1,0:T(8,128)(2,1)S(1)} %get-tuple-element.93), channel_id=1, source_target_pairs={{0,6},{1,7},{2,4},{3,5},{4,2},{5,3},{6,0},{7,1},{8,14},{9,15},{10,... | collective-permute-start | bytes 602120 | tf_op jit(solution)/shard_map/ppermute | solution.py:483
  19.5 2.3 %collective-permute-done.1.refs_2_ = bf16[784,128]{1,0:T(8,128)(2,1)S(1)} collective-permute-done((bf16[784,128]{1,0:T(8,128)(2,1)S(1)}, bf16[784,128]{1,0:T(8,128)(2,1)S(1)}, u32[]{:S(2)}, u32[]{:S(2)}) %collective-permute-start.1) | collective-permute-done | bytes 200736 | tf_op jit(solution)/shard_map/ppermute | solution.py:483
  21.8 2.9 %collective-permute-start.6 = (bf16[784,128]{1,0:T(8,128)(2,1)S(1)}, bf16[784,128]{1,0:T(8,128)(2,1)S(1)}, u32[]{:S(2)}, u32[]{:S(2)}) collective-permute-start(bf16[784,128]{1,0:T(8,128)(2,1)S(1)} %get-tuple-element.102), channel_id=1, source_target_pairs={{0,7},{1,6},{2,5},{3,4},{4,3},{5,2},{6,1},{7,0},{8,15},{9,14},{10,... | collective-permute-start | bytes 602120 | tf_op jit(solution)/shard_map/ppermute | solution.py:483
  24.7 1.2 %collective-permute-done.2.refs_3_ = bf16[784,128]{1,0:T(8,128)(2,1)S(1)} collective-permute-done((bf16[784,128]{1,0:T(8,128)(2,1)S(1)}, bf16[784,128]{1,0:T(8,128)(2,1)S(1)}, u32[]{:S(2)}, u32[]{:S(2)}) %collective-permute-start.2) | collective-permute-done | bytes 200736 | tf_op jit(solution)/shard_map/ppermute | solution.py:483
  25.9 0.0 collective-permute-done.3.refs_1_
  25.9 0.0 copy-done.2
  25.9 0.0 copy-done.4
  25.9 0.0 copy-done.5
  25.9 0.0 copy-start.6
  25.9 1.3 %copy-done.6 = bf16[768,768]{1,0:T(8,128)(2,1)S(1)} copy-done((bf16[768,768]{1,0:T(8,128)(2,1)S(1)}, bf16[768,768]{1,0:T(8,128)(2,1)}, u32[]{:S(2)}) %copy-start.6) | copy-done | bytes 1179672
  27.2 1.3 %copy-done.8 = bf16[768,768]{1,0:T(8,128)(2,1)S(1)} copy-done((bf16[768,768]{1,0:T(8,128)(2,1)S(1)}, bf16[768,768]{1,0:T(8,128)(2,1)}, u32[]{:S(2)}) %copy-start.8) | copy-done | bytes 1179672
  28.5 1.3 %copy-done.10 = bf16[768,768]{1,0:T(8,128)(2,1)S(1)} copy-done((bf16[768,768]{1,0:T(8,128)(2,1)S(1)}, bf16[768,768]{1,0:T(8,128)(2,1)}, u32[]{:S(2)}) %copy-start.10) | copy-done | bytes 1179672
  29.7 6.9 %window_layer.4 = (bf16[8,48,768]{2,1,0:T(8,128)(2,1)S(1)}, bf16[8,48,768]{2,1,0:T(8,128)(2,1)S(1)}, bf16[8,48,768]{2,1,0:T(8,128)(2,1)S(1)}, bf16[8,48,768]{2,1...) custom-call(s32[1]{0:T(128)} %bitcast.me_ref, ...), custom_call_target="tpu_custom_call" | custom-call | flops 4051697664 | bytes 16777216 | tf_op jit(solution)/shard_map/window_layer/pallas_call | solution.py:349
  36.7 0.0 collective-permute-done.4.refs_1_
  36.7 0.0 copy-done.9
  36.7 4.5 %window_layer.5 = (bf16[8,32,768]{2,1,0:T(8,128)(2,1)S(1)}, bf16[8,32,768]{2,1,0:T(8,128)(2,1)S(1)}, bf16[8,32,768]{2,1,0:T(8,128)(2,1)S(1)}, bf16[8,32,768]{2,1...) custom-call(s32[1]{0:T(128)} %bitcast.me_ref, ...), custom_call_target="tpu_custom_call" | custom-call | flops 2315255808 | bytes 16777216 | tf_op jit(solution)/shard_map/window_layer/pallas_call | solution.py:349
  41.2 0.0 collective-permute-done.5.refs_0_
  41.2 2.6 %window_layer.6 = (bf16[8,16,768]{2,1,0:T(8,128)(2,1)S(1)}, bf16[8,16,768]{2,1,0:T(8,128)(2,1)S(1)}, bf16[8,16,768]{2,1,0:T(8,128)(2,1)S(1)}, bf16[8,16,768]{2,1...) custom-call(s32[1]{0:T(128)} %bitcast.me_ref, ...), custom_call_target="tpu_custom_call" | custom-call | flops 1157627904 | bytes 16777216 | tf_op jit(solution)/shard_map/window_layer/pallas_call | solution.py:349
  43.8 0.0 collective-permute-done.6.refs_0_
  43.8 0.0 copy-start.11
  43.8 3.4 %window_layer.7 = (bf16[8,32,768]{2,1,0:T(8,128)(2,1)S(1)}, bf16[4,32,768]{2,1,0:T(8,128)(2,1)S(1)}, bf16[4,32,768]{2,1,0:T(8,128)(2,1)S(1)}, bf16[4,32,768]{2,1,0:T(8,128)(2,1)S(1)}, bf16[8,32,128]{2,1,0:T(8,128)(2,1)S(1)}) custom-call(s32[1]{0:T(128)} %bitcast.me_ref, bf16[784,128]{1,0:T(8,128)(2,1)S(1)} %collective-permute-done.6.refs_0_, ...), custom_call_target="tpu_custom_call" | custom-call | flops 1736441856 | bytes 16777216 | tf_op jit(solution)/shard_map/window_layer/pallas_call | solution.py:349
  47.3 0.0 copy-done.11
  47.3 0.0 copy-start.7
  47.3 2.7 %row_layer.2 = (bf16[4,16,768]{2,1,0:T(8,128)(2,1)S(1)}, bf16[4,16,768]{2,1,0:T(8,128)(2,1)S(1)}, bf16[4,16,768]{2,1,0:T(8,128)(2,1)S(1)}, bf16[4,16,768]{2,1,0:...) custom-call(s32[1]{0:T(128)} %bitcast.me_ref, ...), custom_call_target="tpu_custom_call" | custom-call | bytes 65536 | tf_op jit(solution)/shard_map/row_layer/pallas_call | solution.py:434
  50.0 1.4 %collective-permute-start.7 = (bf16[4,16,768]{2,1,0:T(8,128)(2,1)S(1)}, bf16[4,16,768]{2,1,0:T(8,128)(2,1)S(1)}, u32[]{:S(2)}, u32[]{:S(2)}) collective-permute-start(bf16[4,16,768]{2,1,0:T(8,128)(2,1)S(1)} %get-tuple-element.116), channel_id=1, source_target_pairs={{0,4},{1,5},{2,6},{3,7},{4,0},{5,1},{6,2},{7,3},{8,12},{9,13},{10,... | collective-permute-start | bytes 294920 | tf_op jit(solution)/shard_map/ppermute | solution.py:483
  51.5 1.4 %collective-permute-start.9 = (bf16[4,16,768]{2,1,0:T(8,128)(2,1)S(1)}, bf16[4,16,768]{2,1,0:T(8,128)(2,1)S(1)}, u32[]{:S(2)}, u32[]{:S(2)}) collective-permute-start(bf16[4,16,768]{2,1,0:T(8,128)(2,1)S(1)} %get-tuple-element.119), channel_id=1, source_target_pairs={{0,5},{1,4},{2,7},{3,6},{4,1},{5,0},{6,3},{7,2},{8,13},{9,12},{10,... | collective-permute-start | bytes 294920 | tf_op jit(solution)/shard_map/ppermute | solution.py:483
  52.9 0.0 copy-done.7
  52.9 3.4 %row_layer.3 = (bf16[4,16,768]{2,1,0:T(8,128)(2,1)S(1)}, bf16[4,16,768]{2,1,0:T(8,128)(2,1)S(1)}, bf16[4,16,768]{2,1,0:T(8,128)(2,1)S(1)}, bf16[4,16,768]{2,1,0:...) custom-call(s32[1]{0:T(128)} %bitcast.me_ref, ...), custom_call_target="tpu_custom_call" | custom-call | bytes 65536 | tf_op jit(solution)/shard_map/row_layer/pallas_call | solution.py:434
  56.2 1.7 %collective-permute-start.15 = (bf16[8,16,768]{2,1,0:T(8,128)(2,1)S(1)}, bf16[8,16,768]{2,1,0:T(8,128)(2,1)S(1)}, u32[]{:S(2)}, u32[]{:S(2)}) collective-permute-start(bf16[8,16,768]{2,1,0:T(8,128)(2,1)S(1)} %get-tuple-element.131), channel_id=1, source_target_pairs={{0,1},{1,0},{2,3},{3,2},{4,5},{5,4},{6,7},{7,6},{8,9},{9,8},{10,11... | collective-permute-start | bytes 589832 | tf_op jit(solution)/shard_map/ppermute | solution.py:483
  57.9 0.3 collective-permute-start.16
  58.2 2.6 %collective-permute-start.11 = (bf16[4,16,768]{2,1,0:T(8,128)(2,1)S(1)}, bf16[4,16,768]{2,1,0:T(8,128)(2,1)S(1)}, u32[]{:S(2)}, u32[]{:S(2)}) collective-permute-start(bf16[4,16,768]{2,1,0:T(8,128)(2,1)S(1)} %get-tuple-element.122), channel_id=1, source_target_pairs={{0,6},{1,7},{2,4},{3,5},{4,2},{5,3},{6,0},{7,1},{8,14},{9,15},{10,... | collective-permute-start | bytes 294920 | tf_op jit(solution)/shard_map/ppermute | solution.py:483
  60.8 0.0 collective-permute-done.7.refs_0_
  60.8 1.2 %collective-permute-start.13 = (bf16[4,16,768]{2,1,0:T(8,128)(2,1)S(1)}, bf16[4,16,768]{2,1,0:T(8,128)(2,1)S(1)}, u32[]{:S(2)}, u32[]{:S(2)}) collective-permute-start(bf16[4,16,768]{2,1,0:T(8,128)(2,1)S(1)} %get-tuple-element.125), channel_id=1, source_target_pairs={{0,7},{1,6},{2,5},{3,4},{4,3},{5,2},{6,1},{7,0},{8,15},{9,14},{10,... | collective-permute-start | bytes 294920 | tf_op jit(solution)/shard_map/ppermute | solution.py:483
  62.0 0.0 collective-permute-done.9.refs_1_
  62.0 0.9 %collective-permute-start.17 = (bf16[8,16,768]{2,1,0:T(8,128)(2,1)S(1)}, bf16[8,16,768]{2,1,0:T(8,128)(2,1)S(1)}, u32[]{:S(2)}, u32[]{:S(2)}) collective-permute-start(bf16[8,16,768]{2,1,0:T(8,128)(2,1)S(1)} %get-tuple-element.133), channel_id=1, source_target_pairs={{0,3},{1,2},{2,1},{3,0},{4,7},{5,6},{6,5},{7,4},{8,11},{9,10},{10,... | collective-permute-start | bytes 589832 | tf_op jit(solution)/shard_map/ppermute | solution.py:483
  62.9 5.8 %collective-permute-done.11.refs_2_ = bf16[4,16,768]{2,1,0:T(8,128)(2,1)S(1)} collective-permute-done((bf16[4,16,768]{2,1,0:T(8,128)(2,1)S(1)}, bf16[4,16,768]{2,1,0:T(8,128)(2,1)S(1)}, u32[]{:S(2)}, u32[]{:S(2)}) %collective-permute-start.11) | collective-permute-done | bytes 98336 | tf_op jit(solution)/shard_map/ppermute | solution.py:483
  68.7 0.0 collective-permute-start.8
  68.7 2.0 %collective-permute-done.13.refs_3_ = bf16[4,16,768]{2,1,0:T(8,128)(2,1)S(1)} collective-permute-done((bf16[4,16,768]{2,1,0:T(8,128)(2,1)S(1)}, bf16[4,16,768]{2,1,0:T(8,128)(2,1)S(1)}, u32[]{:S(2)}, u32[]{:S(2)}) %collective-permute-start.13) | collective-permute-done | bytes 98336 | tf_op jit(solution)/shard_map/ppermute | solution.py:483
  70.7 1.6 %collective-permute-start.10 = (bf16[4,16,768]{2,1,0:T(8,128)(2,1)S(1)}, bf16[4,16,768]{2,1,0:T(8,128)(2,1)S(1)}, u32[]{:S(2)}, u32[]{:S(2)}) collective-permute-start(bf16[4,16,768]{2,1,0:T(8,128)(2,1)S(1)} %get-tuple-element.120), channel_id=1, source_target_pairs={{0,5},{1,4},{2,7},{3,6},{4,1},{5,0},{6,3},{7,2},{8,13},{9,12},{10,... | collective-permute-start | bytes 294920 | tf_op jit(solution)/shard_map/ppermute | solution.py:483
  72.4 0.0 collective-permute-done.15.refs_4_
  72.4 0.0 collective-permute-start.12
  72.4 0.0 collective-permute-done.16.refs_5_
  72.4 4.0 %collective-permute-start.14 = (bf16[4,16,768]{2,1,0:T(8,128)(2,1)S(1)}, bf16[4,16,768]{2,1,0:T(8,128)(2,1)S(1)}, u32[]{:S(2)}, u32[]{:S(2)}) collective-permute-start(bf16[4,16,768]{2,1,0:T(8,128)(2,1)S(1)} %get-tuple-element.126), channel_id=1, source_target_pairs={{0,7},{1,6},{2,5},{3,4},{4,3},{5,2},{6,1},{7,0},{8,15},{9,14},{10,... | collective-permute-start | bytes 294920 | tf_op jit(solution)/shard_map/ppermute | solution.py:483
  76.3 0.0 collective-permute-done.17.refs_6_
  76.4 1.1 %place.2.refs_4_ = bf16[64,16,768]{2,1,0:T(8,128)(2,1)} custom-call(s32[1]{0:T(128)} %bitcast.me_ref, bf16[4,16,768]{2,1,0:T(8,128)(2,1)S(1)} %collective-permute-done.7.refs_0_, bf16[4,16,768]{2,1,0:T(8,128)(2,1)S(1)} %collective-permute-done.9.refs_1_, bf16[4,16,768]{2,1,0:T(8,128)(2,1)S(1)} %collective-permute-done.11.refs_2_, ...), custom_call_target="tpu_custom_call" | custom-call | bytes 4194304 | tf_op jit(solution)/shard_map/place/pallas_call | solution.py:468
  77.4 5.4 %collective-permute-done.8.refs_0_ = bf16[4,16,768]{2,1,0:T(8,128)(2,1)S(1)} collective-permute-done((bf16[4,16,768]{2,1,0:T(8,128)(2,1)S(1)}, bf16[4,16,768]{2,1,0:T(8,128)(2,1)S(1)}, u32[]{:S(2)}, u32[]{:S(2)}) %collective-permute-start.8) | collective-permute-done | bytes 98336 | tf_op jit(solution)/shard_map/ppermute | solution.py:483
  82.8 2.0 %collective-permute-done.10.refs_1_ = bf16[4,16,768]{2,1,0:T(8,128)(2,1)S(1)} collective-permute-done((bf16[4,16,768]{2,1,0:T(8,128)(2,1)S(1)}, bf16[4,16,768]{2,1,0:T(8,128)(2,1)S(1)}, u32[]{:S(2)}, u32[]{:S(2)}) %collective-permute-start.10) | collective-permute-done | bytes 98336 | tf_op jit(solution)/shard_map/ppermute | solution.py:483
  84.9 0.0 collective-permute-done.12.refs_2_
  84.9 0.0 collective-permute-done.14.refs_3_
  84.9 0.8 place.3
  (8 shorter events, 0.0 us)
Async XLA Ops:
  0.0 11.2 %copy-start = (bf16[768,768]{1,0:T(8,128)(2,1)S(1)}, bf16[768,768]{1,0:T(8,128)(2,1)}, u32[]{:S(2)}) copy-start(bf16[768,768]{1,0:T(8,128)(2,1)} %refs_9_.7) | copy-start | bytes 3538948
  0.0 0.8 copy-start.12
  2.4 14.3 %collective-permute-start = (bf16[784,128]{1,0:T(8,128)(2,1)S(1)}, bf16[784,128]{1,0:T(8,128)(2,1)S(1)}, u32[]{:S(2)}, u32[]{:S(2)}) collective-permute-start(bf16[784,128]{1,0:T(8,128)(2,1)S(1)} %get-tuple-element.71), channel_id=1, source_target_pairs={{0,4},{1,5},{2,6},{3,7},{4,0},{5,1},{6,2},{7,3},{8,12},{9,13},{10,... | collective-permute-start | bytes 602120 | tf_op jit(solution)/shard_map/ppermute | solution.py:483
  6.5 15.4 %collective-permute-start.1 = (bf16[784,128]{1,0:T(8,128)(2,1)S(1)}, bf16[784,128]{1,0:T(8,128)(2,1)S(1)}, u32[]{:S(2)}, u32[]{:S(2)}) collective-permute-start(bf16[784,128]{1,0:T(8,128)(2,1)S(1)} %get-tuple-element.72), channel_id=1, source_target_pairs={{0,2},{1,3},{2,0},{3,1},{4,6},{5,7},{6,4},{7,5},{8,10},{9,11},{10,... | collective-permute-start | bytes 602120 | tf_op jit(solution)/shard_map/ppermute | solution.py:483
  8.0 17.8 %collective-permute-start.2 = (bf16[784,128]{1,0:T(8,128)(2,1)S(1)}, bf16[784,128]{1,0:T(8,128)(2,1)S(1)}, u32[]{:S(2)}, u32[]{:S(2)}) collective-permute-start(bf16[784,128]{1,0:T(8,128)(2,1)S(1)} %get-tuple-element.73), channel_id=1, source_target_pairs={{0,3},{1,2},{2,1},{3,0},{4,7},{5,6},{6,5},{7,4},{8,11},{9,10},{10,... | collective-permute-start | bytes 602120 | tf_op jit(solution)/shard_map/ppermute | solution.py:483
  9.4 16.4 %collective-permute-start.3 = (bf16[784,128]{1,0:T(8,128)(2,1)S(1)}, bf16[784,128]{1,0:T(8,128)(2,1)S(1)}, u32[]{:S(2)}, u32[]{:S(2)}) collective-permute-start(bf16[784,128]{1,0:T(8,128)(2,1)S(1)} %get-tuple-element.74), channel_id=1, source_target_pairs={{0,1},{1,0},{2,3},{3,2},{4,5},{5,4},{6,7},{7,6},{8,9},{9,8},{10,11... | collective-permute-start | bytes 602120 | tf_op jit(solution)/shard_map/ppermute | solution.py:483
  10.0 26.7 %collective-permute-start.4 = (bf16[784,128]{1,0:T(8,128)(2,1)S(1)}, bf16[784,128]{1,0:T(8,128)(2,1)S(1)}, u32[]{:S(2)}, u32[]{:S(2)}) collective-permute-start(bf16[784,128]{1,0:T(8,128)(2,1)S(1)} %get-tuple-element.84), channel_id=1, source_target_pairs={{0,5},{1,4},{2,7},{3,6},{4,1},{5,0},{6,3},{7,2},{8,13},{9,12},{10,... | collective-permute-start | bytes 602120 | tf_op jit(solution)/shard_map/ppermute | solution.py:483
  11.3 1.3 %copy-start.1 = (bf16[768,768]{1,0:T(8,128)(2,1)S(1)}, bf16[768,768]{1,0:T(8,128)(2,1)}, u32[]{:S(2)}) copy-start(bf16[768,768]{1,0:T(8,128)(2,1)} %refs_10_.7) | copy-start | bytes 3538948
  12.5 1.3 %copy-start.3 = (bf16[768,768]{1,0:T(8,128)(2,1)S(1)}, bf16[768,768]{1,0:T(8,128)(2,1)}, u32[]{:S(2)}) copy-start(bf16[768,768]{1,0:T(8,128)(2,1)} %refs_11_.7) | copy-start | bytes 3538948
  13.8 12.1 %copy-start.2 = (bf16[768,768]{1,0:T(8,128)(2,1)S(1)}, bf16[768,768]{1,0:T(8,128)(2,1)}, u32[]{:S(2)}) copy-start(bf16[768,768]{1,0:T(8,128)(2,1)} %refs_10_.7) | copy-start | bytes 3538948
  13.8 12.1 %copy-start.4 = (bf16[768,768]{1,0:T(8,128)(2,1)S(1)}, bf16[768,768]{1,0:T(8,128)(2,1)}, u32[]{:S(2)}) copy-start(bf16[768,768]{1,0:T(8,128)(2,1)} %refs_11_.7) | copy-start | bytes 3538948
  13.8 12.1 %copy-start.5 = (bf16[768,768]{1,0:T(8,128)(2,1)S(1)}, bf16[768,768]{1,0:T(8,128)(2,1)}, u32[]{:S(2)}) copy-start(bf16[768,768]{1,0:T(8,128)(2,1)} %refs_25_.1) | copy-start | bytes 3538948
  16.7 24.5 %collective-permute-start.5 = (bf16[784,128]{1,0:T(8,128)(2,1)S(1)}, bf16[784,128]{1,0:T(8,128)(2,1)S(1)}, u32[]{:S(2)}, u32[]{:S(2)}) collective-permute-start(bf16[784,128]{1,0:T(8,128)(2,1)S(1)} %get-tuple-element.93), channel_id=1, source_target_pairs={{0,6},{1,7},{2,4},{3,5},{4,2},{5,3},{6,0},{7,1},{8,14},{9,15},{10,... | collective-permute-start | bytes 602120 | tf_op jit(solution)/shard_map/ppermute | solution.py:483
  21.8 22.0 %collective-permute-start.6 = (bf16[784,128]{1,0:T(8,128)(2,1)S(1)}, bf16[784,128]{1,0:T(8,128)(2,1)S(1)}, u32[]{:S(2)}, u32[]{:S(2)}) collective-permute-start(bf16[784,128]{1,0:T(8,128)(2,1)S(1)} %get-tuple-element.102), channel_id=1, source_target_pairs={{0,7},{1,6},{2,5},{3,4},{4,3},{5,2},{6,1},{7,0},{8,15},{9,14},{10,... | collective-permute-start | bytes 602120 | tf_op jit(solution)/shard_map/ppermute | solution.py:483
  25.9 1.3 %copy-start.6 = (bf16[768,768]{1,0:T(8,128)(2,1)S(1)}, bf16[768,768]{1,0:T(8,128)(2,1)}, u32[]{:S(2)}) copy-start(bf16[768,768]{1,0:T(8,128)(2,1)} %refs_26_.1) | copy-start | bytes 3538948
  27.2 1.3 %copy-start.8 = (bf16[768,768]{1,0:T(8,128)(2,1)S(1)}, bf16[768,768]{1,0:T(8,128)(2,1)}, u32[]{:S(2)}) copy-start(bf16[768,768]{1,0:T(8,128)(2,1)} %refs_27_.1) | copy-start | bytes 3538948
  28.5 1.3 %copy-start.10 = (bf16[768,768]{1,0:T(8,128)(2,1)S(1)}, bf16[768,768]{1,0:T(8,128)(2,1)}, u32[]{:S(2)}) copy-start(bf16[768,768]{1,0:T(8,128)(2,1)} %refs_12_.5) | copy-start | bytes 3538948
  29.7 7.0 %copy-start.9 = (bf16[768,768]{1,0:T(8,128)(2,1)S(1)}, bf16[768,768]{1,0:T(8,128)(2,1)}, u32[]{:S(2)}) copy-start(bf16[768,768]{1,0:T(8,128)(2,1)} %refs_27_.1) | copy-start | bytes 3538948
  43.8 3.5 %copy-start.11 = (bf16[768,768]{1,0:T(8,128)(2,1)S(1)}, bf16[768,768]{1,0:T(8,128)(2,1)}, u32[]{:S(2)}) copy-start(bf16[768,768]{1,0:T(8,128)(2,1)} %refs_20_.3) | copy-start | bytes 3538948
  47.3 5.6 %copy-start.7 = (bf16[768,768]{1,0:T(8,128)(2,1)S(1)}, bf16[768,768]{1,0:T(8,128)(2,1)}, u32[]{:S(2)}) copy-start(bf16[768,768]{1,0:T(8,128)(2,1)} %refs_26_.1) | copy-start | bytes 3538948
  50.0 10.7 %collective-permute-start.7 = (bf16[4,16,768]{2,1,0:T(8,128)(2,1)S(1)}, bf16[4,16,768]{2,1,0:T(8,128)(2,1)S(1)}, u32[]{:S(2)}, u32[]{:S(2)}) collective-permute-start(bf16[4,16,768]{2,1,0:T(8,128)(2,1)S(1)} %get-tuple-element.116), channel_id=1, source_target_pairs={{0,4},{1,5},{2,6},{3,7},{4,0},{5,1},{6,2},{7,3},{8,12},{9,13},{10,... | collective-permute-start | bytes 294920 | tf_op jit(solution)/shard_map/ppermute | solution.py:483
  51.5 10.5 %collective-permute-start.9 = (bf16[4,16,768]{2,1,0:T(8,128)(2,1)S(1)}, bf16[4,16,768]{2,1,0:T(8,128)(2,1)S(1)}, u32[]{:S(2)}, u32[]{:S(2)}) collective-permute-start(bf16[4,16,768]{2,1,0:T(8,128)(2,1)S(1)} %get-tuple-element.119), channel_id=1, source_target_pairs={{0,5},{1,4},{2,7},{3,6},{4,1},{5,0},{6,3},{7,2},{8,13},{9,12},{10,... | collective-permute-start | bytes 294920 | tf_op jit(solution)/shard_map/ppermute | solution.py:483
  56.2 16.1 %collective-permute-start.15 = (bf16[8,16,768]{2,1,0:T(8,128)(2,1)S(1)}, bf16[8,16,768]{2,1,0:T(8,128)(2,1)S(1)}, u32[]{:S(2)}, u32[]{:S(2)}) collective-permute-start(bf16[8,16,768]{2,1,0:T(8,128)(2,1)S(1)} %get-tuple-element.131), channel_id=1, source_target_pairs={{0,1},{1,0},{2,3},{3,2},{4,5},{5,4},{6,7},{7,6},{8,9},{9,8},{10,11... | collective-permute-start | bytes 589832 | tf_op jit(solution)/shard_map/ppermute | solution.py:483
  57.9 14.5 %collective-permute-start.16 = (bf16[8,16,768]{2,1,0:T(8,128)(2,1)S(1)}, bf16[8,16,768]{2,1,0:T(8,128)(2,1)S(1)}, u32[]{:S(2)}, u32[]{:S(2)}) collective-permute-start(bf16[8,16,768]{2,1,0:T(8,128)(2,1)S(1)} %get-tuple-element.132), channel_id=1, source_target_pairs={{0,2},{1,3},{2,0},{3,1},{4,6},{5,7},{6,4},{7,5},{8,10},{9,11},{10,... | collective-permute-start | bytes 589832 | tf_op jit(solution)/shard_map/ppermute | solution.py:483
  58.2 10.5 %collective-permute-start.11 = (bf16[4,16,768]{2,1,0:T(8,128)(2,1)S(1)}, bf16[4,16,768]{2,1,0:T(8,128)(2,1)S(1)}, u32[]{:S(2)}, u32[]{:S(2)}) collective-permute-start(bf16[4,16,768]{2,1,0:T(8,128)(2,1)S(1)} %get-tuple-element.122), channel_id=1, source_target_pairs={{0,6},{1,7},{2,4},{3,5},{4,2},{5,3},{6,0},{7,1},{8,14},{9,15},{10,... | collective-permute-start | bytes 294920 | tf_op jit(solution)/shard_map/ppermute | solution.py:483
  60.8 10.0 %collective-permute-start.13 = (bf16[4,16,768]{2,1,0:T(8,128)(2,1)S(1)}, bf16[4,16,768]{2,1,0:T(8,128)(2,1)S(1)}, u32[]{:S(2)}, u32[]{:S(2)}) collective-permute-start(bf16[4,16,768]{2,1,0:T(8,128)(2,1)S(1)} %get-tuple-element.125), channel_id=1, source_target_pairs={{0,7},{1,6},{2,5},{3,4},{4,3},{5,2},{6,1},{7,0},{8,15},{9,14},{10,... | collective-permute-start | bytes 294920 | tf_op jit(solution)/shard_map/ppermute | solution.py:483
  62.0 14.3 %collective-permute-start.17 = (bf16[8,16,768]{2,1,0:T(8,128)(2,1)S(1)}, bf16[8,16,768]{2,1,0:T(8,128)(2,1)S(1)}, u32[]{:S(2)}, u32[]{:S(2)}) collective-permute-start(bf16[8,16,768]{2,1,0:T(8,128)(2,1)S(1)} %get-tuple-element.133), channel_id=1, source_target_pairs={{0,3},{1,2},{2,1},{3,0},{4,7},{5,6},{6,5},{7,4},{8,11},{9,10},{10,... | collective-permute-start | bytes 589832 | tf_op jit(solution)/shard_map/ppermute | solution.py:483
  68.7 14.1 %collective-permute-start.8 = (bf16[4,16,768]{2,1,0:T(8,128)(2,1)S(1)}, bf16[4,16,768]{2,1,0:T(8,128)(2,1)S(1)}, u32[]{:S(2)}, u32[]{:S(2)}) collective-permute-start(bf16[4,16,768]{2,1,0:T(8,128)(2,1)S(1)} %get-tuple-element.117), channel_id=1, source_target_pairs={{0,4},{1,5},{2,6},{3,7},{4,0},{5,1},{6,2},{7,3},{8,12},{9,13},{10,... | collective-permute-start | bytes 294920 | tf_op jit(solution)/shard_map/ppermute | solution.py:483
  70.7 14.1 %collective-permute-start.10 = (bf16[4,16,768]{2,1,0:T(8,128)(2,1)S(1)}, bf16[4,16,768]{2,1,0:T(8,128)(2,1)S(1)}, u32[]{:S(2)}, u32[]{:S(2)}) collective-permute-start(bf16[4,16,768]{2,1,0:T(8,128)(2,1)S(1)} %get-tuple-element.120), channel_id=1, source_target_pairs={{0,5},{1,4},{2,7},{3,6},{4,1},{5,0},{6,3},{7,2},{8,13},{9,12},{10,... | collective-permute-start | bytes 294920 | tf_op jit(solution)/shard_map/ppermute | solution.py:483
  72.4 12.5 %collective-permute-start.12 = (bf16[4,16,768]{2,1,0:T(8,128)(2,1)S(1)}, bf16[4,16,768]{2,1,0:T(8,128)(2,1)S(1)}, u32[]{:S(2)}, u32[]{:S(2)}) collective-permute-start(bf16[4,16,768]{2,1,0:T(8,128)(2,1)S(1)} %get-tuple-element.123), channel_id=1, source_target_pairs={{0,6},{1,7},{2,4},{3,5},{4,2},{5,3},{6,0},{7,1},{8,14},{9,15},{10,... | collective-permute-start | bytes 294920 | tf_op jit(solution)/shard_map/ppermute | solution.py:483
  72.4 12.5 %collective-permute-start.14 = (bf16[4,16,768]{2,1,0:T(8,128)(2,1)S(1)}, bf16[4,16,768]{2,1,0:T(8,128)(2,1)S(1)}, u32[]{:S(2)}, u32[]{:S(2)}) collective-permute-start(bf16[4,16,768]{2,1,0:T(8,128)(2,1)S(1)} %get-tuple-element.126), channel_id=1, source_target_pairs={{0,7},{1,6},{2,5},{3,4},{4,3},{5,2},{6,1},{7,0},{8,15},{9,14},{10,... | collective-permute-start | bytes 294920 | tf_op jit(solution)/shard_map/ppermute | solution.py:483

commit v12 on v11

--- a/solution.py
+++ b/solution.py
@@ -13,7 +13,7 @@
 EPS = 1e-05
 NEG = -1e30
 
-PACK_VMEM = 52 * 1024 * 1024
+PACK_VMEM = (54 * 1024 * 1024, 52 * 1024 * 1024)
 
 PAIRS = [slice(128 * p, 128 * p + 128) for p in range(HEADS // 2)]
 
@@ -209,7 +209,7 @@
             pltpu.VMEM(marks.shape, marks.dtype),
             pltpu.SemaphoreType.DMA((n + 1,)),
         ],
-        compiler_params=pltpu.CompilerParams(vmem_limit_bytes=PACK_VMEM),
+        compiler_params=pltpu.CompilerParams(vmem_limit_bytes=PACK_VMEM[n > 1]),
         cost_estimate=pl.CostEstimate(flops=n * 200000, bytes_accessed=n * 400000, transcendentals=0),
         name="pack",
     )(me, marks, fields)
@@ -490,7 +490,8 @@
     weights = (w_query1, w_key1, w_value1, w_out1, w_query2, w_key2, w_value2)
     weights = (ready(weights[:3]), *weights)
 
-    packed = dict(zip(ORDER, pack(ORDER, me, ocean.T, fields)))
+    packed = {ORDER[0]: pack(ORDER[:1], me, ocean.T, fields)[0]}
+    packed.update(zip(ORDER[1:], pack(ORDER[1:], me, ocean.T, fields)))
     got = {d: exchanged(packed[d], d) if d else packed[d] for d in ORDER}
     got[4], *near = lax.optimization_barrier((got[4], got[2], got[3], got[1]))
     got[2], got[3], got[1] = near

time: 86.1 us -> 92.2 us (1.071)
  starting transfers between devices: 29.6 us -> 33.9 us
  waiting for transfers between devices: 21.7 us -> 25.4 us
  local copies, waits for them, and re-layouts: 7.17 us -> 3.85 us
  Pallas kernels: 27 us -> 28.4 us
    ppermute x18, starting transfers between devices: 29.6 us -> 33.9 us  [exchanged(): return lax.ppermute(piece, 'lon', [(s, s ^ distance) for s in range(count)])]
    ppermute x18, waiting for transfers between devices: 21.7 us -> 25.4 us  [exchanged(): return lax.ppermute(piece, 'lon', [(s, s ^ distance) for s in range(count)])]
    unnamed x26 -> x24, local copies, waits for them, and re-layouts: 7.17 us -> 3.85 us
    pallas_call x1 -> x2, Pallas kernels: 1.56 us -> 3.25 us  [pack(): pl.pallas_call(functools.partial(pack_kernel, distances), out_shape=(piec...]
where the time goes in v12:
time: 92.2 us; the launch traced here: 91.9 us
  starting transfers between devices  33.9 us (37%)
  Pallas kernels  28.4 us (31%)
  waiting for transfers between devices  25.4 us (28%)
  local copies, waits for them, and re-layouts  3.85 us (4%)
    ppermute x18, starting transfers between devices, exchanged(): return lax.ppermute(piece, 'lon', [(s, s ^ distance) for s in range(count)])  33.9 us
    ppermute x18, waiting for transfers between devices, exchanged(): return lax.ppermute(piece, 'lon', [(s, s ^ distance) for s in range(count)])  25.4 us
    pallas_call x4, Pallas kernels, window_layer(): pl.pallas_call(functools.partial(window_kernel, stage), out_shape=outs, i...  17.3 us
    pallas_call x2, Pallas kernels, row_layer(): pl.pallas_call(functools.partial(row_kernel, start, rows), out_shape=(far...  6.01 us
    unnamed x24, local copies, waits for them, and re-layouts  3.85 us
    pallas_call x2, Pallas kernels, pack(): pl.pallas_call(functools.partial(pack_kernel, distances), out_shape=(piec...  3.25 us
  transfers between devices with their start and end apart: 18, of which 7 were waited for; matrix products, arithmetic and copies ran while one was open for 0% of the time, Pallas kernels for 22%

profile of v12, /device:TPU:0, one launch (start us, length us, event | category | flops | bytes accessed | tf_op | source)
XLA Modules:
  0.0 91.9 jit_solution(16848602234353825182)
XLA Ops:
  0.0 0.0 copy-start.11
  0.0 0.0 copy-start.1
  0.0 1.8 %pack.3 = bf16[784,128]{1,0:T(8,128)(2,1)} custom-call(s32[1]{0:T(128)} %bitcast.me_ref, s32[16,64]{1,0:T(8,128)} %bitcast.2, bf16[64,16,768]{2,1,0:T(8,128)(2,1)} %fields_ref.3), custom_call_target="tpu_custom_call" | custom-call | flops 200000 | bytes 400000 | tf_op jit(solution)/shard_map/pack/pallas_call | solution.py:202
  1.8 0.0 copy-start
  1.8 4.1 %collective-permute-start = (bf16[784,128]{1,0:T(8,128)(2,1)}, bf16[784,128]{1,0:T(8,128)(2,1)S(1)}, u32[]{:S(2)}, u32[]{:S(2)}) collective-permute-start(bf16[784,128]{1,0:T(8,128)(2,1)} %pack.3), channel_id=1, source_target_pairs={{0,4},{1,5},{2,6},{3,7},{4,0},{5,1},{6,2},{7,3},{8,12},{9,13},{10,... | collective-permute-start | bytes 602120 | tf_op jit(solution)/shard_map/ppermute | solution.py:483
  5.9 0.0 copy-done.11
  5.9 1.5 %pack.2 = (bf16[784,128]{1,0:T(8,128)(2,1)S(1)}, bf16[784,128]{1,0:T(8,128)(2,1)S(1)}, bf16[784,128]{1,0:T(8,128)(2,1)S(1)}, bf16[784,128]{1,0:T(8,128)(2,1)S(1)...) custom-call(s32[1]{0:T(128)} %bitcast.me_ref, s32[16,64]{1,0:T(8,128)S(1)} %bitcast.3, ...), custom_call_target="tpu_custom_call" | custom-call | flops 1400000 | bytes 2800000 | tf_op jit(solution)/shard_map/pack/pallas_call | solution.py:202
  7.4 1.6 %collective-permute-start.1 = (bf16[784,128]{1,0:T(8,128)(2,1)S(1)}, bf16[784,128]{1,0:T(8,128)(2,1)S(1)}, u32[]{:S(2)}, u32[]{:S(2)}) collective-permute-start(bf16[784,128]{1,0:T(8,128)(2,1)S(1)} %get-tuple-element.70), channel_id=1, source_target_pairs={{0,2},{1,3},{2,0},{3,1},{4,6},{5,7},{6,4},{7,5},{8,10},{9,11},{10,... | collective-permute-start | bytes 602120 | tf_op jit(solution)/shard_map/ppermute | solution.py:483
  9.0 1.4 %collective-permute-start.2 = (bf16[784,128]{1,0:T(8,128)(2,1)S(1)}, bf16[784,128]{1,0:T(8,128)(2,1)S(1)}, u32[]{:S(2)}, u32[]{:S(2)}) collective-permute-start(bf16[784,128]{1,0:T(8,128)(2,1)S(1)} %get-tuple-element.71), channel_id=1, source_target_pairs={{0,3},{1,2},{2,1},{3,0},{4,7},{5,6},{6,5},{7,4},{8,11},{9,10},{10,... | collective-permute-start | bytes 602120 | tf_op jit(solution)/shard_map/ppermute | solution.py:483
  10.4 0.5 collective-permute-start.3
  10.9 1.3 %collective-permute-start.4 = (bf16[784,128]{1,0:T(8,128)(2,1)S(1)}, bf16[784,128]{1,0:T(8,128)(2,1)S(1)}, u32[]{:S(2)}, u32[]{:S(2)}) collective-permute-start(bf16[784,128]{1,0:T(8,128)(2,1)S(1)} %get-tuple-element.82), channel_id=1, source_target_pairs={{0,5},{1,4},{2,7},{3,6},{4,1},{5,0},{6,3},{7,2},{8,13},{9,12},{10,... | collective-permute-start | bytes 602120 | tf_op jit(solution)/shard_map/ppermute | solution.py:483
  12.2 0.0 copy-done.1
  12.2 0.0 copy-done
  12.2 1.3 %copy-done.2 = bf16[768,768]{1,0:T(8,128)(2,1)S(1)} copy-done((bf16[768,768]{1,0:T(8,128)(2,1)S(1)}, bf16[768,768]{1,0:T(8,128)(2,1)}, u32[]{:S(2)}) %copy-start.2) | copy-done | bytes 1179672
  13.5 2.8 %collective-permute-done.refs_0_ = bf16[784,128]{1,0:T(8,128)(2,1)S(1)} collective-permute-done((bf16[784,128]{1,0:T(8,128)(2,1)}, bf16[784,128]{1,0:T(8,128)(2,1)S(1)}, u32[]{:S(2)}, u32[]{:S(2)}) %collective-permute-start) | collective-permute-done | bytes 200736 | tf_op jit(solution)/shard_map/ppermute | solution.py:483
  16.3 2.8 %collective-permute-start.5 = (bf16[784,128]{1,0:T(8,128)(2,1)S(1)}, bf16[784,128]{1,0:T(8,128)(2,1)S(1)}, u32[]{:S(2)}, u32[]{:S(2)}) collective-permute-start(bf16[784,128]{1,0:T(8,128)(2,1)S(1)} %get-tuple-element.91), channel_id=1, source_target_pairs={{0,6},{1,7},{2,4},{3,5},{4,2},{5,3},{6,0},{7,1},{8,14},{9,15},{10,... | collective-permute-start | bytes 602120 | tf_op jit(solution)/shard_map/ppermute | solution.py:483
  19.1 3.7 %collective-permute-done.1.refs_2_ = bf16[784,128]{1,0:T(8,128)(2,1)S(1)} collective-permute-done((bf16[784,128]{1,0:T(8,128)(2,1)S(1)}, bf16[784,128]{1,0:T(8,128)(2,1)S(1)}, u32[]{:S(2)}, u32[]{:S(2)}) %collective-permute-start.1) | collective-permute-done | bytes 200736 | tf_op jit(solution)/shard_map/ppermute | solution.py:483
  22.8 3.4 %collective-permute-start.6 = (bf16[784,128]{1,0:T(8,128)(2,1)S(1)}, bf16[784,128]{1,0:T(8,128)(2,1)S(1)}, u32[]{:S(2)}, u32[]{:S(2)}) collective-permute-start(bf16[784,128]{1,0:T(8,128)(2,1)S(1)} %get-tuple-element.100), channel_id=1, source_target_pairs={{0,7},{1,6},{2,5},{3,4},{4,3},{5,2},{6,1},{7,0},{8,15},{9,14},{10,... | collective-permute-start | bytes 602120 | tf_op jit(solution)/shard_map/ppermute | solution.py:483
  26.2 9.1 %collective-permute-done.2.refs_3_ = bf16[784,128]{1,0:T(8,128)(2,1)S(1)} collective-permute-done((bf16[784,128]{1,0:T(8,128)(2,1)S(1)}, bf16[784,128]{1,0:T(8,128)(2,1)S(1)}, u32[]{:S(2)}, u32[]{:S(2)}) %collective-permute-start.2) | collective-permute-done | bytes 200736 | tf_op jit(solution)/shard_map/ppermute | solution.py:483
  35.3 0.0 collective-permute-done.3.refs_1_
  35.3 0.0 copy-done.3
  35.3 0.0 copy-done.4
  35.3 0.0 copy-done.5
  35.3 0.0 copy-start.6
  35.3 1.3 %copy-done.6 = bf16[768,768]{1,0:T(8,128)(2,1)S(1)} copy-done((bf16[768,768]{1,0:T(8,128)(2,1)S(1)}, bf16[768,768]{1,0:T(8,128)(2,1)}, u32[]{:S(2)}) %copy-start.6) | copy-done | bytes 1179672
  36.5 1.3 %copy-done.8 = bf16[768,768]{1,0:T(8,128)(2,1)S(1)} copy-done((bf16[768,768]{1,0:T(8,128)(2,1)S(1)}, bf16[768,768]{1,0:T(8,128)(2,1)}, u32[]{:S(2)}) %copy-start.8) | copy-done | bytes 1179672
  37.8 6.9 %window_layer.4 = (bf16[8,48,768]{2,1,0:T(8,128)(2,1)S(1)}, bf16[8,48,768]{2,1,0:T(8,128)(2,1)S(1)}, bf16[8,48,768]{2,1,0:T(8,128)(2,1)S(1)}, bf16[8,48,768]{2,1...) custom-call(s32[1]{0:T(128)} %bitcast.me_ref, ...), custom_call_target="tpu_custom_call" | custom-call | flops 4051697664 | bytes 16777216 | tf_op jit(solution)/shard_map/window_layer/pallas_call | solution.py:349
  44.7 0.0 collective-permute-done.4.refs_1_
  44.7 0.0 copy-done.9
  44.7 4.4 %window_layer.5 = (bf16[8,32,768]{2,1,0:T(8,128)(2,1)S(1)}, bf16[8,32,768]{2,1,0:T(8,128)(2,1)S(1)}, bf16[8,32,768]{2,1,0:T(8,128)(2,1)S(1)}, bf16[8,32,768]{2,1...) custom-call(s32[1]{0:T(128)} %bitcast.me_ref, ...), custom_call_target="tpu_custom_call" | custom-call | flops 2315255808 | bytes 16777216 | tf_op jit(solution)/shard_map/window_layer/pallas_call | solution.py:349
  49.1 0.0 collective-permute-done.5.refs_0_
  49.2 2.6 %window_layer.6 = (bf16[8,16,768]{2,1,0:T(8,128)(2,1)S(1)}, bf16[8,16,768]{2,1,0:T(8,128)(2,1)S(1)}, bf16[8,16,768]{2,1,0:T(8,128)(2,1)S(1)}, bf16[8,16,768]{2,1...) custom-call(s32[1]{0:T(128)} %bitcast.me_ref, ...), custom_call_target="tpu_custom_call" | custom-call | flops 1157627904 | bytes 16777216 | tf_op jit(solution)/shard_map/window_layer/pallas_call | solution.py:349
  51.8 0.0 collective-permute-done.6.refs_0_
  51.8 0.0 copy-start.10
  51.8 3.4 %window_layer.7 = (bf16[8,32,768]{2,1,0:T(8,128)(2,1)S(1)}, bf16[4,32,768]{2,1,0:T(8,128)(2,1)S(1)}, bf16[4,32,768]{2,1,0:T(8,128)(2,1)S(1)}, bf16[4,32,768]{2,1,0:T(8,128)(2,1)S(1)}, bf16[8,32,128]{2,1,0:T(8,128)(2,1)S(1)}) custom-call(s32[1]{0:T(128)} %bitcast.me_ref, bf16[784,128]{1,0:T(8,128)(2,1)S(1)} %collective-permute-done.6.refs_0_, ...), custom_call_target="tpu_custom_call" | custom-call | flops 1736441856 | bytes 16777216 | tf_op jit(solution)/shard_map/window_layer/pallas_call | solution.py:349
  55.2 0.0 copy-done.10
  55.2 0.0 copy-start.7
  55.2 2.7 %row_layer.2 = (bf16[4,16,768]{2,1,0:T(8,128)(2,1)S(1)}, bf16[4,16,768]{2,1,0:T(8,128)(2,1)S(1)}, bf16[4,16,768]{2,1,0:T(8,128)(2,1)S(1)}, bf16[4,16,768]{2,1,0:...) custom-call(s32[1]{0:T(128)} %bitcast.me_ref, ...), custom_call_target="tpu_custom_call" | custom-call | bytes 65536 | tf_op jit(solution)/shard_map/row_layer/pallas_call | solution.py:434
  57.9 0.1 collective-permute-start.7
  58.0 2.8 %collective-permute-start.9 = (bf16[4,16,768]{2,1,0:T(8,128)(2,1)S(1)}, bf16[4,16,768]{2,1,0:T(8,128)(2,1)S(1)}, u32[]{:S(2)}, u32[]{:S(2)}) collective-permute-start(bf16[4,16,768]{2,1,0:T(8,128)(2,1)S(1)} %get-tuple-element.117), channel_id=1, source_target_pairs={{0,5},{1,4},{2,7},{3,6},{4,1},{5,0},{6,3},{7,2},{8,13},{9,12},{10,... | collective-permute-start | bytes 294920 | tf_op jit(solution)/shard_map/ppermute | solution.py:483
  60.8 0.0 copy-done.7
  60.8 3.3 %row_layer.3 = (bf16[4,16,768]{2,1,0:T(8,128)(2,1)S(1)}, bf16[4,16,768]{2,1,0:T(8,128)(2,1)S(1)}, bf16[4,16,768]{2,1,0:T(8,128)(2,1)S(1)}, bf16[4,16,768]{2,1,0:...) custom-call(s32[1]{0:T(128)} %bitcast.me_ref, ...), custom_call_target="tpu_custom_call" | custom-call | bytes 65536 | tf_op jit(solution)/shard_map/row_layer/pallas_call | solution.py:434
  64.2 1.6 %collective-permute-start.15 = (bf16[8,16,768]{2,1,0:T(8,128)(2,1)S(1)}, bf16[8,16,768]{2,1,0:T(8,128)(2,1)S(1)}, u32[]{:S(2)}, u32[]{:S(2)}) collective-permute-start(bf16[8,16,768]{2,1,0:T(8,128)(2,1)S(1)} %get-tuple-element.129), channel_id=1, source_target_pairs={{0,1},{1,0},{2,3},{3,2},{4,5},{5,4},{6,7},{7,6},{8,9},{9,8},{10,11... | collective-permute-start | bytes 589832 | tf_op jit(solution)/shard_map/ppermute | solution.py:483
  65.8 0.2 collective-permute-start.16
  66.0 2.3 %collective-permute-start.11 = (bf16[4,16,768]{2,1,0:T(8,128)(2,1)S(1)}, bf16[4,16,768]{2,1,0:T(8,128)(2,1)S(1)}, u32[]{:S(2)}, u32[]{:S(2)}) collective-permute-start(bf16[4,16,768]{2,1,0:T(8,128)(2,1)S(1)} %get-tuple-element.120), channel_id=1, source_target_pairs={{0,6},{1,7},{2,4},{3,5},{4,2},{5,3},{6,0},{7,1},{8,14},{9,15},{10,... | collective-permute-start | bytes 294920 | tf_op jit(solution)/shard_map/ppermute | solution.py:483
  68.3 0.0 collective-permute-done.7.refs_0_
  68.3 1.5 %collective-permute-start.13 = (bf16[4,16,768]{2,1,0:T(8,128)(2,1)S(1)}, bf16[4,16,768]{2,1,0:T(8,128)(2,1)S(1)}, u32[]{:S(2)}, u32[]{:S(2)}) collective-permute-start(bf16[4,16,768]{2,1,0:T(8,128)(2,1)S(1)} %get-tuple-element.123), channel_id=1, source_target_pairs={{0,7},{1,6},{2,5},{3,4},{4,3},{5,2},{6,1},{7,0},{8,15},{9,14},{10,... | collective-permute-start | bytes 294920 | tf_op jit(solution)/shard_map/ppermute | solution.py:483
  69.7 1.5 %collective-permute-done.9.refs_1_ = bf16[4,16,768]{2,1,0:T(8,128)(2,1)S(1)} collective-permute-done((bf16[4,16,768]{2,1,0:T(8,128)(2,1)S(1)}, bf16[4,16,768]{2,1,0:T(8,128)(2,1)S(1)}, u32[]{:S(2)}, u32[]{:S(2)}) %collective-permute-start.9) | collective-permute-done | bytes 98336 | tf_op jit(solution)/shard_map/ppermute | solution.py:483
  71.2 0.0 collective-permute-start.17
  71.2 4.5 %collective-permute-done.11.refs_2_ = bf16[4,16,768]{2,1,0:T(8,128)(2,1)S(1)} collective-permute-done((bf16[4,16,768]{2,1,0:T(8,128)(2,1)S(1)}, bf16[4,16,768]{2,1,0:T(8,128)(2,1)S(1)}, u32[]{:S(2)}, u32[]{:S(2)}) %collective-permute-start.11) | collective-permute-done | bytes 98336 | tf_op jit(solution)/shard_map/ppermute | solution.py:483
  75.7 3.6 %collective-permute-start.8 = (bf16[4,16,768]{2,1,0:T(8,128)(2,1)S(1)}, bf16[4,16,768]{2,1,0:T(8,128)(2,1)S(1)}, u32[]{:S(2)}, u32[]{:S(2)}) collective-permute-start(bf16[4,16,768]{2,1,0:T(8,128)(2,1)S(1)} %get-tuple-element.115), channel_id=1, source_target_pairs={{0,4},{1,5},{2,6},{3,7},{4,0},{5,1},{6,2},{7,3},{8,12},{9,13},{10,... | collective-permute-start | bytes 294920 | tf_op jit(solution)/shard_map/ppermute | solution.py:483
  79.3 0.0 collective-permute-done.13.refs_3_
  79.3 3.1 %collective-permute-start.10 = (bf16[4,16,768]{2,1,0:T(8,128)(2,1)S(1)}, bf16[4,16,768]{2,1,0:T(8,128)(2,1)S(1)}, u32[]{:S(2)}, u32[]{:S(2)}) collective-permute-start(bf16[4,16,768]{2,1,0:T(8,128)(2,1)S(1)} %get-tuple-element.118), channel_id=1, source_target_pairs={{0,5},{1,4},{2,7},{3,6},{4,1},{5,0},{6,3},{7,2},{8,13},{9,12},{10,... | collective-permute-start | bytes 294920 | tf_op jit(solution)/shard_map/ppermute | solution.py:483
  82.4 0.0 collective-permute-done.15.refs_4_
  82.4 1.1 %collective-permute-start.12 = (bf16[4,16,768]{2,1,0:T(8,128)(2,1)S(1)}, bf16[4,16,768]{2,1,0:T(8,128)(2,1)S(1)}, u32[]{:S(2)}, u32[]{:S(2)}) collective-permute-start(bf16[4,16,768]{2,1,0:T(8,128)(2,1)S(1)} %get-tuple-element.121), channel_id=1, source_target_pairs={{0,6},{1,7},{2,4},{3,5},{4,2},{5,3},{6,0},{7,1},{8,14},{9,15},{10,... | collective-permute-start | bytes 294920 | tf_op jit(solution)/shard_map/ppermute | solution.py:483
  83.6 0.0 collective-permute-done.16.refs_5_
  83.6 2.5 %collective-permute-start.14 = (bf16[4,16,768]{2,1,0:T(8,128)(2,1)S(1)}, bf16[4,16,768]{2,1,0:T(8,128)(2,1)S(1)}, u32[]{:S(2)}, u32[]{:S(2)}) collective-permute-start(bf16[4,16,768]{2,1,0:T(8,128)(2,1)S(1)} %get-tuple-element.124), channel_id=1, source_target_pairs={{0,7},{1,6},{2,5},{3,4},{4,3},{5,2},{6,1},{7,0},{8,15},{9,14},{10,... | collective-permute-start | bytes 294920 | tf_op jit(solution)/shard_map/ppermute | solution.py:483
  86.0 0.0 collective-permute-done.17.refs_6_
  86.0 1.1 %place.2.refs_4_ = bf16[64,16,768]{2,1,0:T(8,128)(2,1)} custom-call(s32[1]{0:T(128)} %bitcast.me_ref, bf16[4,16,768]{2,1,0:T(8,128)(2,1)S(1)} %collective-permute-done.7.refs_0_, bf16[4,16,768]{2,1,0:T(8,128)(2,1)S(1)} %collective-permute-done.9.refs_1_, bf16[4,16,768]{2,1,0:T(8,128)(2,1)S(1)} %collective-permute-done.11.refs_2_, ...), custom_call_target="tpu_custom_call" | custom-call | bytes 4194304 | tf_op jit(solution)/shard_map/place/pallas_call | solution.py:468
  87.1 0.0 collective-permute-done.8.refs_0_
  87.1 0.0 collective-permute-done.10.refs_1_
  87.1 1.8 %collective-permute-done.12.refs_2_ = bf16[4,16,768]{2,1,0:T(8,128)(2,1)S(1)} collective-permute-done((bf16[4,16,768]{2,1,0:T(8,128)(2,1)S(1)}, bf16[4,16,768]{2,1,0:T(8,128)(2,1)S(1)}, u32[]{:S(2)}, u32[]{:S(2)}) %collective-permute-start.12) | collective-permute-done | bytes 98336 | tf_op jit(solution)/shard_map/ppermute | solution.py:483
  88.9 2.1 %collective-permute-done.14.refs_3_ = bf16[4,16,768]{2,1,0:T(8,128)(2,1)S(1)} collective-permute-done((bf16[4,16,768]{2,1,0:T(8,128)(2,1)S(1)}, bf16[4,16,768]{2,1,0:T(8,128)(2,1)S(1)}, u32[]{:S(2)}, u32[]{:S(2)}) %collective-permute-start.14) | collective-permute-done | bytes 98336 | tf_op jit(solution)/shard_map/ppermute | solution.py:483
  91.0 0.8 place.3
  (7 shorter events, 0.0 us)
Async XLA Ops:
  0.0 5.9 %copy-start.11 = (s32[64,16]{0,1:T(8,128)S(1)}, s32[64,16]{0,1:T(8,128)}, u32[]{:S(2)}) copy-start(s32[64,16]{0,1:T(8,128)} %param.11) | copy-start | bytes 12292
  0.0 12.2 %copy-start.1 = (bf16[768,768]{1,0:T(8,128)(2,1)S(1)}, bf16[768,768]{1,0:T(8,128)(2,1)}, u32[]{:S(2)}) copy-start(bf16[768,768]{1,0:T(8,128)(2,1)} %refs_10_.7) | copy-start | bytes 3538948
  1.8 10.5 %copy-start = (bf16[768,768]{1,0:T(8,128)(2,1)S(1)}, bf16[768,768]{1,0:T(8,128)(2,1)}, u32[]{:S(2)}) copy-start(bf16[768,768]{1,0:T(8,128)(2,1)} %refs_9_.7) | copy-start | bytes 3538948
  1.8 14.5 %collective-permute-start = (bf16[784,128]{1,0:T(8,128)(2,1)}, bf16[784,128]{1,0:T(8,128)(2,1)S(1)}, u32[]{:S(2)}, u32[]{:S(2)}) collective-permute-start(bf16[784,128]{1,0:T(8,128)(2,1)} %pack.3), channel_id=1, source_target_pairs={{0,4},{1,5},{2,6},{3,7},{4,0},{5,1},{6,2},{7,3},{8,12},{9,13},{10,... | collective-permute-start | bytes 602120 | tf_op jit(solution)/shard_map/ppermute | solution.py:483
  7.4 15.4 %collective-permute-start.1 = (bf16[784,128]{1,0:T(8,128)(2,1)S(1)}, bf16[784,128]{1,0:T(8,128)(2,1)S(1)}, u32[]{:S(2)}, u32[]{:S(2)}) collective-permute-start(bf16[784,128]{1,0:T(8,128)(2,1)S(1)} %get-tuple-element.70), channel_id=1, source_target_pairs={{0,2},{1,3},{2,0},{3,1},{4,6},{5,7},{6,4},{7,5},{8,10},{9,11},{10,... | collective-permute-start | bytes 602120 | tf_op jit(solution)/shard_map/ppermute | solution.py:483
  9.0 26.2 %collective-permute-start.2 = (bf16[784,128]{1,0:T(8,128)(2,1)S(1)}, bf16[784,128]{1,0:T(8,128)(2,1)S(1)}, u32[]{:S(2)}, u32[]{:S(2)}) collective-permute-start(bf16[784,128]{1,0:T(8,128)(2,1)S(1)} %get-tuple-element.71), channel_id=1, source_target_pairs={{0,3},{1,2},{2,1},{3,0},{4,7},{5,6},{6,5},{7,4},{8,11},{9,10},{10,... | collective-permute-start | bytes 602120 | tf_op jit(solution)/shard_map/ppermute | solution.py:483
  10.4 24.8 %collective-permute-start.3 = (bf16[784,128]{1,0:T(8,128)(2,1)S(1)}, bf16[784,128]{1,0:T(8,128)(2,1)S(1)}, u32[]{:S(2)}, u32[]{:S(2)}) collective-permute-start(bf16[784,128]{1,0:T(8,128)(2,1)S(1)} %get-tuple-element.72), channel_id=1, source_target_pairs={{0,1},{1,0},{2,3},{3,2},{4,5},{5,4},{6,7},{7,6},{8,9},{9,8},{10,11... | collective-permute-start | bytes 602120 | tf_op jit(solution)/shard_map/ppermute | solution.py:483
  10.9 33.8 %collective-permute-start.4 = (bf16[784,128]{1,0:T(8,128)(2,1)S(1)}, bf16[784,128]{1,0:T(8,128)(2,1)S(1)}, u32[]{:S(2)}, u32[]{:S(2)}) collective-permute-start(bf16[784,128]{1,0:T(8,128)(2,1)S(1)} %get-tuple-element.82), channel_id=1, source_target_pairs={{0,5},{1,4},{2,7},{3,6},{4,1},{5,0},{6,3},{7,2},{8,13},{9,12},{10,... | collective-permute-start | bytes 602120 | tf_op jit(solution)/shard_map/ppermute | solution.py:483
  12.2 1.3 %copy-start.2 = (bf16[768,768]{1,0:T(8,128)(2,1)S(1)}, bf16[768,768]{1,0:T(8,128)(2,1)}, u32[]{:S(2)}) copy-start(bf16[768,768]{1,0:T(8,128)(2,1)} %refs_11_.7) | copy-start | bytes 3538948
  13.5 21.7 %copy-start.3 = (bf16[768,768]{1,0:T(8,128)(2,1)S(1)}, bf16[768,768]{1,0:T(8,128)(2,1)}, u32[]{:S(2)}) copy-start(bf16[768,768]{1,0:T(8,128)(2,1)} %refs_11_.7) | copy-start | bytes 3538948
  13.5 21.7 %copy-start.4 = (bf16[768,768]{1,0:T(8,128)(2,1)S(1)}, bf16[768,768]{1,0:T(8,128)(2,1)}, u32[]{:S(2)}) copy-start(bf16[768,768]{1,0:T(8,128)(2,1)} %refs_25_.1) | copy-start | bytes 3538948
  13.5 21.7 %copy-start.5 = (bf16[768,768]{1,0:T(8,128)(2,1)S(1)}, bf16[768,768]{1,0:T(8,128)(2,1)}, u32[]{:S(2)}) copy-start(bf16[768,768]{1,0:T(8,128)(2,1)} %refs_26_.1) | copy-start | bytes 3538948
  16.3 32.8 %collective-permute-start.5 = (bf16[784,128]{1,0:T(8,128)(2,1)S(1)}, bf16[784,128]{1,0:T(8,128)(2,1)S(1)}, u32[]{:S(2)}, u32[]{:S(2)}) collective-permute-start(bf16[784,128]{1,0:T(8,128)(2,1)S(1)} %get-tuple-element.91), channel_id=1, source_target_pairs={{0,6},{1,7},{2,4},{3,5},{4,2},{5,3},{6,0},{7,1},{8,14},{9,15},{10,... | collective-permute-start | bytes 602120 | tf_op jit(solution)/shard_map/ppermute | solution.py:483
  22.8 29.0 %collective-permute-start.6 = (bf16[784,128]{1,0:T(8,128)(2,1)S(1)}, bf16[784,128]{1,0:T(8,128)(2,1)S(1)}, u32[]{:S(2)}, u32[]{:S(2)}) collective-permute-start(bf16[784,128]{1,0:T(8,128)(2,1)S(1)} %get-tuple-element.100), channel_id=1, source_target_pairs={{0,7},{1,6},{2,5},{3,4},{4,3},{5,2},{6,1},{7,0},{8,15},{9,14},{10,... | collective-permute-start | bytes 602120 | tf_op jit(solution)/shard_map/ppermute | solution.py:483
  35.3 1.3 %copy-start.6 = (bf16[768,768]{1,0:T(8,128)(2,1)S(1)}, bf16[768,768]{1,0:T(8,128)(2,1)}, u32[]{:S(2)}) copy-start(bf16[768,768]{1,0:T(8,128)(2,1)} %refs_27_.1) | copy-start | bytes 3538948
  36.5 1.3 %copy-start.8 = (bf16[768,768]{1,0:T(8,128)(2,1)S(1)}, bf16[768,768]{1,0:T(8,128)(2,1)}, u32[]{:S(2)}) copy-start(bf16[768,768]{1,0:T(8,128)(2,1)} %refs_12_.5) | copy-start | bytes 3538948
  37.8 6.9 %copy-start.9 = (bf16[768,768]{1,0:T(8,128)(2,1)S(1)}, bf16[768,768]{1,0:T(8,128)(2,1)}, u32[]{:S(2)}) copy-start(bf16[768,768]{1,0:T(8,128)(2,1)} %refs_12_.5) | copy-start | bytes 3538948
  51.8 3.4 %copy-start.10 = (bf16[768,768]{1,0:T(8,128)(2,1)S(1)}, bf16[768,768]{1,0:T(8,128)(2,1)}, u32[]{:S(2)}) copy-start(bf16[768,768]{1,0:T(8,128)(2,1)} %refs_20_.3) | copy-start | bytes 3538948
  55.2 5.6 %copy-start.7 = (bf16[768,768]{1,0:T(8,128)(2,1)S(1)}, bf16[768,768]{1,0:T(8,128)(2,1)}, u32[]{:S(2)}) copy-start(bf16[768,768]{1,0:T(8,128)(2,1)} %refs_27_.1) | copy-start | bytes 3538948
  57.9 10.3 %collective-permute-start.7 = (bf16[4,16,768]{2,1,0:T(8,128)(2,1)S(1)}, bf16[4,16,768]{2,1,0:T(8,128)(2,1)S(1)}, u32[]{:S(2)}, u32[]{:S(2)}) collective-permute-start(bf16[4,16,768]{2,1,0:T(8,128)(2,1)S(1)} %get-tuple-element.114), channel_id=1, source_target_pairs={{0,4},{1,5},{2,6},{3,7},{4,0},{5,1},{6,2},{7,3},{8,12},{9,13},{10,... | collective-permute-start | bytes 294920 | tf_op jit(solution)/shard_map/ppermute | solution.py:483
  58.0 13.2 %collective-permute-start.9 = (bf16[4,16,768]{2,1,0:T(8,128)(2,1)S(1)}, bf16[4,16,768]{2,1,0:T(8,128)(2,1)S(1)}, u32[]{:S(2)}, u32[]{:S(2)}) collective-permute-start(bf16[4,16,768]{2,1,0:T(8,128)(2,1)S(1)} %get-tuple-element.117), channel_id=1, source_target_pairs={{0,5},{1,4},{2,7},{3,6},{4,1},{5,0},{6,3},{7,2},{8,13},{9,12},{10,... | collective-permute-start | bytes 294920 | tf_op jit(solution)/shard_map/ppermute | solution.py:483
  64.2 18.3 %collective-permute-start.15 = (bf16[8,16,768]{2,1,0:T(8,128)(2,1)S(1)}, bf16[8,16,768]{2,1,0:T(8,128)(2,1)S(1)}, u32[]{:S(2)}, u32[]{:S(2)}) collective-permute-start(bf16[8,16,768]{2,1,0:T(8,128)(2,1)S(1)} %get-tuple-element.129), channel_id=1, source_target_pairs={{0,1},{1,0},{2,3},{3,2},{4,5},{5,4},{6,7},{7,6},{8,9},{9,8},{10,11... | collective-permute-start | bytes 589832 | tf_op jit(solution)/shard_map/ppermute | solution.py:483
  65.8 17.8 %collective-permute-start.16 = (bf16[8,16,768]{2,1,0:T(8,128)(2,1)S(1)}, bf16[8,16,768]{2,1,0:T(8,128)(2,1)S(1)}, u32[]{:S(2)}, u32[]{:S(2)}) collective-permute-start(bf16[8,16,768]{2,1,0:T(8,128)(2,1)S(1)} %get-tuple-element.130), channel_id=1, source_target_pairs={{0,2},{1,3},{2,0},{3,1},{4,6},{5,7},{6,4},{7,5},{8,10},{9,11},{10,... | collective-permute-start | bytes 589832 | tf_op jit(solution)/shard_map/ppermute | solution.py:483
  66.0 9.7 %collective-permute-start.11 = (bf16[4,16,768]{2,1,0:T(8,128)(2,1)S(1)}, bf16[4,16,768]{2,1,0:T(8,128)(2,1)S(1)}, u32[]{:S(2)}, u32[]{:S(2)}) collective-permute-start(bf16[4,16,768]{2,1,0:T(8,128)(2,1)S(1)} %get-tuple-element.120), channel_id=1, source_target_pairs={{0,6},{1,7},{2,4},{3,5},{4,2},{5,3},{6,0},{7,1},{8,14},{9,15},{10,... | collective-permute-start | bytes 294920 | tf_op jit(solution)/shard_map/ppermute | solution.py:483
  68.3 11.1 %collective-permute-start.13 = (bf16[4,16,768]{2,1,0:T(8,128)(2,1)S(1)}, bf16[4,16,768]{2,1,0:T(8,128)(2,1)S(1)}, u32[]{:S(2)}, u32[]{:S(2)}) collective-permute-start(bf16[4,16,768]{2,1,0:T(8,128)(2,1)S(1)} %get-tuple-element.123), channel_id=1, source_target_pairs={{0,7},{1,6},{2,5},{3,4},{4,3},{5,2},{6,1},{7,0},{8,15},{9,14},{10,... | collective-permute-start | bytes 294920 | tf_op jit(solution)/shard_map/ppermute | solution.py:483
  71.2 14.8 %collective-permute-start.17 = (bf16[8,16,768]{2,1,0:T(8,128)(2,1)S(1)}, bf16[8,16,768]{2,1,0:T(8,128)(2,1)S(1)}, u32[]{:S(2)}, u32[]{:S(2)}) collective-permute-start(bf16[8,16,768]{2,1,0:T(8,128)(2,1)S(1)} %get-tuple-element.131), channel_id=1, source_target_pairs={{0,3},{1,2},{2,1},{3,0},{4,7},{5,6},{6,5},{7,4},{8,11},{9,10},{10,... | collective-permute-start | bytes 589832 | tf_op jit(solution)/shard_map/ppermute | solution.py:483
  75.7 11.4 %collective-permute-start.8 = (bf16[4,16,768]{2,1,0:T(8,128)(2,1)S(1)}, bf16[4,16,768]{2,1,0:T(8,128)(2,1)S(1)}, u32[]{:S(2)}, u32[]{:S(2)}) collective-permute-start(bf16[4,16,768]{2,1,0:T(8,128)(2,1)S(1)} %get-tuple-element.115), channel_id=1, source_target_pairs={{0,4},{1,5},{2,6},{3,7},{4,0},{5,1},{6,2},{7,3},{8,12},{9,13},{10,... | collective-permute-start | bytes 294920 | tf_op jit(solution)/shard_map/ppermute | solution.py:483
  79.3 7.8 %collective-permute-start.10 = (bf16[4,16,768]{2,1,0:T(8,128)(2,1)S(1)}, bf16[4,16,768]{2,1,0:T(8,128)(2,1)S(1)}, u32[]{:S(2)}, u32[]{:S(2)}) collective-permute-start(bf16[4,16,768]{2,1,0:T(8,128)(2,1)S(1)} %get-tuple-element.118), channel_id=1, source_target_pairs={{0,5},{1,4},{2,7},{3,6},{4,1},{5,0},{6,3},{7,2},{8,13},{9,12},{10,... | collective-permute-start | bytes 294920 | tf_op jit(solution)/shard_map/ppermute | solution.py:483
  82.4 6.5 %collective-permute-start.12 = (bf16[4,16,768]{2,1,0:T(8,128)(2,1)S(1)}, bf16[4,16,768]{2,1,0:T(8,128)(2,1)S(1)}, u32[]{:S(2)}, u32[]{:S(2)}) collective-permute-start(bf16[4,16,768]{2,1,0:T(8,128)(2,1)S(1)} %get-tuple-element.121), channel_id=1, source_target_pairs={{0,6},{1,7},{2,4},{3,5},{4,2},{5,3},{6,0},{7,1},{8,14},{9,15},{10,... | collective-permute-start | bytes 294920 | tf_op jit(solution)/shard_map/ppermute | solution.py:483
  83.6 7.4 %collective-permute-start.14 = (bf16[4,16,768]{2,1,0:T(8,128)(2,1)S(1)}, bf16[4,16,768]{2,1,0:T(8,128)(2,1)S(1)}, u32[]{:S(2)}, u32[]{:S(2)}) collective-permute-start(bf16[4,16,768]{2,1,0:T(8,128)(2,1)S(1)} %get-tuple-element.124), channel_id=1, source_target_pairs={{0,7},{1,6},{2,5},{3,4},{4,3},{5,2},{6,1},{7,0},{8,15},{9,14},{10,... | collective-permute-start | bytes 294920 | tf_op jit(solution)/shard_map/ppermute | solution.py:483

commit v13 on v11

--- a/solution.py
+++ b/solution.py
@@ -488,7 +488,7 @@
 ):
     me = lax.axis_index("lon").astype(jnp.int32).reshape(1)
     weights = (w_query1, w_key1, w_value1, w_out1, w_query2, w_key2, w_value2)
-    weights = (ready(weights[:3]), *weights)
+    weights = (ready(weights[:5]), *weights)
 
     packed = dict(zip(ORDER, pack(ORDER, me, ocean.T, fields)))
     got = {d: exchanged(packed[d], d) if d else packed[d] for d in ORDER}

time: 86.1 us -> 86.2 us (level)
    unnamed x26 -> x28, local copies, waits for them, and re-layouts: 7.17 us -> 7.18 us
  transfers between devices with their start and end apart: 18 -> 18, of which waited for: 7 -> 8; matrix products, arithmetic and copies ran while one was open for 0% -> 0% of each run, Pallas kernels for 22% -> 22%
where the time goes in v13:
time: 86.2 us; the launch traced here: 85.8 us
  starting transfers between devices  30.3 us (35%)
  Pallas kernels  27 us (31%)
  waiting for transfers between devices  21 us (24%)
  local copies, waits for them, and re-layouts  7.18 us (8%)
    ppermute x18, starting transfers between devices, exchanged(): return lax.ppermute(piece, 'lon', [(s, s ^ distance) for s in range(count)])  30.3 us
    ppermute x18, waiting for transfers between devices, exchanged(): return lax.ppermute(piece, 'lon', [(s, s ^ distance) for s in range(count)])  21 us
    pallas_call x4, Pallas kernels, window_layer(): pl.pallas_call(functools.partial(window_kernel, stage), out_shape=outs, i...  17.5 us
    unnamed x28, local copies, waits for them, and re-layouts  7.18 us
    pallas_call x2, Pallas kernels, row_layer(): pl.pallas_call(functools.partial(row_kernel, start, rows), out_shape=(far...  6.11 us
    pallas_call x2, Pallas kernels, place(): pl.pallas_call(functools.partial(place_kernel, spots), out_shape=jax.Shap...  1.84 us
  transfers between devices with their start and end apart: 18, of which 8 were waited for; matrix products, arithmetic and copies ran while one was open for 0% of the time, Pallas kernels for 22%

profile of v13, /device:TPU:0, one launch (start us, length us, event | category | flops | bytes accessed | tf_op | source)
XLA Modules:
  0.0 85.8 jit_solution(13181277262080342913)
XLA Ops:
  0.0 0.0 copy-start
  0.0 0.8 copy-done.13
  0.8 1.6 %pack.1 = (bf16[784,128]{1,0:T(8,128)(2,1)S(1)}, bf16[784,128]{1,0:T(8,128)(2,1)S(1)}, bf16[784,128]{1,0:T(8,128)(2,1)S(1)}, bf16[784,128]{1,0:T(8,128)(2,1)S(1)...) custom-call(s32[1]{0:T(128)} %bitcast.me_ref, ...), custom_call_target="tpu_custom_call" | custom-call | flops 1600000 | bytes 3200000 | tf_op jit(solution)/shard_map/pack/pallas_call | solution.py:202
  2.4 4.1 %collective-permute-start = (bf16[784,128]{1,0:T(8,128)(2,1)S(1)}, bf16[784,128]{1,0:T(8,128)(2,1)S(1)}, u32[]{:S(2)}, u32[]{:S(2)}) collective-permute-start(bf16[784,128]{1,0:T(8,128)(2,1)S(1)} %get-tuple-element.71), channel_id=1, source_target_pairs={{0,4},{1,5},{2,6},{3,7},{4,0},{5,1},{6,2},{7,3},{8,12},{9,13},{10,... | collective-permute-start | bytes 602120 | tf_op jit(solution)/shard_map/ppermute | solution.py:483
  6.5 1.6 %collective-permute-start.1 = (bf16[784,128]{1,0:T(8,128)(2,1)S(1)}, bf16[784,128]{1,0:T(8,128)(2,1)S(1)}, u32[]{:S(2)}, u32[]{:S(2)}) collective-permute-start(bf16[784,128]{1,0:T(8,128)(2,1)S(1)} %get-tuple-element.72), channel_id=1, source_target_pairs={{0,2},{1,3},{2,0},{3,1},{4,6},{5,7},{6,4},{7,5},{8,10},{9,11},{10,... | collective-permute-start | bytes 602120 | tf_op jit(solution)/shard_map/ppermute | solution.py:483
  8.0 1.4 %collective-permute-start.2 = (bf16[784,128]{1,0:T(8,128)(2,1)S(1)}, bf16[784,128]{1,0:T(8,128)(2,1)S(1)}, u32[]{:S(2)}, u32[]{:S(2)}) collective-permute-start(bf16[784,128]{1,0:T(8,128)(2,1)S(1)} %get-tuple-element.73), channel_id=1, source_target_pairs={{0,3},{1,2},{2,1},{3,0},{4,7},{5,6},{6,5},{7,4},{8,11},{9,10},{10,... | collective-permute-start | bytes 602120 | tf_op jit(solution)/shard_map/ppermute | solution.py:483
  9.4 0.5 collective-permute-start.3
  10.0 1.3 %collective-permute-start.4 = (bf16[784,128]{1,0:T(8,128)(2,1)S(1)}, bf16[784,128]{1,0:T(8,128)(2,1)S(1)}, u32[]{:S(2)}, u32[]{:S(2)}) collective-permute-start(bf16[784,128]{1,0:T(8,128)(2,1)S(1)} %get-tuple-element.84), channel_id=1, source_target_pairs={{0,5},{1,4},{2,7},{3,6},{4,1},{5,0},{6,3},{7,2},{8,13},{9,12},{10,... | collective-permute-start | bytes 602120 | tf_op jit(solution)/shard_map/ppermute | solution.py:483
  11.2 0.0 copy-done
  11.3 1.3 %copy-done.1 = bf16[768,768]{1,0:T(8,128)(2,1)S(1)} copy-done((bf16[768,768]{1,0:T(8,128)(2,1)S(1)}, bf16[768,768]{1,0:T(8,128)(2,1)}, u32[]{:S(2)}) %copy-start.1) | copy-done | bytes 1179672
  12.5 1.3 %copy-done.3 = bf16[768,768]{1,0:T(8,128)(2,1)S(1)} copy-done((bf16[768,768]{1,0:T(8,128)(2,1)S(1)}, bf16[768,768]{1,0:T(8,128)(2,1)}, u32[]{:S(2)}) %copy-start.3) | copy-done | bytes 1179672
  13.8 1.3 %copy-done.5 = bf16[768,768]{1,0:T(8,128)(2,1)S(1)} copy-done((bf16[768,768]{1,0:T(8,128)(2,1)S(1)}, bf16[768,768]{1,0:T(8,128)(2,1)}, u32[]{:S(2)}) %copy-start.5) | copy-done | bytes 1179672
  15.1 1.3 %copy-done.7 = bf16[768,768]{1,0:T(8,128)(2,1)S(1)} copy-done((bf16[768,768]{1,0:T(8,128)(2,1)S(1)}, bf16[768,768]{1,0:T(8,128)(2,1)}, u32[]{:S(2)}) %copy-start.7) | copy-done | bytes 1179672
  16.3 0.0 copy-start.9
  16.4 0.3 collective-permute-done.refs_0_
  16.7 3.4 %collective-permute-start.5 = (bf16[784,128]{1,0:T(8,128)(2,1)S(1)}, bf16[784,128]{1,0:T(8,128)(2,1)S(1)}, u32[]{:S(2)}, u32[]{:S(2)}) collective-permute-start(bf16[784,128]{1,0:T(8,128)(2,1)S(1)} %get-tuple-element.93), channel_id=1, source_target_pairs={{0,6},{1,7},{2,4},{3,5},{4,2},{5,3},{6,0},{7,1},{8,14},{9,15},{10,... | collective-permute-start | bytes 602120 | tf_op jit(solution)/shard_map/ppermute | solution.py:483
  20.0 1.8 %collective-permute-done.1.refs_2_ = bf16[784,128]{1,0:T(8,128)(2,1)S(1)} collective-permute-done((bf16[784,128]{1,0:T(8,128)(2,1)S(1)}, bf16[784,128]{1,0:T(8,128)(2,1)S(1)}, u32[]{:S(2)}, u32[]{:S(2)}) %collective-permute-start.1) | collective-permute-done | bytes 200736 | tf_op jit(solution)/shard_map/ppermute | solution.py:483
  21.8 2.9 %collective-permute-start.6 = (bf16[784,128]{1,0:T(8,128)(2,1)S(1)}, bf16[784,128]{1,0:T(8,128)(2,1)S(1)}, u32[]{:S(2)}, u32[]{:S(2)}) collective-permute-start(bf16[784,128]{1,0:T(8,128)(2,1)S(1)} %get-tuple-element.102), channel_id=1, source_target_pairs={{0,7},{1,6},{2,5},{3,4},{4,3},{5,2},{6,1},{7,0},{8,15},{9,14},{10,... | collective-permute-start | bytes 602120 | tf_op jit(solution)/shard_map/ppermute | solution.py:483
  24.7 1.2 %collective-permute-done.2.refs_3_ = bf16[784,128]{1,0:T(8,128)(2,1)S(1)} collective-permute-done((bf16[784,128]{1,0:T(8,128)(2,1)S(1)}, bf16[784,128]{1,0:T(8,128)(2,1)S(1)}, u32[]{:S(2)}, u32[]{:S(2)}) %collective-permute-start.2) | collective-permute-done | bytes 200736 | tf_op jit(solution)/shard_map/ppermute | solution.py:483
  25.9 0.0 collective-permute-done.3.refs_1_
  25.9 0.0 copy-done.2
  25.9 0.0 copy-done.4
  25.9 0.0 copy-done.6
  25.9 0.0 copy-done.8
  25.9 0.0 copy-done.9
  25.9 0.0 copy-start.10
  25.9 1.3 %copy-done.10 = bf16[768,768]{1,0:T(8,128)(2,1)S(1)} copy-done((bf16[768,768]{1,0:T(8,128)(2,1)S(1)}, bf16[768,768]{1,0:T(8,128)(2,1)}, u32[]{:S(2)}) %copy-start.10) | copy-done | bytes 1179672
  27.2 6.9 %window_layer.4 = (bf16[8,48,768]{2,1,0:T(8,128)(2,1)S(1)}, bf16[8,48,768]{2,1,0:T(8,128)(2,1)S(1)}, bf16[8,48,768]{2,1,0:T(8,128)(2,1)S(1)}, bf16[8,48,768]{2,1...) custom-call(s32[1]{0:T(128)} %bitcast.me_ref, ...), custom_call_target="tpu_custom_call" | custom-call | flops 4051697664 | bytes 16777216 | tf_op jit(solution)/shard_map/window_layer/pallas_call | solution.py:349
  34.2 1.0 %collective-permute-done.4.refs_1_ = bf16[784,128]{1,0:T(8,128)(2,1)S(1)} collective-permute-done((bf16[784,128]{1,0:T(8,128)(2,1)S(1)}, bf16[784,128]{1,0:T(8,128)(2,1)S(1)}, u32[]{:S(2)}, u32[]{:S(2)}) %collective-permute-start.4) | collective-permute-done | bytes 200736 | tf_op jit(solution)/shard_map/ppermute | solution.py:483
  35.1 4.5 %window_layer.5 = (bf16[8,32,768]{2,1,0:T(8,128)(2,1)S(1)}, bf16[8,32,768]{2,1,0:T(8,128)(2,1)S(1)}, bf16[8,32,768]{2,1,0:T(8,128)(2,1)S(1)}, bf16[8,32,768]{2,1...) custom-call(s32[1]{0:T(128)} %bitcast.me_ref, ...), custom_call_target="tpu_custom_call" | custom-call | flops 2315255808 | bytes 16777216 | tf_op jit(solution)/shard_map/window_layer/pallas_call | solution.py:349
  39.6 0.0 collective-permute-done.5.refs_0_
  39.6 2.6 %window_layer.6 = (bf16[8,16,768]{2,1,0:T(8,128)(2,1)S(1)}, bf16[8,16,768]{2,1,0:T(8,128)(2,1)S(1)}, bf16[8,16,768]{2,1,0:T(8,128)(2,1)S(1)}, bf16[8,16,768]{2,1...) custom-call(s32[1]{0:T(128)} %bitcast.me_ref, ...), custom_call_target="tpu_custom_call" | custom-call | flops 1157627904 | bytes 16777216 | tf_op jit(solution)/shard_map/window_layer/pallas_call | solution.py:349
  42.2 0.0 collective-permute-done.6.refs_0_
  42.3 0.0 copy-start.12
  42.3 3.4 %window_layer.7 = (bf16[8,32,768]{2,1,0:T(8,128)(2,1)S(1)}, bf16[4,32,768]{2,1,0:T(8,128)(2,1)S(1)}, bf16[4,32,768]{2,1,0:T(8,128)(2,1)S(1)}, bf16[4,32,768]{2,1,0:T(8,128)(2,1)S(1)}, bf16[8,32,128]{2,1,0:T(8,128)(2,1)S(1)}) custom-call(s32[1]{0:T(128)} %bitcast.me_ref, bf16[784,128]{1,0:T(8,128)(2,1)S(1)} %collective-permute-done.6.refs_0_, ...), custom_call_target="tpu_custom_call" | custom-call | flops 1736441856 | bytes 16777216 | tf_op jit(solution)/shard_map/window_layer/pallas_call | solution.py:349
  45.7 0.0 copy-done.12
  45.7 0.0 copy-start.11
  45.7 2.7 %row_layer.2 = (bf16[4,16,768]{2,1,0:T(8,128)(2,1)S(1)}, bf16[4,16,768]{2,1,0:T(8,128)(2,1)S(1)}, bf16[4,16,768]{2,1,0:T(8,128)(2,1)S(1)}, bf16[4,16,768]{2,1,0:...) custom-call(s32[1]{0:T(128)} %bitcast.me_ref, ...), custom_call_target="tpu_custom_call" | custom-call | bytes 65536 | tf_op jit(solution)/shard_map/row_layer/pallas_call | solution.py:434
  48.5 3.0 %collective-permute-start.7 = (bf16[4,16,768]{2,1,0:T(8,128)(2,1)S(1)}, bf16[4,16,768]{2,1,0:T(8,128)(2,1)S(1)}, u32[]{:S(2)}, u32[]{:S(2)}) collective-permute-start(bf16[4,16,768]{2,1,0:T(8,128)(2,1)S(1)} %get-tuple-element.116), channel_id=1, source_target_pairs={{0,4},{1,5},{2,6},{3,7},{4,0},{5,1},{6,2},{7,3},{8,12},{9,13},{10,... | collective-permute-start | bytes 294920 | tf_op jit(solution)/shard_map/ppermute | solution.py:483
  51.5 0.0 collective-permute-start.9
  51.5 0.0 copy-done.11
  51.5 3.4 %row_layer.3 = (bf16[4,16,768]{2,1,0:T(8,128)(2,1)S(1)}, bf16[4,16,768]{2,1,0:T(8,128)(2,1)S(1)}, bf16[4,16,768]{2,1,0:T(8,128)(2,1)S(1)}, bf16[4,16,768]{2,1,0:...) custom-call(s32[1]{0:T(128)} %bitcast.me_ref, ...), custom_call_target="tpu_custom_call" | custom-call | bytes 65536 | tf_op jit(solution)/shard_map/row_layer/pallas_call | solution.py:434
  54.9 1.6 %collective-permute-start.15 = (bf16[8,16,768]{2,1,0:T(8,128)(2,1)S(1)}, bf16[8,16,768]{2,1,0:T(8,128)(2,1)S(1)}, u32[]{:S(2)}, u32[]{:S(2)}) collective-permute-start(bf16[8,16,768]{2,1,0:T(8,128)(2,1)S(1)} %get-tuple-element.131), channel_id=1, source_target_pairs={{0,1},{1,0},{2,3},{3,2},{4,5},{5,4},{6,7},{7,6},{8,9},{9,8},{10,11... | collective-permute-start | bytes 589832 | tf_op jit(solution)/shard_map/ppermute | solution.py:483
  56.5 0.8 collective-permute-start.16
  57.3 3.5 %collective-permute-start.11 = (bf16[4,16,768]{2,1,0:T(8,128)(2,1)S(1)}, bf16[4,16,768]{2,1,0:T(8,128)(2,1)S(1)}, u32[]{:S(2)}, u32[]{:S(2)}) collective-permute-start(bf16[4,16,768]{2,1,0:T(8,128)(2,1)S(1)} %get-tuple-element.122), channel_id=1, source_target_pairs={{0,6},{1,7},{2,4},{3,5},{4,2},{5,3},{6,0},{7,1},{8,14},{9,15},{10,... | collective-permute-start | bytes 294920 | tf_op jit(solution)/shard_map/ppermute | solution.py:483
  60.8 0.0 collective-permute-done.7.refs_0_
  60.8 0.4 collective-permute-start.13
  61.2 0.0 collective-permute-done.9.refs_1_
  61.2 0.2 collective-permute-start.17
  61.4 7.3 %collective-permute-done.11.refs_2_ = bf16[4,16,768]{2,1,0:T(8,128)(2,1)S(1)} collective-permute-done((bf16[4,16,768]{2,1,0:T(8,128)(2,1)S(1)}, bf16[4,16,768]{2,1,0:T(8,128)(2,1)S(1)}, u32[]{:S(2)}, u32[]{:S(2)}) %collective-permute-start.11) | collective-permute-done | bytes 98336 | tf_op jit(solution)/shard_map/ppermute | solution.py:483
  68.7 0.0 collective-permute-start.8
  68.7 2.0 %collective-permute-done.13.refs_3_ = bf16[4,16,768]{2,1,0:T(8,128)(2,1)S(1)} collective-permute-done((bf16[4,16,768]{2,1,0:T(8,128)(2,1)S(1)}, bf16[4,16,768]{2,1,0:T(8,128)(2,1)S(1)}, u32[]{:S(2)}, u32[]{:S(2)}) %collective-permute-start.13) | collective-permute-done | bytes 98336 | tf_op jit(solution)/shard_map/ppermute | solution.py:483
  70.8 0.8 collective-permute-start.10
  71.6 0.0 collective-permute-done.15.refs_4_
  71.6 0.0 collective-permute-start.12
  71.6 0.0 collective-permute-done.16.refs_5_
  71.6 4.8 %collective-permute-start.14 = (bf16[4,16,768]{2,1,0:T(8,128)(2,1)S(1)}, bf16[4,16,768]{2,1,0:T(8,128)(2,1)S(1)}, u32[]{:S(2)}, u32[]{:S(2)}) collective-permute-start(bf16[4,16,768]{2,1,0:T(8,128)(2,1)S(1)} %get-tuple-element.126), channel_id=1, source_target_pairs={{0,7},{1,6},{2,5},{3,4},{4,3},{5,2},{6,1},{7,0},{8,15},{9,14},{10,... | collective-permute-start | bytes 294920 | tf_op jit(solution)/shard_map/ppermute | solution.py:483
  76.4 0.0 collective-permute-done.17.refs_6_
  76.4 1.1 %place.2.refs_4_ = bf16[64,16,768]{2,1,0:T(8,128)(2,1)} custom-call(s32[1]{0:T(128)} %bitcast.me_ref, bf16[4,16,768]{2,1,0:T(8,128)(2,1)S(1)} %collective-permute-done.7.refs_0_, bf16[4,16,768]{2,1,0:T(8,128)(2,1)S(1)} %collective-permute-done.9.refs_1_, bf16[4,16,768]{2,1,0:T(8,128)(2,1)S(1)} %collective-permute-done.11.refs_2_, ...), custom_call_target="tpu_custom_call" | custom-call | bytes 4194304 | tf_op jit(solution)/shard_map/place/pallas_call | solution.py:468
  77.4 5.4 %collective-permute-done.8.refs_0_ = bf16[4,16,768]{2,1,0:T(8,128)(2,1)S(1)} collective-permute-done((bf16[4,16,768]{2,1,0:T(8,128)(2,1)S(1)}, bf16[4,16,768]{2,1,0:T(8,128)(2,1)S(1)}, u32[]{:S(2)}, u32[]{:S(2)}) %collective-permute-start.8) | collective-permute-done | bytes 98336 | tf_op jit(solution)/shard_map/ppermute | solution.py:483
  82.8 2.0 %collective-permute-done.10.refs_1_ = bf16[4,16,768]{2,1,0:T(8,128)(2,1)S(1)} collective-permute-done((bf16[4,16,768]{2,1,0:T(8,128)(2,1)S(1)}, bf16[4,16,768]{2,1,0:T(8,128)(2,1)S(1)}, u32[]{:S(2)}, u32[]{:S(2)}) %collective-permute-start.10) | collective-permute-done | bytes 98336 | tf_op jit(solution)/shard_map/ppermute | solution.py:483
  84.9 0.0 collective-permute-done.12.refs_2_
  84.9 0.0 collective-permute-done.14.refs_3_
  84.9 0.8 place.3
  (10 shorter events, 0.0 us)
Async XLA Ops:
  0.0 11.2 %copy-start = (bf16[768,768]{1,0:T(8,128)(2,1)S(1)}, bf16[768,768]{1,0:T(8,128)(2,1)}, u32[]{:S(2)}) copy-start(bf16[768,768]{1,0:T(8,128)(2,1)} %refs_25_.1) | copy-start | bytes 3538948
  0.0 0.8 copy-start.13
  2.4 14.3 %collective-permute-start = (bf16[784,128]{1,0:T(8,128)(2,1)S(1)}, bf16[784,128]{1,0:T(8,128)(2,1)S(1)}, u32[]{:S(2)}, u32[]{:S(2)}) collective-permute-start(bf16[784,128]{1,0:T(8,128)(2,1)S(1)} %get-tuple-element.71), channel_id=1, source_target_pairs={{0,4},{1,5},{2,6},{3,7},{4,0},{5,1},{6,2},{7,3},{8,12},{9,13},{10,... | collective-permute-start | bytes 602120 | tf_op jit(solution)/shard_map/ppermute | solution.py:483
  6.5 15.4 %collective-permute-start.1 = (bf16[784,128]{1,0:T(8,128)(2,1)S(1)}, bf16[784,128]{1,0:T(8,128)(2,1)S(1)}, u32[]{:S(2)}, u32[]{:S(2)}) collective-permute-start(bf16[784,128]{1,0:T(8,128)(2,1)S(1)} %get-tuple-element.72), channel_id=1, source_target_pairs={{0,2},{1,3},{2,0},{3,1},{4,6},{5,7},{6,4},{7,5},{8,10},{9,11},{10,... | collective-permute-start | bytes 602120 | tf_op jit(solution)/shard_map/ppermute | solution.py:483
  8.0 17.8 %collective-permute-start.2 = (bf16[784,128]{1,0:T(8,128)(2,1)S(1)}, bf16[784,128]{1,0:T(8,128)(2,1)S(1)}, u32[]{:S(2)}, u32[]{:S(2)}) collective-permute-start(bf16[784,128]{1,0:T(8,128)(2,1)S(1)} %get-tuple-element.73), channel_id=1, source_target_pairs={{0,3},{1,2},{2,1},{3,0},{4,7},{5,6},{6,5},{7,4},{8,11},{9,10},{10,... | collective-permute-start | bytes 602120 | tf_op jit(solution)/shard_map/ppermute | solution.py:483
  9.4 16.4 %collective-permute-start.3 = (bf16[784,128]{1,0:T(8,128)(2,1)S(1)}, bf16[784,128]{1,0:T(8,128)(2,1)S(1)}, u32[]{:S(2)}, u32[]{:S(2)}) collective-permute-start(bf16[784,128]{1,0:T(8,128)(2,1)S(1)} %get-tuple-element.74), channel_id=1, source_target_pairs={{0,1},{1,0},{2,3},{3,2},{4,5},{5,4},{6,7},{7,6},{8,9},{9,8},{10,11... | collective-permute-start | bytes 602120 | tf_op jit(solution)/shard_map/ppermute | solution.py:483
  10.0 25.2 %collective-permute-start.4 = (bf16[784,128]{1,0:T(8,128)(2,1)S(1)}, bf16[784,128]{1,0:T(8,128)(2,1)S(1)}, u32[]{:S(2)}, u32[]{:S(2)}) collective-permute-start(bf16[784,128]{1,0:T(8,128)(2,1)S(1)} %get-tuple-element.84), channel_id=1, source_target_pairs={{0,5},{1,4},{2,7},{3,6},{4,1},{5,0},{6,3},{7,2},{8,13},{9,12},{10,... | collective-permute-start | bytes 602120 | tf_op jit(solution)/shard_map/ppermute | solution.py:483
  11.3 1.3 %copy-start.1 = (bf16[768,768]{1,0:T(8,128)(2,1)S(1)}, bf16[768,768]{1,0:T(8,128)(2,1)}, u32[]{:S(2)}) copy-start(bf16[768,768]{1,0:T(8,128)(2,1)} %refs_9_.7) | copy-start | bytes 3538948
  12.5 1.3 %copy-start.3 = (bf16[768,768]{1,0:T(8,128)(2,1)S(1)}, bf16[768,768]{1,0:T(8,128)(2,1)}, u32[]{:S(2)}) copy-start(bf16[768,768]{1,0:T(8,128)(2,1)} %refs_10_.7) | copy-start | bytes 3538948
  13.8 1.3 %copy-start.5 = (bf16[768,768]{1,0:T(8,128)(2,1)S(1)}, bf16[768,768]{1,0:T(8,128)(2,1)}, u32[]{:S(2)}) copy-start(bf16[768,768]{1,0:T(8,128)(2,1)} %refs_11_.7) | copy-start | bytes 3538948
  15.1 1.3 %copy-start.7 = (bf16[768,768]{1,0:T(8,128)(2,1)S(1)}, bf16[768,768]{1,0:T(8,128)(2,1)}, u32[]{:S(2)}) copy-start(bf16[768,768]{1,0:T(8,128)(2,1)} %refs_12_.5) | copy-start | bytes 3538948
  16.3 9.6 %copy-start.2 = (bf16[768,768]{1,0:T(8,128)(2,1)S(1)}, bf16[768,768]{1,0:T(8,128)(2,1)}, u32[]{:S(2)}) copy-start(bf16[768,768]{1,0:T(8,128)(2,1)} %refs_9_.7) | copy-start | bytes 3538948
  16.3 9.6 %copy-start.4 = (bf16[768,768]{1,0:T(8,128)(2,1)S(1)}, bf16[768,768]{1,0:T(8,128)(2,1)}, u32[]{:S(2)}) copy-start(bf16[768,768]{1,0:T(8,128)(2,1)} %refs_10_.7) | copy-start | bytes 3538948
  16.3 9.6 %copy-start.6 = (bf16[768,768]{1,0:T(8,128)(2,1)S(1)}, bf16[768,768]{1,0:T(8,128)(2,1)}, u32[]{:S(2)}) copy-start(bf16[768,768]{1,0:T(8,128)(2,1)} %refs_11_.7) | copy-start | bytes 3538948
  16.3 9.6 %copy-start.8 = (bf16[768,768]{1,0:T(8,128)(2,1)S(1)}, bf16[768,768]{1,0:T(8,128)(2,1)}, u32[]{:S(2)}) copy-start(bf16[768,768]{1,0:T(8,128)(2,1)} %refs_12_.5) | copy-start | bytes 3538948
  16.3 9.6 %copy-start.9 = (bf16[768,768]{1,0:T(8,128)(2,1)S(1)}, bf16[768,768]{1,0:T(8,128)(2,1)}, u32[]{:S(2)}) copy-start(bf16[768,768]{1,0:T(8,128)(2,1)} %refs_26_.1) | copy-start | bytes 3538948
  16.7 22.9 %collective-permute-start.5 = (bf16[784,128]{1,0:T(8,128)(2,1)S(1)}, bf16[784,128]{1,0:T(8,128)(2,1)S(1)}, u32[]{:S(2)}, u32[]{:S(2)}) collective-permute-start(bf16[784,128]{1,0:T(8,128)(2,1)S(1)} %get-tuple-element.93), channel_id=1, source_target_pairs={{0,6},{1,7},{2,4},{3,5},{4,2},{5,3},{6,0},{7,1},{8,14},{9,15},{10,... | collective-permute-start | bytes 602120 | tf_op jit(solution)/shard_map/ppermute | solution.py:483
  21.8 20.4 %collective-permute-start.6 = (bf16[784,128]{1,0:T(8,128)(2,1)S(1)}, bf16[784,128]{1,0:T(8,128)(2,1)S(1)}, u32[]{:S(2)}, u32[]{:S(2)}) collective-permute-start(bf16[784,128]{1,0:T(8,128)(2,1)S(1)} %get-tuple-element.102), channel_id=1, source_target_pairs={{0,7},{1,6},{2,5},{3,4},{4,3},{5,2},{6,1},{7,0},{8,15},{9,14},{10,... | collective-permute-start | bytes 602120 | tf_op jit(solution)/shard_map/ppermute | solution.py:483
  25.9 1.3 %copy-start.10 = (bf16[768,768]{1,0:T(8,128)(2,1)S(1)}, bf16[768,768]{1,0:T(8,128)(2,1)}, u32[]{:S(2)}) copy-start(bf16[768,768]{1,0:T(8,128)(2,1)} %refs_27_.1) | copy-start | bytes 3538948
  42.3 3.5 %copy-start.12 = (bf16[768,768]{1,0:T(8,128)(2,1)S(1)}, bf16[768,768]{1,0:T(8,128)(2,1)}, u32[]{:S(2)}) copy-start(bf16[768,768]{1,0:T(8,128)(2,1)} %refs_20_.3) | copy-start | bytes 3538948
  45.7 5.8 %copy-start.11 = (bf16[768,768]{1,0:T(8,128)(2,1)S(1)}, bf16[768,768]{1,0:T(8,128)(2,1)}, u32[]{:S(2)}) copy-start(bf16[768,768]{1,0:T(8,128)(2,1)} %refs_27_.1) | copy-start | bytes 3538948
  48.5 12.3 %collective-permute-start.7 = (bf16[4,16,768]{2,1,0:T(8,128)(2,1)S(1)}, bf16[4,16,768]{2,1,0:T(8,128)(2,1)S(1)}, u32[]{:S(2)}, u32[]{:S(2)}) collective-permute-start(bf16[4,16,768]{2,1,0:T(8,128)(2,1)S(1)} %get-tuple-element.116), channel_id=1, source_target_pairs={{0,4},{1,5},{2,6},{3,7},{4,0},{5,1},{6,2},{7,3},{8,12},{9,13},{10,... | collective-permute-start | bytes 294920 | tf_op jit(solution)/shard_map/ppermute | solution.py:483
  51.5 9.7 %collective-permute-start.9 = (bf16[4,16,768]{2,1,0:T(8,128)(2,1)S(1)}, bf16[4,16,768]{2,1,0:T(8,128)(2,1)S(1)}, u32[]{:S(2)}, u32[]{:S(2)}) collective-permute-start(bf16[4,16,768]{2,1,0:T(8,128)(2,1)S(1)} %get-tuple-element.119), channel_id=1, source_target_pairs={{0,5},{1,4},{2,7},{3,6},{4,1},{5,0},{6,3},{7,2},{8,13},{9,12},{10,... | collective-permute-start | bytes 294920 | tf_op jit(solution)/shard_map/ppermute | solution.py:483
  54.9 16.7 %collective-permute-start.15 = (bf16[8,16,768]{2,1,0:T(8,128)(2,1)S(1)}, bf16[8,16,768]{2,1,0:T(8,128)(2,1)S(1)}, u32[]{:S(2)}, u32[]{:S(2)}) collective-permute-start(bf16[8,16,768]{2,1,0:T(8,128)(2,1)S(1)} %get-tuple-element.131), channel_id=1, source_target_pairs={{0,1},{1,0},{2,3},{3,2},{4,5},{5,4},{6,7},{7,6},{8,9},{9,8},{10,11... | collective-permute-start | bytes 589832 | tf_op jit(solution)/shard_map/ppermute | solution.py:483
  56.5 15.1 %collective-permute-start.16 = (bf16[8,16,768]{2,1,0:T(8,128)(2,1)S(1)}, bf16[8,16,768]{2,1,0:T(8,128)(2,1)S(1)}, u32[]{:S(2)}, u32[]{:S(2)}) collective-permute-start(bf16[8,16,768]{2,1,0:T(8,128)(2,1)S(1)} %get-tuple-element.132), channel_id=1, source_target_pairs={{0,2},{1,3},{2,0},{3,1},{4,6},{5,7},{6,4},{7,5},{8,10},{9,11},{10,... | collective-permute-start | bytes 589832 | tf_op jit(solution)/shard_map/ppermute | solution.py:483
  57.3 11.4 %collective-permute-start.11 = (bf16[4,16,768]{2,1,0:T(8,128)(2,1)S(1)}, bf16[4,16,768]{2,1,0:T(8,128)(2,1)S(1)}, u32[]{:S(2)}, u32[]{:S(2)}) collective-permute-start(bf16[4,16,768]{2,1,0:T(8,128)(2,1)S(1)} %get-tuple-element.122), channel_id=1, source_target_pairs={{0,6},{1,7},{2,4},{3,5},{4,2},{5,3},{6,0},{7,1},{8,14},{9,15},{10,... | collective-permute-start | bytes 294920 | tf_op jit(solution)/shard_map/ppermute | solution.py:483
  60.8 10.0 %collective-permute-start.13 = (bf16[4,16,768]{2,1,0:T(8,128)(2,1)S(1)}, bf16[4,16,768]{2,1,0:T(8,128)(2,1)S(1)}, u32[]{:S(2)}, u32[]{:S(2)}) collective-permute-start(bf16[4,16,768]{2,1,0:T(8,128)(2,1)S(1)} %get-tuple-element.125), channel_id=1, source_target_pairs={{0,7},{1,6},{2,5},{3,4},{4,3},{5,2},{6,1},{7,0},{8,15},{9,14},{10,... | collective-permute-start | bytes 294920 | tf_op jit(solution)/shard_map/ppermute | solution.py:483
  61.2 15.1 %collective-permute-start.17 = (bf16[8,16,768]{2,1,0:T(8,128)(2,1)S(1)}, bf16[8,16,768]{2,1,0:T(8,128)(2,1)S(1)}, u32[]{:S(2)}, u32[]{:S(2)}) collective-permute-start(bf16[8,16,768]{2,1,0:T(8,128)(2,1)S(1)} %get-tuple-element.133), channel_id=1, source_target_pairs={{0,3},{1,2},{2,1},{3,0},{4,7},{5,6},{6,5},{7,4},{8,11},{9,10},{10,... | collective-permute-start | bytes 589832 | tf_op jit(solution)/shard_map/ppermute | solution.py:483
  68.7 14.1 %collective-permute-start.8 = (bf16[4,16,768]{2,1,0:T(8,128)(2,1)S(1)}, bf16[4,16,768]{2,1,0:T(8,128)(2,1)S(1)}, u32[]{:S(2)}, u32[]{:S(2)}) collective-permute-start(bf16[4,16,768]{2,1,0:T(8,128)(2,1)S(1)} %get-tuple-element.117), channel_id=1, source_target_pairs={{0,4},{1,5},{2,6},{3,7},{4,0},{5,1},{6,2},{7,3},{8,12},{9,13},{10,... | collective-permute-start | bytes 294920 | tf_op jit(solution)/shard_map/ppermute | solution.py:483
  70.8 14.1 %collective-permute-start.10 = (bf16[4,16,768]{2,1,0:T(8,128)(2,1)S(1)}, bf16[4,16,768]{2,1,0:T(8,128)(2,1)S(1)}, u32[]{:S(2)}, u32[]{:S(2)}) collective-permute-start(bf16[4,16,768]{2,1,0:T(8,128)(2,1)S(1)} %get-tuple-element.120), channel_id=1, source_target_pairs={{0,5},{1,4},{2,7},{3,6},{4,1},{5,0},{6,3},{7,2},{8,13},{9,12},{10,... | collective-permute-start | bytes 294920 | tf_op jit(solution)/shard_map/ppermute | solution.py:483
  71.6 13.3 %collective-permute-start.12 = (bf16[4,16,768]{2,1,0:T(8,128)(2,1)S(1)}, bf16[4,16,768]{2,1,0:T(8,128)(2,1)S(1)}, u32[]{:S(2)}, u32[]{:S(2)}) collective-permute-start(bf16[4,16,768]{2,1,0:T(8,128)(2,1)S(1)} %get-tuple-element.123), channel_id=1, source_target_pairs={{0,6},{1,7},{2,4},{3,5},{4,2},{5,3},{6,0},{7,1},{8,14},{9,15},{10,... | collective-permute-start | bytes 294920 | tf_op jit(solution)/shard_map/ppermute | solution.py:483
  71.6 13.3 %collective-permute-start.14 = (bf16[4,16,768]{2,1,0:T(8,128)(2,1)S(1)}, bf16[4,16,768]{2,1,0:T(8,128)(2,1)S(1)}, u32[]{:S(2)}, u32[]{:S(2)}) collective-permute-start(bf16[4,16,768]{2,1,0:T(8,128)(2,1)S(1)} %get-tuple-element.126), channel_id=1, source_target_pairs={{0,7},{1,6},{2,5},{3,4},{4,3},{5,2},{6,1},{7,0},{8,15},{9,14},{10,... | collective-permute-start | bytes 294920 | tf_op jit(solution)/shard_map/ppermute | solution.py:483
